TPU v7x, 32 devices: a whole 2x2x4 slice. The times are simulated.
32 devices in a mesh: dp: 8 (over z, y), tensor: 4 (over x, core).
Axes of the slice: x: 2, y: 2, z: 4, core: 2. Of those that a mesh axis runs over, the one named last changes fastest.
Arguments:
- tokens: bfloat16 [20480, 768], P(('dp', 'tensor')), may hold values from -6 to 6
- w_query: bfloat16 [768, 768], P(None, 'tensor'), may hold values from -0.3125 to 0.3125
- w_key: bfloat16 [768, 768], P(None, 'tensor'), may hold values from -0.3125 to 0.3125
- w_value: bfloat16 [768, 768], P(None, 'tensor'), may hold values from -0.21875 to 0.21875
- conv_weight: float32 [12, 33], P('tensor'), may hold values from -1.25 to 1.25
- w_out: bfloat16 [768, 768], replicated, may hold values from -0.4375 to 0.4375
- gain_one: float32 [768], replicated, may hold values from 0.5 to 1.5
- shift_one: float32 [768], replicated, may hold values from -3 to 3
- w_up: bfloat16 [768, 3072], P(None, 'tensor'), may hold values from -0.21875 to 0.21875
- w_down: bfloat16 [3072, 768], P('tensor'), may hold values from -0.15625 to 0.15625
- gain_two: float32 [768], replicated, may hold values from 0.5 to 1.5
- shift_two: float32 [768], replicated, may hold values from -3 to 3
- lengths: int32 [8, 3], P('dp'), may hold values from 64 to 2432, as said below
- grad_output: bfloat16 [20480, 768], P(('dp', 'tensor')), may hold values from -6 to 6
Outputs:
- output: float32 [20480, 768], P(('dp', 'tensor'))
- grad_tokens: float32 [20480, 768], P(('dp', 'tensor'))
- grad_w_query: float32 [768, 768], P(None, 'tensor')
- grad_w_key: float32 [768, 768], P(None, 'tensor')
- grad_w_value: float32 [768, 768], P(None, 'tensor')
- grad_conv: float32 [12, 33], P('tensor')
- grad_w_out: float32 [768, 768], replicated
- grad_gain_one: float32 [768], replicated
- grad_shift_one: float32 [768], replicated
- grad_w_up: float32 [768, 3072], P(None, 'tensor')
- grad_w_down: float32 [3072, 768], P('tensor')
- grad_gain_two: float32 [768], replicated
- grad_shift_two: float32 [768], replicated
Inputs may be any that keep to these rules, and one draw needn't show every extreme that they name: Row g lists the lengths of the 3 sequences of group g, laid end to end over its 2560 tokens; they sum to 2560.
All inputs are finite; a program needn't handle non-finite values.
Results may differ from a plain program's by a relative error of at most 0.02.
The roundings to bfloat16 on the way count: a program that leaves them out, or rounds other values in their place, can miss the bound.
Values may be sent and summed in bfloat16 or wider, within the bound.
No kernel may reach another device: no remote copies, remote signals or barrier semaphores. Data moves between devices by JAX's collectives and lax.ppermute only.
A program may use at most 256 MiB of HBM per device.

v0:
```python
import jax
import jax.numpy as jnp
from jax import lax
from jax.sharding import PartitionSpec as P

HEAD = 64
LANDMARKS = 64
NS_ITERS = 6
KERNEL = 33
SEQS = 3
MARKS = 192


TOP_PRECISION = lax.Precision.HIGHEST


def group_layout(length_row, group_size):
    seq_ends = jnp.cumsum(length_row)
    seq_starts = seq_ends - length_row
    places = jnp.arange(group_size, dtype=jnp.int32)
    sequence = jnp.sum((places[:, None] >= seq_ends[None, :]).astype(jnp.int32), axis=1)
    member = (sequence[:, None] == jnp.arange(SEQS, dtype=jnp.int32)[None, :]).astype(jnp.int32)
    own_start = jnp.sum(member * seq_starts[None, :], axis=1)
    own_length = jnp.sum(member * length_row[None, :], axis=1)
    within = places - own_start
    segment = ((within + 1) * LANDMARKS + own_length - 1) // own_length - 1
    return (sequence, sequence * LANDMARKS + segment)


def softmax_keep(scores, allowed):
    masked = jnp.where(allowed, scores, -1e30)
    row_top = jnp.max(masked, axis=-1, keepdims=True)
    raised = jnp.where(allowed, jnp.exp(masked - row_top), 0.0)
    row_total = jnp.sum(raised, axis=-1, keepdims=True)
    return (raised / row_total, row_top + jnp.log(row_total))


def softmax_again(scores, allowed, log_total):
    return jnp.where(allowed, jnp.exp(jnp.where(allowed, scores, -1e30) - log_total), 0.0)


def softmax_back(probs, grad_probs):
    return probs * (grad_probs - jnp.sum(grad_probs * probs, axis=-1, keepdims=True))


def iterative_pseudoinverse(kernel):
    identity = jnp.eye(kernel.shape[-1], dtype=kernel.dtype)
    column_top = jnp.max(jnp.sum(kernel, axis=1), axis=-1)[:, None, None]
    approx = jnp.swapaxes(kernel, 1, 2) / column_top
    for sweep_step in range(NS_ITERS):
        product = jnp.einsum("hij,hjk->hik", kernel, approx, precision=TOP_PRECISION)
        bracket = 7.0 * identity - product
        bracket = 15.0 * identity - jnp.einsum(
            "hij,hjk->hik", product, bracket, precision=TOP_PRECISION
        )
        bracket = 13.0 * identity - jnp.einsum(
            "hij,hjk->hik", product, bracket, precision=TOP_PRECISION
        )
        approx = 0.25 * jnp.einsum("hij,hjk->hik", approx, bracket, precision=TOP_PRECISION)
    return approx


def convolve(values, conv_weight, sequence):
    reach = KERNEL // 2
    size_rows = values.shape[0]
    padded = jnp.pad(values, ((reach, reach), (0, 0), (0, 0)))
    seq_padded = jnp.pad(sequence, (reach, reach), constant_values=-1)
    summed = jnp.zeros_like(values)
    for offset in range(KERNEL):
        same_seq = (seq_padded[offset : offset + size_rows] == sequence)[:, None, None]
        shifted = jnp.where(same_seq, padded[offset : offset + size_rows], 0.0)
        summed = summed + shifted * conv_weight[:, offset][None, :, None]
    return summed


def unit_norm(values):
    row_mean = jnp.mean(values, axis=-1, keepdims=True)
    centered = values - row_mean
    spread = jnp.mean(centered * centered, axis=-1, keepdims=True)
    recip = lax.rsqrt(spread + 1e-05)
    return (centered * recip, recip)


def unit_back(cotangent_normalized_entry, unit_values, recip):
    mean_grad = jnp.mean(cotangent_normalized_entry, axis=-1, keepdims=True)
    mean_cross = jnp.mean(cotangent_normalized_entry * unit_values, axis=-1, keepdims=True)
    return recip * (cotangent_normalized_entry - mean_grad - unit_values * mean_cross)


def gelu_exact(values):
    return jax.nn.gelu(values, approximate=False)


def shards(
    tokens,
    w_query,
    w_key,
    w_value,
    conv_weight,
    w_out,
    gain_one,
    shift_one,
    w_up,
    w_down,
    gain_two,
    shift_two,
    lengths,
    grad_output,
):
    qk_scale = HEAD ** (-0.25)
    group_tokens = lax.all_gather(tokens, "tensor", axis=0, tiled=True)
    group_size = group_tokens.shape[0]
    heads_here = w_query.shape[1] // HEAD
    query_low = (
        jnp.dot(group_tokens, w_query, preferred_element_type=jnp.float32) * qk_scale
    ).astype(jnp.bfloat16)
    key_low = (jnp.dot(group_tokens, w_key, preferred_element_type=jnp.float32) * qk_scale).astype(
        jnp.bfloat16
    )
    value_low = jnp.dot(group_tokens, w_value, preferred_element_type=jnp.float32).astype(
        jnp.bfloat16
    )
    query_head_rows = query_low.reshape(group_size, heads_here, HEAD)
    key_head_rows = key_low.reshape(group_size, heads_here, HEAD)
    value_head_rows = value_low.reshape(group_size, heads_here, HEAD)
    sequence, landmark = group_layout(lengths[0], group_size)
    marks = jnp.arange(MARKS, dtype=jnp.int32)
    mark_seq = marks // LANDMARKS
    pool_mask = landmark[None, :] == marks[:, None]
    landmark_pooling = pool_mask.astype(jnp.bfloat16)
    pooling_window = pool_mask.astype(jnp.float32)
    token_counts = jnp.sum(pooling_window, axis=1)[:, None, None]
    query_landmarks = (
        jnp.einsum(
            "br,rwi->bwi", landmark_pooling, query_head_rows, preferred_element_type=jnp.float32
        )
        / token_counts
    ).astype(jnp.bfloat16)
    key_landmarks = (
        jnp.einsum(
            "br,rwi->bwi", landmark_pooling, key_head_rows, preferred_element_type=jnp.float32
        )
        / token_counts
    ).astype(jnp.bfloat16)
    local_neighbour_response = (sequence[:, None] == mark_seq[None, :])[None]
    near_back = jnp.swapaxes(local_neighbour_response, 1, 2)
    block_layer = (mark_seq[:, None] == mark_seq[None, :])[None]
    target_score_rows = jnp.einsum(
        "tfu,kfu->ftk", query_head_rows, key_landmarks, preferred_element_type=jnp.float32
    )
    to_probs, to_log = softmax_keep(target_score_rows, local_neighbour_response)
    target_landmark_scores = to_probs.astype(jnp.bfloat16)
    landmark_mixing = softmax_keep(
        jnp.einsum(
            "jos,eos->oje", query_landmarks, key_landmarks, preferred_element_type=jnp.float32
        ),
        block_layer,
    )[0]
    source_score_rows = jnp.einsum(
        "oeu,peu->eop", query_landmarks, key_head_rows, preferred_element_type=jnp.float32
    )
    from_probs, from_log = softmax_keep(source_score_rows, near_back)
    source_landmark_scores = from_probs.astype(jnp.bfloat16)
    landmark_digest = jnp.einsum(
        "uca,aue->uce", source_landmark_scores, value_head_rows, preferred_element_type=jnp.float32
    )
    pseudoinverse_matrix, inverse_pull = jax.vjp(iterative_pseudoinverse, landmark_mixing)
    anchor_values_pooled = jnp.einsum(
        "kej,kjq->keq", pseudoinverse_matrix, landmark_digest, precision=TOP_PRECISION
    ).astype(jnp.bfloat16)
    blended_output = jnp.einsum(
        "lvk,lko->vlo",
        target_landmark_scores,
        anchor_values_pooled,
        preferred_element_type=jnp.float32,
    )
    value_wide = value_head_rows.astype(jnp.float32)
    smooth, conv_pull = jax.vjp(
        lambda conv_values, conv_taps: convolve(conv_values, conv_taps, sequence),
        value_wide,
        conv_weight,
    )
    context = (blended_output + smooth).astype(jnp.bfloat16).reshape(group_size, heads_here * HEAD)
    context_rows = lax.all_to_all(context, "tensor", split_axis=0, concat_axis=1, tiled=True)
    resid = tokens.astype(jnp.float32) + jnp.dot(
        context_rows, w_out, preferred_element_type=jnp.float32
    )
    unit_one, recip_one = unit_norm(resid)
    normed = unit_one * gain_one + shift_one
    normed_low = normed.astype(jnp.bfloat16)
    normed_group = lax.all_gather(normed_low, "tensor", axis=0, tiled=True)
    preactivation_feedforward = jnp.dot(normed_group, w_up, preferred_element_type=jnp.float32)
    hidden = gelu_exact(preactivation_feedforward).astype(jnp.bfloat16)
    branch = lax.psum_scatter(
        jnp.dot(hidden, w_down, preferred_element_type=jnp.float32).astype(jnp.bfloat16),
        "tensor",
        scatter_dimension=0,
        tiled=True,
    ).astype(jnp.float32)
    unit_two, recip_two = unit_norm(normed + branch)
    output = unit_two * gain_two + shift_two
    grad_top = grad_output.astype(jnp.float32)
    grad_gain_two = jnp.sum(grad_top * unit_two, axis=0)
    grad_shift_two = jnp.sum(grad_top, axis=0)
    grad_summed = unit_back(grad_top * gain_two, unit_two, recip_two)
    grad_branch = grad_summed.astype(jnp.bfloat16)
    gelu_pull = jax.vjp(gelu_exact, preactivation_feedforward)[1]
    branch_group = lax.all_gather(grad_branch, "tensor", axis=0, tiled=True)
    grad_down = jnp.einsum("gf,gd->fd", hidden, branch_group, preferred_element_type=jnp.float32)
    grad_hidden = jnp.einsum("gd,fd->gf", branch_group, w_down, preferred_element_type=jnp.float32)
    grad_pre = gelu_pull(grad_hidden)[0].astype(jnp.bfloat16)
    grad_up = jnp.einsum("gd,gf->df", normed_group, grad_pre, preferred_element_type=jnp.float32)
    grad_normed_branch = lax.psum_scatter(
        jnp.einsum("gf,df->gd", grad_pre, w_up, preferred_element_type=jnp.float32).astype(
            jnp.bfloat16
        ),
        "tensor",
        scatter_dimension=0,
        tiled=True,
    ).astype(jnp.float32)
    grad_normed = grad_summed + grad_normed_branch
    grad_gain_one = jnp.sum(grad_normed * unit_one, axis=0)
    grad_shift_one = jnp.sum(grad_normed, axis=0)
    grad_resid = unit_back(grad_normed * gain_one, unit_one, recip_one)
    grad_attended = grad_resid.astype(jnp.bfloat16)
    grad_w_out = jnp.einsum(
        "te,td->ed", context_rows, grad_attended, preferred_element_type=jnp.float32
    )
    grad_rows_ctx = jnp.einsum(
        "td,ed->te", grad_attended, w_out, preferred_element_type=jnp.float32
    ).astype(jnp.bfloat16)
    grad_context = lax.all_to_all(grad_rows_ctx, "tensor", split_axis=1, concat_axis=0, tiled=True)
    derivative_per_attention_slice = grad_context.reshape(group_size, heads_here, HEAD)
    to_again = softmax_again(
        jnp.einsum(
            "tfu,kfu->ftk", query_head_rows, key_landmarks, preferred_element_type=jnp.float32
        ),
        local_neighbour_response,
        to_log,
    )
    from_again = softmax_again(
        jnp.einsum(
            "oeu,peu->eop", query_landmarks, key_head_rows, preferred_element_type=jnp.float32
        ),
        near_back,
        from_log,
    )
    grad_to = jnp.einsum(
        "mnk,nhk->nmh",
        derivative_per_attention_slice,
        anchor_values_pooled,
        preferred_element_type=jnp.float32,
    )
    gradient_landmark = jnp.einsum(
        "uox,ouc->uxc",
        to_again.astype(jnp.bfloat16),
        derivative_per_attention_slice,
        preferred_element_type=jnp.float32,
    )
    gradient_pseudoinverse = jnp.einsum(
        "ybx,ytx->ybt", gradient_landmark, landmark_digest, precision=TOP_PRECISION
    )
    gradient_digest = jnp.einsum(
        "fbc,fbp->fcp", pseudoinverse_matrix, gradient_landmark, precision=TOP_PRECISION
    ).astype(jnp.bfloat16)
    grad_among = inverse_pull(gradient_pseudoinverse)[0]
    gradient_mixing_scores = softmax_back(landmark_mixing, grad_among)
    grad_q_land = jnp.einsum(
        "afi,iay->fay",
        gradient_mixing_scores,
        key_landmarks.astype(jnp.float32),
        precision=TOP_PRECISION,
    )
    grad_k_land = jnp.einsum(
        "xcr,cxj->rxj",
        gradient_mixing_scores,
        query_landmarks.astype(jnp.float32),
        precision=TOP_PRECISION,
    )
    grad_from = jnp.einsum(
        "sjb,zsb->sjz", gradient_digest, value_head_rows, preferred_element_type=jnp.float32
    )
    grad_value = jnp.einsum(
        "bet,bek->tbk",
        from_again.astype(jnp.bfloat16),
        gradient_digest,
        preferred_element_type=jnp.float32,
    )
    gradient_source_scores = softmax_back(from_again, grad_from).astype(jnp.bfloat16)
    grad_q_land = grad_q_land + jnp.einsum(
        "xft,txz->fxz", gradient_source_scores, key_head_rows, preferred_element_type=jnp.float32
    )
    gradient_key_rows = jnp.einsum(
        "jyc,yjs->cjs", gradient_source_scores, query_landmarks, preferred_element_type=jnp.float32
    )
    gradient_target_scores = softmax_back(to_again, grad_to).astype(jnp.bfloat16)
    gradient_query_rows = jnp.einsum(
        "upk,kuj->puj", gradient_target_scores, key_landmarks, preferred_element_type=jnp.float32
    )
    grad_k_land = grad_k_land + jnp.einsum(
        "euo,ueb->oeb", gradient_target_scores, query_head_rows, preferred_element_type=jnp.float32
    )
    grad_value_conv, grad_conv = conv_pull(derivative_per_attention_slice.astype(jnp.float32))
    broadcast_query = (
        lax.optimization_barrier(grad_q_land.astype(jnp.bfloat16)).astype(jnp.float32)
        / token_counts
    )
    broadcast_key = (
        lax.optimization_barrier(grad_k_land.astype(jnp.bfloat16)).astype(jnp.float32)
        / token_counts
    )
    gradient_query_rows = gradient_query_rows + jnp.einsum(
        "uc,ufo->cfo", pooling_window, broadcast_query, precision=TOP_PRECISION
    )
    gradient_key_rows = gradient_key_rows + jnp.einsum(
        "uc,ufo->cfo", pooling_window, broadcast_key, precision=TOP_PRECISION
    )
    grad_value = grad_value + grad_value_conv
    grad_q_low = gradient_query_rows.astype(jnp.bfloat16).reshape(group_size, heads_here * HEAD)
    grad_k_low = gradient_key_rows.astype(jnp.bfloat16).reshape(group_size, heads_here * HEAD)
    grad_v_low = grad_value.astype(jnp.bfloat16).reshape(group_size, heads_here * HEAD)
    grad_w_query = (
        jnp.einsum("gd,ge->de", group_tokens, grad_q_low, preferred_element_type=jnp.float32)
        * qk_scale
    )
    grad_w_key = (
        jnp.einsum("gd,ge->de", group_tokens, grad_k_low, preferred_element_type=jnp.float32)
        * qk_scale
    )
    grad_w_value = jnp.einsum(
        "gd,ge->de", group_tokens, grad_v_low, preferred_element_type=jnp.float32
    )
    scaled = jnp.einsum("ge,de->gd", grad_q_low, w_query, preferred_element_type=jnp.float32)
    scaled = scaled + jnp.einsum("ge,de->gd", grad_k_low, w_key, preferred_element_type=jnp.float32)
    grad_tokens = grad_resid + lax.psum_scatter(
        (
            scaled * qk_scale
            + jnp.einsum("ge,de->gd", grad_v_low, w_value, preferred_element_type=jnp.float32)
        ).astype(jnp.bfloat16),
        "tensor",
        scatter_dimension=0,
        tiled=True,
    ).astype(jnp.float32)
    grad_w_query, grad_w_key, grad_w_value, grad_conv, grad_up, grad_down = lax.psum(
        (grad_w_query, grad_w_key, grad_w_value, grad_conv, grad_up, grad_down), "dp"
    )
    grad_w_out, grad_gain_one, grad_shift_one, grad_gain_two, grad_shift_two = lax.psum(
        (grad_w_out, grad_gain_one, grad_shift_one, grad_gain_two, grad_shift_two), ("dp", "tensor")
    )
    return (
        output,
        grad_tokens,
        grad_w_query,
        grad_w_key,
        grad_w_value,
        grad_conv,
        grad_w_out,
        grad_gain_one,
        grad_shift_one,
        grad_up,
        grad_down,
        grad_gain_two,
        grad_shift_two,
    )


def solution(mesh):
    in_specs = (
        P(("dp", "tensor"), None),
        P(None, "tensor"),
        P(None, "tensor"),
        P(None, "tensor"),
        P("tensor", None),
        P(),
        P(),
        P(),
        P(None, "tensor"),
        P("tensor", None),
        P(),
        P(),
        P("dp", None),
        P(("dp", "tensor"), None),
    )
    out_specs = (
        P(("dp", "tensor"), None),
        P(("dp", "tensor"), None),
        P(None, "tensor"),
        P(None, "tensor"),
        P(None, "tensor"),
        P("tensor", None),
        P(),
        P(),
        P(),
        P(None, "tensor"),
        P("tensor", None),
        P(),
        P(),
    )
    return jax.shard_map(shards, mesh=mesh, in_specs=in_specs, out_specs=out_specs, check_vma=False)
```

profile of v0, /device:TPU:0, one launch (start us, length us, event | category | flops | bytes accessed | tf_op | source)
XLA Modules:
  0.0 962.5 jit_solution(17809063656849623296)
XLA Ops:
  9.7 2.2 slice_reduce_fusion.31
  11.9 2.5 slice_reduce_fusion.32
  21.5 23.8 %all-gather.4.cloned.1.call-done = bf16[2560,768]{1,0:T(8,128)(2,1)} async-done(((bf16[640,768]{1,0:T(8,128)(2,1)}), bf16[2560,768]{1,0:T(8,128)(2,1)}) %all-gather.4.cloned.1.call-update) | async-done | bytes 3932176 | tf_op jit(solution)/shard_map/all_gather | solution.py:111
  45.4 3.7 fusion.19
  50.2 1.4 fusion.18
  55.0 2.2 fusion.176
  85.7 1.5 fusion.6
  88.2 1.8 fusion.30
  95.4 20.6 %fusion.14 = bf16[2560,3,64]{0,2,1:T(8,128)(2,1)} fusion(bf16[3,192,64]{1,2,0:T(8,128)(2,1)S(1)} %convolution_convert_fusion.5, f32[3,2560,192]{1,2,0:T(8,128)} %copy-done.5, f32[3,2560]{1,0:T(4,128)S(1)} %fusion.7, f32[3,2560]{1,0:T(4,128)S(1)} %get-tuple-element.222, pred[2560,192]{0,1:T(8,128)(4,1)S(1)} %copy-done.41, ...), kind=kOutput, calls=%fused_computation.111 | convolution fusion | flops 243302400 | bytes 9556364 | tf_op jit(solution)/shard_map/lvk,lko->vlo/dot_general | solution.py:171
  116.0 2.7 all_to_all.26
  118.7 1.5 copy.97
  120.2 16.2 %all_to_all.35 = bf16[4,640,192]{1,2,0:T(8,128)(2,1)S(1)} all-to-all(bf16[4,640,192]{1,2,0:T(8,128)(2,1)S(1)} %copy.97), channel_id=1, replica_groups=mesh['dp'=8,'tensor'=4] {'tensor'}, dimensions={0} | all-to-all | bytes 1966080 | tf_op jit(solution)/shard_map/all_to_all | solution.py:184
  140.1 33.1 %all-gather.6.cloned.1.call-done = bf16[2560,768]{1,0:T(8,128)(2,1)} async-done(((bf16[640,768]{1,0:T(8,128)(2,1)}), bf16[2560,768]{1,0:T(8,128)(2,1)}) %all-gather.6.cloned.1.call-update) | async-done | bytes 3932176 | tf_op jit(solution)/shard_map/all_gather | solution.py:191
  173.2 22.1 %multiply_convert_fusion = (bf16[2560,768]{1,0:T(8,128)(2,1)S(1)}, f32[2560,768]{1,0:T(8,128)}, f32[2560,768]{1,0:T(8,128)}) fusion(bf16[2560,768]{1,0:T(8,128)(2,1)} %all-gather.6.cloned.1.call-done, bf16[768,768]{1,0:T(8,128)(2,1)S(1)} %copy-done), kind=kOutput, calls=%fused_computation.69 | convolution fusion | flops 3147694080 | bytes 24772608 | tf_op jit(solution)/shard_map/dot_general | solution.py:192
  195.4 1.9 copy-done.236
  197.3 4.7 convolution_convert_fusion.1
  202.1 43.0 %reduce-scatter.4.cloned.1.call-done = bf16[640,768]{1,0:T(8,128)(2,1)} async-done(((bf16[2560,768]{1,0:T(8,128)(2,1)}), bf16[640,768]{1,0:T(8,128)(2,1)}) %reduce-scatter.4.cloned.1.call-update) | async-done | bytes 983056 | tf_op jit(solution)/shard_map/reduce_scatter | solution.py:194
  245.1 2.5 fusion.179
  250.2 3.0 fusion.177
  253.3 33.1 %all-gather.8.cloned.1.call-done = bf16[2560,768]{1,0:T(8,128)(2,1)} async-done(((bf16[640,768]{1,0:T(8,128)(2,1)}), bf16[2560,768]{1,0:T(8,128)(2,1)}) %all-gather.8.cloned.1.call-update) | async-done | bytes 3932176 | tf_op jit(solution)/shard_map/all_gather | solution.py:208
  286.4 10.8 %add_convert_fusion.1 = bf16[2560,768]{1,0:T(8,128)(2,1)S(1)} fusion(f32[2560,768]{1,0:T(8,128)} %get-tuple-element.143, f32[2560,768]{1,0:T(8,128)} %get-tuple-element.226, bf16[2560,768]{1,0:T(8,128)(2,1)} %all-gather.8.cloned.1.call-done, bf16[768,768]{1,0:T(8,128)(2,1)} %param.23), kind=kOutput, calls=%fused_computation.68 | convolution fusion | flops 3047424000 | bytes 24772608 | tf_op jit(solution)/shard_map/gd,fd->gf/dot_general | solution.py:210
  297.3 1.9 copy-done.237
  299.2 4.7 convolution_convert_fusion
  305.9 41.1 %reduce-scatter.6.cloned.1.call-done = bf16[640,768]{1,0:T(8,128)(2,1)} async-done(((bf16[2560,768]{1,0:T(8,128)(2,1)}), bf16[640,768]{1,0:T(8,128)(2,1)}) %reduce-scatter.6.cloned.1.call-update) | async-done | bytes 983056 | tf_op jit(solution)/shard_map/reduce_scatter | solution.py:213
  347.0 4.1 multiply_reduce_fusion.2
  355.4 3.5 all-to-all-start.1
  359.6 13.0 %all-to-all-done.1 = bf16[640,4,192]{0,2,1:T(8,128)(2,1)S(1)} async-done(((bf16[640,4,192]{0,2,1:T(8,128)(2,1)}), bf16[640,4,192]{0,2,1:T(8,128)(2,1)S(1)}, u32[]{:S(2)}, u32[]{:S(2)}) %all-to-all-start.1) | async-done | bytes 983072 | tf_op jit(solution)/shard_map/all_to_all | solution.py:232
  373.6 1.7 copy.99
  375.3 2.0 reshape.499
  377.3 4.0 fusion.21
  393.0 1.5 convolution_negate_fusion.13
  404.9 1.6 convolution_negate_fusion.8
  419.1 1.6 convolution_negate_fusion.2
  431.0 4.7 multiply_reduce_fusion.1
  436.0 6.8 fusion.97
  443.0 5.8 fusion.57
  449.1 7.1 fusion.38
  456.3 7.1 fusion.48
  463.5 6.1 multiply_convert_fusion.2
  469.5 3.0 fusion.124
  472.6 2.2 multiply_reduce_fusion
  474.8 2.1 multiply_convert_fusion.1
  482.0 4.4 fusion.205
  486.4 4.3 fusion.204
  490.7 24.8 %pad_add_fusion = f32[2592,3,64]{0,2,1:T(8,128)} fusion(f32[2560,3,64]{0,2,1:T(8,128)} %get-tuple-element.178, f32[2560,3,64]{0,2,1:T(8,128)} %get-tuple-element.177, f32[2560,3,64]{0,2,1:T(8,128)} %get-tuple-element.176, f32[2560,3,64]{0,2,1:T(8,128)} %get-tuple-element.175, f32[2560,3,64]{0,2,1:T(8,128)} %get-tuple-element.174, ...), kind=kLoop, calls=%fused_computation.133 | loop fusion | flops 12939264 | bytes 55074816 | tf_op jit(solution)/shard_map/transpose(jvp())/add_any | solution.py:71
  515.5 11.4 %fusion.17 = bf16[2560,3,64]{0,2,1:T(8,128)(2,1)S(1)} fusion(bf16[3,192,64]{1,2,0:T(8,128)(2,1)S(1)} %convolution_convert_fusion.4, f32[3,192,2560]{2,1,0:T(8,128)} %copy-done.2, f32[3,192]{1,0:T(4,128)S(1)} %log_add_fusion.1, pred[192,2560]{1,0:T(8,128)(4,1)} %compare_bitcast_fusion, f32[2560,3,64]{0,2,1:T(8,128)} %get-tuple-element.150, ...), kind=kOutput, calls=%fused_computation.114 | convolution fusion | flops 197099520 | bytes 21211392 | tf_op jit(solution)/shard_map/bet,bek->tbk/dot_general | solution.py:283
  527.9 3.5 add_convert_fusion
  531.5 8.1 fusion.207
  539.6 2.5 fusion.145
  542.5 8.1 fusion.206
  550.6 1.8 convolution_bitcast_fusion.4
  552.4 1.7 fusion.120
  554.1 1.7 fusion.121
  556.6 39.9 %all-reduce.68 = (f32[768]{0:T(1024)}, f32[768]{0:T(1024)}, f32[768]{0:T(1024)}, f32[768]{0:T(1024)}) all-reduce(f32[768]{0:T(1024)S(1)} %copy-done.180, f32[768]{0:T(1024)S(1)} %copy-done.181, f32[768]{0:T(1024)S(1)} %copy-done.177, f32[768]{0:T(1024)S(1)} %copy-done.178), channel_id=1, replica_groups=mesh['dp'=8,'tensor'=4] {'dp','tensor'}, use_global_device_ids=true, to_apply=%region_69.70 | all-reduce | flops 3072 | bytes 24576 | tf_op jit(solution)/shard_map/psum | solution.py:347
  599.6 5.1 fusion.79
  604.7 5.1 fusion.88
  609.7 5.1 fusion.70
  614.9 37.4 %psum.80 = f32[3,33]{0,1:T(8,128)S(1)} all-reduce(f32[3,33]{0,1:T(8,128)S(1)} %pad_add_fusion.7), channel_id=1, replica_groups=mesh['dp'=8,'tensor'=4] {'dp'}, use_global_device_ids=true, to_apply=%region_66.67 | all-reduce | flops 99 | bytes 792 | tf_op jit(solution)/shard_map/psum | solution.py:344
  653.0 3.3 convert_add_fusion
  656.2 61.0 %all-reduce.73.cloned.1.call-done = f32[768,768]{1,0:T(8,128)} async-done(((f32[768,768]{1,0:T(8,128)}), f32[768,768]{1,0:T(8,128)}) %all-reduce.73.cloned.1.call-update) | async-done | bytes 2359312 | tf_op jit(solution)/shard_map/psum | solution.py:347
  717.3 225.7 %all-reduce.75.cloned.1.call-done = (f32[768,192]{0,1:T(8,128)}, f32[768,192]{0,1:T(8,128)}, f32[768,192]{0,1:T(8,128)}, f32[768,768]{1,0:T(8,128)}, f32[768,768]{1,0:T(8,128)}) async-done(((f32[768,192]{0,1:T(8,128)}, f32[768,192]{0,1:T(8,128)}, f32[768,192]{0,1:T(8,128)}, f32[768,768]{1,0:T(8,128)}, f32[768,768]{1,0:T(8,128)}), (f32[768,192]{0,1:T(8,128)}, f32[768,192]{0,1:T(8,128)}, ...) | async-done | bytes 6488080 | tf_op jit(solution)/shard_map/psum | solution.py:344
  943.0 1.9 copy.278
  944.9 1.9 copy.279
  946.9 1.9 copy.280
  (641 shorter events, 123.4 us)
Async XLA Ops:
  7.2 166.1 %copy-start = (bf16[768,768]{1,0:T(8,128)(2,1)S(1)}, bf16[768,768]{1,0:T(8,128)(2,1)}, u32[]{:S(2)}) copy-start(bf16[768,768]{1,0:T(8,128)(2,1)} %param.22) | copy-start | bytes 3538948
  7.2 38.2 %copy-start.106 = (bf16[768,192]{0,1:T(8,128)(2,1)S(1)}, bf16[768,192]{0,1:T(8,128)(2,1)}, u32[]{:S(2)}) copy-start(bf16[768,192]{0,1:T(8,128)(2,1)} %param.16) | copy-start | bytes 884740
  7.2 38.2 %all-gather.4.cloned.1.call-start = ((), (), s32[]{:S(2)}) async-start(), calls=%async_computation.5 | async-start | bytes 4915200 | tf_op jit(solution)/shard_map/all_gather | solution.py:111
  7.9 165.3 %all-gather.6.cloned.1.call-start = ((), (), s32[]{:S(2)}) async-start(), calls=%async_computation.6 | async-start | bytes 4915200 | tf_op jit(solution)/shard_map/all_gather | solution.py:191
  8.9 43.7 %copy-start.103 = (pred[192,192]{0,1:T(8,128)(4,1)}, pred[192,192]{0,1:T(8,128)(4,1)S(1)}, u32[]{:S(2)}) copy-start(pred[192,192]{0,1:T(8,128)(4,1)S(1)} %copy.88) | copy-start | bytes 110596
  16.0 62.5 %copy-start.13 = (f32[192,192]{1,0:T(8,128)}, f32[192,192]{1,0:T(8,128)S(1)}, u32[]{:S(2)}) copy-start(f32[192,192]{1,0:T(8,128)S(1)} %get-tuple-element.235) | copy-start | bytes 442372
  16.2 35.5 %copy-start.112 = (s32[2560]{0:T(1024)}, s32[2560]{0:T(1024)S(1)}, u32[]{:S(2)}) copy-start(s32[2560]{0:T(1024)S(1)} %fusion.168) | copy-start | bytes 30724
  16.5 35.7 %copy-start.192 = (f32[192]{0:T(256)}, f32[192]{0:T(256)S(1)}, u32[]{:S(2)}) copy-start(f32[192]{0:T(256)S(1)} %convert_reduce_fusion.1) | copy-start | bytes 2308
  52.6 6.9 copy-start.67
  52.6 6.9 copy-start.119
  54.2 23.0 %copy-start.3 = (f32[3,192,192]{1,2,0:T(8,128)}, f32[3,192,192]{1,2,0:T(8,128)S(1)}, u32[]{:S(2)}) copy-start(f32[3,192,192]{1,2,0:T(8,128)S(1)} %get-tuple-element.145) | copy-start | bytes 1327108
  81.2 8.7 copy-start.65
  118.7 17.6 %copy-start.102 = (bf16[640,768]{1,0:T(8,128)(2,1)S(1)}, bf16[640,768]{1,0:T(8,128)(2,1)}, u32[]{:S(2)}) copy-start(bf16[640,768]{1,0:T(8,128)(2,1)} %param.14) | copy-start | bytes 2949124
  118.7 17.6 %copy-start.233 = (bf16[768,768]{1,0:T(8,128)(2,1)S(1)}, bf16[768,768]{1,0:T(8,128)(2,1)}, u32[]{:S(2)}) copy-start(bf16[768,768]{1,0:T(8,128)(2,1)} %param.19) | copy-start | bytes 3538948
  140.1 105.0 %reduce-scatter.4.cloned.1.call-start = ((), (), s32[]{:S(2)}) async-start(), calls=%async_computation.7 | async-start | bytes 4915200 | tf_op jit(solution)/shard_map/reduce_scatter | solution.py:194
  173.2 24.0 %copy-start.232 = (bf16[768,768]{1,0:T(8,128)(2,1)S(1)}, bf16[768,768]{1,0:T(8,128)(2,1)}, u32[]{:S(2)}) copy-start(bf16[768,768]{1,0:T(8,128)(2,1)} %param.23) | copy-start | bytes 3538948
  202.0 84.4 %all-gather.8.cloned.1.call-start = ((), (), s32[]{:S(2)}) async-start(), calls=%async_computation.8 | async-start | bytes 4915200 | tf_op jit(solution)/shard_map/all_gather | solution.py:208
  253.3 93.7 %reduce-scatter.6.cloned.1.call-start = ((), (), s32[]{:S(2)}) async-start(), calls=%async_computation.9 | async-start | bytes 4915200 | tf_op jit(solution)/shard_map/reduce_scatter | solution.py:213
  355.4 17.2 %all-to-all-start.1 = ((bf16[640,4,192]{0,2,1:T(8,128)(2,1)}), bf16[640,4,192]{0,2,1:T(8,128)(2,1)S(1)}, u32[]{:S(2)}, u32[]{:S(2)}) async-start(bf16[640,4,192]{0,2,1:T(8,128)(2,1)} %bitcast.348), calls=%async_computation.3 | async-start | bytes 1966080 | tf_op jit(solution)/shard_map/all_to_all | solution.py:232
  358.9 294.1 %reduce-scatter.8.cloned.1.call-start = ((), (), s32[]{:S(2)}) async-start(), calls=%async_computation.10 | async-start | bytes 4915200 | tf_op jit(solution)/shard_map/reduce_scatter | solution.py:335
  359.6 17.7 %copy-start.104 = (f32[3,2560]{1,0:T(4,128)}, f32[3,2560]{1,0:T(4,128)S(1)}, u32[]{:S(2)}) copy-start(f32[3,2560]{1,0:T(4,128)S(1)} %log_add_fusion) | copy-start | bytes 92164
  435.9 6.9 copy-start.124
  435.9 6.9 copy-start.126
  435.9 6.9 copy-start.128
  435.9 6.9 copy-start.130
  435.9 6.9 copy-start.132
  435.9 6.9 copy-start.197
  435.9 6.9 copy-start.199
  435.9 6.9 copy-start.201
  435.9 6.9 copy-start.203
  436.0 6.9 copy-start.205
  436.0 6.9 copy-start.207
  436.0 6.9 copy-start.209
  436.0 6.9 copy-start.211
  448.9 7.3 copy-start.138
  448.9 7.2 copy-start.154
  448.9 7.2 copy-start.158
  448.9 7.2 copy-start.160
  448.9 7.2 copy-start.162
  449.0 7.2 copy-start.164
  449.0 7.2 copy-start.166
  449.0 7.2 copy-start.168
  449.0 7.2 copy-start.170
  449.0 7.2 copy-start.213
  449.0 7.2 copy-start.215
  449.0 7.2 copy-start.216
  449.0 7.2 copy-start.217
  449.0 7.2 copy-start.218
  449.0 7.2 copy-start.219
  449.1 7.2 copy-start.220
  456.3 16.2 %slice-start = ((s8[5898240]{0:T(1024)(128)(4,1)}), s8[4194304]{0:T(1024)(128)(4,1)S(1)}, s32[]{:S(2)}) async-start(s8[5898240]{0:T(1024)(128)(4,1)} %bitcast.325), calls=%async_computation.13 | async-start | bytes 8388608
  463.5 6.1 copy-start.89
  463.5 9.1 slice-start.1
  479.9 6.5 copy-start.43
  515.5 12.4 %copy-start.8 = (f32[2560,768]{1,0:T(8,128)S(1)}, f32[2560,768]{1,0:T(8,128)}, u32[]{:S(2)}) copy-start(f32[2560,768]{1,0:T(8,128)} %fusion.205) | copy-start | bytes 23592964
  515.5 12.4 %copy-start.9 = (f32[2560,768]{1,0:T(8,128)S(1)}, f32[2560,768]{1,0:T(8,128)}, u32[]{:S(2)}) copy-start(f32[2560,768]{1,0:T(8,128)} %fusion.204) | copy-start | bytes 23592964
  515.5 12.4 %copy-start.111 = (bf16[768,192]{0,1:T(8,128)(2,1)S(1)}, bf16[768,192]{0,1:T(8,128)(2,1)}, u32[]{:S(2)}) copy-start(bf16[768,192]{0,1:T(8,128)(2,1)} %param.17) | copy-start | bytes 884740
  531.4 185.9 %all-reduce.73.cloned.1.call-start = ((), (), s32[]{:S(2)}) async-start(), calls=%async_computation.11 | async-start | bytes 4718592 | tf_op jit(solution)/shard_map/psum | solution.py:347
  531.4 8.2 copy-start.32
  531.5 8.1 copy-start.86
  542.1 400.9 %all-reduce.75.cloned.1.call-start = ((), (), s32[]{:S(2)}) async-start(), calls=%async_computation.12 | async-start | bytes 12976128 | tf_op jit(solution)/shard_map/psum | solution.py:344
  542.4 8.2 copy-start.12
  542.4 8.2 copy-start.51
  717.3 231.5 %copy-start.97 = (f32[768,768]{1,0:T(8,128)S(1)}, f32[768,768]{1,0:T(8,128)}, u32[]{:S(2)}) copy-start(f32[768,768]{1,0:T(8,128)} %all-reduce.73.cloned.1.call-done) | copy-start | bytes 7077892
  (187 other events, 489.6 us)
Sparse Core Ops, SparseCore 0:
  9.6 35.7 all-gather.3
  140.2 33.0 all-gather.5
  202.1 42.9 reduce-scatter.3
  253.4 32.9 all-gather.7
  304.1 42.8 reduce-scatter.5
  531.5 43.5 reduce-scatter.7
  582.2 135.0 all-reduce.72
  723.4 219.6 all-reduce.74
where the time goes:
time: 972 us; the launch traced here: 962 us
  waiting for transfers between devices  475 us (49%)
  matrix products  214 us (22%)
  other arithmetic  109 us (11%)
  blocking collectives  93.5 us (10%)
  local copies, waits for them, and re-layouts  47.9 us (5%)
  between operations  18.3 us (2%)
    psum x1, waiting for transfers between devices, shards(): lax.psum((grad_w_query, grad_w_key, grad_w_value, grad_conv, grad_up, gra...  226 us
    psum x1, waiting for transfers between devices, shards(): lax.psum((grad_w_out, grad_gain_one, grad_shift_one, grad_gain_two, grad_...  61 us
    reduce_scatter x1, waiting for transfers between devices, shards(): lax.psum_scatter(jnp.dot(hidden, w_down, preferred_element_type=jnp.float...  43 us
    reduce_scatter x1, waiting for transfers between devices, shards(): lax.psum_scatter(jnp.einsum('gf,df->gd', grad_pre, w_up, preferred_elemen...  41.1 us
    psum x1, blocking collectives, shards(): lax.psum((grad_w_out, grad_gain_one, grad_shift_one, grad_gain_two, grad_...  39.9 us
    psum x1, blocking collectives, shards(): lax.psum((grad_w_query, grad_w_key, grad_w_value, grad_conv, grad_up, gra...  37.4 us
    unnamed x491, local copies, waits for them, and re-layouts  33.7 us
    dot_general x36, matrix products, iterative_pseudoinverse(): jnp.einsum('hij,hjk->hik', product, bracket, precision=TOP_PRECISION)  33.5 us
  transfers between devices with their start and end apart: 9, of which 8 were waited for; matrix products, arithmetic and copies ran while one was open for 6% of the time, Pallas kernels for 0%

commit v1 on v0

v1 whole, which is shorter than its diff:
```python
import jax
import jax.numpy as jnp
from jax import lax
from jax.experimental import pallas as pl
from jax.experimental.pallas import tpu as pltpu
from jax.sharding import PartitionSpec as P

HEAD = 64
LANDMARKS = 64
NS_ITERS = 6
KERNEL = 33
SEQS = 3
MARKS = 192
REACH = KERNEL // 2
PAD = 128
BAND_IN = 512
BAND_OUT = 256
TILE = 512
VMEM_LIMIT = 60 * 1024 * 1024
F32 = jnp.float32
BF16 = jnp.bfloat16


def dot_nn(a, b):
    return lax.dot_general(a, b, (((1,), (0,)), ((), ())), preferred_element_type=F32)


def dot_nt(a, b):
    return lax.dot_general(a, b, (((1,), (1,)), ((), ())), preferred_element_type=F32)


def dot_tn(a, b):
    return lax.dot_general(a, b, (((0,), (0,)), ((), ())), preferred_element_type=F32)


def split_low(a):
    high = a.astype(BF16)
    return (high, (a - high.astype(F32)).astype(BF16))


def dot_three(a, b, dot=dot_nn):
    a_high, a_low = a
    b_high, b_low = b
    return dot(a_high, b_high) + (dot(a_high, b_low) + dot(a_low, b_high))


def block_mask(dtype):
    rows = lax.broadcasted_iota(jnp.int32, (MARKS, MARKS), 0) // LANDMARKS
    columns = lax.broadcasted_iota(jnp.int32, (MARKS, MARKS), 1) // LANDMARKS
    return jnp.where(rows == columns, 1.0, 0.0).astype(dtype)


def spread(packed, mask):
    return jnp.concatenate([packed] * SEQS, axis=0) * mask


def spread_split(packed, mask):
    high, low = split_low(packed)
    return (spread(high, mask), spread(low, mask))


def fold(blocks):
    return (
        blocks[:LANDMARKS] + blocks[LANDMARKS : 2 * LANDMARKS] + blocks[2 * LANDMARKS :]
    )


def packed_identity():
    rows = lax.broadcasted_iota(jnp.int32, (LANDMARKS, MARKS), 0)
    columns = lax.broadcasted_iota(jnp.int32, (LANDMARKS, MARKS), 1) % LANDMARKS
    return jnp.where(rows == columns, 1.0, 0.0).astype(F32)


def sequence_of(places, first_end, second_end):
    return (places >= first_end).astype(jnp.int32) + (places >= second_end).astype(jnp.int32)


def pooling_tile(start, width, ends):
    first_end, second_end, group_size = ends
    places = start + lax.broadcasted_iota(jnp.int32, (1, width), 1)
    sequence = sequence_of(places, first_end, second_end)
    own_start = jnp.where(sequence == 0, 0, jnp.where(sequence == 1, first_end, second_end))
    own_end = jnp.where(
        sequence == 0, first_end, jnp.where(sequence == 1, second_end, group_size)
    )
    own_length = (own_end - own_start).astype(F32)
    within = places - own_start
    numerator = ((within + 1) * LANDMARKS - 1).astype(F32) + own_length + 0.5
    segment = jnp.floor(numerator / own_length).astype(jnp.int32) - 1
    landmark = sequence * LANDMARKS + segment
    marks = lax.broadcasted_iota(jnp.int32, (MARKS, width), 0)
    return jnp.where(marks == landmark, 1.0, 0.0).astype(BF16)


def own_tokens_tile(start, width, ends):
    places = start + lax.broadcasted_iota(jnp.int32, (1, width), 1)
    sequence = sequence_of(places, ends[0], ends[1])
    marks = lax.broadcasted_iota(jnp.int32, (MARKS, width), 0) // LANDMARKS
    return marks == sequence


def landmark_counts(ends, axis):
    first_end, second_end, group_size = ends
    shape = (1, MARKS) if axis == 1 else (MARKS, 1)
    marks = lax.broadcasted_iota(jnp.int32, shape, axis)
    sequence = marks // LANDMARKS
    k = marks % LANDMARKS
    own_length = jnp.where(
        sequence == 0,
        first_end,
        jnp.where(sequence == 1, second_end - first_end, group_size - second_end),
    )
    upper = lax.shift_right_logical((k + 1) * own_length, 6)
    return (upper - lax.shift_right_logical(k * own_length, 6)).astype(F32)


def band_mask(start, ends):
    into = start - PAD + lax.broadcasted_iota(jnp.int32, (BAND_IN, 1), 0)
    out = start + lax.broadcasted_iota(jnp.int32, (1, BAND_OUT), 1)
    return sequence_of(into, ends[0], ends[1]) == sequence_of(out, ends[0], ends[1])


def ends_of(scalars, group_size):
    first_end = scalars[0]
    return (first_end, first_end + scalars[1], group_size)


def lane_slice(start, width):
    return pl.ds(pl.multiple_of(start, 128), width)


def attend_kernel(
    heads,
    scalars,
    x0,
    x1,
    x2,
    x3,
    w_t,
    bands,
    qkv_t,
    c0,
    c1,
    c2,
    c3,
    land_t,
    mark_values_out,
    summary_out,
    steps_out,
    among_out,
    inverse_out,
    lse_to,
    lse_from,
    context_t,
    scores,
    pooled,
    mvt_scratch,
):
    width = heads * HEAD
    block = x0.shape[0]
    group_size = 4 * block
    ends = ends_of(scalars, group_size)
    me = scalars[3]
    qk_scale = HEAD ** (-0.25)
    tiles = group_size // TILE

    qkv_t[:, :PAD] = jnp.zeros((3 * width, PAD), BF16)
    qkv_t[:, PAD + group_size :] = jnp.zeros((3 * width, PAD), BF16)
    for at, x in enumerate((x0, x1, x2, x3)):
        offset = PAD + (me ^ at) * block

        @pl.loop(0, 3)
        def _(part):
            rows = pl.ds(pl.multiple_of(part * width, width), width)
            product = dot_nt(w_t[rows, :], x[...])
            scale = jnp.where(part < 2, qk_scale, 1.0).astype(F32)
            qkv_t[rows, lane_slice(offset, block)] = (product * scale).astype(BF16)

    pooled[...] = jnp.zeros_like(pooled)

    @pl.loop(0, tiles)
    def _(i):
        pool = pooling_tile(i * TILE, TILE, ends)
        pooled[...] += dot_nt(qkv_t[: 2 * width, lane_slice(PAD + i * TILE, TILE)], pool)

    pooled[...] = pooled[...] / landmark_counts(ends, 1)
    land_t[...] = pooled[...].astype(BF16)

    mask_f = block_mask(F32)
    mask_b = block_mask(BF16)
    eye = packed_identity()
    summaries = []
    amongs = []
    packs = []
    approxes = []
    key_lands = []
    for h in range(heads):
        head_rows = slice(h * HEAD, (h + 1) * HEAD)
        key_rows = slice(width + h * HEAD, width + (h + 1) * HEAD)
        value_rows = slice(2 * width + h * HEAD, 2 * width + (h + 1) * HEAD)
        q_land = land_t[head_rows, :].astype(F32).T.astype(BF16)
        k_land = land_t[key_rows, :].astype(F32).T.astype(BF16)
        key_lands.append(k_land)

        def score_pass(i, top):
            raw = dot_nn(q_land, qkv_t[key_rows, lane_slice(PAD + i * TILE, TILE)])
            masked = jnp.where(own_tokens_tile(i * TILE, TILE, ends), raw, -1e30)
            scores[:, lane_slice(i * TILE, TILE)] = masked
            return jnp.maximum(top, jnp.max(masked, axis=1, keepdims=True))

        top = lax.fori_loop(0, tiles, score_pass, jnp.full((MARKS, 1), -1e30, F32))

        def raise_pass(i, total):
            at = lane_slice(i * TILE, TILE)
            raised = jnp.exp(scores[:, at] - top)
            scores[:, at] = raised
            return total + jnp.sum(raised, axis=1, keepdims=True)

        total = lax.fori_loop(0, tiles, raise_pass, jnp.zeros((MARKS, 1), F32))
        recip = 1.0 / total
        lse_from[h] = jnp.broadcast_to(top + jnp.log(total), (MARKS, 128))

        def summary_pass(i, summed):
            low = (scores[:, lane_slice(i * TILE, TILE)] * recip).astype(BF16)
            return summed + dot_nt(low, qkv_t[value_rows, lane_slice(PAD + i * TILE, TILE)])

        summary = lax.fori_loop(0, tiles, summary_pass, jnp.zeros((MARKS, HEAD), F32))
        summary_out[h] = summary
        summaries.append(summary)

        raw = dot_nn(q_land, land_t[key_rows, :])
        masked = jnp.where(mask_f > 0.0, raw, -1e30)
        row_top = jnp.max(masked, axis=1, keepdims=True)
        raised = jnp.exp(masked - row_top)
        among = raised / jnp.sum(raised, axis=1, keepdims=True)
        column_top = jnp.max(jnp.sum(among, axis=0, keepdims=True), axis=1, keepdims=True)
        packed = fold(among)
        among_out[h] = packed
        amongs.append(split_low(packed))
        approxes.append(fold(among.T) / column_top)

    for step in range(NS_ITERS):
        product = [
            dot_three(amongs[h], spread_split(approxes[h], mask_b)) for h in range(heads)
        ]
        split = [split_low(product[h]) for h in range(heads)]
        bracket = [7.0 * eye - product[h] for h in range(heads)]
        second = [
            15.0 * eye - dot_three(split[h], spread_split(bracket[h], mask_b))
            for h in range(heads)
        ]
        third = [
            13.0 * eye - dot_three(split[h], spread_split(second[h], mask_b))
            for h in range(heads)
        ]
        for h in range(heads):
            steps_out[h, 4 * step] = approxes[h]
            steps_out[h, 4 * step + 1] = product[h]
            steps_out[h, 4 * step + 2] = second[h]
            steps_out[h, 4 * step + 3] = third[h]
        approxes = [
            0.25 * dot_three(split_low(approxes[h]), spread_split(third[h], mask_b))
            for h in range(heads)
        ]

    for h in range(heads):
        inverse_out[h] = approxes[h]
        mark_values = dot_three(
            spread_split(approxes[h], mask_b), split_low(summaries[h])
        )
        mark_values_out[h] = mark_values.astype(BF16)
        mvt_scratch[h] = mark_values.astype(BF16).astype(F32).T.astype(BF16)

    @pl.loop(0, group_size // BAND_OUT)
    def _(i):
        start = i * BAND_OUT
        near = own_tokens_tile(start, BAND_OUT, ends)
        same = jnp.where(band_mask(start, ends), 1.0, 0.0).astype(BF16)
        for h in range(heads):
            head_rows = slice(h * HEAD, (h + 1) * HEAD)
            value_rows = slice(2 * width + h * HEAD, 2 * width + (h + 1) * HEAD)
            raw = dot_nn(key_lands[h], qkv_t[head_rows, lane_slice(PAD + start, BAND_OUT)])
            masked = jnp.where(near, raw, -1e30)
            top = jnp.max(masked, axis=0, keepdims=True)
            raised = jnp.exp(masked - top)
            total = jnp.sum(raised, axis=0, keepdims=True)
            lse_to[h : h + 1, lane_slice(start, BAND_OUT)] = top + jnp.log(total)
            low = (raised * (1.0 / total)).astype(BF16)
            window = qkv_t[value_rows, lane_slice(start, BAND_IN)]
            blended = dot_nn(mvt_scratch[h], low)
            smooth = dot_nn(window, bands[h, 0] * same) + dot_nn(window, bands[h, 1] * same)
            context_t[head_rows, lane_slice(start, BAND_OUT)] = (blended + smooth).astype(BF16)

    for at, out in enumerate((c0, c1, c2, c3)):
        out[...] = context_t[:, lane_slice((me ^ at) * block, block)]


def attend(scalars, blocks, w_t, bands):
    block = blocks[0].shape[0]
    group_size = 4 * block
    width = w_t.shape[0] // 3
    heads = width // HEAD
    out_shape = (
        jax.ShapeDtypeStruct((3 * width, group_size + 2 * PAD), BF16),
        *[jax.ShapeDtypeStruct((width, block), BF16) for _ in range(4)],
        jax.ShapeDtypeStruct((2 * width, MARKS), BF16),
        jax.ShapeDtypeStruct((heads, MARKS, HEAD), BF16),
        jax.ShapeDtypeStruct((heads, MARKS, HEAD), F32),
        jax.ShapeDtypeStruct((heads, 4 * NS_ITERS, LANDMARKS, MARKS), F32),
        jax.ShapeDtypeStruct((heads, LANDMARKS, MARKS), F32),
        jax.ShapeDtypeStruct((heads, LANDMARKS, MARKS), F32),
        jax.ShapeDtypeStruct((heads, group_size), F32),
        jax.ShapeDtypeStruct((heads, MARKS, 128), F32),
    )
    vmem = pl.BlockSpec(memory_space=pltpu.VMEM)

    def kernel(*refs):
        attend_kernel(heads, *refs)

    return pl.pallas_call(
        kernel,
        name="attend",
        out_shape=out_shape,
        in_specs=[pl.BlockSpec(memory_space=pltpu.SMEM)] + [vmem] * 6,
        out_specs=[vmem] * len(out_shape),
        scratch_shapes=[
            pltpu.VMEM((width, group_size), BF16),
            pltpu.VMEM((MARKS, group_size), F32),
            pltpu.VMEM((2 * width, MARKS), F32),
            pltpu.VMEM((heads, HEAD, MARKS), BF16),
        ],
        compiler_params=pltpu.CompilerParams(vmem_limit_bytes=VMEM_LIMIT),
        cost_estimate=pl.CostEstimate(
            flops=15_000_000_000, bytes_accessed=20_000_000, transcendentals=4_000_000
        ),
    )(scalars, *blocks, w_t, bands)


def attend_back_kernel(
    heads,
    scalars,
    qkv_t,
    land_t,
    mark_values_in,
    summary_in,
    steps_in,
    among_in,
    inverse_in,
    lse_to,
    lse_from,
    bands,
    g0,
    g1,
    g2,
    g3,
    x0,
    x1,
    x2,
    x3,
    w_t,
    grad_w_t,
    grad_conv,
    d0,
    d1,
    d2,
    d3,
    context_grad,
    grad_qkv,
    partial_query,
    partial_key,
    partial_value,
    grad_q_land,
    grad_k_land,
    grad_mark,
    correlation,
):
    width = heads * HEAD
    block = x0.shape[0]
    group_size = 4 * block
    ends = ends_of(scalars, group_size)
    me = scalars[3]
    qk_scale = HEAD ** (-0.25)
    tiles = group_size // TILE

    context_grad[:, :PAD] = jnp.zeros((width, PAD), BF16)
    context_grad[:, PAD + group_size :] = jnp.zeros((width, PAD), BF16)
    for at, g in enumerate((g0, g1, g2, g3)):
        context_grad[:, lane_slice(PAD + (me ^ at) * block, block)] = g[...]

    mask_f = block_mask(F32)
    mask_b = block_mask(BF16)
    lands = []
    for h in range(heads):
        q_land_t = land_t[h * HEAD : (h + 1) * HEAD, :]
        k_land_t = land_t[width + h * HEAD : width + (h + 1) * HEAD, :]
        lands.append(
            (
                q_land_t,
                k_land_t,
                q_land_t.astype(F32).T.astype(BF16),
                k_land_t.astype(F32).T.astype(BF16),
            )
        )

    grad_k_land[...] = jnp.zeros_like(grad_k_land)
    grad_mark[...] = jnp.zeros_like(grad_mark)
    grad_q_land[...] = jnp.zeros_like(grad_q_land)

    @pl.loop(0, tiles)
    def _(i):
        at = lane_slice(i * TILE, TILE)
        padded = lane_slice(PAD + i * TILE, TILE)
        near = own_tokens_tile(i * TILE, TILE, ends)
        for h in range(heads):
            head_rows = slice(h * HEAD, (h + 1) * HEAD)
            q_land_t, k_land_t, q_land, k_land = lands[h]
            query = qkv_t[head_rows, padded]
            out_grad = context_grad[head_rows, padded]
            raw = dot_nn(k_land, query)
            probs = jnp.exp(jnp.where(near, raw, -1e30) - lse_to[h : h + 1, at])
            grad_to = dot_nn(mark_values_in[h], out_grad)
            inner = jnp.sum(grad_to * probs, axis=0, keepdims=True)
            grad_scores = (probs * (grad_to - inner)).astype(BF16)
            grad_mark[h] += dot_nt(probs.astype(BF16), out_grad)
            grad_k_land[h] += dot_nt(grad_scores, query)
            partial_query[head_rows, at] = dot_nn(k_land_t, grad_scores)

    grad_summaries = []
    offsets = []
    carried = []
    among_grads = []
    for h in range(heads):
        mark = grad_mark[h]
        mark_split = split_low(mark)
        summary = summary_in[h]
        carried.append(fold(dot_three(split_low(summary), mark_split, dot_nt) * mask_f))
        inverse_blocks = spread(inverse_in[h], mask_f).T
        grad_summary = dot_three(split_low(inverse_blocks), mark_split)
        grad_low = grad_summary.astype(BF16)
        grad_summaries.append((grad_low, grad_low.astype(F32).T.astype(BF16)))
        offsets.append(jnp.sum(grad_low.astype(F32) * summary, axis=1, keepdims=True))

    @pl.loop(0, tiles)
    def _(i):
        at = lane_slice(i * TILE, TILE)
        padded = lane_slice(PAD + i * TILE, TILE)
        near = own_tokens_tile(i * TILE, TILE, ends)
        for h in range(heads):
            head_rows = slice(h * HEAD, (h + 1) * HEAD)
            key_rows = slice(width + h * HEAD, width + (h + 1) * HEAD)
            value_rows = slice(2 * width + h * HEAD, 2 * width + (h + 1) * HEAD)
            q_land_t, k_land_t, q_land, k_land = lands[h]
            key = qkv_t[key_rows, padded]
            value = qkv_t[value_rows, padded]
            raw = dot_nn(q_land, key)
            lse = jnp.concatenate([lse_from[h]] * (TILE // 128), axis=1)
            probs = jnp.exp(jnp.where(near, raw, -1e30) - lse)
            grad_low, grad_low_t = grad_summaries[h]
            grad_from = dot_nn(grad_low, value)
            grad_scores = (probs * (grad_from - offsets[h])).astype(BF16)
            partial_value[head_rows, at] = dot_nn(grad_low_t, probs.astype(BF16))
            grad_q_land[h] += dot_nt(grad_scores, key)
            partial_key[head_rows, at] = dot_nn(q_land_t, grad_scores)

    eye = packed_identity()
    among_split = [split_low(among_in[h]) for h in range(heads)]
    for step in reversed(range(NS_ITERS)):
        for h in range(heads):
            approx = steps_in[h, 4 * step]
            product = steps_in[h, 4 * step + 1]
            second = steps_in[h, 4 * step + 2]
            third = steps_in[h, 4 * step + 3]
            first = 7.0 * eye - product
            approx_split = split_low(approx)
            approx_wide = tuple(spread(a, mask_b) for a in approx_split)
            product_wide = spread_split(product, mask_b)
            grad = carried[h]
            grad_third = 0.25 * dot_three(split_low(grad), approx_wide)
            third_split = split_low(grad_third)
            grad_second = -dot_three(third_split, product_wide)
            second_split = split_low(grad_second)
            grad_first = -dot_three(second_split, product_wide)
            grad_product = -(
                grad_first
                + dot_three(
                    split_low(second), tuple(spread(a, mask_b) for a in third_split)
                )
                + dot_three(
                    split_low(first), tuple(spread(a, mask_b) for a in second_split)
                )
            )
            product_split = split_low(grad_product)
            among_part = dot_three(
                approx_split, tuple(spread(a, mask_b) for a in product_split)
            )
            if step == NS_ITERS - 1:
                among_grads.append(among_part)
            else:
                among_grads[h] = among_grads[h] + among_part
            carried[h] = 0.25 * dot_three(
                split_low(third), spread_split(grad, mask_b)
            ) + dot_three(
                product_split, tuple(spread(a, mask_b) for a in among_split[h])
            )

    land_grads = []
    for h in range(heads):
        q_land_t, k_land_t, q_land, k_land = lands[h]
        among = spread(among_in[h], mask_f)
        column_sums = jnp.sum(among, axis=0, keepdims=True)
        column_top = jnp.max(column_sums, axis=1, keepdims=True)
        start = steps_in[h, 0]
        start_grad = carried[h]
        start_blocks = spread(start, mask_f).T
        top_grad = -jnp.sum(
            jnp.sum(start_grad * fold(start_blocks), axis=1, keepdims=True),
            axis=0,
            keepdims=True,
        ) / column_top
        at_top = jnp.where(column_sums == column_top, 1.0, 0.0)
        shared = top_grad * at_top / jnp.sum(at_top, axis=1, keepdims=True)
        among_grad = spread(among_grads[h], mask_f).T + (
            spread(start_grad, mask_f) / column_top + shared * mask_f
        )
        inner = jnp.sum(among_grad * among, axis=1, keepdims=True)
        grad_scores = among * (among_grad - inner)
        high, low = split_low(grad_scores)
        back_high, back_low = split_low(grad_scores.T)
        q_total = grad_q_land[h] + (dot_nn(high, k_land) + dot_nn(low, k_land))
        k_total = grad_k_land[h] + (dot_nn(back_high, q_land) + dot_nn(back_low, q_land))
        counts = landmark_counts(ends, 0)
        q_share = q_total.astype(BF16).astype(F32) / counts
        k_share = k_total.astype(BF16).astype(F32) / counts
        land_grads.append((split_low(q_share.T), split_low(k_share.T)))

    correlation[...] = jnp.zeros_like(correlation)

    @pl.loop(0, group_size // BAND_OUT)
    def _(i):
        start = i * BAND_OUT
        at = lane_slice(start, BAND_OUT)
        padded = lane_slice(PAD + start, BAND_OUT)
        around = lane_slice(start, BAND_IN)
        pool = pooling_tile(start, BAND_OUT, ends)
        same = band_mask(start, ends)
        same_f = jnp.where(same, 1.0, 0.0)
        same_b = same_f.astype(BF16)
        for h in range(heads):
            head_rows = slice(h * HEAD, (h + 1) * HEAD)
            key_rows = slice(width + h * HEAD, width + (h + 1) * HEAD)
            value_rows = slice(2 * width + h * HEAD, 2 * width + (h + 1) * HEAD)
            (q_high, q_low), (k_high, k_low) = land_grads[h]
            query = partial_query[head_rows, at] + (dot_nn(q_high, pool) + dot_nn(q_low, pool))
            key = partial_key[head_rows, at] + (dot_nn(k_high, pool) + dot_nn(k_low, pool))
            window = context_grad[head_rows, around]
            value = partial_value[head_rows, at] + (
                dot_nn(window, bands[h, 0] * same_b) + dot_nn(window, bands[h, 1] * same_b)
            )
            grad_qkv[head_rows, at] = query.astype(BF16)
            grad_qkv[key_rows, at] = key.astype(BF16)
            grad_qkv[value_rows, at] = value.astype(BF16)
            across = dot_tn(qkv_t[value_rows, around], context_grad[head_rows, padded])
            across = across * same_f
            correlation[h, 0] += across[:128, :128] + across[128:256, 128:]
            correlation[h, 1] += across[128:256, :128] + across[256:384, 128:]
            correlation[h, 2] += across[256:384, :128] + across[384:, 128:]

    apart = lax.broadcasted_iota(jnp.int32, (128, 128), 0) - lax.broadcasted_iota(
        jnp.int32, (128, 128), 1
    )
    lanes = lax.broadcasted_iota(jnp.int32, (8, 128), 1)
    rows = lax.broadcasted_iota(jnp.int32, (8, 128), 0)
    taps = jnp.zeros((8, 128), F32)
    for h in range(heads):
        for tap in range(KERNEL):
            away = tap - REACH
            picked = jnp.where(apart == away, correlation[h, 1], 0.0)
            if away < 0:
                picked += jnp.where(apart == away + 128, correlation[h, 0], 0.0)
            if away > 0:
                picked += jnp.where(apart == away - 128, correlation[h, 2], 0.0)
            total = jnp.sum(
                jnp.sum(picked, axis=0, keepdims=True), axis=1, keepdims=True
            )
            taps = taps + jnp.where((lanes == tap) & (rows == h), total, 0.0)
    grad_conv[...] = taps

    grad_w_t[...] = jnp.zeros_like(grad_w_t)
    for at, (x, d) in enumerate(((x0, d0), (x1, d1), (x2, d2), (x3, d3))):
        offset = (me ^ at) * block

        @pl.loop(0, 3)
        def _(part):
            rows = pl.ds(pl.multiple_of(part * width, width), width)
            grad_w_t[rows, :] += dot_nn(grad_qkv[rows, lane_slice(offset, block)], x[...])

        @pl.loop(0, block // 128)
        def _(piece):
            lanes = lane_slice(offset + piece * 128, 128)
            scaled = dot_tn(grad_qkv[: 2 * width, lanes], w_t[: 2 * width, :])
            plain = dot_tn(grad_qkv[2 * width :, lanes], w_t[2 * width :, :])
            d[pl.ds(pl.multiple_of(piece * 128, 128), 128), :] = (
                scaled * qk_scale + plain
            ).astype(BF16)

    grad_w_t[: 2 * width, :] = grad_w_t[: 2 * width, :] * qk_scale


def attend_back(scalars, saved, bands, grads, blocks, w_t):
    block, features = blocks[0].shape
    group_size = 4 * block
    width = w_t.shape[0] // 3
    heads = width // HEAD
    out_shape = (
        jax.ShapeDtypeStruct((3 * width, features), F32),
        jax.ShapeDtypeStruct((8, 128), F32),
        *[jax.ShapeDtypeStruct((block, features), BF16) for _ in range(4)],
    )
    vmem = pl.BlockSpec(memory_space=pltpu.VMEM)

    def kernel(*refs):
        attend_back_kernel(heads, *refs)

    operands = (scalars, *saved, bands, *grads, *blocks, w_t)
    return pl.pallas_call(
        kernel,
        name="attend_back",
        out_shape=out_shape,
        in_specs=[pl.BlockSpec(memory_space=pltpu.SMEM)] + [vmem] * (len(operands) - 1),
        out_specs=[vmem] * len(out_shape),
        scratch_shapes=[
            pltpu.VMEM((width, group_size + 2 * PAD), BF16),
            pltpu.VMEM((3 * width, group_size), BF16),
            pltpu.VMEM((width, group_size), F32),
            pltpu.VMEM((width, group_size), F32),
            pltpu.VMEM((width, group_size), F32),
            pltpu.VMEM((heads, MARKS, HEAD), F32),
            pltpu.VMEM((heads, MARKS, HEAD), F32),
            pltpu.VMEM((heads, MARKS, HEAD), F32),
            pltpu.VMEM((heads, 3, 128, 128), F32),
        ],
        compiler_params=pltpu.CompilerParams(vmem_limit_bytes=VMEM_LIMIT),
        cost_estimate=pl.CostEstimate(
            flops=30_000_000_000, bytes_accessed=40_000_000, transcendentals=4_000_000
        ),
    )(*operands)


def gelu_and_slope(values):
    z = jnp.abs(values) * 0.7071067811865476
    t = pl.reciprocal(1.0 + 0.5 * z)
    poly = t * 0.17087277 - 0.82215223
    for coefficient in (
        1.48851587,
        -1.13520398,
        0.27886807,
        -0.18628806,
        0.09678418,
        0.37409196,
        1.00002368,
        -1.26551223,
    ):
        poly = poly * t + coefficient
    bell = jnp.exp(-z * z)
    half_tail = (0.5 * t) * jnp.exp(poly) * bell
    below = jnp.where(values >= 0.0, 1.0 - half_tail, half_tail)
    return values * below, below + values * (bell * 0.3989422804014327)


def unit_norm(values):
    row_mean = jnp.mean(values, axis=-1, keepdims=True)
    centered = values - row_mean
    spread_out = jnp.mean(centered * centered, axis=-1, keepdims=True)
    recip = lax.rsqrt(spread_out + 1e-05)
    return (centered * recip, recip)


def unit_back(grad, unit, recip):
    mean_grad = jnp.mean(grad, axis=-1, keepdims=True)
    mean_cross = jnp.mean(grad * unit, axis=-1, keepdims=True)
    return recip * (grad - mean_grad - unit * mean_cross)


ROWS = 128
UNITS = 256


def feed_kernel(
    scalars,
    c0,
    c1,
    c2,
    c3,
    tokens,
    grad_output,
    w_out,
    norms,
    up0,
    up1,
    up2,
    up3,
    down0,
    down1,
    down2,
    down3,
    output,
    normed_out,
    branch_grad_out,
    resid_grad_out,
    grad_w_out,
    norm_grads,
    g0,
    g1,
    g2,
    g3,
    normed,
    unit_one,
    recip_one,
    hidden,
    slope,
    summed_grad,
    attended_grad,
):
    me = scalars[3]
    width, block = c0.shape
    features = tokens.shape[1]
    units = up0.shape[1]
    ups = (up0, up1, up2, up3)
    downs = (down0, down1, down2, down3)
    gain_one, shift_one = norms[0:1, :], norms[1:2, :]
    gain_two, shift_two = norms[2:3, :], norms[3:4, :]
    pieces = block // ROWS
    norm_grads[...] = jnp.zeros_like(norm_grads)

    def rows_of(i):
        return pl.ds(pl.multiple_of(i * ROWS, ROWS), ROWS)

    def weight_rows(at):
        return pl.ds(pl.multiple_of((me ^ at) * width, width), width)

    @pl.loop(0, pieces)
    def _(i):
        rows = rows_of(i)
        resid = tokens[rows, :].astype(F32)
        for at, c in enumerate((c0, c1, c2, c3)):
            resid += dot_tn(c[:, rows], w_out[weight_rows(at), :])
        unit, recip = unit_norm(resid)
        unit_one[rows, :] = unit
        recip_one[rows, :] = jnp.broadcast_to(recip, (ROWS, 128))
        value = unit * gain_one + shift_one
        normed[rows, :] = value
        normed_out[rows, :] = value.astype(BF16)

    for s, up in enumerate(ups):

        @pl.loop(0, units // UNITS)
        def _(j):
            columns = lane_slice(j * UNITS, UNITS)
            target = lane_slice(s * units + j * UNITS, UNITS)
            value, derivative = gelu_and_slope(dot_nn(normed_out[...], up[:, columns]))
            hidden[:, target] = value.astype(BF16)
            slope[:, target] = derivative

    @pl.loop(0, pieces)
    def _(i):
        rows = rows_of(i)
        total = normed[rows, :]
        for s, down in enumerate(downs):
            total += dot_nn(hidden[rows, s * units : (s + 1) * units], down[...])
        unit, recip = unit_norm(total)
        output[rows, :] = unit * gain_two + shift_two
        top = grad_output[rows, :].astype(F32)
        norm_grads[2:3, :] += jnp.sum(top * unit, axis=0, keepdims=True)
        norm_grads[3:4, :] += jnp.sum(top, axis=0, keepdims=True)
        grad = unit_back(top * gain_two, unit, recip)
        summed_grad[rows, :] = grad
        branch_grad_out[rows, :] = grad.astype(BF16)

    for s, down in enumerate(downs):

        @pl.loop(0, units // UNITS)
        def _(j):
            target = lane_slice(s * units + j * UNITS, UNITS)
            grad = dot_nt(
                branch_grad_out[...], down[pl.ds(pl.multiple_of(j * UNITS, UNITS), UNITS), :]
            )
            hidden[:, target] = (slope[:, target] * grad).astype(BF16)

    @pl.loop(0, pieces)
    def _(i):
        rows = rows_of(i)
        total = summed_grad[rows, :]
        for s, up in enumerate(ups):
            total += dot_nt(hidden[rows, s * units : (s + 1) * units], up[...])
        unit = unit_one[rows, :]
        norm_grads[0:1, :] += jnp.sum(total * unit, axis=0, keepdims=True)
        norm_grads[1:2, :] += jnp.sum(total, axis=0, keepdims=True)
        grad = unit_back(total * gain_one, unit, recip_one[rows, :1])
        resid_grad_out[rows, :] = grad
        attended_grad[rows, :] = grad.astype(BF16)

    for at, (c, g) in enumerate(((c0, g0), (c1, g1), (c2, g2), (c3, g3))):
        rows = weight_rows(at)
        g[...] = dot_nt(w_out[rows, :], attended_grad[...]).astype(BF16)
        grad_w_out[rows, :] = dot_nn(c[...], attended_grad[...])


def feed(scalars, contexts, tokens, grad_output, w_out, norms, ups, downs):
    width, block = contexts[0].shape
    features = tokens.shape[1]
    units = ups[0].shape[1]
    out_shape = (
        jax.ShapeDtypeStruct((block, features), F32),
        jax.ShapeDtypeStruct((block, features), BF16),
        jax.ShapeDtypeStruct((block, features), BF16),
        jax.ShapeDtypeStruct((block, features), F32),
        jax.ShapeDtypeStruct((features, features), F32),
        jax.ShapeDtypeStruct((8, features), F32),
        *[jax.ShapeDtypeStruct((width, block), BF16) for _ in range(4)],
    )
    vmem = pl.BlockSpec(memory_space=pltpu.VMEM)
    operands = (scalars, *contexts, tokens, grad_output, w_out, norms, *ups, *downs)
    return pl.pallas_call(
        feed_kernel,
        name="feed",
        out_shape=out_shape,
        in_specs=[pl.BlockSpec(memory_space=pltpu.SMEM)] + [vmem] * (len(operands) - 1),
        out_specs=[vmem] * len(out_shape),
        scratch_shapes=[
            pltpu.VMEM((block, features), F32),
            pltpu.VMEM((block, features), F32),
            pltpu.VMEM((block, 128), F32),
            pltpu.VMEM((block, 4 * units), BF16),
            pltpu.VMEM((block, 4 * units), F32),
            pltpu.VMEM((block, features), F32),
            pltpu.VMEM((block, features), BF16),
        ],
        compiler_params=pltpu.CompilerParams(vmem_limit_bytes=VMEM_LIMIT),
        cost_estimate=pl.CostEstimate(
            flops=25_000_000_000, bytes_accessed=30_000_000, transcendentals=6_000_000
        ),
    )(*operands)


def feed_weights_kernel(
    n0, n1, n2, n3, b0, b1, b2, b3, up, down, grad_up, grad_down, up_total, down_total
):
    units = up.shape[1]
    for at, (n, b) in enumerate(((n0, b0), (n1, b1), (n2, b2), (n3, b3))):

        @pl.loop(0, units // UNITS)
        def _(j):
            columns = lane_slice(j * UNITS, UNITS)
            rows = pl.ds(pl.multiple_of(j * UNITS, UNITS), UNITS)
            value, derivative = gelu_and_slope(dot_nn(n[...], up[:, columns]))
            grad_hidden = dot_nt(b[...], down[rows, :])
            grad_pre = (derivative * grad_hidden).astype(BF16)
            down_part = dot_tn(value.astype(BF16), b[...])
            up_part = dot_tn(n[...], grad_pre)
            if at == 0:
                down_total[rows, :] = down_part
                up_total[:, columns] = up_part
            elif at < 3:
                down_total[rows, :] += down_part
                up_total[:, columns] += up_part
            else:
                grad_down[rows, :] = (down_total[rows, :] + down_part).astype(BF16)
                grad_up[:, columns] = (up_total[:, columns] + up_part).astype(BF16)


def feed_weights(normeds, branch_grads, up, down):
    features, units = up.shape
    vmem = pl.BlockSpec(memory_space=pltpu.VMEM)
    return pl.pallas_call(
        feed_weights_kernel,
        name="feed_weights",
        out_shape=(
            jax.ShapeDtypeStruct((features, units), BF16),
            jax.ShapeDtypeStruct((units, features), BF16),
        ),
        in_specs=[vmem] * 10,
        out_specs=[vmem] * 2,
        scratch_shapes=[
            pltpu.VMEM((features, units), F32),
            pltpu.VMEM((units, features), F32),
        ],
        compiler_params=pltpu.CompilerParams(vmem_limit_bytes=VMEM_LIMIT),
        cost_estimate=pl.CostEstimate(
            flops=18_000_000_000, bytes_accessed=12_000_000, transcendentals=6_000_000
        ),
    )(*normeds, *branch_grads, up, down)


def to_partner(array, axis, size, bit):
    return lax.ppermute(array, axis, [(i, i ^ bit) for i in range(size)])


def gather_tensor(array):
    one = to_partner(array, "tensor", 4, 1)
    two = to_partner(array, "tensor", 4, 2)
    three = to_partner(two, "tensor", 4, 1)
    return (array, one, two, three)


def exchange_tensor(blocks):
    return (
        blocks[0],
        to_partner(blocks[1], "tensor", 4, 1),
        to_partner(blocks[2], "tensor", 4, 2),
        to_partner(blocks[3], "tensor", 4, 3),
    )


def make_bands(conv_weight):
    apart = (
        lax.broadcasted_iota(jnp.int32, (BAND_IN, BAND_OUT), 0)
        - PAD
        - lax.broadcasted_iota(jnp.int32, (BAND_IN, BAND_OUT), 1)
        + REACH
    )
    band = jnp.zeros((conv_weight.shape[0], BAND_IN, BAND_OUT), F32)
    for tap in range(KERNEL):
        band = jnp.where(apart[None] == tap, conv_weight[:, tap][:, None, None], band)
    return jnp.stack(split_low(band), axis=1)


def sum_dp(array, size):
    me = lax.axis_index("dp")
    bits = [1 << b for b in range(size.bit_length() - 1)]
    for bit in bits:
        half = array.shape[0] // 2
        low, high = array[:half], array[half:]
        mine = (me & bit) != 0
        got = to_partner(jnp.where(mine, low, high), "dp", size, bit)
        array = (jnp.where(mine, high, low).astype(F32) + got.astype(F32)).astype(array.dtype)
    for bit in reversed(bits):
        mine = (me & bit) != 0
        got = to_partner(array, "dp", size, bit)
        array = jnp.concatenate(
            [jnp.where(mine, got, array), jnp.where(mine, array, got)], axis=0
        )
    return array


def solution(mesh):
    dp_size = mesh.shape["dp"]

    def shards(
        tokens,
        w_query,
        w_key,
        w_value,
        conv_weight,
        w_out,
        gain_one,
        shift_one,
        w_up,
        w_down,
        gain_two,
        shift_two,
        lengths,
        grad_output,
    ):
        width = w_query.shape[1]
        heads = width // HEAD
        features = tokens.shape[1]
        me = lax.axis_index("tensor").astype(jnp.int32)
        scalars = jnp.concatenate([lengths[0], me[None]])
        blocks = gather_tensor(tokens)
        w_t = jnp.concatenate([w_query.T, w_key.T, w_value.T], axis=0)
        bands = make_bands(conv_weight)
        bands_back = make_bands(conv_weight[:, ::-1])
        norms = jnp.stack([gain_one, shift_one, gain_two, shift_two])
        ups = gather_tensor(w_up)
        downs = gather_tensor(w_down)

        attended = attend(scalars, blocks, w_t, bands)
        saved = (attended[0], *attended[5:])
        contexts = exchange_tensor(attended[1:5])
        (
            output,
            normed_low,
            branch_grad,
            resid_grad,
            grad_w_out,
            norm_grads,
            *context_grads,
        ) = feed(scalars, contexts, tokens, grad_output, w_out, norms, ups, downs)
        context_grads = exchange_tensor(context_grads)
        normeds = gather_tensor(normed_low)
        branch_grads = gather_tensor(branch_grad)
        grad_up, grad_down = feed_weights(normeds, branch_grads, w_up, w_down)
        ffn_grads = sum_dp(jnp.concatenate([grad_up, grad_down], axis=0), dp_size)

        grad_w_t, taps, *token_grads = attend_back(
            scalars, saved, bands_back, context_grads, blocks, w_t
        )
        got = (
            to_partner(token_grads[1], "tensor", 4, 1),
            to_partner(token_grads[3], "tensor", 4, 1),
        )
        away = (token_grads[2].astype(F32) + got[1].astype(F32)).astype(BF16)
        here = token_grads[0].astype(F32) + got[0].astype(F32)
        arrived = to_partner(away, "tensor", 4, 2)
        grad_tokens = resid_grad + here + arrived.astype(F32)

        qkv_grads = sum_dp(grad_w_t.astype(BF16), dp_size)
        taps = lax.psum(taps, "dp")
        small = lax.psum(
            jnp.concatenate([grad_w_out, norm_grads], axis=0).astype(BF16), ("dp", "tensor")
        ).astype(F32)
        qkv_wide = qkv_grads.astype(F32)
        return (
            output,
            grad_tokens,
            qkv_wide[:width].T,
            qkv_wide[width : 2 * width].T,
            qkv_wide[2 * width :].T,
            taps[:heads, :KERNEL],
            small[:features],
            small[features],
            small[features + 1],
            ffn_grads[:features].astype(F32),
            ffn_grads[features:].astype(F32),
            small[features + 2],
            small[features + 3],
        )

    rows = P(("dp", "tensor"), None)
    columns = P(None, "tensor")
    in_specs = (
        rows,
        columns,
        columns,
        columns,
        P("tensor", None),
        P(),
        P(),
        P(),
        columns,
        P("tensor", None),
        P(),
        P(),
        P("dp", None),
        rows,
    )
    out_specs = (
        rows,
        rows,
        columns,
        columns,
        columns,
        P("tensor", None),
        P(),
        P(),
        P(),
        columns,
        P("tensor", None),
        P(),
        P(),
    )
    return jax.shard_map(shards, mesh=mesh, in_specs=in_specs, out_specs=out_specs, check_vma=False)
```

time: 972 us -> 602 us (0.62)
  matrix products: 214 us -> 0 us
  Pallas kernels: 0 us -> 172 us
  waiting for transfers between devices: 475 us -> 305 us
  blocking collectives: 93.5 us -> 21.5 us
  other arithmetic: 109 us -> 37.2 us
  local copies, waits for them, and re-layouts: 47.9 us -> 11.4 us
  starting transfers between devices: 4.09 us -> 30.9 us
    ppermute x0 -> x36, waiting for transfers between devices: none -> 212 us  [to_partner(): return lax.ppermute(array, axis, [(i, i ^ bit) for i in range(size)])]
    dot_general x108 -> x0, matrix products: 211 us -> none  [the longest x36 33.5 us: iterative_pseudoinverse(): jnp.einsum('hij,hjk->hik', product, bracket, precision=TOP_PRECISION)]
    psum x2 -> x1, waiting for transfers between devices: 287 us -> 93 us  [shards(): lax.psum(jnp.concatenate([grad_w_out, norm_grads], axis=0).astype(BF16),...]
    pallas_call x0 -> x4, Pallas kernels: none -> 172 us  [the longest x1 57 us: attend_back(): pl.pallas_call(kernel, name='attend_back', out_shape=out_shape, in_specs=...]
    all_gather x3 -> x0, waiting for transfers between devices: 90.1 us -> none  [the longest x1 33.1 us: shards(): normed_group = lax.all_gather(normed_low, 'tensor', axis=0, tiled=True)]
    reduce_scatter x3 -> x0, waiting for transfers between devices: 84.1 us -> none  [the longest x1 43 us: shards(): lax.psum_scatter(jnp.dot(hidden, w_down, preferred_element_type=jnp.float...]
    psum x2 -> x1, blocking collectives: 77.4 us -> 21.5 us  [shards(): taps = lax.psum(taps, 'dp')]
    reduce_sum x19 -> x0, other arithmetic: 37.4 us -> none  [the longest x6 22.4 us: convolve(): summed = summed + shifted * conv_weight[:, offset][None, :, None]]
  transfers between devices with their start and end apart: 9 -> 37, of which waited for: 8 -> 17; matrix products, arithmetic and copies ran while one was open for 6% -> 7% of each run, Pallas kernels for 0% -> 16%
where the time goes in v1:
time: 602 us; the launch traced here: 593 us
  waiting for transfers between devices  305 us (51%)
  Pallas kernels  172 us (29%)
  other arithmetic  37.2 us (6%)
  starting transfers between devices  30.9 us (5%)
  blocking collectives  21.5 us (4%)
  between operations  15.4 us (3%)
  local copies, waits for them, and re-layouts  11.4 us (2%)
    ppermute x36, waiting for transfers between devices, to_partner(): return lax.ppermute(array, axis, [(i, i ^ bit) for i in range(size)])  212 us
    psum x1, waiting for transfers between devices, shards(): lax.psum(jnp.concatenate([grad_w_out, norm_grads], axis=0).astype(BF16),...  93 us
    pallas_call x1, Pallas kernels, attend_back(): pl.pallas_call(kernel, name='attend_back', out_shape=out_shape, in_specs=...  57 us
    pallas_call x1, Pallas kernels, feed(): pl.pallas_call(feed_kernel, name='feed', out_shape=out_shape, in_specs=[p...  47.2 us
    pallas_call x1, Pallas kernels, attend(): pl.pallas_call(kernel, name='attend', out_shape=out_shape, in_specs=[pl.B...  37.6 us
    ppermute x36, starting transfers between devices, to_partner(): return lax.ppermute(array, axis, [(i, i ^ bit) for i in range(size)])  30.9 us
    pallas_call x1, Pallas kernels, feed_weights(): pl.pallas_call(feed_weights_kernel, name='feed_weights', out_shape=(jax.S...  30.3 us
    psum x1, blocking collectives, shards(): taps = lax.psum(taps, 'dp')  21.5 us
  transfers between devices with their start and end apart: 37, of which 17 were waited for; matrix products, arithmetic and copies ran while one was open for 7% of the time, Pallas kernels for 16%

profile of v1, /device:TPU:0, one launch (start us, length us, event | category | flops | bytes accessed | tf_op | source)
XLA Modules:
  0.0 593.0 jit_solution(713491544171701754)
XLA Ops:
  7.2 3.0 collective-permute-start.1
  10.7 1.7 collective-permute-start.10
  12.5 1.6 slice_reduce_fusion.35
  14.1 1.9 slice_reduce_fusion.36
  16.2 1.2 pad_add_fusion.refs_0_.scalars
  17.4 2.1 pad_maximum_fusion.4.refs_5_.refs_19_
  19.5 3.3 fusion.32
  23.0 10.1 %collective-permute-done.1.refs_3_.refs_17_ = bf16[640,768]{1,0:T(8,128)(2,1)} collective-permute-done((bf16[640,768]{1,0:T(8,128)(2,1)}, bf16[640,768]{1,0:T(8,128)(2,1)}, u32[]{:S(2)}, u32[]{:S(2)}) %collective-permute-start.1) | collective-permute-done | bytes 983072 | tf_op jit(solution)/shard_map/ppermute | solution.py:895
  33.3 5.0 subtract_convert_fusion.1
  38.4 1.3 pad_maximum_fusion.refs_6_
  40.6 17.8 %collective-permute-done.7.up2 = bf16[768,768]{1,0:T(8,128)(2,1)} collective-permute-done((bf16[768,768]{1,0:T(8,128)(2,1)}, bf16[768,768]{1,0:T(8,128)(2,1)}, u32[]{:S(2)}, u32[]{:S(2)}) %collective-permute-start.7) | collective-permute-done | bytes 1179680 | tf_op jit(solution)/shard_map/ppermute | solution.py:895
  58.4 24.4 %collective-permute-done.10.down2 = bf16[768,768]{1,0:T(8,128)(2,1)} collective-permute-done((bf16[768,768]{1,0:T(8,128)(2,1)}, bf16[768,768]{1,0:T(8,128)(2,1)}, u32[]{:S(2)}, u32[]{:S(2)}) %collective-permute-start.10) | collective-permute-done | bytes 1179680 | tf_op jit(solution)/shard_map/ppermute | solution.py:895
  82.9 37.6 %attend.1 = (bf16[576,2816]{1,0:T(8,128)(2,1)}, bf16[192,640]{1,0:T(8,128)(2,1)}, bf16[192,640]{1,0:T(8,128)(2,1)}, bf16[192,640]{1,0:T(8,128)(2,1)}, bf16[192,6...) custom-call(s32[4]{0:T(128)} %pad_add_fusion.refs_0_.scalars, ...), custom_call_target="tpu_custom_call" | custom-call | flops 15000000512 | bytes 20000000 | tf_op jit(solution)/shard_map/attend/pallas_call | solution.py:320
  120.4 0.5 collective-permute-start.3
  120.9 1.7 collective-permute-start.4
  122.8 0.6 pad_maximum_fusion.8.norms
  123.4 6.7 %collective-permute-done.4.c2 = bf16[192,640]{1,0:T(8,128)(2,1)} collective-permute-done((bf16[192,640]{1,0:T(8,128)(2,1)}, bf16[192,640]{1,0:T(8,128)(2,1)}, u32[]{:S(2)}, u32[]{:S(2)}) %collective-permute-start.4) | collective-permute-done | bytes 245792 | tf_op jit(solution)/shard_map/ppermute | solution.py:895
  130.1 3.6 collective-permute-done.5.c3
  133.7 0.7 copy-done.48
  134.4 47.2 %feed.1 = (f32[640,768]{1,0:T(8,128)}, bf16[640,768]{1,0:T(8,128)(2,1)}, bf16[640,768]{1,0:T(8,128)(2,1)}, f32[640,768]{1,0:T(8,128)}, f32[768,768]{1,0:T(8,128)...) custom-call(s32[4]{0:T(128)} %pad_add_fusion.refs_0_.scalars, ...), custom_call_target="tpu_custom_call" | custom-call | flops 24999999488 | bytes 30000000 | tf_op jit(solution)/shard_map/feed/pallas_call | solution.py:823
  181.6 0.5 collective-permute-start.12
  182.1 1.7 collective-permute-start.13
  183.9 1.4 collective-permute-start.25
  185.3 0.6 collective-permute-start.28
  185.9 6.4 %subtract_convert_fusion = (bf16[3,1,512,256]{3,2,1,0:T(8,128)(2,1)S(1)}, bf16[3,1,512,256]{3,2,1,0:T(8,128)(2,1)S(1)}) fusion(f32[3]{0:T(128)S(1)} %get-tuple-element.79, pred[512,256]{1,0:T(8,128)(4,1)S(1)} %get-tuple-element.132, f32[3]{0:T(128)S(1)} %get-tuple-element.98, pred[512,256]{1,0:T(8,128)(4,1)S(1)} %get-tuple-element.133, ...), kind=kLoop, calls=%fused_computation.5 | loop fusion | flops 14548992 | bytes 5898636 | tf_op jit(solution)/shard_map/convert_element_type | solution.py:38
  192.3 1.3 pad_maximum_fusion.1.refs_10_
  193.9 0.5 collective-permute-start.27
  194.4 23.2 %collective-permute-done.25.n2 = bf16[640,768]{1,0:T(8,128)(2,1)} collective-permute-done((bf16[640,768]{1,0:T(8,128)(2,1)}, bf16[640,768]{1,0:T(8,128)(2,1)}, u32[]{:S(2)}, u32[]{:S(2)}) %collective-permute-start.25) | collective-permute-done | bytes 983072 | tf_op jit(solution)/shard_map/ppermute | solution.py:895
  217.6 20.2 %collective-permute-done.28.b2 = bf16[640,768]{1,0:T(8,128)(2,1)} collective-permute-done((bf16[640,768]{1,0:T(8,128)(2,1)}, bf16[640,768]{1,0:T(8,128)(2,1)}, u32[]{:S(2)}, u32[]{:S(2)}) %collective-permute-start.28) | collective-permute-done | bytes 983072 | tf_op jit(solution)/shard_map/ppermute | solution.py:895
  237.8 57.0 %attend_back.1 = (f32[576,768]{1,0:T(8,128)}, f32[8,128]{1,0:T(8,128)}, bf16[640,768]{1,0:T(8,128)(2,1)}, bf16[640,768]{1,0:T(8,128)(2,1)}, bf16[640,768]{1,0:T(8,128)(2,1)}, /*index=5*/bf16[640,768]{1,0:T(8,128)(2,1)}) custom-call(s32[4]{0:T(128)} %pad_add_fusion.refs_0_.scalars, bf16[576,2816]{1,0:T(8,128)(2,1)} %get-tuple-element.50.refs_1_, ...), custom_call_target="tpu_custom_call" | custom-call | flops 30000001024 | bytes 40000000 | tf_op jit(solution)/shard_map/attend_back/pallas_call | solution.py:625
  294.8 1.6 convert_element_type.168
  296.4 0.9 copy-done.46
  297.3 30.3 %feed_weights.1 = (bf16[768,768]{1,0:T(8,128)(2,1)}, bf16[768,768]{1,0:T(8,128)(2,1)}) custom-call(bf16[640,768]{1,0:T(8,128)(2,1)} %get-tuple-element.71.n0, bf16[640,768]{1,0:T(8,128)(2,1)} %copy-done.46, bf16[640,768]{1,0:T(8,128)(2,1)} %collective-permute-done.25.n2, bf16[640,768]{1,0:T(8,128)(2,1)} %collective-permute-done.26.n3, ...), custom_call_target="tpu_custom_call" | custom-call | flops 17999998976 | bytes 12000000 | tf_op jit(solution)/shard_map/feed_weights/pallas_call | solution.py:874
  327.6 2.6 broadcast_select_fusion
  330.2 1.8 collective-permute-start.30
  332.0 0.8 broadcast_select_fusion.6
  333.2 35.2 %collective-permute-done.18 = bf16[288,768]{1,0:T(8,128)(2,1)} collective-permute-done((bf16[288,768]{1,0:T(8,128)(2,1)}, bf16[288,768]{1,0:T(8,128)(2,1)}, u32[]{:S(2)}, u32[]{:S(2)}) %collective-permute-start.18) | collective-permute-done | bytes 442400 | tf_op jit(solution)/shard_map/ppermute | solution.py:895
  368.4 1.2 add_convert_fusion.3
  369.6 1.9 collective-permute-start.19
  371.5 1.8 add_convert_fusion
  373.6 1.1 pad_maximum_fusion.2
  374.8 3.2 collective-permute-done.19
  378.1 0.7 broadcast_select_fusion.15
  378.8 2.8 collective-permute-start.20
  381.6 13.1 %collective-permute-done.31 = bf16[384,768]{1,0:T(8,128)(2,1)S(1)} collective-permute-done((bf16[384,768]{1,0:T(8,128)(2,1)S(1)}, bf16[384,768]{1,0:T(8,128)(2,1)S(1)}, u32[]{:S(2)}, u32[]{:S(2)}) %collective-permute-start.31) | collective-permute-done | bytes 589856 | tf_op jit(solution)/shard_map/ppermute | solution.py:895
  394.9 2.8 collective-permute-start.32
  397.7 21.5 %psum.14 = f32[8,128]{1,0:T(8,128)S(1)} all-reduce(f32[8,128]{1,0:T(8,128)S(1)} %copy-done.43), channel_id=1, replica_groups=mesh['dp'=8,'tensor'=4] {'dp'}, use_global_device_ids=true, to_apply=%region_0.1 | all-reduce | flops 1024 | bytes 8192 | tf_op jit(solution)/shard_map/psum | solution.py:1008
  419.2 0.6 slice.264
  420.3 93.0 %all-reduce.2.cloned.1.call-done = bf16[776,768]{1,0:T(8,128)(2,1)} async-done(((bf16[776,768]{1,0:T(8,128)(2,1)}), bf16[776,768]{1,0:T(8,128)(2,1)}) %all-reduce.2.cloned.1.call-update) | async-done | bytes 1191952 | tf_op jit(solution)/shard_map/psum | solution.py:1009
  513.3 2.9 slice.283
  516.5 2.7 collective-permute-start.21
  519.7 11.5 %collective-permute-done.21 = bf16[72,768]{1,0:T(8,128)(2,1)S(1)} collective-permute-done((bf16[72,768]{1,0:T(8,128)(2,1)S(1)}, bf16[72,768]{1,0:T(8,128)(2,1)S(1)}, u32[]{:S(2)}, u32[]{:S(2)}) %collective-permute-start.21) | collective-permute-done | bytes 110624 | tf_op jit(solution)/shard_map/ppermute | solution.py:895
  531.4 6.2 %collective-permute-done.33 = bf16[192,768]{1,0:T(8,128)(2,1)S(1)} collective-permute-done((bf16[192,768]{1,0:T(8,128)(2,1)S(1)}, bf16[192,768]{1,0:T(8,128)(2,1)S(1)}, u32[]{:S(2)}, u32[]{:S(2)}) %collective-permute-start.33) | collective-permute-done | bytes 294944 | tf_op jit(solution)/shard_map/ppermute | solution.py:895
  538.1 1.5 collective-permute-start.17
  539.6 2.7 collective-permute-done.22
  542.4 1.5 collective-permute-start.23
  543.9 10.9 %collective-permute-done.34 = bf16[384,768]{1,0:T(8,128)(2,1)S(1)} collective-permute-done((bf16[384,768]{1,0:T(8,128)(2,1)S(1)}, bf16[384,768]{1,0:T(8,128)(2,1)S(1)}, u32[]{:S(2)}, u32[]{:S(2)}) %collective-permute-start.34) | collective-permute-done | bytes 589856 | tf_op jit(solution)/shard_map/ppermute | solution.py:895
  555.2 1.5 collective-permute-start.35
  556.7 0.6 slice_reduce_fusion
  557.6 1.2 slice_bitcast_fusion
  558.9 2.9 collective-permute-done.17
  561.8 1.7 convert_add_fusion
  563.5 19.6 %collective-permute-done.35 = bf16[768,768]{1,0:T(8,128)(2,1)S(1)} collective-permute-done((bf16[768,768]{1,0:T(8,128)(2,1)S(1)}, bf16[768,768]{1,0:T(8,128)(2,1)S(1)}, u32[]{:S(2)}, u32[]{:S(2)}) %collective-permute-start.35) | collective-permute-done | bytes 1179680 | tf_op jit(solution)/shard_map/ppermute | solution.py:895
  583.1 2.6 select_convert_fusion
  (163 shorter events, 5.6 us)
Async XLA Ops:
  7.2 506.1 %all-reduce.2.cloned.1.call-start = ((), (), s32[]{:S(2)}) async-start(), calls=%async_computation | async-start | bytes 2383872 | tf_op jit(solution)/shard_map/psum | solution.py:1009
  7.2 25.9 %collective-permute-start.1 = (bf16[640,768]{1,0:T(8,128)(2,1)}, bf16[640,768]{1,0:T(8,128)(2,1)}, u32[]{:S(2)}, u32[]{:S(2)}) collective-permute-start(bf16[640,768]{1,0:T(8,128)(2,1)} %refs_15_.1), channel_id=1, source_target_pairs={{0,2},{1,3},{2,0},{3,1},{4,6},{5,7},{6,4},{7,5},{8,10},{9,11},{10,... | collective-permute-start | bytes 2949128 | tf_op jit(solution)/shard_map/ppermute | solution.py:895
  10.2 29.5 %collective-permute-start = (bf16[640,768]{1,0:T(8,128)(2,1)}, bf16[640,768]{1,0:T(8,128)(2,1)}, u32[]{:S(2)}, u32[]{:S(2)}) collective-permute-start(bf16[640,768]{1,0:T(8,128)(2,1)} %refs_15_.1), channel_id=1, source_target_pairs={{0,1},{1,0},{2,3},{3,2},{4,5},{5,4},{6,7},{7,6},{8,9},{9,8},{10,11... | collective-permute-start | bytes 2949128 | tf_op jit(solution)/shard_map/ppermute | solution.py:895
  10.2 48.2 %collective-permute-start.7 = (bf16[768,768]{1,0:T(8,128)(2,1)}, bf16[768,768]{1,0:T(8,128)(2,1)}, u32[]{:S(2)}, u32[]{:S(2)}) collective-permute-start(bf16[768,768]{1,0:T(8,128)(2,1)} %up.1), channel_id=1, source_target_pairs={{0,2},{1,3},{2,0},{3,1},{4,6},{5,7},{6,4},{7,5},{8,10},{9,11},{10,... | collective-permute-start | bytes 3538952 | tf_op jit(solution)/shard_map/ppermute | solution.py:895
  10.4 110.5 %collective-permute-start.6 = (bf16[768,768]{1,0:T(8,128)(2,1)}, bf16[768,768]{1,0:T(8,128)(2,1)}, u32[]{:S(2)}, u32[]{:S(2)}) collective-permute-start(bf16[768,768]{1,0:T(8,128)(2,1)} %up.1), channel_id=1, source_target_pairs={{0,1},{1,0},{2,3},{3,2},{4,5},{5,4},{6,7},{7,6},{8,9},{9,8},{10,11... | collective-permute-start | bytes 3538952 | tf_op jit(solution)/shard_map/ppermute | solution.py:895
  10.7 72.1 %collective-permute-start.10 = (bf16[768,768]{1,0:T(8,128)(2,1)}, bf16[768,768]{1,0:T(8,128)(2,1)}, u32[]{:S(2)}, u32[]{:S(2)}) collective-permute-start(bf16[768,768]{1,0:T(8,128)(2,1)} %down.1), channel_id=1, source_target_pairs={{0,2},{1,3},{2,0},{3,1},{4,6},{5,7},{6,4},{7,5},{8,10},{9,11},{10,... | collective-permute-start | bytes 3538952 | tf_op jit(solution)/shard_map/ppermute | solution.py:895
  16.0 17.1 %copy-start.22 = (f32[3]{0:T(128)}, f32[3]{0:T(128)S(1)}, u32[]{:S(2)}) copy-start(f32[3]{0:T(128)S(1)} %get-tuple-element.81) | copy-start | bytes 40
  16.0 17.1 %copy-start.23 = (f32[3]{0:T(128)}, f32[3]{0:T(128)S(1)}, u32[]{:S(2)}) copy-start(f32[3]{0:T(128)S(1)} %get-tuple-element.82) | copy-start | bytes 40
  16.0 17.1 %copy-start.24 = (f32[3]{0:T(128)}, f32[3]{0:T(128)S(1)}, u32[]{:S(2)}) copy-start(f32[3]{0:T(128)S(1)} %get-tuple-element.83) | copy-start | bytes 40
  16.0 17.1 %copy-start.25 = (f32[3]{0:T(128)}, f32[3]{0:T(128)S(1)}, u32[]{:S(2)}) copy-start(f32[3]{0:T(128)S(1)} %get-tuple-element.84) | copy-start | bytes 40
  16.0 17.1 %copy-start.26 = (f32[3]{0:T(128)}, f32[3]{0:T(128)S(1)}, u32[]{:S(2)}) copy-start(f32[3]{0:T(128)S(1)} %get-tuple-element.85) | copy-start | bytes 40
  16.0 17.1 %copy-start.27 = (f32[3]{0:T(128)}, f32[3]{0:T(128)S(1)}, u32[]{:S(2)}) copy-start(f32[3]{0:T(128)S(1)} %get-tuple-element.86) | copy-start | bytes 40
  16.0 17.1 %copy-start.28 = (f32[3]{0:T(128)}, f32[3]{0:T(128)S(1)}, u32[]{:S(2)}) copy-start(f32[3]{0:T(128)S(1)} %get-tuple-element.87) | copy-start | bytes 40
  16.1 17.1 %copy-start.29 = (f32[3]{0:T(128)}, f32[3]{0:T(128)S(1)}, u32[]{:S(2)}) copy-start(f32[3]{0:T(128)S(1)} %get-tuple-element.88) | copy-start | bytes 40
  16.1 17.1 %copy-start.30 = (f32[3]{0:T(128)}, f32[3]{0:T(128)S(1)}, u32[]{:S(2)}) copy-start(f32[3]{0:T(128)S(1)} %get-tuple-element.89) | copy-start | bytes 40
  16.1 17.1 %copy-start.31 = (f32[3]{0:T(128)}, f32[3]{0:T(128)S(1)}, u32[]{:S(2)}) copy-start(f32[3]{0:T(128)S(1)} %get-tuple-element.90) | copy-start | bytes 40
  16.1 17.1 %copy-start.32 = (f32[3]{0:T(128)}, f32[3]{0:T(128)S(1)}, u32[]{:S(2)}) copy-start(f32[3]{0:T(128)S(1)} %get-tuple-element.91) | copy-start | bytes 40
  16.1 17.1 %copy-start.33 = (f32[3]{0:T(128)}, f32[3]{0:T(128)S(1)}, u32[]{:S(2)}) copy-start(f32[3]{0:T(128)S(1)} %get-tuple-element.92) | copy-start | bytes 40
  16.1 17.1 %copy-start.34 = (f32[3]{0:T(128)}, f32[3]{0:T(128)S(1)}, u32[]{:S(2)}) copy-start(f32[3]{0:T(128)S(1)} %get-tuple-element.93) | copy-start | bytes 40
  16.1 17.1 %copy-start.35 = (f32[3]{0:T(128)}, f32[3]{0:T(128)S(1)}, u32[]{:S(2)}) copy-start(f32[3]{0:T(128)S(1)} %get-tuple-element.94) | copy-start | bytes 40
  16.1 17.1 %copy-start.36 = (f32[3]{0:T(128)}, f32[3]{0:T(128)S(1)}, u32[]{:S(2)}) copy-start(f32[3]{0:T(128)S(1)} %get-tuple-element.95) | copy-start | bytes 40
  16.1 17.1 %copy-start.37 = (f32[3]{0:T(128)}, f32[3]{0:T(128)S(1)}, u32[]{:S(2)}) copy-start(f32[3]{0:T(128)S(1)} %get-tuple-element.96) | copy-start | bytes 40
  16.1 17.1 %copy-start.38 = (f32[3]{0:T(128)}, f32[3]{0:T(128)S(1)}, u32[]{:S(2)}) copy-start(f32[3]{0:T(128)S(1)} %get-tuple-element.97) | copy-start | bytes 40
  22.9 15.4 %copy-start.5 = (pred[512,256]{1,0:T(8,128)(4,1)}, pred[512,256]{1,0:T(8,128)(4,1)S(1)}, u32[]{:S(2)}) copy-start(pred[512,256]{1,0:T(8,128)(4,1)S(1)} %get-tuple-element.150) | copy-start | bytes 393220
  22.9 15.4 %copy-start.6 = (pred[512,256]{1,0:T(8,128)(4,1)}, pred[512,256]{1,0:T(8,128)(4,1)S(1)}, u32[]{:S(2)}) copy-start(pred[512,256]{1,0:T(8,128)(4,1)S(1)} %get-tuple-element.151) | copy-start | bytes 393220
  33.1 49.7 %collective-permute-start.2 = (bf16[640,768]{1,0:T(8,128)(2,1)}, bf16[640,768]{1,0:T(8,128)(2,1)}, u32[]{:S(2)}, u32[]{:S(2)}) collective-permute-start(bf16[640,768]{1,0:T(8,128)(2,1)} %collective-permute-done.1.refs_3_.refs_17_), channel_id=1, source_target_pairs={{0,1},{1,0},{2,3},{3,2},{4,5},{5,4},{6,7},{7,6},{8,9},{9,8},{10,11... | collective-permute-start | bytes 2949128 | tf_op jit(solution)/shard_map/ppermute | solution.py:895
  39.7 83.0 %copy-start.39 = (f32[768]{0:T(1024)S(1)}, f32[768]{0:T(1024)}, u32[]{:S(2)}) copy-start(f32[768]{0:T(1024)} %param.20) | copy-start | bytes 9220
  39.7 83.0 %copy-start.40 = (f32[768]{0:T(1024)S(1)}, f32[768]{0:T(1024)}, u32[]{:S(2)}) copy-start(f32[768]{0:T(1024)} %param.21) | copy-start | bytes 9220
  39.7 83.0 %copy-start.41 = (f32[768]{0:T(1024)S(1)}, f32[768]{0:T(1024)}, u32[]{:S(2)}) copy-start(f32[768]{0:T(1024)} %param.24) | copy-start | bytes 9220
  39.7 83.1 %copy-start.42 = (f32[768]{0:T(1024)S(1)}, f32[768]{0:T(1024)}, u32[]{:S(2)}) copy-start(f32[768]{0:T(1024)} %param.25) | copy-start | bytes 9220
  40.1 82.5 %collective-permute-start.9 = (bf16[768,768]{1,0:T(8,128)(2,1)S(1)}, bf16[768,768]{1,0:T(8,128)(2,1)}, u32[]{:S(2)}, u32[]{:S(2)}) collective-permute-start(bf16[768,768]{1,0:T(8,128)(2,1)S(1)} %copy-done.44), channel_id=1, source_target_pairs={{0,1},{1,0},{2,3},{3,2},{4,5},{5,4},{6,7},{7,6},{8,9},{9,8},{10,11... | collective-permute-start | bytes 3538952 | tf_op jit(solution)/shard_map/ppermute | solution.py:895
  58.4 75.3 %collective-permute-start.8 = (bf16[768,768]{1,0:T(8,128)(2,1)}, bf16[768,768]{1,0:T(8,128)(2,1)}, u32[]{:S(2)}, u32[]{:S(2)}) collective-permute-start(bf16[768,768]{1,0:T(8,128)(2,1)} %collective-permute-done.7.up2), channel_id=1, source_target_pairs={{0,1},{1,0},{2,3},{3,2},{4,5},{5,4},{6,7},{7,6},{8,9},{9,8},{10,11... | collective-permute-start | bytes 3538952 | tf_op jit(solution)/shard_map/ppermute | solution.py:895
  82.9 50.9 %collective-permute-start.11 = (bf16[768,768]{1,0:T(8,128)(2,1)}, bf16[768,768]{1,0:T(8,128)(2,1)}, u32[]{:S(2)}, u32[]{:S(2)}) collective-permute-start(bf16[768,768]{1,0:T(8,128)(2,1)} %collective-permute-done.10.down2), channel_id=1, source_target_pairs={{0,1},{1,0},{2,3},{3,2},{4,5},{5,4},{6,7},{7,6},{8,9},{9,8},{10,11... | collective-permute-start | bytes 3538952 | tf_op jit(solution)/shard_map/ppermute | solution.py:895
  120.4 3.0 collective-permute-start.3
  120.9 9.1 %collective-permute-start.4 = (bf16[192,640]{1,0:T(8,128)(2,1)}, bf16[192,640]{1,0:T(8,128)(2,1)}, u32[]{:S(2)}, u32[]{:S(2)}) collective-permute-start(bf16[192,640]{1,0:T(8,128)(2,1)} %get-tuple-element.46), channel_id=1, source_target_pairs={{0,2},{1,3},{2,0},{3,1},{4,6},{5,7},{6,4},{7,5},{8,10},{9,11},{10,... | collective-permute-start | bytes 737288 | tf_op jit(solution)/shard_map/ppermute | solution.py:895
  122.7 11.0 %collective-permute-start.5 = (bf16[192,640]{1,0:T(8,128)(2,1)}, bf16[192,640]{1,0:T(8,128)(2,1)S(1)}, u32[]{:S(2)}, u32[]{:S(2)}) collective-permute-start(bf16[192,640]{1,0:T(8,128)(2,1)} %get-tuple-element.47), channel_id=1, source_target_pairs={{0,3},{1,2},{2,1},{3,0},{4,7},{5,6},{6,5},{7,4},{8,11},{9,10},{10,... | collective-permute-start | bytes 737288 | tf_op jit(solution)/shard_map/ppermute | solution.py:895
  181.6 12.0 %collective-permute-start.12 = (bf16[192,640]{1,0:T(8,128)(2,1)}, bf16[192,640]{1,0:T(8,128)(2,1)}, u32[]{:S(2)}, u32[]{:S(2)}) collective-permute-start(bf16[192,640]{1,0:T(8,128)(2,1)} %get-tuple-element.60), channel_id=1, source_target_pairs={{0,1},{1,0},{2,3},{3,2},{4,5},{5,4},{6,7},{7,6},{8,9},{9,8},{10,11... | collective-permute-start | bytes 737288 | tf_op jit(solution)/shard_map/ppermute | solution.py:895
  182.1 11.7 %collective-permute-start.13 = (bf16[192,640]{1,0:T(8,128)(2,1)}, bf16[192,640]{1,0:T(8,128)(2,1)}, u32[]{:S(2)}, u32[]{:S(2)}) collective-permute-start(bf16[192,640]{1,0:T(8,128)(2,1)} %get-tuple-element.61), channel_id=1, source_target_pairs={{0,2},{1,3},{2,0},{3,1},{4,6},{5,7},{6,4},{7,5},{8,10},{9,11},{10,... | collective-permute-start | bytes 737288 | tf_op jit(solution)/shard_map/ppermute | solution.py:895
  183.9 53.9 %collective-permute-start.14 = (bf16[192,640]{1,0:T(8,128)(2,1)}, bf16[192,640]{1,0:T(8,128)(2,1)}, u32[]{:S(2)}, u32[]{:S(2)}) collective-permute-start(bf16[192,640]{1,0:T(8,128)(2,1)} %get-tuple-element.62), channel_id=1, source_target_pairs={{0,3},{1,2},{2,1},{3,0},{4,7},{5,6},{6,5},{7,4},{8,11},{9,10},{10,... | collective-permute-start | bytes 737288 | tf_op jit(solution)/shard_map/ppermute | solution.py:895
  183.9 33.7 %collective-permute-start.25 = (bf16[640,768]{1,0:T(8,128)(2,1)}, bf16[640,768]{1,0:T(8,128)(2,1)}, u32[]{:S(2)}, u32[]{:S(2)}) collective-permute-start(bf16[640,768]{1,0:T(8,128)(2,1)} %get-tuple-element.71.n0), channel_id=1, source_target_pairs={{0,2},{1,3},{2,0},{3,1},{4,6},{5,7},{6,4},{7,5},{8,10},{9,11},{10,... | collective-permute-start | bytes 2949128 | tf_op jit(solution)/shard_map/ppermute | solution.py:895
  185.3 52.5 %collective-permute-start.28 = (bf16[640,768]{1,0:T(8,128)(2,1)}, bf16[640,768]{1,0:T(8,128)(2,1)}, u32[]{:S(2)}, u32[]{:S(2)}) collective-permute-start(bf16[640,768]{1,0:T(8,128)(2,1)} %get-tuple-element.72.b0), channel_id=1, source_target_pairs={{0,2},{1,3},{2,0},{3,1},{4,6},{5,7},{6,4},{7,5},{8,10},{9,11},{10,... | collective-permute-start | bytes 2949128 | tf_op jit(solution)/shard_map/ppermute | solution.py:895
  193.9 102.5 %collective-permute-start.24 = (bf16[640,768]{1,0:T(8,128)(2,1)S(1)}, bf16[640,768]{1,0:T(8,128)(2,1)S(1)}, u32[]{:S(2)}, u32[]{:S(2)}) collective-permute-start(bf16[640,768]{1,0:T(8,128)(2,1)S(1)} %copy-done.45), channel_id=1, source_target_pairs={{0,1},{1,0},{2,3},{3,2},{4,5},{5,4},{6,7},{7,6},{8,9},{9,8},{10,11... | collective-permute-start | bytes 2949128 | tf_op jit(solution)/shard_map/ppermute | solution.py:895
  193.9 102.5 %collective-permute-start.27 = (bf16[640,768]{1,0:T(8,128)(2,1)}, bf16[640,768]{1,0:T(8,128)(2,1)}, u32[]{:S(2)}, u32[]{:S(2)}) collective-permute-start(bf16[640,768]{1,0:T(8,128)(2,1)} %get-tuple-element.72.b0), channel_id=1, source_target_pairs={{0,1},{1,0},{2,3},{3,2},{4,5},{5,4},{6,7},{7,6},{8,9},{9,8},{10,11... | collective-permute-start | bytes 2949128 | tf_op jit(solution)/shard_map/ppermute | solution.py:895
  217.6 78.8 %collective-permute-start.26 = (bf16[640,768]{1,0:T(8,128)(2,1)}, bf16[640,768]{1,0:T(8,128)(2,1)}, u32[]{:S(2)}, u32[]{:S(2)}) collective-permute-start(bf16[640,768]{1,0:T(8,128)(2,1)} %collective-permute-done.25.n2), channel_id=1, source_target_pairs={{0,1},{1,0},{2,3},{3,2},{4,5},{5,4},{6,7},{7,6},{8,9},{9,8},{10,11... | collective-permute-start | bytes 2949128 | tf_op jit(solution)/shard_map/ppermute | solution.py:895
  237.8 58.6 %collective-permute-start.29 = (bf16[640,768]{1,0:T(8,128)(2,1)}, bf16[640,768]{1,0:T(8,128)(2,1)}, u32[]{:S(2)}, u32[]{:S(2)}) collective-permute-start(bf16[640,768]{1,0:T(8,128)(2,1)} %collective-permute-done.28.b2), channel_id=1, source_target_pairs={{0,1},{1,0},{2,3},{3,2},{4,5},{5,4},{6,7},{7,6},{8,9},{9,8},{10,11... | collective-permute-start | bytes 2949128 | tf_op jit(solution)/shard_map/ppermute | solution.py:895
  330.2 41.3 %collective-permute-start.30 = (bf16[768,768]{1,0:T(8,128)(2,1)}, bf16[768,768]{1,0:T(8,128)(2,1)}, u32[]{:S(2)}, u32[]{:S(2)}) collective-permute-start(bf16[768,768]{1,0:T(8,128)(2,1)} %broadcast_select_fusion), channel_id=1, source_target_pairs={{0,4},{4,0},{8,12},{12,8},{16,20},{20,16},{24,28},{28,24},{1,5},{5... | collective-permute-start | bytes 3538952 | tf_op jit(solution)/shard_map/ppermute | solution.py:895
  332.8 35.6 %collective-permute-start.18 = (bf16[288,768]{1,0:T(8,128)(2,1)}, bf16[288,768]{1,0:T(8,128)(2,1)}, u32[]{:S(2)}, u32[]{:S(2)}) collective-permute-start(bf16[288,768]{1,0:T(8,128)(2,1)} %broadcast_select_fusion.6), channel_id=1, source_target_pairs={{0,4},{4,0},{8,12},{12,8},{16,20},{20,16},{24,28},{28,24},{1,5},{5... | collective-permute-start | bytes 1327112 | tf_op jit(solution)/shard_map/ppermute | solution.py:895
  333.2 38.3 %copy-start.1 = (bf16[768,768]{1,0:T(8,128)(2,1)S(1)}, bf16[768,768]{1,0:T(8,128)(2,1)}, u32[]{:S(2)}) copy-start(bf16[768,768]{1,0:T(8,128)(2,1)} %get-tuple-element.74) | copy-start | bytes 3538948
  333.2 38.3 %copy-start.2 = (bf16[768,768]{1,0:T(8,128)(2,1)S(1)}, bf16[768,768]{1,0:T(8,128)(2,1)}, u32[]{:S(2)}) copy-start(bf16[768,768]{1,0:T(8,128)(2,1)} %get-tuple-element.73) | copy-start | bytes 3538948
  369.6 8.4 %collective-permute-start.19 = (bf16[144,768]{1,0:T(8,128)(2,1)S(1)}, bf16[144,768]{1,0:T(8,128)(2,1)S(1)}, u32[]{:S(2)}, u32[]{:S(2)}) collective-permute-start(bf16[144,768]{1,0:T(8,128)(2,1)S(1)} %broadcast_select_fusion.12), channel_id=1, source_target_pairs={{0,8},{4,12},{8,0},{12,4},{16,24},{20,28},{24,16},{28,20},{1,9},{5... | collective-permute-start | bytes 663560 | tf_op jit(solution)/shard_map/ppermute | solution.py:895
  373.4 21.3 %collective-permute-start.31 = (bf16[384,768]{1,0:T(8,128)(2,1)S(1)}, bf16[384,768]{1,0:T(8,128)(2,1)S(1)}, u32[]{:S(2)}, u32[]{:S(2)}) collective-permute-start(bf16[384,768]{1,0:T(8,128)(2,1)S(1)} %broadcast_select_fusion.3), channel_id=1, source_target_pairs={{0,8},{4,12},{8,0},{12,4},{16,24},{20,28},{24,16},{28,20},{1,9},{5... | collective-permute-start | bytes 1769480 | tf_op jit(solution)/shard_map/ppermute | solution.py:895
  378.8 19.0 %copy-start.43 = (f32[8,128]{1,0:T(8,128)S(1)}, f32[8,128]{1,0:T(8,128)}, u32[]{:S(2)}) copy-start(f32[8,128]{1,0:T(8,128)} %get-tuple-element.68) | copy-start | bytes 12292
  378.8 137.7 %collective-permute-start.20 = (bf16[72,768]{1,0:T(8,128)(2,1)}, bf16[72,768]{1,0:T(8,128)(2,1)S(1)}, u32[]{:S(2)}, u32[]{:S(2)}) collective-permute-start(bf16[72,768]{1,0:T(8,128)(2,1)} %broadcast_select_fusion.15), channel_id=1, source_target_pairs={{0,16},{4,20},{8,24},{12,28},{16,0},{20,4},{24,8},{28,12},{1,17},{... | collective-permute-start | bytes 331784 | tf_op jit(solution)/shard_map/ppermute | solution.py:895
  394.9 124.3 %collective-permute-start.32 = (bf16[192,768]{1,0:T(8,128)(2,1)S(1)}, bf16[192,768]{1,0:T(8,128)(2,1)S(1)}, u32[]{:S(2)}, u32[]{:S(2)}) collective-permute-start(bf16[192,768]{1,0:T(8,128)(2,1)S(1)} %broadcast_select_fusion.9), channel_id=1, source_target_pairs={{0,16},{4,20},{8,24},{12,28},{16,0},{20,4},{24,8},{28,12},{1,17},{... | collective-permute-start | bytes 884744 | tf_op jit(solution)/shard_map/ppermute | solution.py:895
  419.8 139.1 %collective-permute-start.15 = (bf16[640,768]{1,0:T(8,128)(2,1)}, bf16[640,768]{1,0:T(8,128)(2,1)S(1)}, u32[]{:S(2)}, u32[]{:S(2)}) collective-permute-start(bf16[640,768]{1,0:T(8,128)(2,1)} %get-tuple-element.64), channel_id=1, source_target_pairs={{0,1},{1,0},{2,3},{3,2},{4,5},{5,4},{6,7},{7,6},{8,9},{9,8},{10,11... | collective-permute-start | bytes 2949128 | tf_op jit(solution)/shard_map/ppermute | solution.py:895
  419.8 117.9 %collective-permute-start.16 = (bf16[640,768]{1,0:T(8,128)(2,1)}, bf16[640,768]{1,0:T(8,128)(2,1)S(1)}, u32[]{:S(2)}, u32[]{:S(2)}) collective-permute-start(bf16[640,768]{1,0:T(8,128)(2,1)} %get-tuple-element.66), channel_id=1, source_target_pairs={{0,1},{1,0},{2,3},{3,2},{4,5},{5,4},{6,7},{7,6},{8,9},{9,8},{10,11... | collective-permute-start | bytes 2949128 | tf_op jit(solution)/shard_map/ppermute | solution.py:895
  516.5 14.7 %collective-permute-start.21 = (bf16[72,768]{1,0:T(8,128)(2,1)S(1)}, bf16[72,768]{1,0:T(8,128)(2,1)S(1)}, u32[]{:S(2)}, u32[]{:S(2)}) collective-permute-start(bf16[72,768]{1,0:T(8,128)(2,1)S(1)} %add_convert_fusion.6), channel_id=1, source_target_pairs={{0,16},{4,20},{8,24},{12,28},{16,0},{20,4},{24,8},{28,12},{1,17},{... | collective-permute-start | bytes 331784 | tf_op jit(solution)/shard_map/ppermute | solution.py:895
  519.3 18.4 %copy-start.20 = (bf16[640,768]{1,0:T(8,128)(2,1)S(1)}, bf16[640,768]{1,0:T(8,128)(2,1)}, u32[]{:S(2)}) copy-start(bf16[640,768]{1,0:T(8,128)(2,1)} %get-tuple-element.65) | copy-start | bytes 2949124
  519.3 18.2 %collective-permute-start.33 = (bf16[192,768]{1,0:T(8,128)(2,1)S(1)}, bf16[192,768]{1,0:T(8,128)(2,1)S(1)}, u32[]{:S(2)}, u32[]{:S(2)}) collective-permute-start(bf16[192,768]{1,0:T(8,128)(2,1)S(1)} %add_convert_fusion.4), channel_id=1, source_target_pairs={{0,16},{4,20},{8,24},{12,28},{16,0},{20,4},{24,8},{28,12},{1,17},{... | collective-permute-start | bytes 884744 | tf_op jit(solution)/shard_map/ppermute | solution.py:895
  531.3 11.0 %collective-permute-start.22 = (bf16[144,768]{1,0:T(8,128)(2,1)S(1)}, bf16[144,768]{1,0:T(8,128)(2,1)S(1)}, u32[]{:S(2)}, u32[]{:S(2)}) collective-permute-start(bf16[144,768]{1,0:T(8,128)(2,1)S(1)} %pad_maximum_fusion.7), channel_id=1, source_target_pairs={{0,8},{4,12},{8,0},{12,4},{16,24},{20,28},{24,16},{28,20},{1,9},{5... | collective-permute-start | bytes 663560 | tf_op jit(solution)/shard_map/ppermute | solution.py:895
  537.7 17.2 %collective-permute-start.34 = (bf16[384,768]{1,0:T(8,128)(2,1)S(1)}, bf16[384,768]{1,0:T(8,128)(2,1)S(1)}, u32[]{:S(2)}, u32[]{:S(2)}) collective-permute-start(bf16[384,768]{1,0:T(8,128)(2,1)S(1)} %pad_maximum_fusion.5), channel_id=1, source_target_pairs={{0,8},{4,12},{8,0},{12,4},{16,24},{20,28},{24,16},{28,20},{1,9},{5... | collective-permute-start | bytes 1769480 | tf_op jit(solution)/shard_map/ppermute | solution.py:895
  538.1 23.7 %collective-permute-start.17 = (bf16[640,768]{1,0:T(8,128)(2,1)S(1)}, bf16[640,768]{1,0:T(8,128)(2,1)S(1)}, u32[]{:S(2)}, u32[]{:S(2)}) collective-permute-start(bf16[640,768]{1,0:T(8,128)(2,1)S(1)} %add_convert_fusion.1), channel_id=1, source_target_pairs={{0,2},{1,3},{2,0},{3,1},{4,6},{5,7},{6,4},{7,5},{8,10},{9,11},{10,... | collective-permute-start | bytes 2949128 | tf_op jit(solution)/shard_map/ppermute | solution.py:895
  542.4 14.9 %collective-permute-start.23 = (bf16[288,768]{1,0:T(8,128)(2,1)S(1)}, bf16[288,768]{1,0:T(8,128)(2,1)S(1)}, u32[]{:S(2)}, u32[]{:S(2)}) collective-permute-start(bf16[288,768]{1,0:T(8,128)(2,1)S(1)} %pad_maximum_fusion.6), channel_id=1, source_target_pairs={{0,4},{4,0},{8,12},{12,8},{16,20},{20,16},{24,28},{28,24},{1,5},{5... | collective-permute-start | bytes 1327112 | tf_op jit(solution)/shard_map/ppermute | solution.py:895
  555.2 28.0 %collective-permute-start.35 = (bf16[768,768]{1,0:T(8,128)(2,1)S(1)}, bf16[768,768]{1,0:T(8,128)(2,1)S(1)}, u32[]{:S(2)}, u32[]{:S(2)}) collective-permute-start(bf16[768,768]{1,0:T(8,128)(2,1)S(1)} %pad_maximum_fusion.3), channel_id=1, source_target_pairs={{0,4},{4,0},{8,12},{12,8},{16,20},{20,16},{24,28},{28,24},{1,5},{5... | collective-permute-start | bytes 3538952 | tf_op jit(solution)/shard_map/ppermute | solution.py:895
  (22 other events, 222.1 us)
Sparse Core Ops, SparseCore 0:
  374.9 138.3 all-reduce.1

commit v2 on v0

v2 whole, which is shorter than its diff:
```python
import jax
import jax.numpy as jnp
from jax import lax
from jax.experimental import pallas as pl
from jax.experimental.pallas import tpu as pltpu
from jax.sharding import PartitionSpec as P

HEAD = 64
LANDMARKS = 64
NS_ITERS = 6
KERNEL = 33
SEQS = 3
MARKS = 192
REACH = KERNEL // 2
PAD = 128
BAND_IN = 512
BAND_OUT = 256
TILE = 512
AHEAD = 20
VMEM_LIMIT = 60 * 1024 * 1024
F32 = jnp.float32
BF16 = jnp.bfloat16


def dot_nn(a, b):
    return lax.dot_general(a, b, (((1,), (0,)), ((), ())), preferred_element_type=F32)


def dot_nt(a, b):
    return lax.dot_general(a, b, (((1,), (1,)), ((), ())), preferred_element_type=F32)


def dot_tn(a, b):
    return lax.dot_general(a, b, (((0,), (0,)), ((), ())), preferred_element_type=F32)


def split_low(a):
    high = a.astype(BF16)
    return (high, (a - high.astype(F32)).astype(BF16))


def dot_three(a, b, dot=dot_nn):
    a_high, a_low = a
    b_high, b_low = b
    return dot(a_high, b_high) + (dot(a_high, b_low) + dot(a_low, b_high))


def block_mask(dtype):
    rows = lax.broadcasted_iota(jnp.int32, (MARKS, MARKS), 0) // LANDMARKS
    columns = lax.broadcasted_iota(jnp.int32, (MARKS, MARKS), 1) // LANDMARKS
    return jnp.where(rows == columns, 1.0, 0.0).astype(dtype)


def spread(packed, mask):
    return jnp.concatenate([packed] * SEQS, axis=0) * mask


def spread_split(packed, mask):
    high, low = split_low(packed)
    return (spread(high, mask), spread(low, mask))


def fold(blocks):
    return (
        blocks[:LANDMARKS] + blocks[LANDMARKS : 2 * LANDMARKS] + blocks[2 * LANDMARKS :]
    )


def packed_identity():
    rows = lax.broadcasted_iota(jnp.int32, (LANDMARKS, MARKS), 0)
    columns = lax.broadcasted_iota(jnp.int32, (LANDMARKS, MARKS), 1) % LANDMARKS
    return jnp.where(rows == columns, 1.0, 0.0).astype(F32)


def sequence_of(places, first_end, second_end):
    return (places >= first_end).astype(jnp.int32) + (places >= second_end).astype(jnp.int32)


def lane_slice(start, width):
    return pl.ds(pl.multiple_of(start, 128), width)


def row_block(i, size):
    return pl.ds(pl.multiple_of(i * size, size), size)


class Layout:
    def __init__(self, scalars, group_size):
        self.first_end = scalars[0]
        self.second_end = scalars[0] + scalars[1]
        self.group_size = group_size
        self.tiles = group_size // TILE
        last = [
            (self.first_end - 1) // TILE,
            (self.second_end - 1) // TILE,
            self.tiles - 1,
        ]
        self.first_tile = [0, self.first_end // TILE, self.second_end // TILE]
        counts = [b - a + 1 for a, b in zip(self.first_tile, last, strict=True)]
        self.before = [0, counts[0], counts[0] + counts[1]]
        self.pairs = counts[0] + counts[1] + counts[2]

    def pick(self, sequence, values):
        return jnp.where(
            sequence == 0, values[0], jnp.where(sequence == 1, values[1], values[2])
        )

    def pair(self, p):
        sequence = (p >= self.before[1]).astype(jnp.int32) + (p >= self.before[2]).astype(
            jnp.int32
        )
        tile = p - self.pick(sequence, self.before) + self.pick(sequence, self.first_tile)
        start = self.pick(sequence, [0, self.first_end, self.second_end])
        end = self.pick(sequence, [self.first_end, self.second_end, self.group_size])
        return sequence, tile, start, end

    def own(self, tile, start, end):
        places = tile * TILE + lax.broadcasted_iota(jnp.int32, (LANDMARKS, TILE), 1)
        return (places >= start) & (places < end)

    def pool(self, tile, start, end):
        places = tile * TILE + lax.broadcasted_iota(jnp.int32, (1, TILE), 1)
        length = jnp.full((1, TILE), end - start, jnp.int32).astype(F32)
        numerator = ((places - start + 1) * LANDMARKS - 1).astype(F32) + length + 0.5
        segment = jnp.floor(numerator / length).astype(jnp.int32) - 1
        segment = jnp.where((places >= start) & (places < end), segment, -1)
        marks = lax.broadcasted_iota(jnp.int32, (LANDMARKS, TILE), 0)
        return jnp.where(marks == segment, 1.0, 0.0).astype(BF16)

    def counts(self):
        marks = lax.broadcasted_iota(jnp.int32, (MARKS, 1), 0)
        sequence = marks // LANDMARKS
        k = marks % LANDMARKS
        length = self.pick(
            sequence,
            [
                self.first_end,
                self.second_end - self.first_end,
                self.group_size - self.second_end,
            ],
        )
        upper = lax.shift_right_logical((k + 1) * length, 6)
        return (upper - lax.shift_right_logical(k * length, 6)).astype(F32)

    def same(self, start):
        into = start - PAD + lax.broadcasted_iota(jnp.int32, (BAND_IN, 1), 0)
        out = start + lax.broadcasted_iota(jnp.int32, (1, BAND_OUT), 1)
        return sequence_of(into, self.first_end, self.second_end) == sequence_of(
            out, self.first_end, self.second_end
        )


class Joined:
    def __init__(self, *pieces):
        self.pieces = pieces
        first = pieces[0][0]
        self.shape = (sum(rows for _, _, rows in pieces), first.shape[1])
        self.dtype = first.dtype

    def copies(self, sources, local):
        pairs, at = [], 0
        for source, (_, start, rows) in zip(sources, self.pieces, strict=True):
            pairs.append((source.at[start : start + rows, :], local.at[at : at + rows, :]))
            at += rows
        return pairs


class Io:
    def __init__(self, copies, inputs, outputs, targets, in_sems, out_sems):
        self.inputs, self.outputs = inputs, outputs
        self.arriving = [
            [
                pltpu.make_async_copy(source, local, in_sems.at[at])
                for source, local, at in group
            ]
            for group in copies
        ]
        self.leaving = [
            pltpu.make_async_copy(local, target, out_sems.at[i])
            for i, (local, target) in enumerate(zip(outputs, targets, strict=True))
        ]
        self.sent = set()
        self.started = 0
        self.waited = set()
        self.start_to(AHEAD)

    def start_to(self, end):
        for group in self.arriving[self.started : end]:
            for copy in group:
                copy.start()
        self.started = max(self.started, min(end, len(self.arriving)))

    def need(self, *which):
        self.start_to(max(which) + 1 + AHEAD)
        for i in which:
            if i not in self.waited:
                self.waited.add(i)
                for copy in self.arriving[i]:
                    copy.wait()
        return [self.inputs[i] for i in which]

    def send(self, *which):
        for i in which:
            self.sent.add(i)
            self.leaving[i].start()

    def close(self):
        self.need(*range(len(self.arriving)))
        self.send(*[i for i in range(len(self.leaving)) if i not in self.sent])
        for copy in self.leaving:
            copy.wait()


def local_call(kernel, name, scalars, operands, out_shape, scratch, gigaflops):
    anywhere = pl.BlockSpec(memory_space=pl.ANY)
    flat = [
        a
        for o in operands
        for a in ([piece[0] for piece in o.pieces] if isinstance(o, Joined) else [o])
    ]
    moved = sum(x.size * x.dtype.itemsize for x in (*flat, *out_shape))
    n_in, n_out, n_flat = len(operands), len(out_shape), len(flat)

    def body(scalar_ref, *refs):
        sources, refs = refs[:n_flat], refs[n_flat:]
        targets, refs = refs[:n_out], refs[n_out:]
        inputs, refs = refs[:n_in], refs[n_in:]
        outputs, refs = refs[:n_out], refs[n_out:]
        copies, at = [], 0
        for o, local in zip(operands, inputs, strict=True):
            count = len(o.pieces) if isinstance(o, Joined) else 1
            mine = sources[at : at + count]
            pairs = o.copies(mine, local) if isinstance(o, Joined) else [(mine[0], local)]
            copies.append([(a, b, at + i) for i, (a, b) in enumerate(pairs)])
            at += count
        io = Io(copies, inputs, outputs, targets, refs[0], refs[1])
        kernel(io, scalar_ref, *refs[2:])
        io.close()

    return pl.pallas_call(
        body,
        name=name,
        out_shape=out_shape,
        in_specs=[pl.BlockSpec(memory_space=pltpu.SMEM)] + [anywhere] * n_flat,
        out_specs=[anywhere] * n_out,
        scratch_shapes=[
            *[pltpu.VMEM(x.shape, x.dtype) for x in operands],
            *[pltpu.VMEM(x.shape, x.dtype) for x in out_shape],
            pltpu.SemaphoreType.DMA((n_flat,)),
            pltpu.SemaphoreType.DMA((n_out,)),
            *scratch,
        ],
        compiler_params=pltpu.CompilerParams(vmem_limit_bytes=VMEM_LIMIT),
        cost_estimate=pl.CostEstimate(
            flops=gigaflops * 1_000_000_000, bytes_accessed=moved, transcendentals=0
        ),
    )(scalars, *flat)


def shape_of(dtype, *shape):
    return jax.ShapeDtypeStruct(shape, dtype)


def wide(narrow):
    return jnp.concatenate([narrow] * (TILE // 128), axis=1)


def attend_kernel(
    io,
    scalars,
    context,
    scores,
    pooled,
    tops,
    totals,
    q_lands,
    k_lands,
    mvts,
):
    w_t, bands = io.inputs[0], io.inputs[5]
    qkv_t, c0, c1, c2, c3, land_out, mark_values_out, summary_out = io.outputs[:8]
    steps_out, among_out, inverse_out, lse_to, lse_from = io.outputs[8:]
    width = w_t.shape[0] // 3
    heads = width // HEAD
    block = io.inputs[1].shape[0]
    group_size = 4 * block
    layout = Layout(scalars, group_size)
    me = scalars[3]
    qk_scale = HEAD ** (-0.25)

    qkv_t[:, :PAD] = jnp.zeros((3 * width, PAD), BF16)
    qkv_t[:, PAD + group_size :] = jnp.zeros((3 * width, PAD), BF16)
    io.need(0)
    for at in range(4):
        x = io.need(1 + at)[0]
        lanes = lane_slice(PAD + (me ^ at) * block, block)
        qkv_t[: 2 * width, lanes] = (dot_nt(w_t[: 2 * width, :], x[...]) * qk_scale).astype(BF16)
        qkv_t[2 * width :, lanes] = dot_nt(w_t[2 * width :, :], x[...]).astype(BF16)
    io.send(0)

    pooled[...] = jnp.zeros_like(pooled)

    @pl.loop(0, layout.pairs)
    def _(p):
        sequence, tile, start, end = layout.pair(p)
        rows = row_block(sequence, LANDMARKS)
        pool = layout.pool(tile, start, end)
        pooled[rows, :] += dot_nt(pool, qkv_t[: 2 * width, lane_slice(PAD + tile * TILE, TILE)])

    pooled[...] = pooled[...] / layout.counts()
    land_t = pooled[...].T.astype(BF16)
    land_out[...] = land_t
    for h in range(heads):
        q_lands[h] = pooled[:, h * HEAD : (h + 1) * HEAD].astype(BF16)
        k_lands[h] = pooled[:, width + h * HEAD : width + (h + 1) * HEAD].astype(BF16)
    io.send(5)

    tops[...] = jnp.full(tops.shape, -1e30, F32)
    totals[...] = jnp.zeros_like(totals)
    summary_out[...] = jnp.zeros_like(summary_out)

    each = range(heads)

    def part_rows(part, h):
        return slice(part * width + h * HEAD, part * width + (h + 1) * HEAD)

    @pl.loop(0, layout.pairs)
    def _(p):
        sequence, tile, start, end = layout.pair(p)
        rows = row_block(sequence, LANDMARKS)
        own = layout.own(tile, start, end)
        padded = lane_slice(PAD + tile * TILE, TILE)
        raw = [dot_nn(q_lands[h, rows, :], qkv_t[part_rows(1, h), padded]) for h in each]
        masked = [jnp.where(own, raw[h], -1e30) for h in each]
        top = [tops[h, rows, :] for h in each]
        for lane in range(0, TILE, 128):
            top = [jnp.maximum(top[h], masked[h][:, lane : lane + 128]) for h in each]
        for h in each:
            scores[h, :, lane_slice(p * TILE, TILE)] = masked[h]
            tops[h, rows, :] = top[h]

    for h in range(heads):
        tops[h] = jnp.broadcast_to(jnp.max(tops[h], axis=1, keepdims=True), (MARKS, 128))

    @pl.loop(0, layout.pairs)
    def _(p):
        sequence, _, _, _ = layout.pair(p)
        rows = row_block(sequence, LANDMARKS)
        at = lane_slice(p * TILE, TILE)
        raised = [jnp.exp(scores[h, :, at] - wide(tops[h, rows, :])) for h in each]
        total = [totals[h, rows, :] for h in each]
        for lane in range(0, TILE, 128):
            total = [total[h] + raised[h][:, lane : lane + 128] for h in each]
        for h in each:
            scores[h, :, at] = raised[h]
            totals[h, rows, :] = total[h]

    for h in range(heads):
        total = jnp.broadcast_to(jnp.sum(totals[h], axis=1, keepdims=True), (MARKS, 128))
        lse_from[h] = tops[h] + jnp.log(total)
        totals[h] = 1.0 / total

    @pl.loop(0, layout.pairs)
    def _(p):
        sequence, tile, _, _ = layout.pair(p)
        rows = row_block(sequence, LANDMARKS)
        at = lane_slice(p * TILE, TILE)
        padded = lane_slice(PAD + tile * TILE, TILE)
        low = [(scores[h, :, at] * wide(totals[h, rows, :])).astype(BF16) for h in each]
        part = [dot_nt(low[h], qkv_t[part_rows(2, h), padded]) for h in each]
        part = [summary_out[h, rows, :] + part[h] for h in each]
        for h in each:
            summary_out[h, rows, :] = part[h]

    io.send(7, 12)
    mask_f = block_mask(F32)
    mask_b = block_mask(BF16)
    eye = packed_identity()
    amongs = []
    approxes = []
    for h in range(heads):
        raw = dot_nt(q_lands[h], k_lands[h])
        masked = jnp.where(mask_f > 0.0, raw, -1e30)
        row_top = jnp.max(masked, axis=1, keepdims=True)
        raised = jnp.exp(masked - row_top)
        among = raised / jnp.sum(raised, axis=1, keepdims=True)
        column_top = jnp.max(jnp.sum(among, axis=0, keepdims=True), axis=1, keepdims=True)
        packed = fold(among)
        among_out[h] = packed
        amongs.append(split_low(packed))
        approxes.append(fold(among.T) / column_top)

    for step in range(NS_ITERS):
        product = [
            dot_three(amongs[h], spread_split(approxes[h], mask_b)) for h in range(heads)
        ]
        split = [split_low(product[h]) for h in range(heads)]
        bracket = [7.0 * eye - product[h] for h in range(heads)]
        second = [
            15.0 * eye - dot_three(split[h], spread_split(bracket[h], mask_b))
            for h in range(heads)
        ]
        third = [
            13.0 * eye - dot_three(split[h], spread_split(second[h], mask_b))
            for h in range(heads)
        ]
        for h in range(heads):
            steps_out[h, 4 * step] = approxes[h]
            steps_out[h, 4 * step + 1] = product[h]
            steps_out[h, 4 * step + 2] = second[h]
            steps_out[h, 4 * step + 3] = third[h]
        approxes = [
            0.25 * dot_three(split_low(approxes[h]), spread_split(third[h], mask_b))
            for h in range(heads)
        ]

    for h in range(heads):
        inverse_out[h] = approxes[h]
        mark_values = dot_three(
            spread_split(approxes[h], mask_b), split_low(summary_out[h])
        )
        mark_values_out[h] = mark_values.astype(BF16)
        for s in range(SEQS):
            part = mark_values[s * LANDMARKS : (s + 1) * LANDMARKS, :]
            mvts[SEQS * h + s] = part.T.astype(BF16)
    io.send(6, 8, 9, 10)
    io.need(5)

    @pl.loop(0, group_size // BAND_OUT)
    def _(i):
        start = i * BAND_OUT
        same = jnp.where(layout.same(start), 1.0, 0.0).astype(BF16)
        smooth = [
            dot_nn(qkv_t[part_rows(2, h), lane_slice(start, BAND_IN)], bands[h] * same)
            for h in each
        ]
        for h in each:
            context[part_rows(0, h), lane_slice(start, BAND_OUT)] = smooth[h]

    @pl.loop(0, layout.pairs)
    def _(p):
        sequence, tile, start, end = layout.pair(p)
        rows = row_block(sequence, LANDMARKS)
        own = layout.own(tile, start, end)
        at = lane_slice(tile * TILE, TILE)
        padded = lane_slice(PAD + tile * TILE, TILE)
        raw = [dot_nn(k_lands[h, rows, :], qkv_t[part_rows(0, h), padded]) for h in each]
        top = [jnp.max(raw[h], axis=0, keepdims=True) for h in each]
        raised = [jnp.exp(raw[h] - top[h]) for h in each]
        total = [jnp.sum(raised[h], axis=0, keepdims=True) for h in each]
        low = [
            jnp.where(own, raised[h] * (1.0 / total[h]), 0.0).astype(BF16) for h in each
        ]
        blended = [dot_nn(mvts[SEQS * h + sequence], low[h]) for h in each]
        blended = [context[part_rows(0, h), at] + blended[h] for h in each]
        lse = [
            jnp.where(own[:1], top[h] + jnp.log(total[h]), lse_to[h : h + 1, at]) for h in each
        ]
        for h in each:
            lse_to[h : h + 1, at] = lse[h]
            context[part_rows(0, h), at] = blended[h]

    for at, out in enumerate((c0, c1, c2, c3)):
        out[...] = context[:, lane_slice((me ^ at) * block, block)].astype(BF16)


def attend(scalars, blocks, w_t, bands):
    block = blocks[0].shape[0]
    group_size = 4 * block
    width = w_t.shape[0] // 3
    heads = width // HEAD
    most_pairs = group_size // TILE + SEQS - 1
    return local_call(
        attend_kernel,
        "attend",
        scalars,
        (w_t, *blocks, bands),
        (
            shape_of(BF16, 3 * width, group_size + 2 * PAD),
            *[shape_of(BF16, width, block) for _ in range(4)],
            shape_of(BF16, 2 * width, MARKS),
            shape_of(BF16, heads, MARKS, HEAD),
            shape_of(F32, heads, MARKS, HEAD),
            shape_of(F32, heads, 4 * NS_ITERS, LANDMARKS, MARKS),
            shape_of(F32, heads, LANDMARKS, MARKS),
            shape_of(F32, heads, LANDMARKS, MARKS),
            shape_of(F32, heads, group_size),
            shape_of(F32, heads, MARKS, 128),
        ),
        [
            pltpu.VMEM((width, group_size), F32),
            pltpu.VMEM((heads, LANDMARKS, most_pairs * TILE), F32),
            pltpu.VMEM((MARKS, 2 * width), F32),
            pltpu.VMEM((heads, MARKS, 128), F32),
            pltpu.VMEM((heads, MARKS, 128), F32),
            pltpu.VMEM((heads, MARKS, HEAD), BF16),
            pltpu.VMEM((heads, MARKS, HEAD), BF16),
            pltpu.VMEM((SEQS * heads, HEAD, LANDMARKS), BF16),
        ],
        30,
    )


def attend_back_kernel(
    io,
    scalars,
    context_grad,
    partial_value,
    correlation,
    q_lands,
    k_lands,
    q_lands_t,
    k_lands_t,
    grad_summaries,
    grad_summaries_t,
    offsets,
):
    g_refs = io.inputs[:4]
    qkv_t, land_t, mark_values_in, summary_in = io.inputs[4:8]
    inverse_in, lse_to, lse_from = io.inputs[8:11]
    bands = io.inputs[11]
    grad_value, taps_out, partial_query, partial_key = io.outputs[:4]
    grad_q_land, grad_k_land, grad_mark = io.outputs[4:]
    width, block = g_refs[0].shape
    heads = width // HEAD
    group_size = 4 * block
    layout = Layout(scalars, group_size)
    me = scalars[3]
    each = range(heads)

    def part_rows(part, h):
        return slice(part * width + h * HEAD, part * width + (h + 1) * HEAD)

    io.need(*range(11))
    context_grad[:, :PAD] = jnp.zeros((width, PAD), BF16)
    context_grad[:, PAD + group_size :] = jnp.zeros((width, PAD), BF16)
    for at, g in enumerate(g_refs):
        context_grad[:, lane_slice(PAD + (me ^ at) * block, block)] = g[...]

    for h in range(heads):
        q_t = land_t[h * HEAD : (h + 1) * HEAD, :].astype(F32)
        k_t = land_t[width + h * HEAD : width + (h + 1) * HEAD, :].astype(F32)
        q_lands[h] = q_t.T.astype(BF16)
        k_lands[h] = k_t.T.astype(BF16)
        for s in range(SEQS):
            columns = slice(s * LANDMARKS, (s + 1) * LANDMARKS)
            q_lands_t[SEQS * h + s] = q_t[:, columns].astype(BF16)
            k_lands_t[SEQS * h + s] = k_t[:, columns].astype(BF16)

    for ref in (grad_k_land, grad_mark, grad_q_land, partial_query, partial_key, partial_value):
        ref[...] = jnp.zeros_like(ref)

    @pl.loop(0, layout.pairs)
    def _(p):
        sequence, tile, start, end = layout.pair(p)
        rows = row_block(sequence, LANDMARKS)
        own = layout.own(tile, start, end)
        at = lane_slice(tile * TILE, TILE)
        padded = lane_slice(PAD + tile * TILE, TILE)
        query = [qkv_t[part_rows(0, h), padded] for h in each]
        out_grad = [context_grad[part_rows(0, h), padded] for h in each]
        raw = [dot_nn(k_lands[h, rows, :], query[h]) for h in each]
        grad_to = [dot_nn(mark_values_in[h, rows, :], out_grad[h]) for h in each]
        probs = [
            jnp.exp(jnp.where(own, raw[h] - lse_to[h : h + 1, at], -1e30)) for h in each
        ]
        inner = [jnp.sum(grad_to[h] * probs[h], axis=0, keepdims=True) for h in each]
        grad_scores = [(probs[h] * (grad_to[h] - inner[h])).astype(BF16) for h in each]
        mark_part = [
            grad_mark[h, rows, :] + dot_nt(probs[h].astype(BF16), out_grad[h]) for h in each
        ]
        land_part = [
            grad_k_land[h, rows, :] + dot_nt(grad_scores[h], query[h]) for h in each
        ]
        query_part = [
            partial_query[part_rows(0, h), at]
            + dot_nn(k_lands_t[SEQS * h + sequence], grad_scores[h])
            for h in each
        ]
        for h in each:
            grad_mark[h, rows, :] = mark_part[h]
            grad_k_land[h, rows, :] = land_part[h]
            partial_query[part_rows(0, h), at] = query_part[h]

    io.send(2, 5, 6)
    mask_f = block_mask(F32)
    for h in range(heads):
        mark_split = split_low(grad_mark[h])
        summary = summary_in[h]
        inverse_blocks = spread(inverse_in[h], mask_f).T
        grad_summary = dot_three(split_low(inverse_blocks), mark_split)
        grad_low = grad_summary.astype(BF16)
        grad_summaries[h] = grad_low
        exact = grad_low.astype(F32)
        for s in range(SEQS):
            part = exact[s * LANDMARKS : (s + 1) * LANDMARKS, :]
            grad_summaries_t[SEQS * h + s] = part.T.astype(BF16)
        inner = jnp.sum(exact * summary, axis=1, keepdims=True)
        offsets[h] = jnp.broadcast_to(inner, (MARKS, 128))

    @pl.loop(0, layout.pairs)
    def _(p):
        sequence, tile, start, end = layout.pair(p)
        rows = row_block(sequence, LANDMARKS)
        own = layout.own(tile, start, end)
        at = lane_slice(tile * TILE, TILE)
        padded = lane_slice(PAD + tile * TILE, TILE)
        key = [qkv_t[part_rows(1, h), padded] for h in each]
        value = [qkv_t[part_rows(2, h), padded] for h in each]
        raw = [dot_nn(q_lands[h, rows, :], key[h]) for h in each]
        grad_from = [dot_nn(grad_summaries[h, rows, :], value[h]) for h in each]
        probs = [
            jnp.exp(jnp.where(own, raw[h] - wide(lse_from[h, rows, :]), -1e30)) for h in each
        ]
        grad_scores = [
            (probs[h] * (grad_from[h] - wide(offsets[h, rows, :]))).astype(BF16) for h in each
        ]
        value_part = [
            partial_value[part_rows(0, h), padded]
            + dot_nn(grad_summaries_t[SEQS * h + sequence], probs[h].astype(BF16))
            for h in each
        ]
        land_part = [grad_q_land[h, rows, :] + dot_nt(grad_scores[h], key[h]) for h in each]
        key_part = [
            partial_key[part_rows(0, h), at]
            + dot_nn(q_lands_t[SEQS * h + sequence], grad_scores[h])
            for h in each
        ]
        for h in each:
            partial_value[part_rows(0, h), padded] = value_part[h]
            grad_q_land[h, rows, :] = land_part[h]
            partial_key[part_rows(0, h), at] = key_part[h]

    io.send(3, 4)

    correlation[...] = jnp.zeros_like(correlation)
    io.need(11)

    @pl.loop(0, group_size // BAND_OUT)
    def _(i):
        start = i * BAND_OUT
        padded = lane_slice(PAD + start, BAND_OUT)
        around = lane_slice(start, BAND_IN)
        same = jnp.where(layout.same(start), 1.0, 0.0)
        same_b = same.astype(BF16)
        out_grad = [context_grad[part_rows(0, h), padded] for h in each]
        value_part = [
            partial_value[part_rows(0, h), around] + dot_nt(out_grad[h], bands[h] * same_b)
            for h in each
        ]
        across = [
            dot_tn(qkv_t[part_rows(2, h), around], out_grad[h]) * same for h in each
        ]
        parts = [
            (
                a[:128, :128] + a[128:256, 128:],
                a[128:256, :128] + a[256:384, 128:],
                a[256:384, :128] + a[384:, 128:],
            )
            for a in across
        ]
        for h in each:
            partial_value[part_rows(0, h), around] = value_part[h]
            for at in range(3):
                correlation[h, at] += parts[h][at]

    grad_value[...] = partial_value[:, PAD : PAD + group_size].astype(BF16)
    io.send(0)
    apart = lax.broadcasted_iota(jnp.int32, (128, 128), 0) - lax.broadcasted_iota(
        jnp.int32, (128, 128), 1
    )
    lanes = lax.broadcasted_iota(jnp.int32, (8, 128), 1)
    rows = lax.broadcasted_iota(jnp.int32, (8, 128), 0)
    taps = jnp.zeros((8, 128), F32)
    for h in range(heads):
        for tap in range(KERNEL):
            away = tap - REACH
            picked = jnp.where(apart == away, correlation[h, 1], 0.0)
            if away < 0:
                picked += jnp.where(apart == away + 128, correlation[h, 0], 0.0)
            if away > 0:
                picked += jnp.where(apart == away - 128, correlation[h, 2], 0.0)
            total = jnp.sum(
                jnp.sum(picked, axis=0, keepdims=True), axis=1, keepdims=True
            )
            taps = taps + jnp.where((lanes == tap) & (rows == h), total, 0.0)
    taps_out[...] = taps


def attend_steps_kernel(group_size, io, scalars):
    grad_mark_in, summary_in, among_in, steps_in = io.inputs[:4]
    land_t, grad_q_land, grad_k_land = io.inputs[4:]
    shares = io.outputs[0]
    heads = summary_in.shape[0]
    width = heads * HEAD
    layout = Layout(scalars, group_size)
    each = range(heads)
    mask_f = block_mask(F32)
    mask_b = block_mask(BF16)
    io.need(0, 1, 2)
    carried = [
        fold(dot_three(split_low(summary_in[h]), split_low(grad_mark_in[h]), dot_nt) * mask_f)
        for h in each
    ]
    io.need(*range(3, 7))
    eye = packed_identity()

    def spread_both(pair):
        return tuple(spread(a, mask_b) for a in pair)

    among_wide = [spread_split(among_in[h], mask_b) for h in each]
    among_grads = [jnp.zeros((LANDMARKS, MARKS), F32) for _ in each]
    for step in reversed(range(NS_ITERS)):
        approx = [split_low(steps_in[h, 4 * step]) for h in each]
        product = [steps_in[h, 4 * step + 1] for h in each]
        product_wide = [spread_split(product[h], mask_b) for h in each]
        grad = [split_low(carried[h]) for h in each]
        third = [
            split_low(0.25 * dot_three(grad[h], spread_both(approx[h]))) for h in each
        ]
        through = [
            dot_three(split_low(steps_in[h, 4 * step + 3]), spread_both(grad[h])) for h in each
        ]
        second = [split_low(-dot_three(third[h], product_wide[h])) for h in each]
        from_third = [
            dot_three(split_low(steps_in[h, 4 * step + 2]), spread_both(third[h]))
            for h in each
        ]
        first = [dot_three(second[h], product_wide[h]) for h in each]
        from_second = [
            dot_three(split_low(7.0 * eye - product[h]), spread_both(second[h])) for h in each
        ]
        grad_product = [
            split_low(first[h] - from_third[h] - from_second[h]) for h in each
        ]
        carried = [
            0.25 * through[h] + dot_three(grad_product[h], among_wide[h]) for h in each
        ]
        among_grads = [
            among_grads[h] + dot_three(approx[h], spread_both(grad_product[h])) for h in each
        ]

    for h in each:
        among = spread(among_in[h], mask_f)
        column_sums = jnp.sum(among, axis=0, keepdims=True)
        column_top = jnp.max(column_sums, axis=1, keepdims=True)
        start_grad = carried[h]
        start_blocks = spread(steps_in[h, 0], mask_f).T
        top_grad = -jnp.sum(
            jnp.sum(start_grad * fold(start_blocks), axis=1, keepdims=True),
            axis=0,
            keepdims=True,
        ) / column_top
        at_top = jnp.where(column_sums == column_top, 1.0, 0.0)
        shared = top_grad * at_top / jnp.sum(at_top, axis=1, keepdims=True)
        among_grad = spread(among_grads[h], mask_f).T + (
            spread(start_grad, mask_f) / column_top + shared * mask_f
        )
        inner = jnp.sum(among_grad * among, axis=1, keepdims=True)
        grad_scores = among * (among_grad - inner)
        high, low = split_low(grad_scores)
        back_high, back_low = split_low(grad_scores.T)
        q_land = land_t[h * HEAD : (h + 1) * HEAD, :].astype(F32).T.astype(BF16)
        k_land = land_t[width + h * HEAD : width + (h + 1) * HEAD, :].astype(F32).T.astype(BF16)
        q_total = grad_q_land[h] + (dot_nn(high, k_land) + dot_nn(low, k_land))
        k_total = grad_k_land[h] + (dot_nn(back_high, q_land) + dot_nn(back_low, q_land))
        counts = layout.counts()
        for which, total in enumerate((q_total, k_total)):
            share = total.astype(BF16).astype(F32) / counts
            for s in range(SEQS):
                part = share[s * LANDMARKS : (s + 1) * LANDMARKS, :].T
                shares[which, SEQS * h + s] = part.astype(BF16)


def attend_grads_kernel(io, scalars, grad_qkv, grad_w_t):
    grad_value, taps, partial_query, partial_key, shares, w_t = io.inputs[:6]
    x_refs = io.inputs[6:]
    low_out, high_out, d_refs = io.outputs[0], io.outputs[1], io.outputs[2:]
    width, group_size = partial_query.shape
    heads = width // HEAD
    block, features = x_refs[0].shape
    half = low_out.shape[0]
    me = scalars[3]
    qk_scale = HEAD ** (-0.25)
    layout = Layout(scalars, group_size)
    each = range(heads)

    def part_rows(part, h):
        return slice(part * width + h * HEAD, part * width + (h + 1) * HEAD)

    io.need(0, 2, 3, 4)

    @pl.loop(0, layout.pairs)
    def _(p):
        sequence, tile, start, end = layout.pair(p)
        at = lane_slice(tile * TILE, TILE)
        pool = layout.pool(tile, start, end)
        query = [
            partial_query[part_rows(0, h), at] + dot_nn(shares[0, SEQS * h + sequence], pool)
            for h in each
        ]
        key = [
            partial_key[part_rows(0, h), at] + dot_nn(shares[1, SEQS * h + sequence], pool)
            for h in each
        ]
        for h in each:
            partial_query[part_rows(0, h), at] = query[h]
            partial_key[part_rows(0, h), at] = key[h]

    grad_qkv[:width, :] = partial_query[...].astype(BF16)
    grad_qkv[width : 2 * width, :] = partial_key[...].astype(BF16)
    grad_qkv[2 * width :, :] = grad_value[...]

    io.need(1, 5)
    for at in (3, 1, 2, 0):
        x = io.need(6 + at)[0]
        lanes = lane_slice((me ^ at) * block, block)
        part = dot_nn(grad_qkv[:, lanes], x[...])
        if at == 3:
            grad_w_t[...] = part
        else:
            grad_w_t[...] += part

    def put(start, value):
        end = start + value.shape[0]
        if start < half:
            low_out[start : min(end, half), :] = value[: min(end, half) - start]
        if end > half:
            high_out[max(start, half) - half : end - half, :] = value[max(start, half) - start :]

    put(0, (grad_w_t[: 2 * width] * qk_scale).astype(BF16))
    put(2 * width, grad_w_t[2 * width :].astype(BF16))
    put(3 * width, jnp.zeros((2 * half - 3 * width, features), BF16))
    start = 3 * width - half
    high_out[start : start + 16, :128] = jnp.concatenate(
        [taps[...], jnp.zeros((8, 128), F32)], axis=0
    ).astype(BF16)
    io.send(0, 1)

    for at in (3, 1, 2, 0):
        d = d_refs[at]
        lanes = lane_slice((me ^ at) * block, block)
        scaled = dot_tn(grad_qkv[: 2 * width, lanes], w_t[: 2 * width, :])
        plain = dot_tn(grad_qkv[2 * width :, lanes], w_t[2 * width :, :])
        d[...] = (scaled * qk_scale + plain).astype(BF16)
        io.send(2 + at)


def attend_back(scalars, saved, grads, bands):
    qkv_t, land_t, mark_values, summary, steps, among, inverse, lse_to, lse_from = saved
    width, block = grads[0].shape
    group_size = 4 * block
    heads = width // HEAD
    lands = pltpu.VMEM((heads, MARKS, HEAD), BF16)
    lands_t = pltpu.VMEM((SEQS * heads, HEAD, LANDMARKS), BF16)
    return local_call(
        attend_back_kernel,
        "attend_back",
        scalars,
        (*grads, qkv_t, land_t, mark_values, summary, inverse, lse_to, lse_from, bands),
        (
            shape_of(BF16, width, group_size),
            shape_of(F32, 8, 128),
            shape_of(F32, width, group_size),
            shape_of(F32, width, group_size),
            *[shape_of(F32, heads, MARKS, HEAD) for _ in range(3)],
        ),
        [
            pltpu.VMEM((width, group_size + 2 * PAD), BF16),
            pltpu.VMEM((width, group_size + 2 * PAD), F32),
            pltpu.VMEM((heads, 3, 128, 128), F32),
            lands,
            lands,
            lands_t,
            lands_t,
            lands,
            lands_t,
            pltpu.VMEM((heads, MARKS, 128), F32),
        ],
        8,
    )


def attend_steps(scalars, saved, passed):
    qkv_t, land_t, mark_values, summary, steps, among, inverse, lse_to, lse_from = saved
    grad_q_land, grad_k_land, grad_mark = passed[4:]
    heads = summary.shape[0]

    def kernel(*refs):
        attend_steps_kernel(qkv_t.shape[1] - 2 * PAD, *refs)

    return local_call(
        kernel,
        "attend_steps",
        scalars,
        (grad_mark, summary, among, steps, land_t, grad_q_land, grad_k_land),
        (shape_of(BF16, 2, SEQS * heads, HEAD, LANDMARKS),),
        [],
        5,
    )[0]


def attend_grads(scalars, passed, shares, blocks, w_t, multiple):
    grad_value, taps, partial_query, partial_key = passed[:4]
    block, features = blocks[0].shape
    width, group_size = partial_query.shape
    heads = width // HEAD
    half = -(-(w_t.shape[0] + 16) // (2 * multiple)) * multiple
    return local_call(
        attend_grads_kernel,
        "attend_grads",
        scalars,
        (
            grad_value,
            taps,
            partial_query,
            partial_key,
            shares,
            w_t,
            *blocks,
        ),
        (
            shape_of(BF16, half, features),
            shape_of(BF16, half, features),
            *[shape_of(BF16, block, features) for _ in range(4)],
        ),
        [
            pltpu.VMEM((3 * width, group_size), BF16),
            pltpu.VMEM(w_t.shape, F32),
        ],
        8,
    )


def gelu_and_slope(values):
    z = jnp.abs(values) * 0.7071067811865476
    t = pl.reciprocal(1.0 + 0.3275911 * z)
    poly = t * 1.061405429 - 1.453152027
    for coefficient in (1.421413741, -0.284496736, 0.254829592):
        poly = poly * t + coefficient
    bell = jnp.exp(-z * z)
    half_tail = (0.5 * t) * poly * bell
    below = jnp.where(values >= 0.0, 1.0 - half_tail, half_tail)
    return values * below, below + values * (bell * 0.3989422804014327)


def unit_norm(values):
    row_mean = jnp.mean(values, axis=-1, keepdims=True)
    centered = values - row_mean
    spread_out = jnp.mean(centered * centered, axis=-1, keepdims=True)
    recip = lax.rsqrt(spread_out + 1e-05)
    return (centered * recip, recip)


def unit_back(grad, unit, recip):
    mean_grad = jnp.mean(grad, axis=-1, keepdims=True)
    mean_cross = jnp.mean(grad * unit, axis=-1, keepdims=True)
    return recip * (grad - mean_grad - unit * mean_cross)


ROWS = 320
UNITS = 768


def norm_in_kernel(io, scalars):
    contexts, (tokens, w_out, norms) = io.inputs[:4], io.inputs[4:]
    normed_out, unit_one, recip_one = io.outputs
    me = scalars[3]
    width, block = contexts[0].shape
    io.need(*range(7))

    @pl.loop(0, block // 128)
    def _(i):
        rows = row_block(i, 128)
        resid = tokens[rows, :].astype(F32)
        for at, c in enumerate(contexts):
            resid += dot_tn(c[:, rows], w_out[row_block(me ^ at, width), :])
        unit, recip = unit_norm(resid)
        unit_one[rows, :] = unit
        recip_one[rows, :] = jnp.broadcast_to(recip, (128, 128))
        normed_out[rows, :] = (unit * norms[0:1, :] + norms[1:2, :]).astype(BF16)


def feed_kernel(io, scalars, hidden):
    normed_low, norms = io.inputs[:2]
    ups, downs = io.inputs[2:6], io.inputs[6:10]
    unit_one, grad_output = io.inputs[10:]
    output, slope, summed_grad, branch_grad, norm_grads = io.outputs
    block, features = normed_low.shape
    units = ups[0].shape[0]
    norm_grads[...] = jnp.zeros_like(norm_grads)
    io.need(0, 1)

    for s, up in enumerate(ups):
        io.need(2 + s)

        @pl.loop(0, units // UNITS)
        def _(j):
            target = lane_slice(s * units + j * UNITS, UNITS)
            value, derivative = gelu_and_slope(
                dot_nt(normed_low[...], up[row_block(j, UNITS), :])
            )
            hidden[:, target] = value.astype(BF16)
            slope[:, target] = derivative.astype(BF16)

    io.send(1)
    io.need(*range(6, 12))

    @pl.loop(0, block // ROWS)
    def _(i):
        rows = row_block(i, ROWS)
        total = unit_one[rows, :] * norms[0:1, :] + norms[1:2, :]
        for s, down in enumerate(downs):
            total += dot_nn(hidden[rows, s * units : (s + 1) * units], down[...])
        unit, recip = unit_norm(total)
        output[rows, :] = unit * norms[2:3, :] + norms[3:4, :]
        top = grad_output[rows, :].astype(F32)
        norm_grads[0:1, :] += jnp.sum(top * unit, axis=0, keepdims=True)
        norm_grads[1:2, :] += jnp.sum(top, axis=0, keepdims=True)
        grad = unit_back(top * norms[2:3, :], unit, recip)
        summed_grad[rows, :] = grad
        branch_grad[rows, :] = grad.astype(BF16)


def feed_back_kernel(io, scalars, grad_pre, attended_grad):
    branch_grad, norms = io.inputs[:2]
    downs, slope = io.inputs[2:6], io.inputs[6]
    ups = io.inputs[7:11]
    summed_grad, unit_one, recip_one, w_out = io.inputs[11:15]
    contexts = io.inputs[15:19]
    resid_grad, grad_w_out, norm_grads = io.outputs[:3]
    targets = io.outputs[3:]
    me = scalars[3]
    width, block = contexts[0].shape
    units = ups[0].shape[0]
    norm_grads[...] = jnp.zeros_like(norm_grads)
    io.need(0, 1, 2, 6)

    for s, down in enumerate(downs):
        io.need(2 + s)

        @pl.loop(0, units // UNITS)
        def _(j):
            target = lane_slice(s * units + j * UNITS, UNITS)
            grad = dot_nt(branch_grad[...], down[row_block(j, UNITS), :])
            grad_pre[:, target] = (slope[:, target] * grad).astype(BF16)

    io.need(*range(7, 19))

    @pl.loop(0, block // ROWS)
    def _(i):
        rows = row_block(i, ROWS)
        total = summed_grad[rows, :]
        for s, up in enumerate(ups):
            total += dot_nn(grad_pre[rows, s * units : (s + 1) * units], up[...])
        unit = unit_one[rows, :]
        norm_grads[0:1, :] += jnp.sum(total * unit, axis=0, keepdims=True)
        norm_grads[1:2, :] += jnp.sum(total, axis=0, keepdims=True)
        grad = unit_back(total * norms[0:1, :], unit, recip_one[rows, :1])
        resid_grad[rows, :] = grad
        attended_grad[rows, :] = grad.astype(BF16)

    for at in (3, 2, 1, 0):
        rows = row_block(me ^ at, width)
        targets[at][...] = dot_nt(w_out[rows, :], attended_grad[...]).astype(BF16)
        io.send(3 + at)
    for at, c in enumerate(contexts):
        rows = row_block(me ^ at, width)
        grad_w_out[rows, :] = dot_nn(c[...], attended_grad[...]).astype(BF16)


def norm_in(scalars, contexts, tokens, w_out, norms):
    block, features = tokens.shape
    return local_call(
        norm_in_kernel,
        "norm_in",
        scalars,
        (*contexts, tokens, w_out, norms),
        (
            shape_of(BF16, block, features),
            shape_of(F32, block, features),
            shape_of(F32, block, 128),
        ),
        [],
        6,
    )


def feed(scalars, normed_low, unit_one, grad_output, norms, ups, downs):
    block, features = normed_low.shape
    units = ups[0].shape[0]
    return local_call(
        feed_kernel,
        "feed",
        scalars,
        (normed_low, norms, *ups, *downs, unit_one, grad_output),
        (
            shape_of(F32, block, features),
            shape_of(BF16, block, 4 * units),
            shape_of(F32, block, features),
            shape_of(BF16, block, features),
            shape_of(F32, 8, features),
        ),
        [pltpu.VMEM((block, 4 * units), BF16)],
        22,
    )


def feed_back(scalars, fed, unit_one, recip_one, contexts, w_out, norms, ups, downs):
    slope, summed_grad, branch_grad = fed
    width, block = contexts[0].shape
    features = w_out.shape[0]
    units = ups[0].shape[0]
    return local_call(
        feed_back_kernel,
        "feed_back",
        scalars,
        (
            branch_grad,
            norms,
            *downs,
            slope,
            *ups,
            summed_grad,
            unit_one,
            recip_one,
            w_out,
            *contexts,
        ),
        (
            shape_of(F32, block, features),
            shape_of(BF16, features, features),
            shape_of(F32, 8, features),
            *[shape_of(BF16, width, block) for _ in range(4)],
        ),
        [
            pltpu.VMEM((block, 4 * units), BF16),
            pltpu.VMEM((block, features), BF16),
        ],
        20,
    )


def feed_weights_kernel(io, scalars, pre, grad_hidden, up_total, down_total):
    up, down = io.inputs[0], io.inputs[1]
    grad_up, grad_down = io.outputs
    units = up.shape[1]

    def into(at, j):
        n, b = io.inputs[2 + 2 * at], io.inputs[3 + 2 * at]
        columns = lane_slice(j * UNITS, UNITS)
        pre[at % 2, :, columns] = dot_nn(n[...], up[:, columns])
        grad_hidden[at % 2, :, columns] = dot_nt(b[...], down[row_block(j, UNITS), :])

    def out_of(at, j):
        n, b = io.inputs[2 + 2 * at], io.inputs[3 + 2 * at]
        columns = lane_slice(j * UNITS, UNITS)
        rows = row_block(j, UNITS)
        value, derivative = gelu_and_slope(pre[at % 2, :, columns])
        grad_pre = (derivative * grad_hidden[at % 2, :, columns]).astype(BF16)
        down_part = dot_tn(value.astype(BF16), b[...])
        up_part = dot_tn(grad_pre, n[...])
        if at == 0:
            down_total[rows, :] = down_part
            up_total[rows, :] = up_part
        elif at < 3:
            down_total[rows, :] += down_part
            up_total[rows, :] += up_part
        else:
            grad_down[rows, :] = (down_total[rows, :] + down_part).astype(BF16)
            grad_up[:, columns] = (up_total[rows, :] + up_part).T.astype(BF16)

    io.need(0, 1)
    for at in range(5):
        if at < 4:
            io.need(2 + 2 * at, 3 + 2 * at)

        @pl.loop(0, units // UNITS)
        def _(j):
            if at < 4:
                into(at, j)
            if at > 0:
                out_of(at - 1, j)


def feed_weights(scalars, normeds, branch_grads, up, down):
    features, units = up.shape
    block = normeds[0].shape[0]
    between = [a for pair in zip(normeds, branch_grads, strict=True) for a in pair]
    return local_call(
        feed_weights_kernel,
        "feed_weights",
        scalars,
        (up, down, *between),
        (shape_of(BF16, features, units), shape_of(BF16, units, features)),
        [
            pltpu.VMEM((2, block, units), F32),
            pltpu.VMEM((2, block, units), F32),
            pltpu.VMEM((units, features), F32),
            pltpu.VMEM((units, features), F32),
        ],
        25,
    )


def to_partner(array, axis, size, bit):
    return lax.ppermute(array, axis, [(i, i ^ bit) for i in range(size)])


def exchange_tensor(blocks):
    return (
        blocks[0],
        to_partner(blocks[1], "tensor", 4, 1),
        to_partner(blocks[2], "tensor", 4, 2),
        to_partner(blocks[3], "tensor", 4, 3),
    )


def make_bands(conv_weight):
    apart = (
        lax.broadcasted_iota(jnp.int32, (BAND_IN, BAND_OUT), 0)
        - PAD
        - lax.broadcasted_iota(jnp.int32, (BAND_IN, BAND_OUT), 1)
        + REACH
    )
    band = jnp.zeros((conv_weight.shape[0], BAND_IN, BAND_OUT), F32)
    for tap in range(KERNEL):
        band = jnp.where(apart[None] == tap, conv_weight[:, tap][:, None, None], band)
    return band.astype(BF16)


def after(array, *others):
    return lax.optimization_barrier((array, *others))[0]


def hop(arrays, axis, size, bit):
    columns = arrays[0].shape[-1]
    flat = [a.reshape(-1, columns) for a in arrays]
    got = to_partner(jnp.concatenate(flat, axis=0) if len(flat) > 1 else flat[0], axis, size, bit)
    parts, start = [], 0
    for array, rows in zip(arrays, flat, strict=True):
        parts.append(got[start : start + rows.shape[0]].reshape(array.shape))
        start += rows.shape[0]
    return parts


def is_upper(axis, bit):
    return (lax.axis_index(axis) & bit) != 0


def halve(array, axis, bit):
    rows = array.shape[-2] // 2
    low, high = array[..., :rows, :], array[..., rows:, :]
    upper = is_upper(axis, bit)
    return jnp.where(upper, high, low), jnp.where(upper, low, high)


def add(kept, got):
    return (kept.astype(F32) + got.astype(F32)).astype(kept.dtype)


def rejoin(array, got, axis, bit):
    upper = is_upper(axis, bit)
    return jnp.concatenate(
        [jnp.where(upper, got, array), jnp.where(upper, array, got)], axis=-2
    )


def solution(mesh):
    dp_size = mesh.shape["dp"]
    first, second, *others = [1 << b for b in range(dp_size.bit_length() - 1)]

    def dp_hop(arrays, bit):
        return hop(arrays, "dp", dp_size, bit)

    def shards(
        tokens,
        w_query,
        w_key,
        w_value,
        conv_weight,
        w_out,
        gain_one,
        shift_one,
        w_up,
        w_down,
        gain_two,
        shift_two,
        lengths,
        grad_output,
    ):
        width = w_query.shape[1]
        heads = width // HEAD
        features, units = w_up.shape
        me = lax.axis_index("tensor").astype(jnp.int32)
        scalars = jnp.concatenate([lengths[0], me[None]])
        w_t = jnp.concatenate([w_query.T, w_key.T, w_value.T], axis=0)
        bands = make_bands(conv_weight)
        norms = jnp.stack([gain_one, shift_one, gain_two, shift_two])
        tokens_two = to_partner(tokens, "tensor", 4, 2)
        tokens_one = to_partner(tokens, "tensor", 4, 1)
        weights = jnp.concatenate([w_up.T, w_down], axis=0)
        weights_one = to_partner(weights, "tensor", 4, 1)
        turn = lax.axis_index("dp") & 1
        half_units = units // 2
        weights_half = jnp.concatenate(
            [
                lax.dynamic_slice_in_dim(weights, start + turn * half_units, half_units, axis=0)
                for start in (0, units)
            ],
            axis=0,
        )
        tokens_two = after(tokens_two, bands, w_t, weights_half)
        blocks = (tokens, tokens_one, tokens_two, to_partner(tokens_two, "tensor", 4, 1))
        across = to_partner(after(weights_half, tokens_two), "tensor", 4, 2)

        attended = attend(scalars, blocks, w_t, bands)
        saved = (attended[0], *attended[5:])
        contexts = exchange_tensor(attended[1:5])
        across = after(across, attended[1])
        on = to_partner(across, "dp", dp_size, 1)
        normed_low, unit_one, recip_one = norm_in(scalars, contexts, tokens, w_out, norms)
        normed_two = to_partner(normed_low, "tensor", 4, 2)
        on = after(on, normed_low)

        def core_hop(array):
            return to_partner(array, "tensor", 4, 1)

        across_one, on_one = core_hop(across), core_hop(on)
        ups, downs = [
            (
                Joined((weights, which * units, units)),
                Joined((weights_one, which * units, units)),
                Joined(*[(a, which * half_units, half_units) for a in (across, on)]),
                Joined(*[(a, which * half_units, half_units) for a in (across_one, on_one)]),
            )
            for which in (0, 1)
        ]
        output, slope, summed_grad, branch_grad, norm_grads_two = feed(
            scalars, normed_low, unit_one, grad_output, norms, ups, downs
        )
        branch_two = to_partner(branch_grad, "tensor", 4, 2)
        branch_one = core_hop(branch_grad)
        normed_one = core_hop(normed_low)
        resid_grad, grad_w_out, norm_grads_one, *context_grads = feed_back(
            scalars,
            (slope, summed_grad, branch_grad),
            unit_one,
            recip_one,
            contexts,
            w_out,
            norms,
            ups,
            downs,
        )
        context_grads = exchange_tensor(context_grads)
        norm_rows = jnp.concatenate([norm_grads_one, norm_grads_two], axis=0)
        least = max(dp_size, 32)
        part = -(-(features + norm_rows.shape[0]) // (8 * least)) * least
        spare = jnp.zeros((8 * part - features - norm_rows.shape[0], features), BF16)
        small_kept, small_sent = halve(
            jnp.concatenate([grad_w_out, norm_rows.astype(BF16), spare], axis=0), "tensor", 1
        )
        small_got = core_hop(small_sent)
        normed_two, branch_two = after(normed_two, resid_grad), after(branch_two, resid_grad)
        normeds = (normed_low, normed_one, normed_two, core_hop(normed_two))
        branch_grads = (branch_grad, branch_one, branch_two, core_hop(branch_two))
        small = add(small_kept, after(small_got, branch_two))
        small_kept, small_sent = halve(small, "tensor", 2)
        small_got = to_partner(small_sent, "tensor", 4, 2)
        grad_up, grad_down = feed_weights(scalars, normeds, branch_grads, w_up, w_down)
        small = add(small_kept, after(small_got, grad_up))
        up = jnp.concatenate([grad_up, small[:part]], axis=0)
        down = jnp.concatenate([grad_down, small[part:]], axis=0)
        up_kept, up_sent = halve(up, "dp", first)
        down_kept, down_sent = halve(down, "dp", second)
        (up_got,), (down_got,) = dp_hop([up_sent], first), dp_hop([down_sent], second)
        context_grads = [after(context_grads[0], up_sent, down_sent), *context_grads[1:]]

        passed = attend_back(scalars, saved, context_grads, bands)
        up_kept, up_sent = halve(add(up_kept, after(up_got, passed[0])), "dp", second)
        down_kept, down_sent = halve(add(down_kept, after(down_got, passed[0])), "dp", first)
        (up_got,), (down_got,) = dp_hop([up_sent], second), dp_hop([down_sent], first)
        passed = [*passed[:6], after(passed[6], up_sent, down_sent)]
        shares = attend_steps(scalars, saved, passed)
        both = jnp.stack(
            [add(up_kept, after(up_got, shares)), add(down_kept, after(down_got, shares))]
        )
        kept, sent = halve(both, "dp", others[0])
        (got,) = dp_hop([sent], others[0])
        shares = after(shares, sent)
        low, high, *token_grads = attend_grads(
            scalars, passed, shares, blocks, w_t, max(dp_size, 16)
        )
        both = add(kept, after(got, low))
        for bit in others[1:]:
            kept, sent = halve(both, "dp", bit)
            (got,) = dp_hop([sent], bit)
            both = add(kept, got)
        low, high = after(low, both), after(high, both)
        both_got = dp_hop([both], others[-1])[0]
        low_kept, low_sent = halve(low, "dp", first)
        high_kept, high_sent = halve(high, "dp", second)
        (low_got,), (high_got,) = dp_hop([low_sent], first), dp_hop([high_sent], second)
        token_got = (core_hop(token_grads[3]), core_hop(token_grads[1]))
        away = add(token_grads[2], after(token_got[0], low_sent, high_sent))
        arrived = to_partner(away, "tensor", 4, 2)
        low_kept, low_sent = halve(add(low_kept, after(low_got, away)), "dp", second)
        high_kept, high_sent = halve(add(high_kept, after(high_got, away)), "dp", first)
        (low_got,), (high_got,) = dp_hop([low_sent], second), dp_hop([high_sent], first)
        both = rejoin(both, after(both_got, low_sent, high_sent), "dp", others[-1])
        for bit in reversed(others[:-1]):
            (got,) = dp_hop([both], bit)
            both = rejoin(both, got, "dp", bit)
        up, down = both[0], both[1]
        (up_got,), (down_got,) = dp_hop([up], second), dp_hop([down], first)
        wide = jnp.stack(
            [add(low_kept, after(low_got, both)), add(high_kept, after(high_got, both))]
        )
        for bit in others:
            (got,) = dp_hop([wide], bit)
            wide = add(wide, got)
        up = rejoin(up, after(up_got, wide), "dp", second)
        down = rejoin(down, after(down_got, wide), "dp", first)
        (up_got,), (down_got,) = dp_hop([up], first), dp_hop([down], second)
        wide = after(wide, up, down)
        low, high = wide[0], wide[1]
        (low_got,), (high_got,) = dp_hop([low], second), dp_hop([high], first)
        low, high = rejoin(low, low_got, "dp", second), rejoin(high, high_got, "dp", first)
        (low_got,), (high_got,) = dp_hop([low], first), dp_hop([high], second)
        up = rejoin(up, after(up_got, low), "dp", first)
        down = rejoin(down, after(down_got, low), "dp", second)
        small = jnp.concatenate([up[features:], down[units:]], axis=0)
        small = rejoin(small, to_partner(small, "tensor", 4, 2), "tensor", 2)
        small = rejoin(small, core_hop(small), "tensor", 1).astype(F32)
        here = token_grads[0].astype(F32) + token_got[1].astype(F32)
        grad_tokens = resid_grad + here + after(arrived, low_sent).astype(F32)
        qkv_wide = jnp.concatenate(
            [
                rejoin(low, low_got, "dp", first),
                rejoin(high, high_got, "dp", second),
            ],
            axis=0,
        ).astype(F32)
        grad_up, grad_down = up[:features].astype(F32), down[:units].astype(F32)
        return (
            output,
            grad_tokens,
            qkv_wide[:width].T,
            qkv_wide[width : 2 * width].T,
            qkv_wide[2 * width : 3 * width].T,
            qkv_wide[3 * width : 3 * width + heads, :KERNEL],
            small[:features],
            small[features],
            small[features + 1],
            grad_up,
            grad_down,
            small[features + 8],
            small[features + 9],
        )

    rows = P(("dp", "tensor"), None)
    columns = P(None, "tensor")
    in_specs = (
        rows,
        columns,
        columns,
        columns,
        P("tensor", None),
        P(),
        P(),
        P(),
        columns,
        P("tensor", None),
        P(),
        P(),
        P("dp", None),
        rows,
    )
    out_specs = (
        rows,
        rows,
        columns,
        columns,
        columns,
        P("tensor", None),
        P(),
        P(),
        P(),
        columns,
        P("tensor", None),
        P(),
        P(),
    )
    return jax.shard_map(shards, mesh=mesh, in_specs=in_specs, out_specs=out_specs, check_vma=False)
```

time: 972 us -> 311 us (0.32)
  waiting for transfers between devices: 475 us -> 71.2 us
  matrix products: 214 us -> 0 us
  Pallas kernels: 0 us -> 140 us
  blocking collectives: 93.5 us -> 0 us
  other arithmetic: 109 us -> 35 us
  starting transfers between devices: 4.09 us -> 45.4 us
  local copies, waits for them, and re-layouts: 47.9 us -> 14.1 us
  between operations: 18.3 us -> 2 us
    psum x2 -> x0, waiting for transfers between devices: 287 us -> none  [the longest x1 226 us: shards(): lax.psum((grad_w_query, grad_w_key, grad_w_value, grad_conv, grad_up, gra...]
    dot_general x108 -> x0, matrix products: 211 us -> none  [the longest x36 33.5 us: iterative_pseudoinverse(): jnp.einsum('hij,hjk->hik', product, bracket, precision=TOP_PRECISION)]
    pallas_call x0 -> x8, Pallas kernels: none -> 140 us  [local_call(): pl.pallas_call(body, name=name, out_shape=out_shape, in_specs=[pl.BlockSp...]
    all_gather x3 -> x0, waiting for transfers between devices: 90.1 us -> none  [the longest x1 33.1 us: shards(): normed_group = lax.all_gather(normed_low, 'tensor', axis=0, tiled=True)]
    reduce_scatter x3 -> x0, waiting for transfers between devices: 84.1 us -> none  [the longest x1 43 us: shards(): lax.psum_scatter(jnp.dot(hidden, w_down, preferred_element_type=jnp.float...]
    psum x2 -> x0, blocking collectives: 77.4 us -> none  [the longest x1 39.9 us: shards(): lax.psum((grad_w_out, grad_gain_one, grad_shift_one, grad_gain_two, grad_...]
    ppermute x0 -> x46, waiting for transfers between devices: none -> 71.2 us  [to_partner(): return lax.ppermute(array, axis, [(i, i ^ bit) for i in range(size)])]
    ppermute x0 -> x46, starting transfers between devices: none -> 45.4 us  [to_partner(): return lax.ppermute(array, axis, [(i, i ^ bit) for i in range(size)])]
  transfers between devices with their start and end apart: 9 -> 46, of which waited for: 8 -> 20; matrix products, arithmetic and copies ran while one was open for 6% -> 13% of each run, Pallas kernels for 0% -> 46%
where the time goes in v2:
time: 311 us; the launch traced here: 308 us
  Pallas kernels  140 us (45%)
  waiting for transfers between devices  71.2 us (23%)
  starting transfers between devices  45.4 us (15%)
  other arithmetic  35 us (11%)
  local copies, waits for them, and re-layouts  14.1 us (5%)
    pallas_call x8, Pallas kernels, local_call(): pl.pallas_call(body, name=name, out_shape=out_shape, in_specs=[pl.BlockSp...  140 us
    ppermute x46, waiting for transfers between devices, to_partner(): return lax.ppermute(array, axis, [(i, i ^ bit) for i in range(size)])  71.2 us
    ppermute x46, starting transfers between devices, to_partner(): return lax.ppermute(array, axis, [(i, i ^ bit) for i in range(size)])  45.4 us
    convert_element_type x1, other arithmetic, make_bands(): return band.astype(BF16)  6.7 us
    unnamed x131, local copies, waits for them, and re-layouts  6.39 us
  transfers between devices with their start and end apart: 46, of which 20 were waited for; matrix products, arithmetic and copies ran while one was open for 13% of the time, Pallas kernels for 46%

profile of v2, /device:TPU:0, one launch (start us, length us, event | category | flops | bytes accessed | tf_op | source)
XLA Modules:
  0.0 308.1 jit_solution(15105088229018363115)
XLA Ops:
  0.6 3.0 collective-permute-start.1
  3.7 2.5 slice_reduce_fusion.32
  6.1 2.2 slice_reduce_fusion.31
  8.3 4.5 %fusion.37 = (pred[512,256]{1,0:T(8,128)(4,1)}, pred[512,256]{1,0:T(8,128)(4,1)}, pred[512,256]{1,0:T(8,128)(4,1)}, pred[512,256]{1,0:T(8,128)(4,1)}, pred[512,2...) fusion(s32[512]{0:T(512)S(1)} %iota_add_fusion), kind=kLoop, calls=%fused_computation.85 | loop fusion | flops 4587520 | bytes 4327424 | tf_op jit(solution)/shard_map/eq | solution.py:1228
  14.1 1.6 fusion.3
  16.2 1.0 pad_maximum_fusion.4.refs_0_.refs_5_
  18.3 6.7 %select_convert_fusion.refs_5_.refs_11_ = bf16[3,512,256]{2,1,0:T(8,128)(2,1)} fusion(bf16[3]{0:T(256)(128)(2,1)} %get-tuple-element.194, bf16[3]{0:T(256)(128)(2,1)} %get-tuple-element.195, bf16[3]{0:T(256)(128)(2,1)S(1)} %get-tuple-element.164, bf16[3]{0:T(256)(128)(2,1)S(1)} %get-tuple-element.165, bf16[3]{0:T(256)(128)(2,1)S(1)} %get-tuple-element.166, ...), kind=kLoop, calls=%fused_computation.9 | loop fusion | flops 12976128 | bytes 5112006 | tf_op jit(solution)/shard_map/convert_element_type | solution.py:1229
  25.7 1.2 pad_add_fusion.scalar_ref
  27.0 1.7 collective-permute-start.7
  28.7 26.1 %attend.1 = (bf16[576,2816]{1,0:T(8,128)(2,1)}, bf16[192,640]{1,0:T(8,128)(2,1)}, bf16[192,640]{1,0:T(8,128)(2,1)}, bf16[192,640]{1,0:T(8,128)(2,1)}, bf16[192,6...) custom-call(s32[4]{0:T(128)} %pad_add_fusion.scalar_ref, ...), custom_call_target="tpu_custom_call" | custom-call | flops 30000001024 | bytes 14358528 | tf_op jit(solution)/shard_map/attend/pallas_call | solution.py:240
  55.5 1.8 collective-permute-start.8
  57.3 1.6 pad_maximum_fusion.refs_2_.refs_8_.refs_9_
  59.4 1.5 collective-permute-start.4
  61.6 1.8 collective-permute-done.3.refs_1_.refs_20_
  63.8 4.4 %collective-permute-done.4.refs_2_.refs_21_ = bf16[192,640]{1,0:T(8,128)(2,1)S(1)} collective-permute-done((bf16[192,640]{1,0:T(8,128)(2,1)S(1)}, bf16[192,640]{1,0:T(8,128)(2,1)S(1)}, u32[]{:S(2)}, u32[]{:S(2)}) %collective-permute-start.4) | collective-permute-done | bytes 245792 | tf_op jit(solution)/shard_map/ppermute | solution.py:1207
  68.2 3.6 %collective-permute-done.5.refs_3_.refs_22_ = bf16[192,640]{1,0:T(8,128)(2,1)} collective-permute-done((bf16[192,640]{1,0:T(8,128)(2,1)S(1)}, bf16[192,640]{1,0:T(8,128)(2,1)}, u32[]{:S(2)}, u32[]{:S(2)}) %collective-permute-start.5) | collective-permute-done | bytes 245792 | tf_op jit(solution)/shard_map/ppermute | solution.py:1207
  71.8 7.5 %norm_in.1 = (bf16[640,768]{1,0:T(8,128)(2,1)}, f32[640,768]{1,0:T(8,128)}, f32[640,128]{1,0:T(8,128)}) custom-call(s32[4]{0:T(128)} %pad_add_fusion.scalar_ref, bf16[192,640]{1,0:T(8,128)(2,1)} %get-tuple-element.87.refs_0_.refs_19_, bf16[192,640]{1,0:T(8,128)(2,1)} %copy-done.60, bf16[192,640]{1,0:T(8,128)(2,1)} %copy-done.61, ...), custom_call_target="tpu_custom_call" | custom-call | flops 6000000000 | bytes 6434816 | tf_op jit(solution)/shard_map/norm_in/pallas_call | solution.py:240
  79.4 4.0 %collective-permute-done.8.refs_5_.refs_11_.refs_12_ = bf16[768,768]{1,0:T(8,128)(2,1)S(1)} collective-permute-done((bf16[768,768]{1,0:T(8,128)(2,1)}, bf16[768,768]{1,0:T(8,128)(2,1)S(1)}, u32[]{:S(2)}, u32[]{:S(2)}) %collective-permute-start.8) | collective-permute-done | bytes 1179680 | tf_op jit(solution)/shard_map/ppermute | solution.py:1207
  83.5 1.7 collective-permute-start.13
  85.2 1.2 collective-permute-done.10.refs_7_.refs_13_.refs_14_
  86.6 19.0 %feed.1 = (f32[640,768]{1,0:T(8,128)}, bf16[640,3072]{1,0:T(8,128)(2,1)}, f32[640,768]{1,0:T(8,128)}, bf16[640,768]{1,0:T(8,128)(2,1)}, f32[8,768]{1,0:T(8,128)}) custom-call(s32[4]{0:T(128)} %pad_add_fusion.scalar_ref, bf16[640,768]{1,0:T(8,128)(2,1)} %get-tuple-element.91.refs_0_.refs_2_, f32[4,768]{1,0:T(4,128)} %pad_maximum_fusion.18.refs_6_.refs_1_, ...), custom_call_target="tpu_custom_call" | custom-call | flops 22000001024 | bytes 31690752 | tf_op jit(solution)/shard_map/feed/pallas_call | solution.py:240
  105.6 1.6 collective-permute-start.14
  107.2 17.4 %feed_back.1 = (f32[640,768]{1,0:T(8,128)}, bf16[768,768]{1,0:T(8,128)(2,1)}, f32[8,768]{1,0:T(8,128)}, bf16[192,640]{1,0:T(8,128)(2,1)}, bf16[192,640]{1,0:T(8,...) custom-call(s32[4]{0:T(128)} %pad_add_fusion.scalar_ref, ...), custom_call_target="tpu_custom_call" | custom-call | flops 20000000000 | bytes 34377728 | tf_op jit(solution)/shard_map/feed_back/pallas_call | solution.py:240
  125.5 1.5 broadcast_select_fusion.2
  128.0 1.9 collective-permute-done.14.refs_7_
  131.1 1.3 collective-permute-start.20
  132.3 1.6 collective-permute-done.15.refs_8_
  134.1 1.5 collective-permute-start.18
  135.7 24.1 %feed_weights.1 = (bf16[768,768]{1,0:T(8,128)(2,1)}, bf16[768,768]{1,0:T(8,128)(2,1)}) custom-call(s32[4]{0:T(128)} %pad_add_fusion.scalar_ref, bf16[768,768]{1,0:T(8,128)(2,1)} %refs_0_.1, bf16[768,768]{1,0:T(8,128)(2,1)} %refs_1_.3, bf16[640,768]{1,0:T(8,128)(2,1)} %get-tuple-element.91.refs_0_.refs_2_, ...), custom_call_target="tpu_custom_call" | custom-call | flops 24999999488 | bytes 12582912 | tf_op jit(solution)/shard_map/feed_weights/pallas_call | solution.py:240
  160.0 1.0 copy-done.2
  161.0 1.0 broadcast_select_fusion.5
  162.0 1.6 collective-permute-start.23
  163.6 1.1 broadcast_select_fusion.8
  164.7 1.5 collective-permute-start.22
  166.2 19.6 %attend_back.1 = (bf16[192,2560]{1,0:T(8,128)(2,1)}, f32[8,128]{1,0:T(8,128)}, f32[192,2560]{1,0:T(8,128)}, f32[192,2560]{1,0:T(8,128)}, f32[3,192,64]{2,1,0:T(8...) custom-call(s32[4]{0:T(128)} %pad_add_fusion.scalar_ref, bf16[192,640]{1,0:T(8,128)(2,1)} %get-tuple-element.112.refs_0_, ...), custom_call_target="tpu_custom_call" | custom-call | flops 8000000000 | bytes 11216896 | tf_op jit(solution)/shard_map/attend_back/pallas_call | solution.py:240
  186.7 1.3 add_convert_fusion.2
  190.1 11.4 %attend_steps.1.refs_4_ = bf16[2,9,64,64]{3,2,1,0:T(8,128)(2,1)} custom-call(s32[4]{0:T(128)} %pad_add_fusion.scalar_ref, f32[3,192,64]{2,1,0:T(8,128)} %get-tuple-element.130.refs_0_, f32[3,192,64]{2,1,0:T(8,128)} %get-tuple-element.119.refs_7_.refs_1_, f32[3,64,192]{2,1,0:T(8,128)} %get-tuple-element.131.refs_2_, ...), custom_call_target="tpu_custom_call" | custom-call | flops 5000000000 | bytes 4571136 | tf_op jit(solution)/shard_map/attend_steps/pallas_call | solution.py:240
  201.9 2.7 collective-permute-start.28
  204.5 15.3 %attend_grads.1 = (bf16[304,768]{1,0:T(8,128)(2,1)}, bf16[304,768]{1,0:T(8,128)(2,1)}, bf16[640,768]{1,0:T(8,128)(2,1)}, bf16[640,768]{1,0:T(8,128)(2,1)}, bf16[...) custom-call(s32[4]{0:T(128)} %pad_add_fusion.scalar_ref, bf16[192,2560]{1,0:T(8,128)(2,1)} %get-tuple-element.123.refs_0_, ...), custom_call_target="tpu_custom_call" | custom-call | flops 8000000000 | bytes 14749696 | tf_op jit(solution)/shard_map/attend_grads/pallas_call | solution.py:240
  220.8 1.7 collective-permute-start.33
  222.5 1.6 collective-permute-start.30
  225.0 1.2 add_convert_fusion
  226.2 4.0 %collective-permute-done.33 = bf16[152,768]{1,0:T(8,128)(2,1)S(1)} collective-permute-done((bf16[152,768]{1,0:T(8,128)(2,1)S(1)}, bf16[152,768]{1,0:T(8,128)(2,1)S(1)}, u32[]{:S(2)}, u32[]{:S(2)}) %collective-permute-start.33) | collective-permute-done | bytes 233504 | tf_op jit(solution)/shard_map/ppermute | solution.py:1207
  231.5 1.7 collective-permute-start.34
  233.2 8.4 %collective-permute-done.32 = bf16[224,768]{1,0:T(8,128)(2,1)S(1)} collective-permute-done((bf16[224,768]{1,0:T(8,128)(2,1)S(1)}, bf16[224,768]{1,0:T(8,128)(2,1)S(1)}, u32[]{:S(2)}, u32[]{:S(2)}) %collective-permute-start.32) | collective-permute-done | bytes 344096 | tf_op jit(solution)/shard_map/ppermute | solution.py:1207
  242.2 1.0 collective-permute-start.37
  243.2 1.9 collective-permute-start.36
  245.1 7.9 %collective-permute-done.35 = bf16[152,768]{1,0:T(8,128)(2,1)S(1)} collective-permute-done((bf16[152,768]{1,0:T(8,128)(2,1)S(1)}, bf16[152,768]{1,0:T(8,128)(2,1)S(1)}, u32[]{:S(2)}, u32[]{:S(2)}) %collective-permute-start.35) | collective-permute-done | bytes 233504 | tf_op jit(solution)/shard_map/ppermute | solution.py:1207
  253.1 2.7 collective-permute-done.36
  256.3 1.6 collective-permute-start.40
  257.8 3.2 %collective-permute-done.38 = bf16[76,768]{1,0:T(8,128)(2,1)S(1)} collective-permute-done((bf16[76,768]{1,0:T(8,128)(2,1)S(1)}, bf16[76,768]{1,0:T(8,128)(2,1)S(1)}, u32[]{:S(2)}, u32[]{:S(2)}) %collective-permute-start.38) | collective-permute-done | bytes 116768 | tf_op jit(solution)/shard_map/ppermute | solution.py:1207
  262.0 1.7 collective-permute-start.39
  263.7 2.2 collective-permute-start.43
  267.2 1.0 collective-permute-done.39
  268.2 3.5 %collective-permute-start.41 = (bf16[152,768]{1,0:T(8,128)(2,1)S(1)}, bf16[152,768]{1,0:T(8,128)(2,1)S(1)}, u32[]{:S(2)}, u32[]{:S(2)}) collective-permute-start(bf16[152,768]{1,0:T(8,128)(2,1)S(1)} %pad_maximum_fusion.17), channel_id=1, source_target_pairs={{0,8},{4,12},{8,0},{12,4},{16,24},{20,28},{24,16},{28,20},{1,9},{5... | collective-permute-start | bytes 700424 | tf_op jit(solution)/shard_map/ppermute | solution.py:1207
  271.8 9.6 %collective-permute-done.41 = bf16[152,768]{1,0:T(8,128)(2,1)S(1)} collective-permute-done((bf16[152,768]{1,0:T(8,128)(2,1)S(1)}, bf16[152,768]{1,0:T(8,128)(2,1)S(1)}, u32[]{:S(2)}, u32[]{:S(2)}) %collective-permute-start.41) | collective-permute-done | bytes 233504 | tf_op jit(solution)/shard_map/ppermute | solution.py:1207
  281.8 2.2 collective-permute-done.42
  284.3 1.6 collective-permute-start.44
  286.0 1.2 slice_bitcast_fusion
  287.3 11.2 %collective-permute-done.44 = bf16[256,768]{1,0:T(8,128)(2,1)S(1)} collective-permute-done((bf16[256,768]{1,0:T(8,128)(2,1)S(1)}, bf16[256,768]{1,0:T(8,128)(2,1)S(1)}, u32[]{:S(2)}, u32[]{:S(2)}) %collective-permute-start.44) | collective-permute-done | bytes 393248 | tf_op jit(solution)/shard_map/ppermute | solution.py:1207
  300.4 1.7 convert_add_fusion
  302.0 1.6 fusion
  303.6 1.6 fusion.1
  306.3 1.6 slice.320
  (242 shorter events, 22.9 us)
Async XLA Ops:
  0.6 25.1 %collective-permute-start.1 = (bf16[640,768]{1,0:T(8,128)(2,1)}, bf16[640,768]{1,0:T(8,128)(2,1)}, u32[]{:S(2)}, u32[]{:S(2)}) collective-permute-start(bf16[640,768]{1,0:T(8,128)(2,1)} %refs_6_.1), channel_id=1, source_target_pairs={{0,2},{1,3},{2,0},{3,1},{4,6},{5,7},{6,4},{7,5},{8,10},{9,11},{10,... | collective-permute-start | bytes 2949128 | tf_op jit(solution)/shard_map/ppermute | solution.py:1207
  3.6 25.1 %collective-permute-start = (bf16[640,768]{1,0:T(8,128)(2,1)}, bf16[640,768]{1,0:T(8,128)(2,1)}, u32[]{:S(2)}, u32[]{:S(2)}) collective-permute-start(bf16[640,768]{1,0:T(8,128)(2,1)} %refs_6_.1), channel_id=1, source_target_pairs={{0,1},{1,0},{2,3},{3,2},{4,5},{5,4},{6,7},{7,6},{8,9},{9,8},{10,11... | collective-permute-start | bytes 2949128 | tf_op jit(solution)/shard_map/ppermute | solution.py:1207
  8.3 4.5 %copy-start.7 = (bf16[768,768]{1,0:T(8,128)(2,1)S(1)}, bf16[768,768]{1,0:T(8,128)(2,1)}, u32[]{:S(2)}) copy-start(bf16[768,768]{1,0:T(8,128)(2,1)} %refs_0_.1) | copy-start | bytes 3538948
  14.1 3.1 %copy-start.44 = (pred[512,256]{1,0:T(8,128)(4,1)S(1)}, pred[512,256]{1,0:T(8,128)(4,1)}, u32[]{:S(2)}) copy-start(pred[512,256]{1,0:T(8,128)(4,1)} %get-tuple-element.263) | copy-start | bytes 393220
  25.7 3.0 collective-permute-start.2
  27.0 28.5 %collective-permute-start.7 = (bf16[768,768]{1,0:T(8,128)(2,1)S(1)}, bf16[768,768]{1,0:T(8,128)(2,1)}, u32[]{:S(2)}, u32[]{:S(2)}) collective-permute-start(bf16[768,768]{1,0:T(8,128)(2,1)S(1)} %pad_maximum_fusion.3), channel_id=1, source_target_pairs={{0,2},{1,3},{2,0},{3,1},{4,6},{5,7},{6,4},{7,5},{8,10},{9,11},{10,... | collective-permute-start | bytes 3538952 | tf_op jit(solution)/shard_map/ppermute | solution.py:1207
  55.4 3.4 %copy-start.64 = (bf16[192,640]{1,0:T(8,128)(2,1)S(1)}, bf16[192,640]{1,0:T(8,128)(2,1)}, u32[]{:S(2)}) copy-start(bf16[192,640]{1,0:T(8,128)(2,1)} %get-tuple-element.88) | copy-start | bytes 737284
  55.5 3.9 %copy-start.63 = (bf16[192,640]{1,0:T(8,128)(2,1)S(1)}, bf16[192,640]{1,0:T(8,128)(2,1)}, u32[]{:S(2)}) copy-start(bf16[192,640]{1,0:T(8,128)(2,1)} %get-tuple-element.89) | copy-start | bytes 737284
  55.5 5.4 %copy-start.62 = (bf16[192,640]{1,0:T(8,128)(2,1)S(1)}, bf16[192,640]{1,0:T(8,128)(2,1)}, u32[]{:S(2)}) copy-start(bf16[192,640]{1,0:T(8,128)(2,1)} %get-tuple-element.90) | copy-start | bytes 737284
  55.5 5.4 %copy-start.49 = (f32[768]{0:T(1024)S(1)}, f32[768]{0:T(1024)}, u32[]{:S(2)}) copy-start(f32[768]{0:T(1024)} %param.20) | copy-start | bytes 9220
  55.5 5.5 %copy-start.50 = (f32[768]{0:T(1024)S(1)}, f32[768]{0:T(1024)}, u32[]{:S(2)}) copy-start(f32[768]{0:T(1024)} %param.21) | copy-start | bytes 9220
  55.5 5.5 %copy-start.51 = (f32[768]{0:T(1024)S(1)}, f32[768]{0:T(1024)}, u32[]{:S(2)}) copy-start(f32[768]{0:T(1024)} %param.24) | copy-start | bytes 9220
  55.5 5.5 %copy-start.52 = (f32[768]{0:T(1024)S(1)}, f32[768]{0:T(1024)}, u32[]{:S(2)}) copy-start(f32[768]{0:T(1024)} %param.25) | copy-start | bytes 9220
  55.5 27.9 %collective-permute-start.8 = (bf16[768,768]{1,0:T(8,128)(2,1)}, bf16[768,768]{1,0:T(8,128)(2,1)S(1)}, u32[]{:S(2)}, u32[]{:S(2)}) collective-permute-start(bf16[768,768]{1,0:T(8,128)(2,1)} %collective-permute-done.7.refs_4_.refs_10_.refs_11_), channel_id=1, source_target_pairs={{0,4},{4,0},{8,12},{12,8},{16,20},{20,16},{24,28},{28,24},{1,5},{5... | collective-permute-start | bytes 3538952 | tf_op jit(solution)/shard_map/ppermute | solution.py:1207
  58.9 26.3 %collective-permute-start.6 = (bf16[1536,768]{1,0:T(8,128)(2,1)}, bf16[1536,768]{1,0:T(8,128)(2,1)S(1)}, u32[]{:S(2)}, u32[]{:S(2)}) collective-permute-start(bf16[1536,768]{1,0:T(8,128)(2,1)} %pad_maximum_fusion.refs_2_.refs_8_.refs_9_), channel_id=1, source_target_pairs={{0,1},{1,0},{2,3},{3,2},{4,5},{5,4},{6,7},{7,6},{8,9},{9,8},{10,11... | collective-permute-start | bytes 7077896 | tf_op jit(solution)/shard_map/ppermute | solution.py:1207
  58.9 4.5 %collective-permute-start.3 = (bf16[192,640]{1,0:T(8,128)(2,1)S(1)}, bf16[192,640]{1,0:T(8,128)(2,1)S(1)}, u32[]{:S(2)}, u32[]{:S(2)}) collective-permute-start(bf16[192,640]{1,0:T(8,128)(2,1)S(1)} %copy-done.64), channel_id=1, source_target_pairs={{0,1},{1,0},{2,3},{3,2},{4,5},{5,4},{6,7},{7,6},{8,9},{9,8},{10,11... | collective-permute-start | bytes 737288 | tf_op jit(solution)/shard_map/ppermute | solution.py:1207
  59.4 8.8 %collective-permute-start.4 = (bf16[192,640]{1,0:T(8,128)(2,1)S(1)}, bf16[192,640]{1,0:T(8,128)(2,1)S(1)}, u32[]{:S(2)}, u32[]{:S(2)}) collective-permute-start(bf16[192,640]{1,0:T(8,128)(2,1)S(1)} %copy-done.63), channel_id=1, source_target_pairs={{0,2},{1,3},{2,0},{3,1},{4,6},{5,7},{6,4},{7,5},{8,10},{9,11},{10,... | collective-permute-start | bytes 737288 | tf_op jit(solution)/shard_map/ppermute | solution.py:1207
  60.9 10.9 %collective-permute-start.5 = (bf16[192,640]{1,0:T(8,128)(2,1)S(1)}, bf16[192,640]{1,0:T(8,128)(2,1)}, u32[]{:S(2)}, u32[]{:S(2)}) collective-permute-start(bf16[192,640]{1,0:T(8,128)(2,1)S(1)} %copy-done.62), channel_id=1, source_target_pairs={{0,3},{1,2},{2,1},{3,0},{4,7},{5,6},{6,5},{7,4},{8,11},{9,10},{10,... | collective-permute-start | bytes 737288 | tf_op jit(solution)/shard_map/ppermute | solution.py:1207
  63.4 8.4 %copy-start.60 = (bf16[192,640]{1,0:T(8,128)(2,1)}, bf16[192,640]{1,0:T(8,128)(2,1)S(1)}, u32[]{:S(2)}) copy-start(bf16[192,640]{1,0:T(8,128)(2,1)S(1)} %collective-permute-done.3.refs_1_.refs_20_) | copy-start | bytes 737284
  63.4 21.8 %collective-permute-start.9 = (bf16[768,768]{1,0:T(8,128)(2,1)}, bf16[768,768]{1,0:T(8,128)(2,1)}, u32[]{:S(2)}, u32[]{:S(2)}) collective-permute-start(bf16[768,768]{1,0:T(8,128)(2,1)} %collective-permute-done.7.refs_4_.refs_10_.refs_11_), channel_id=1, source_target_pairs={{0,1},{1,0},{2,3},{3,2},{4,5},{5,4},{6,7},{7,6},{8,9},{9,8},{10,11... | collective-permute-start | bytes 3538952 | tf_op jit(solution)/shard_map/ppermute | solution.py:1207
  68.2 3.6 %copy-start.61 = (bf16[192,640]{1,0:T(8,128)(2,1)}, bf16[192,640]{1,0:T(8,128)(2,1)S(1)}, u32[]{:S(2)}) copy-start(bf16[192,640]{1,0:T(8,128)(2,1)S(1)} %collective-permute-done.4.refs_2_.refs_21_) | copy-start | bytes 737284
  83.4 3.0 copy-start.58
  83.4 3.0 collective-permute-start.10
  83.5 44.1 %collective-permute-start.13 = (bf16[640,768]{1,0:T(8,128)(2,1)}, bf16[640,768]{1,0:T(8,128)(2,1)}, u32[]{:S(2)}, u32[]{:S(2)}) collective-permute-start(bf16[640,768]{1,0:T(8,128)(2,1)} %get-tuple-element.91.refs_0_.refs_2_), channel_id=1, source_target_pairs={{0,2},{1,3},{2,0},{3,1},{4,6},{5,7},{6,4},{7,5},{8,10},{9,11},{10,... | collective-permute-start | bytes 2949128 | tf_op jit(solution)/shard_map/ppermute | solution.py:1207
  105.6 24.3 %collective-permute-start.14 = (bf16[640,768]{1,0:T(8,128)(2,1)}, bf16[640,768]{1,0:T(8,128)(2,1)}, u32[]{:S(2)}, u32[]{:S(2)}) collective-permute-start(bf16[640,768]{1,0:T(8,128)(2,1)} %get-tuple-element.97.refs_0_.refs_3_), channel_id=1, source_target_pairs={{0,2},{1,3},{2,0},{3,1},{4,6},{5,7},{6,4},{7,5},{8,10},{9,11},{10,... | collective-permute-start | bytes 2949128 | tf_op jit(solution)/shard_map/ppermute | solution.py:1207
  107.2 18.3 %copy-start.48 = (f32[8,768]{1,0:T(8,128)S(1)}, f32[8,768]{1,0:T(8,128)}, u32[]{:S(2)}) copy-start(f32[8,768]{1,0:T(8,128)} %get-tuple-element.108) | copy-start | bytes 73732
  124.6 5.8 %copy-start = (bf16[768,768]{1,0:T(8,128)(2,1)S(1)}, bf16[768,768]{1,0:T(8,128)(2,1)}, u32[]{:S(2)}) copy-start(bf16[768,768]{1,0:T(8,128)(2,1)} %get-tuple-element.106) | copy-start | bytes 3538948
  127.0 2.9 collective-permute-start.17
  127.0 4.0 %collective-permute-start.11 = (bf16[640,768]{1,0:T(8,128)(2,1)}, bf16[640,768]{1,0:T(8,128)(2,1)}, u32[]{:S(2)}, u32[]{:S(2)}) collective-permute-start(bf16[640,768]{1,0:T(8,128)(2,1)} %get-tuple-element.91.refs_0_.refs_2_), channel_id=1, source_target_pairs={{0,1},{1,0},{2,3},{3,2},{4,5},{5,4},{6,7},{7,6},{8,9},{9,8},{10,11... | collective-permute-start | bytes 2949128 | tf_op jit(solution)/shard_map/ppermute | solution.py:1207
  127.5 6.6 %collective-permute-start.12 = (bf16[640,768]{1,0:T(8,128)(2,1)}, bf16[640,768]{1,0:T(8,128)(2,1)}, u32[]{:S(2)}, u32[]{:S(2)}) collective-permute-start(bf16[640,768]{1,0:T(8,128)(2,1)} %get-tuple-element.97.refs_0_.refs_3_), channel_id=1, source_target_pairs={{0,1},{1,0},{2,3},{3,2},{4,5},{5,4},{6,7},{7,6},{8,9},{9,8},{10,11... | collective-permute-start | bytes 2949128 | tf_op jit(solution)/shard_map/ppermute | solution.py:1207
  127.6 6.3 %collective-permute-start.15 = (bf16[640,768]{1,0:T(8,128)(2,1)}, bf16[640,768]{1,0:T(8,128)(2,1)}, u32[]{:S(2)}, u32[]{:S(2)}) collective-permute-start(bf16[640,768]{1,0:T(8,128)(2,1)} %collective-permute-done.13.refs_6_), channel_id=1, source_target_pairs={{0,1},{1,0},{2,3},{3,2},{4,5},{5,4},{6,7},{7,6},{8,9},{9,8},{10,11... | collective-permute-start | bytes 2949128 | tf_op jit(solution)/shard_map/ppermute | solution.py:1207
  129.9 5.8 %collective-permute-start.16 = (bf16[640,768]{1,0:T(8,128)(2,1)}, bf16[640,768]{1,0:T(8,128)(2,1)}, u32[]{:S(2)}, u32[]{:S(2)}) collective-permute-start(bf16[640,768]{1,0:T(8,128)(2,1)} %collective-permute-done.14.refs_7_), channel_id=1, source_target_pairs={{0,1},{1,0},{2,3},{3,2},{4,5},{5,4},{6,7},{7,6},{8,9},{9,8},{10,11... | collective-permute-start | bytes 2949128 | tf_op jit(solution)/shard_map/ppermute | solution.py:1207
  129.9 36.3 %collective-permute-start.19 = (bf16[192,640]{1,0:T(8,128)(2,1)}, bf16[192,640]{1,0:T(8,128)(2,1)}, u32[]{:S(2)}, u32[]{:S(2)}) collective-permute-start(bf16[192,640]{1,0:T(8,128)(2,1)} %get-tuple-element.113), channel_id=1, source_target_pairs={{0,1},{1,0},{2,3},{3,2},{4,5},{5,4},{6,7},{7,6},{8,9},{9,8},{10,11... | collective-permute-start | bytes 737288 | tf_op jit(solution)/shard_map/ppermute | solution.py:1207
  131.1 35.1 %collective-permute-start.20 = (bf16[192,640]{1,0:T(8,128)(2,1)}, bf16[192,640]{1,0:T(8,128)(2,1)}, u32[]{:S(2)}, u32[]{:S(2)}) collective-permute-start(bf16[192,640]{1,0:T(8,128)(2,1)} %get-tuple-element.114), channel_id=1, source_target_pairs={{0,2},{1,3},{2,0},{3,1},{4,6},{5,7},{6,4},{7,5},{8,10},{9,11},{10,... | collective-permute-start | bytes 737288 | tf_op jit(solution)/shard_map/ppermute | solution.py:1207
  133.9 32.3 %collective-permute-start.21 = (bf16[192,640]{1,0:T(8,128)(2,1)}, bf16[192,640]{1,0:T(8,128)(2,1)}, u32[]{:S(2)}, u32[]{:S(2)}) collective-permute-start(bf16[192,640]{1,0:T(8,128)(2,1)} %get-tuple-element.115), channel_id=1, source_target_pairs={{0,3},{1,2},{2,1},{3,0},{4,7},{5,6},{6,5},{7,4},{8,11},{9,10},{10,... | collective-permute-start | bytes 737288 | tf_op jit(solution)/shard_map/ppermute | solution.py:1207
  134.1 25.6 %collective-permute-start.18 = (bf16[256,768]{1,0:T(8,128)(2,1)S(1)}, bf16[256,768]{1,0:T(8,128)(2,1)S(1)}, u32[]{:S(2)}, u32[]{:S(2)}) collective-permute-start(bf16[256,768]{1,0:T(8,128)(2,1)S(1)} %broadcast_select_fusion.11), channel_id=1, source_target_pairs={{0,2},{1,3},{2,0},{3,1},{4,6},{5,7},{6,4},{7,5},{8,10},{9,11},{10,... | collective-permute-start | bytes 1179656 | tf_op jit(solution)/shard_map/ppermute | solution.py:1207
  160.0 3.6 %copy-start.1 = (bf16[768,768]{1,0:T(8,128)(2,1)S(1)}, bf16[768,768]{1,0:T(8,128)(2,1)}, u32[]{:S(2)}) copy-start(bf16[768,768]{1,0:T(8,128)(2,1)} %get-tuple-element.105) | copy-start | bytes 3538948
  162.0 23.8 %collective-permute-start.23 = (bf16[448,768]{1,0:T(8,128)(2,1)}, bf16[448,768]{1,0:T(8,128)(2,1)S(1)}, u32[]{:S(2)}, u32[]{:S(2)}) collective-permute-start(bf16[448,768]{1,0:T(8,128)(2,1)} %broadcast_select_fusion.5), channel_id=1, source_target_pairs={{0,8},{4,12},{8,0},{12,4},{16,24},{20,28},{24,16},{28,20},{1,9},{5... | collective-permute-start | bytes 2064392 | tf_op jit(solution)/shard_map/ppermute | solution.py:1207
  164.7 24.2 %collective-permute-start.22 = (bf16[448,768]{1,0:T(8,128)(2,1)}, bf16[448,768]{1,0:T(8,128)(2,1)S(1)}, u32[]{:S(2)}, u32[]{:S(2)}) collective-permute-start(bf16[448,768]{1,0:T(8,128)(2,1)} %broadcast_select_fusion.8), channel_id=1, source_target_pairs={{0,4},{4,0},{8,12},{12,8},{16,20},{20,16},{24,28},{28,24},{1,5},{5... | collective-permute-start | bytes 2064392 | tf_op jit(solution)/shard_map/ppermute | solution.py:1207
  189.1 12.4 %collective-permute-start.24 = (bf16[224,768]{1,0:T(8,128)(2,1)S(1)}, bf16[224,768]{1,0:T(8,128)(2,1)S(1)}, u32[]{:S(2)}, u32[]{:S(2)}) collective-permute-start(bf16[224,768]{1,0:T(8,128)(2,1)S(1)} %broadcast_select_fusion.20), channel_id=1, source_target_pairs={{0,8},{4,12},{8,0},{12,4},{16,24},{20,28},{24,16},{28,20},{1,9},{5... | collective-permute-start | bytes 1032200 | tf_op jit(solution)/shard_map/ppermute | solution.py:1207
  189.6 12.0 %collective-permute-start.25 = (bf16[224,768]{1,0:T(8,128)(2,1)}, bf16[224,768]{1,0:T(8,128)(2,1)S(1)}, u32[]{:S(2)}, u32[]{:S(2)}) collective-permute-start(bf16[224,768]{1,0:T(8,128)(2,1)} %broadcast_select_fusion.17), channel_id=1, source_target_pairs={{0,4},{4,0},{8,12},{12,8},{16,20},{20,16},{24,28},{28,24},{1,5},{5... | collective-permute-start | bytes 1032200 | tf_op jit(solution)/shard_map/ppermute | solution.py:1207
  201.9 18.1 %collective-permute-start.28 = (bf16[224,768]{1,0:T(8,128)(2,1)S(1)}, bf16[224,768]{1,0:T(8,128)(2,1)S(1)}, u32[]{:S(2)}, u32[]{:S(2)}) collective-permute-start(bf16[224,768]{1,0:T(8,128)(2,1)S(1)} %bitcast.44), channel_id=1, source_target_pairs={{0,16},{4,20},{8,24},{12,28},{16,0},{20,4},{24,8},{28,12},{1,17},{... | collective-permute-start | bytes 1032200 | tf_op jit(solution)/shard_map/ppermute | solution.py:1207
  219.8 5.2 %copy-start.10 = (bf16[640,768]{1,0:T(8,128)(2,1)S(1)}, bf16[640,768]{1,0:T(8,128)(2,1)}, u32[]{:S(2)}) copy-start(bf16[640,768]{1,0:T(8,128)(2,1)} %get-tuple-element.140) | copy-start | bytes 2949124
  219.8 5.2 %collective-permute-start.27 = (bf16[640,768]{1,0:T(8,128)(2,1)}, bf16[640,768]{1,0:T(8,128)(2,1)S(1)}, u32[]{:S(2)}, u32[]{:S(2)}) collective-permute-start(bf16[640,768]{1,0:T(8,128)(2,1)} %get-tuple-element.141), channel_id=1, source_target_pairs={{0,1},{1,0},{2,3},{3,2},{4,5},{5,4},{6,7},{7,6},{8,9},{9,8},{10,11... | collective-permute-start | bytes 2949128 | tf_op jit(solution)/shard_map/ppermute | solution.py:1207
  220.8 9.4 %collective-permute-start.33 = (bf16[152,768]{1,0:T(8,128)(2,1)S(1)}, bf16[152,768]{1,0:T(8,128)(2,1)S(1)}, u32[]{:S(2)}, u32[]{:S(2)}) collective-permute-start(bf16[152,768]{1,0:T(8,128)(2,1)S(1)} %broadcast_select_fusion.23), channel_id=1, source_target_pairs={{0,8},{4,12},{8,0},{12,4},{16,24},{20,28},{24,16},{28,20},{1,9},{5... | collective-permute-start | bytes 700424 | tf_op jit(solution)/shard_map/ppermute | solution.py:1207
  222.5 7.8 %collective-permute-start.30 = (bf16[152,768]{1,0:T(8,128)(2,1)S(1)}, bf16[152,768]{1,0:T(8,128)(2,1)S(1)}, u32[]{:S(2)}, u32[]{:S(2)}) collective-permute-start(bf16[152,768]{1,0:T(8,128)(2,1)S(1)} %broadcast_select_fusion.26), channel_id=1, source_target_pairs={{0,4},{4,0},{8,12},{12,8},{16,20},{20,16},{24,28},{28,24},{1,5},{5... | collective-permute-start | bytes 700424 | tf_op jit(solution)/shard_map/ppermute | solution.py:1207
  224.1 17.5 %collective-permute-start.32 = (bf16[224,768]{1,0:T(8,128)(2,1)S(1)}, bf16[224,768]{1,0:T(8,128)(2,1)S(1)}, u32[]{:S(2)}, u32[]{:S(2)}) collective-permute-start(bf16[224,768]{1,0:T(8,128)(2,1)S(1)} %bitcast.45), channel_id=1, source_target_pairs={{0,16},{4,20},{8,24},{12,28},{16,0},{20,4},{24,8},{28,12},{1,17},{... | collective-permute-start | bytes 1032200 | tf_op jit(solution)/shard_map/ppermute | solution.py:1207
  230.5 11.4 %collective-permute-start.31 = (bf16[76,768]{1,0:T(8,128)(2,1)S(1)}, bf16[76,768]{1,0:T(8,128)(2,1)S(1)}, u32[]{:S(2)}, u32[]{:S(2)}) collective-permute-start(bf16[76,768]{1,0:T(8,128)(2,1)S(1)} %broadcast_select_fusion.32), channel_id=1, source_target_pairs={{0,8},{4,12},{8,0},{12,4},{16,24},{20,28},{24,16},{28,20},{1,9},{5... | collective-permute-start | bytes 350216 | tf_op jit(solution)/shard_map/ppermute | solution.py:1207
  231.5 10.5 %collective-permute-start.34 = (bf16[76,768]{1,0:T(8,128)(2,1)S(1)}, bf16[76,768]{1,0:T(8,128)(2,1)S(1)}, u32[]{:S(2)}, u32[]{:S(2)}) collective-permute-start(bf16[76,768]{1,0:T(8,128)(2,1)S(1)} %broadcast_select_fusion.29), channel_id=1, source_target_pairs={{0,4},{4,0},{8,12},{12,8},{16,20},{20,16},{24,28},{28,24},{1,5},{5... | collective-permute-start | bytes 350216 | tf_op jit(solution)/shard_map/ppermute | solution.py:1207
  242.1 10.9 %collective-permute-start.35 = (bf16[152,768]{1,0:T(8,128)(2,1)S(1)}, bf16[152,768]{1,0:T(8,128)(2,1)S(1)}, u32[]{:S(2)}, u32[]{:S(2)}) collective-permute-start(bf16[152,768]{1,0:T(8,128)(2,1)S(1)} %reshape.513), channel_id=1, source_target_pairs={{0,16},{4,20},{8,24},{12,28},{16,0},{20,4},{24,8},{28,12},{1,17},{... | collective-permute-start | bytes 700424 | tf_op jit(solution)/shard_map/ppermute | solution.py:1207
  242.2 10.9 %collective-permute-start.37 = (bf16[224,768]{1,0:T(8,128)(2,1)S(1)}, bf16[224,768]{1,0:T(8,128)(2,1)S(1)}, u32[]{:S(2)}, u32[]{:S(2)}) collective-permute-start(bf16[224,768]{1,0:T(8,128)(2,1)S(1)} %get-tuple-element.211), channel_id=1, source_target_pairs={{0,4},{4,0},{8,12},{12,8},{16,20},{20,16},{24,28},{28,24},{1,5},{5... | collective-permute-start | bytes 1032200 | tf_op jit(solution)/shard_map/ppermute | solution.py:1207
  243.2 12.7 %collective-permute-start.36 = (bf16[224,768]{1,0:T(8,128)(2,1)S(1)}, bf16[224,768]{1,0:T(8,128)(2,1)S(1)}, u32[]{:S(2)}, u32[]{:S(2)}) collective-permute-start(bf16[224,768]{1,0:T(8,128)(2,1)S(1)} %get-tuple-element.212), channel_id=1, source_target_pairs={{0,8},{4,12},{8,0},{12,4},{16,24},{20,28},{24,16},{28,20},{1,9},{5... | collective-permute-start | bytes 1032200 | tf_op jit(solution)/shard_map/ppermute | solution.py:1207
  256.0 9.8 %copy-start.59 = (bf16[640,768]{1,0:T(8,128)(2,1)S(1)}, bf16[640,768]{1,0:T(8,128)(2,1)}, u32[]{:S(2)}) copy-start(bf16[640,768]{1,0:T(8,128)(2,1)} %get-tuple-element.139) | copy-start | bytes 2949124
  256.0 9.8 %copy-start.9 = (bf16[640,768]{1,0:T(8,128)(2,1)S(1)}, bf16[640,768]{1,0:T(8,128)(2,1)}, u32[]{:S(2)}) copy-start(bf16[640,768]{1,0:T(8,128)(2,1)} %add_convert_fusion) | copy-start | bytes 2949124
  256.1 4.9 %collective-permute-start.38 = (bf16[76,768]{1,0:T(8,128)(2,1)S(1)}, bf16[76,768]{1,0:T(8,128)(2,1)S(1)}, u32[]{:S(2)}, u32[]{:S(2)}) collective-permute-start(bf16[76,768]{1,0:T(8,128)(2,1)S(1)} %get-tuple-element.229), channel_id=1, source_target_pairs={{0,8},{4,12},{8,0},{12,4},{16,24},{20,28},{24,16},{28,20},{1,9},{5... | collective-permute-start | bytes 350216 | tf_op jit(solution)/shard_map/ppermute | solution.py:1207
  256.3 5.7 %collective-permute-start.40 = (bf16[76,768]{1,0:T(8,128)(2,1)S(1)}, bf16[76,768]{1,0:T(8,128)(2,1)S(1)}, u32[]{:S(2)}, u32[]{:S(2)}) collective-permute-start(bf16[76,768]{1,0:T(8,128)(2,1)S(1)} %get-tuple-element.230), channel_id=1, source_target_pairs={{0,4},{4,0},{8,12},{12,8},{16,20},{20,16},{24,28},{28,24},{1,5},{5... | collective-permute-start | bytes 350216 | tf_op jit(solution)/shard_map/ppermute | solution.py:1207
  262.0 6.1 %collective-permute-start.39 = (bf16[152,768]{1,0:T(8,128)(2,1)S(1)}, bf16[152,768]{1,0:T(8,128)(2,1)S(1)}, u32[]{:S(2)}, u32[]{:S(2)}) collective-permute-start(bf16[152,768]{1,0:T(8,128)(2,1)S(1)} %pad_maximum_fusion.16), channel_id=1, source_target_pairs={{0,4},{4,0},{8,12},{12,8},{16,20},{20,16},{24,28},{28,24},{1,5},{5... | collective-permute-start | bytes 700424 | tf_op jit(solution)/shard_map/ppermute | solution.py:1207
  263.7 17.8 %collective-permute-start.43 = (bf16[448,768]{1,0:T(8,128)(2,1)S(1)}, bf16[448,768]{1,0:T(8,128)(2,1)S(1)}, u32[]{:S(2)}, u32[]{:S(2)}) collective-permute-start(bf16[448,768]{1,0:T(8,128)(2,1)S(1)} %get-tuple-element.265), channel_id=1, source_target_pairs={{0,8},{4,12},{8,0},{12,4},{16,24},{20,28},{24,16},{28,20},{1,9},{5... | collective-permute-start | bytes 2064392 | tf_op jit(solution)/shard_map/ppermute | solution.py:1207
  265.9 33.5 %collective-permute-start.26 = (bf16[640,768]{1,0:T(8,128)(2,1)S(1)}, bf16[640,768]{1,0:T(8,128)(2,1)S(1)}, u32[]{:S(2)}, u32[]{:S(2)}) collective-permute-start(bf16[640,768]{1,0:T(8,128)(2,1)S(1)} %copy-done.59), channel_id=1, source_target_pairs={{0,1},{1,0},{2,3},{3,2},{4,5},{5,4},{6,7},{7,6},{8,9},{9,8},{10,11... | collective-permute-start | bytes 2949128 | tf_op jit(solution)/shard_map/ppermute | solution.py:1207
  265.9 33.5 %collective-permute-start.29 = (bf16[640,768]{1,0:T(8,128)(2,1)S(1)}, bf16[640,768]{1,0:T(8,128)(2,1)S(1)}, u32[]{:S(2)}, u32[]{:S(2)}) collective-permute-start(bf16[640,768]{1,0:T(8,128)(2,1)S(1)} %copy-done.9), channel_id=1, source_target_pairs={{0,2},{1,3},{2,0},{3,1},{4,6},{5,7},{6,4},{7,5},{8,10},{9,11},{10,... | collective-permute-start | bytes 2949128 | tf_op jit(solution)/shard_map/ppermute | solution.py:1207
  266.4 17.5 %collective-permute-start.42 = (bf16[448,768]{1,0:T(8,128)(2,1)S(1)}, bf16[448,768]{1,0:T(8,128)(2,1)S(1)}, u32[]{:S(2)}, u32[]{:S(2)}) collective-permute-start(bf16[448,768]{1,0:T(8,128)(2,1)S(1)} %get-tuple-element.264), channel_id=1, source_target_pairs={{0,4},{4,0},{8,12},{12,8},{16,20},{20,16},{24,28},{28,24},{1,5},{5... | collective-permute-start | bytes 2064392 | tf_op jit(solution)/shard_map/ppermute | solution.py:1207
  268.2 13.2 %collective-permute-start.41 = (bf16[152,768]{1,0:T(8,128)(2,1)S(1)}, bf16[152,768]{1,0:T(8,128)(2,1)S(1)}, u32[]{:S(2)}, u32[]{:S(2)}) collective-permute-start(bf16[152,768]{1,0:T(8,128)(2,1)S(1)} %pad_maximum_fusion.17), channel_id=1, source_target_pairs={{0,8},{4,12},{8,0},{12,4},{16,24},{20,28},{24,16},{28,20},{1,9},{5... | collective-permute-start | bytes 700424 | tf_op jit(solution)/shard_map/ppermute | solution.py:1207
  284.3 14.2 %collective-permute-start.44 = (bf16[256,768]{1,0:T(8,128)(2,1)S(1)}, bf16[256,768]{1,0:T(8,128)(2,1)S(1)}, u32[]{:S(2)}, u32[]{:S(2)}) collective-permute-start(bf16[256,768]{1,0:T(8,128)(2,1)S(1)} %pad_maximum_fusion.13), channel_id=1, source_target_pairs={{0,2},{1,3},{2,0},{3,1},{4,6},{5,7},{6,4},{7,5},{8,10},{9,11},{10,... | collective-permute-start | bytes 1179656 | tf_op jit(solution)/shard_map/ppermute | solution.py:1207
  298.7 6.5 %collective-permute-start.45 = (bf16[512,768]{1,0:T(8,128)(2,1)S(1)}, bf16[512,768]{1,0:T(8,128)(2,1)S(1)}, u32[]{:S(2)}, u32[]{:S(2)}) collective-permute-start(bf16[512,768]{1,0:T(8,128)(2,1)S(1)} %pad_maximum_fusion.8), channel_id=1, source_target_pairs={{0,1},{1,0},{2,3},{3,2},{4,5},{5,4},{6,7},{7,6},{8,9},{9,8},{10,11... | collective-permute-start | bytes 2359304 | tf_op jit(solution)/shard_map/ppermute | solution.py:1207
  (47 other events, 83.5 us)

commit v3 on v2

--- a/solution.py
+++ b/solution.py
@@ -15,7 +15,7 @@
 PAD = 128
 BAND_IN = 512
 BAND_OUT = 256
-TILE = 512
+TILE = 640
 AHEAD = 20
 VMEM_LIMIT = 60 * 1024 * 1024
 F32 = jnp.float32
@@ -969,16 +969,13 @@
     width, block = contexts[0].shape
     io.need(*range(7))
 
-    @pl.loop(0, block // 128)
-    def _(i):
-        rows = row_block(i, 128)
-        resid = tokens[rows, :].astype(F32)
-        for at, c in enumerate(contexts):
-            resid += dot_tn(c[:, rows], w_out[row_block(me ^ at, width), :])
-        unit, recip = unit_norm(resid)
-        unit_one[rows, :] = unit
-        recip_one[rows, :] = jnp.broadcast_to(recip, (128, 128))
-        normed_out[rows, :] = (unit * norms[0:1, :] + norms[1:2, :]).astype(BF16)
+    resid = tokens[...].astype(F32)
+    for at, c in enumerate(contexts):
+        resid += dot_tn(c[...], w_out[row_block(me ^ at, width), :])
+    unit, recip = unit_norm(resid)
+    unit_one[...] = unit
+    recip_one[...] = jnp.broadcast_to(recip, (block, 128))
+    normed_out[...] = (unit * norms[0:1, :] + norms[1:2, :]).astype(BF16)
 
 
 def feed_kernel(io, scalars, hidden):
@@ -1310,7 +1307,7 @@
             ],
             axis=0,
         )
-        tokens_two = after(tokens_two, bands, w_t, weights_half)
+        tokens_two = after(tokens_two, bands, w_t, weights_half, weights, norms)
         blocks = (tokens, tokens_one, tokens_two, to_partner(tokens_two, "tensor", 4, 1))
         across = to_partner(after(weights_half, tokens_two), "tensor", 4, 2)
 
@@ -1370,8 +1367,19 @@
         small_got = to_partner(small_sent, "tensor", 4, 2)
         grad_up, grad_down = feed_weights(scalars, normeds, branch_grads, w_up, w_down)
         small = add(small_kept, after(small_got, grad_up))
-        up = jnp.concatenate([grad_up, small[:part]], axis=0)
-        down = jnp.concatenate([grad_down, small[part:]], axis=0)
+
+        def with_part(grad, rows):
+            pieces = [a.reshape(dp_size, -1, features) for a in (grad, rows)]
+            return jnp.concatenate(pieces, axis=1).reshape(-1, features)
+
+        def without_part(array):
+            pieces = array.reshape(-1, (units + part) // dp_size, features)
+            cut = units // dp_size
+            return [
+                a.reshape(-1, features) for a in (pieces[:, :cut], pieces[:, cut:])
+            ]
+
+        up, down = with_part(grad_up, small[:part]), with_part(grad_down, small[part:])
         up_kept, up_sent = halve(up, "dp", first)
         down_kept, down_sent = halve(down, "dp", second)
         (up_got,), (down_got,) = dp_hop([up_sent], first), dp_hop([down_sent], second)
@@ -1414,27 +1422,40 @@
             both = rejoin(both, got, "dp", bit)
         up, down = both[0], both[1]
         (up_got,), (down_got,) = dp_hop([up], second), dp_hop([down], first)
-        wide = jnp.stack(
-            [add(low_kept, after(low_got, both)), add(high_kept, after(high_got, both))]
+        wide = jnp.stack([add(low_kept, low_got), add(high_kept, high_got)])
+        kept_wide = wide
+        (wide_got,) = dp_hop([wide], others[0])
+        up = rejoin(up, after(up_got, arrived), "dp", second)
+        down = rejoin(down, down_got, "dp", first)
+        (up, small_up), (down, small_down) = without_part(up), without_part(down)
+        (up_got,), (down_got,) = dp_hop([up], first), dp_hop([down], second)
+        wide = add(kept_wide, after(wide_got, up, down))
+        for bit in others[1:]:
+            (wide_got,) = dp_hop([wide], bit)
+            wide = add(wide, wide_got)
+        low, high = wide[0], wide[1]
+        low_got, down_part_got = dp_hop([low, small_down], second)
+        high_got, up_part_got = dp_hop([high, small_up], first)
+        here = token_grads[0].astype(F32) + token_got[1].astype(F32)
+        grad_tokens = resid_grad + here + after(arrived, low, high).astype(F32)
+        small = jnp.concatenate(
+            [
+                rejoin(small_up, up_part_got, "dp", first),
+                rejoin(small_down, down_part_got, "dp", second),
+            ],
+            axis=0,
         )
-        for bit in others:
-            (got,) = dp_hop([wide], bit)
-            wide = add(wide, got)
-        up = rejoin(up, after(up_got, wide), "dp", second)
-        down = rejoin(down, after(down_got, wide), "dp", first)
-        (up_got,), (down_got,) = dp_hop([up], first), dp_hop([down], second)
-        wide = after(wide, up, down)
-        low, high = wide[0], wide[1]
-        (low_got,), (high_got,) = dp_hop([low], second), dp_hop([high], first)
+        small_got = to_partner(small, "tensor", 4, 2)
         low, high = rejoin(low, low_got, "dp", second), rejoin(high, high_got, "dp", first)
         (low_got,), (high_got,) = dp_hop([low], first), dp_hop([high], second)
-        up = rejoin(up, after(up_got, low), "dp", first)
-        down = rejoin(down, after(down_got, low), "dp", second)
-        small = jnp.concatenate([up[features:], down[units:]], axis=0)
-        small = rejoin(small, to_partner(small, "tensor", 4, 2), "tensor", 2)
-        small = rejoin(small, core_hop(small), "tensor", 1).astype(F32)
-        here = token_grads[0].astype(F32) + token_got[1].astype(F32)
-        grad_tokens = resid_grad + here + after(arrived, low_sent).astype(F32)
+        grad_up = rejoin(up, after(up_got, low), "dp", first).astype(F32)
+        grad_down = rejoin(down, after(down_got, high), "dp", second).astype(F32)
+        small = rejoin(small, after(small_got, low, high), "tensor", 2)
+        small_got = core_hop(small)
+        low_got, high_got = after(low_got, grad_up), after(high_got, grad_down)
+        small = rejoin(small, small_got, "tensor", 1)
+        grad_w_out = small[:features].astype(F32)
+        norm_rows = small[features : features + 16].astype(F32)
         qkv_wide = jnp.concatenate(
             [
                 rejoin(low, low_got, "dp", first),
@@ -1442,7 +1463,6 @@
             ],
             axis=0,
         ).astype(F32)
-        grad_up, grad_down = up[:features].astype(F32), down[:units].astype(F32)
         return (
             output,
             grad_tokens,
@@ -1450,13 +1470,13 @@
             qkv_wide[width : 2 * width].T,
             qkv_wide[2 * width : 3 * width].T,
             qkv_wide[3 * width : 3 * width + heads, :KERNEL],
-            small[:features],
-            small[features],
-            small[features + 1],
+            grad_w_out,
+            norm_rows[0],
+            norm_rows[1],
             grad_up,
             grad_down,
-            small[features + 8],
-            small[features + 9],
+            norm_rows[8],
+            norm_rows[9],
         )
 
     rows = P(("dp", "tensor"), None)

time: 311 us -> 296 us (0.952); the launches traced: 308 us -> 299 us
  Pallas kernels: 140 us -> 150 us
  starting transfers between devices: 45.4 us -> 37 us
  waiting for transfers between devices: 71.2 us -> 64.3 us
    pallas_call x8, Pallas kernels: 140 us -> 150 us  [local_call(): pl.pallas_call(body, name=name, out_shape=out_shape, in_specs=[pl.BlockSp...]
    ppermute x46, starting transfers between devices: 45.4 us -> 37 us  [to_partner(): return lax.ppermute(array, axis, [(i, i ^ bit) for i in range(size)])]
    ppermute x46, waiting for transfers between devices: 71.2 us -> 64.3 us  [to_partner(): return lax.ppermute(array, axis, [(i, i ^ bit) for i in range(size)])]
    unnamed x131 -> x121, local copies, waits for them, and re-layouts: 6.39 us -> 3.04 us
  transfers between devices with their start and end apart: 46 -> 46, of which waited for: 20 -> 17; matrix products, arithmetic and copies ran while one was open for 13% -> 13% of each run, Pallas kernels for 46% -> 50%
where the time goes in v3:
time: 296 us; the launch traced here: 299 us
  Pallas kernels  150 us (51%)
  waiting for transfers between devices  64.3 us (22%)
  starting transfers between devices  37 us (12%)
  other arithmetic  33.7 us (11%)
  local copies, waits for them, and re-layouts  11.5 us (4%)
    pallas_call x8, Pallas kernels, local_call(): pl.pallas_call(body, name=name, out_shape=out_shape, in_specs=[pl.BlockSp...  150 us
    ppermute x46, waiting for transfers between devices, to_partner(): return lax.ppermute(array, axis, [(i, i ^ bit) for i in range(size)])  64.3 us
    ppermute x46, starting transfers between devices, to_partner(): return lax.ppermute(array, axis, [(i, i ^ bit) for i in range(size)])  37 us
    convert_element_type x1, other arithmetic, make_bands(): return band.astype(BF16)  6.74 us
  transfers between devices with their start and end apart: 46, of which 17 were waited for; matrix products, arithmetic and copies ran while one was open for 13% of the time, Pallas kernels for 50%

profile of v3, /device:TPU:0, one launch (start us, length us, event | category | flops | bytes accessed | tf_op | source)
XLA Modules:
  0.0 298.8 jit_solution(17481841441002828584)
XLA Ops:
  0.6 3.0 %collective-permute-start.1 = (bf16[640,768]{1,0:T(8,128)(2,1)}, bf16[640,768]{1,0:T(8,128)(2,1)}, u32[]{:S(2)}, u32[]{:S(2)}) collective-permute-start(bf16[640,768]{1,0:T(8,128)(2,1)} %refs_6_.1), channel_id=1, source_target_pairs={{0,2},{1,3},{2,0},{3,1},{4,6},{5,7},{6,4},{7,5},{8,10},{9,11},{10,... | collective-permute-start | bytes 2949128 | tf_op jit(solution)/shard_map/ppermute | solution.py:1204
  3.7 2.5 slice_reduce_fusion.36
  6.1 2.2 slice_reduce_fusion.35
  8.3 4.4 %fusion.40 = (pred[512,256]{1,0:T(8,128)(4,1)}, pred[512,256]{1,0:T(8,128)(4,1)}, pred[512,256]{1,0:T(8,128)(4,1)}, pred[512,256]{1,0:T(8,128)(4,1)}, pred[512,2...) fusion(s32[512]{0:T(512)S(1)} %iota_add_fusion), kind=kLoop, calls=%fused_computation.91 | loop fusion | flops 4587520 | bytes 4327424 | tf_op jit(solution)/shard_map/eq | solution.py:1225
  12.8 1.0 copy.28
  14.1 1.6 pad_maximum_fusion.refs_2_.refs_8_.refs_9_
  15.6 1.6 fusion.6
  17.8 1.0 pad_maximum_fusion.3.refs_0_.refs_5_
  18.7 0.6 pad_maximum_fusion.19.refs_6_.refs_1_
  19.9 6.7 %select_convert_fusion.refs_5_.refs_11_ = bf16[3,512,256]{2,1,0:T(8,128)(2,1)} fusion(bf16[3]{0:T(256)(128)(2,1)} %get-tuple-element.194, bf16[3]{0:T(256)(128)(2,1)} %get-tuple-element.195, bf16[3]{0:T(256)(128)(2,1)S(1)} %copy-done.53, bf16[3]{0:T(256)(128)(2,1)S(1)} %copy-done.54, bf16[3]{0:T(256)(128)(2,1)S(1)} %copy-done.55, ...), kind=kLoop, calls=%fused_computation.8 | loop fusion | flops 12976128 | bytes 5112006 | tf_op jit(solution)/shard_map/convert_element_type | solution.py:1226
  28.1 1.7 collective-permute-done.2.refs_4_.refs_9_
  29.8 37.1 %attend.1 = (bf16[576,2816]{1,0:T(8,128)(2,1)}, bf16[192,640]{1,0:T(8,128)(2,1)}, bf16[192,640]{1,0:T(8,128)(2,1)}, bf16[192,640]{1,0:T(8,128)(2,1)}, bf16[192,6...) custom-call(s32[4]{0:T(128)} %pad_add_fusion.scalar_ref, ...), custom_call_target="tpu_custom_call" | custom-call | flops 30000001024 | bytes 14358528 | tf_op jit(solution)/shard_map/attend/pallas_call | solution.py:240
  66.9 1.6 collective-permute-start.8
  69.6 0.8 collective-permute-start.5
  70.4 2.9 collective-permute-done.3.refs_1_.refs_20_
  73.7 4.3 %collective-permute-done.4.refs_2_.refs_21_ = bf16[192,640]{1,0:T(8,128)(2,1)S(1)} collective-permute-done((bf16[192,640]{1,0:T(8,128)(2,1)}, bf16[192,640]{1,0:T(8,128)(2,1)S(1)}, u32[]{:S(2)}, u32[]{:S(2)}) %collective-permute-start.4) | collective-permute-done | bytes 245792 | tf_op jit(solution)/shard_map/ppermute | solution.py:1204
  78.0 3.6 %collective-permute-done.5.refs_3_.refs_22_ = bf16[192,640]{1,0:T(8,128)(2,1)} collective-permute-done((bf16[192,640]{1,0:T(8,128)(2,1)}, bf16[192,640]{1,0:T(8,128)(2,1)}, u32[]{:S(2)}, u32[]{:S(2)}) %collective-permute-start.5) | collective-permute-done | bytes 245792 | tf_op jit(solution)/shard_map/ppermute | solution.py:1204
  81.7 6.3 %norm_in.1 = (bf16[640,768]{1,0:T(8,128)(2,1)}, f32[640,768]{1,0:T(8,128)}, f32[640,128]{1,0:T(8,128)}) custom-call(s32[4]{0:T(128)} %pad_add_fusion.scalar_ref, bf16[192,640]{1,0:T(8,128)(2,1)} %get-tuple-element.87.refs_0_.refs_19_, bf16[192,640]{1,0:T(8,128)(2,1)} %copy-done.57, bf16[192,640]{1,0:T(8,128)(2,1)} %copy-done.58, ...), custom_call_target="tpu_custom_call" | custom-call | flops 6000000000 | bytes 6434816 | tf_op jit(solution)/shard_map/norm_in/pallas_call | solution.py:240
  87.9 7.5 %collective-permute-done.8.refs_5_.refs_11_.refs_12_ = bf16[768,768]{1,0:T(8,128)(2,1)S(1)} collective-permute-done((bf16[768,768]{1,0:T(8,128)(2,1)}, bf16[768,768]{1,0:T(8,128)(2,1)S(1)}, u32[]{:S(2)}, u32[]{:S(2)}) %collective-permute-start.8) | collective-permute-done | bytes 1179680 | tf_op jit(solution)/shard_map/ppermute | solution.py:1204
  95.9 2.5 collective-permute-done.10.refs_7_.refs_13_.refs_14_
  98.4 19.4 %feed.1 = (f32[640,768]{1,0:T(8,128)}, bf16[640,3072]{1,0:T(8,128)(2,1)}, f32[640,768]{1,0:T(8,128)}, bf16[640,768]{1,0:T(8,128)(2,1)}, f32[8,768]{1,0:T(8,128)}) custom-call(s32[4]{0:T(128)} %pad_add_fusion.scalar_ref, bf16[640,768]{1,0:T(8,128)(2,1)} %get-tuple-element.91.refs_0_.refs_2_, f32[4,768]{1,0:T(4,128)} %pad_maximum_fusion.19.refs_6_.refs_1_, ...), custom_call_target="tpu_custom_call" | custom-call | flops 22000001024 | bytes 31690752 | tf_op jit(solution)/shard_map/feed/pallas_call | solution.py:240
  118.2 17.5 %feed_back.1 = (f32[640,768]{1,0:T(8,128)}, bf16[768,768]{1,0:T(8,128)(2,1)}, f32[8,768]{1,0:T(8,128)}, bf16[192,640]{1,0:T(8,128)(2,1)}, bf16[192,640]{1,0:T(8,...) custom-call(s32[4]{0:T(128)} %pad_add_fusion.scalar_ref, ...), custom_call_target="tpu_custom_call" | custom-call | flops 20000000000 | bytes 34377728 | tf_op jit(solution)/shard_map/feed_back/pallas_call | solution.py:240
  135.8 0.8 convert.8
  136.7 1.5 broadcast_select_fusion.2
  139.2 2.8 collective-permute-done.14.refs_7_
  142.9 1.0 collective-permute-start.20
  143.9 1.2 collective-permute-done.15.refs_8_
  145.1 1.4 collective-permute-start.21
  146.8 23.9 %feed_weights.1 = (bf16[768,768]{1,0:T(8,128)(2,1)}, bf16[768,768]{1,0:T(8,128)(2,1)}) custom-call(s32[4]{0:T(128)} %pad_add_fusion.scalar_ref, bf16[768,768]{1,0:T(8,128)(2,1)} %refs_0_.1, bf16[768,768]{1,0:T(8,128)(2,1)} %refs_1_.3, bf16[640,768]{1,0:T(8,128)(2,1)} %get-tuple-element.91.refs_0_.refs_2_, ...), custom_call_target="tpu_custom_call" | custom-call | flops 24999999488 | bytes 12582912 | tf_op jit(solution)/shard_map/feed_weights/pallas_call | solution.py:240
  170.9 1.1 copy-done.8
  172.3 1.8 collective-permute-start.23
  174.3 1.6 collective-permute-start.22
  175.9 19.4 %attend_back.1 = (bf16[192,2560]{1,0:T(8,128)(2,1)}, f32[8,128]{1,0:T(8,128)}, f32[192,2560]{1,0:T(8,128)}, f32[192,2560]{1,0:T(8,128)}, f32[3,192,64]{2,1,0:T(8...) custom-call(s32[4]{0:T(128)} %pad_add_fusion.scalar_ref, bf16[192,640]{1,0:T(8,128)(2,1)} %get-tuple-element.112.refs_0_, ...), custom_call_target="tpu_custom_call" | custom-call | flops 8000000000 | bytes 11216896 | tf_op jit(solution)/shard_map/attend_back/pallas_call | solution.py:240
  196.8 11.4 %attend_steps.1.refs_4_ = bf16[2,9,64,64]{3,2,1,0:T(8,128)(2,1)} custom-call(s32[4]{0:T(128)} %pad_add_fusion.scalar_ref, f32[3,192,64]{2,1,0:T(8,128)} %get-tuple-element.130.refs_0_, f32[3,192,64]{2,1,0:T(8,128)} %get-tuple-element.119.refs_7_.refs_1_, f32[3,64,192]{2,1,0:T(8,128)} %get-tuple-element.131.refs_2_, ...), custom_call_target="tpu_custom_call" | custom-call | flops 5000000000 | bytes 4571136 | tf_op jit(solution)/shard_map/attend_steps/pallas_call | solution.py:240
  208.6 2.8 collective-permute-start.28
  211.4 15.2 %attend_grads.1 = (bf16[304,768]{1,0:T(8,128)(2,1)}, bf16[304,768]{1,0:T(8,128)(2,1)}, bf16[640,768]{1,0:T(8,128)(2,1)}, bf16[640,768]{1,0:T(8,128)(2,1)}, bf16[...) custom-call(s32[4]{0:T(128)} %pad_add_fusion.scalar_ref, bf16[192,2560]{1,0:T(8,128)(2,1)} %get-tuple-element.123.refs_0_, ...), custom_call_target="tpu_custom_call" | custom-call | flops 8000000000 | bytes 14749696 | tf_op jit(solution)/shard_map/attend_grads/pallas_call | solution.py:240
  227.6 1.6 collective-permute-start.30
  229.2 1.6 collective-permute-start.32
  230.9 1.0 collective-permute-start.35
  231.9 1.2 add_convert_fusion
  233.1 1.5 collective-permute-start.29
  235.2 4.6 %collective-permute-done.32 = bf16[152,768]{1,0:T(8,128)(2,1)S(1)} collective-permute-done((bf16[152,768]{1,0:T(8,128)(2,1)S(1)}, bf16[152,768]{1,0:T(8,128)(2,1)S(1)}, u32[]{:S(2)}, u32[]{:S(2)}) %collective-permute-start.32) | collective-permute-done | bytes 233504 | tf_op jit(solution)/shard_map/ppermute | solution.py:1204
  240.0 0.6 collective-permute-start.33
  240.6 7.9 %collective-permute-done.35 = bf16[224,768]{1,0:T(8,128)(2,1)S(1)} collective-permute-done((bf16[224,768]{1,0:T(8,128)(2,1)S(1)}, bf16[224,768]{1,0:T(8,128)(2,1)S(1)}, u32[]{:S(2)}, u32[]{:S(2)}) %collective-permute-start.35) | collective-permute-done | bytes 344096 | tf_op jit(solution)/shard_map/ppermute | solution.py:1204
  249.5 0.7 reshape.563
  250.3 1.7 collective-permute-start.34
  251.9 5.2 %collective-permute-done.37 = bf16[224,768]{1,0:T(8,128)(2,1)S(1)} collective-permute-done((bf16[224,768]{1,0:T(8,128)(2,1)S(1)}, bf16[224,768]{1,0:T(8,128)(2,1)S(1)}, u32[]{:S(2)}, u32[]{:S(2)}) %collective-permute-start.37) | collective-permute-done | bytes 344096 | tf_op jit(solution)/shard_map/ppermute | solution.py:1204
  257.4 5.6 %collective-permute-done.34 = bf16[152,768]{1,0:T(8,128)(2,1)} collective-permute-done((bf16[152,768]{1,0:T(8,128)(2,1)}, bf16[152,768]{1,0:T(8,128)(2,1)}, u32[]{:S(2)}, u32[]{:S(2)}) %collective-permute-start.34) | collective-permute-done | bytes 233504 | tf_op jit(solution)/shard_map/ppermute | solution.py:1204
  263.0 1.0 reshape.564
  264.0 0.7 collective-permute-done.36
  264.6 1.0 broadcast_select_fusion.21
  265.8 1.6 collective-permute-start.40
  268.1 1.5 collective-permute-start.38
  269.7 1.8 convert_add_fusion
  271.5 10.1 %collective-permute-done.41 = bf16[140,768]{1,0:T(8,128)(2,1)S(1)} collective-permute-done((bf16[140,768]{1,0:T(8,128)(2,1)S(1)}, bf16[140,768]{1,0:T(8,128)(2,1)S(1)}, u32[]{:S(2)}, u32[]{:S(2)}) %collective-permute-start.41) | collective-permute-done | bytes 215072 | tf_op jit(solution)/shard_map/ppermute | solution.py:1204
  281.7 2.3 collective-permute-start.44
  284.0 1.6 collective-permute-start.39
  285.9 1.1 broadcast_select_fusion.8
  287.0 1.6 maximum_convert_fusion.1
  288.6 3.2 %collective-permute-done.42 = bf16[152,768]{1,0:T(8,128)(2,1)S(1)} collective-permute-done((bf16[152,768]{1,0:T(8,128)(2,1)S(1)}, bf16[152,768]{1,0:T(8,128)(2,1)S(1)}, u32[]{:S(2)}, u32[]{:S(2)}) %collective-permute-start.42) | collective-permute-done | bytes 233504 | tf_op jit(solution)/shard_map/ppermute | solution.py:1204
  291.9 1.6 maximum_convert_fusion
  294.7 1.2 slice_bitcast_fusion
  296.4 1.6 fusion.2
  298.0 0.6 slice_reduce_fusion
  (238 shorter events, 15.3 us)
Async XLA Ops:
  0.6 26.0 %collective-permute-start.1 = (bf16[640,768]{1,0:T(8,128)(2,1)}, bf16[640,768]{1,0:T(8,128)(2,1)}, u32[]{:S(2)}, u32[]{:S(2)}) collective-permute-start(bf16[640,768]{1,0:T(8,128)(2,1)} %refs_6_.1), channel_id=1, source_target_pairs={{0,2},{1,3},{2,0},{3,1},{4,6},{5,7},{6,4},{7,5},{8,10},{9,11},{10,... | collective-permute-start | bytes 2949128 | tf_op jit(solution)/shard_map/ppermute | solution.py:1204
  3.6 24.4 %collective-permute-start = (bf16[640,768]{1,0:T(8,128)(2,1)}, bf16[640,768]{1,0:T(8,128)(2,1)}, u32[]{:S(2)}, u32[]{:S(2)}) collective-permute-start(bf16[640,768]{1,0:T(8,128)(2,1)} %refs_6_.1), channel_id=1, source_target_pairs={{0,1},{1,0},{2,3},{3,2},{4,5},{5,4},{6,7},{7,6},{8,9},{9,8},{10,11... | collective-permute-start | bytes 2949128 | tf_op jit(solution)/shard_map/ppermute | solution.py:1204
  8.3 4.5 %copy-start.6 = (bf16[768,768]{1,0:T(8,128)(2,1)S(1)}, bf16[768,768]{1,0:T(8,128)(2,1)}, u32[]{:S(2)}) copy-start(bf16[768,768]{1,0:T(8,128)(2,1)} %refs_0_.1) | copy-start | bytes 3538948
  15.6 3.7 %copy-start.43 = (pred[512,256]{1,0:T(8,128)(4,1)S(1)}, pred[512,256]{1,0:T(8,128)(4,1)}, u32[]{:S(2)}) copy-start(pred[512,256]{1,0:T(8,128)(4,1)} %get-tuple-element.271) | copy-start | bytes 393220
  17.6 2.3 copy-start.42
  17.6 2.3 copy-start.52
  17.6 2.3 copy-start.53
  17.6 2.3 copy-start.54
  19.9 7.3 %copy-start.59 = (s32[1,3]{1,0:T(1,128)S(1)}, s32[1,3]{1,0:T(1,128)}, u32[]{:S(2)}) copy-start(s32[1,3]{1,0:T(1,128)} %param.26) | copy-start | bytes 40
  26.7 3.1 %collective-permute-start.2 = (bf16[640,768]{1,0:T(8,128)(2,1)}, bf16[640,768]{1,0:T(8,128)(2,1)}, u32[]{:S(2)}, u32[]{:S(2)}) collective-permute-start(bf16[640,768]{1,0:T(8,128)(2,1)} %collective-permute-done.1.refs_3_.refs_8_), channel_id=1, source_target_pairs={{0,1},{1,0},{2,3},{3,2},{4,5},{5,4},{6,7},{7,6},{8,9},{9,8},{10,11... | collective-permute-start | bytes 2949128 | tf_op jit(solution)/shard_map/ppermute | solution.py:1204
  27.8 40.7 %copy-start.2 = (bf16[1536,768]{1,0:T(8,128)(2,1)S(1)}, bf16[1536,768]{1,0:T(8,128)(2,1)}, u32[]{:S(2)}) copy-start(bf16[1536,768]{1,0:T(8,128)(2,1)} %pad_maximum_fusion.refs_2_.refs_8_.refs_9_) | copy-start | bytes 7077892
  27.8 39.1 %collective-permute-start.7 = (bf16[768,768]{1,0:T(8,128)(2,1)S(1)}, bf16[768,768]{1,0:T(8,128)(2,1)}, u32[]{:S(2)}, u32[]{:S(2)}) collective-permute-start(bf16[768,768]{1,0:T(8,128)(2,1)S(1)} %pad_maximum_fusion.2), channel_id=1, source_target_pairs={{0,2},{1,3},{2,0},{3,1},{4,6},{5,7},{6,4},{7,5},{8,10},{9,11},{10,... | collective-permute-start | bytes 3538952 | tf_op jit(solution)/shard_map/ppermute | solution.py:1204
  66.9 28.5 %collective-permute-start.8 = (bf16[768,768]{1,0:T(8,128)(2,1)}, bf16[768,768]{1,0:T(8,128)(2,1)S(1)}, u32[]{:S(2)}, u32[]{:S(2)}) collective-permute-start(bf16[768,768]{1,0:T(8,128)(2,1)} %collective-permute-done.7.refs_4_.refs_10_.refs_11_), channel_id=1, source_target_pairs={{0,4},{4,0},{8,12},{12,8},{16,20},{20,16},{24,28},{28,24},{1,5},{5... | collective-permute-start | bytes 3538952 | tf_op jit(solution)/shard_map/ppermute | solution.py:1204
  68.5 27.4 %collective-permute-start.6 = (bf16[1536,768]{1,0:T(8,128)(2,1)S(1)}, bf16[1536,768]{1,0:T(8,128)(2,1)}, u32[]{:S(2)}, u32[]{:S(2)}) collective-permute-start(bf16[1536,768]{1,0:T(8,128)(2,1)S(1)} %copy-done.2), channel_id=1, source_target_pairs={{0,1},{1,0},{2,3},{3,2},{4,5},{5,4},{6,7},{7,6},{8,9},{9,8},{10,11... | collective-permute-start | bytes 7077896 | tf_op jit(solution)/shard_map/ppermute | solution.py:1204
  68.6 4.7 %collective-permute-start.3 = (bf16[192,640]{1,0:T(8,128)(2,1)}, bf16[192,640]{1,0:T(8,128)(2,1)S(1)}, u32[]{:S(2)}, u32[]{:S(2)}) collective-permute-start(bf16[192,640]{1,0:T(8,128)(2,1)} %get-tuple-element.88), channel_id=1, source_target_pairs={{0,1},{1,0},{2,3},{3,2},{4,5},{5,4},{6,7},{7,6},{8,9},{9,8},{10,11... | collective-permute-start | bytes 737288 | tf_op jit(solution)/shard_map/ppermute | solution.py:1204
  69.0 9.0 %collective-permute-start.4 = (bf16[192,640]{1,0:T(8,128)(2,1)}, bf16[192,640]{1,0:T(8,128)(2,1)S(1)}, u32[]{:S(2)}, u32[]{:S(2)}) collective-permute-start(bf16[192,640]{1,0:T(8,128)(2,1)} %get-tuple-element.89), channel_id=1, source_target_pairs={{0,2},{1,3},{2,0},{3,1},{4,6},{5,7},{6,4},{7,5},{8,10},{9,11},{10,... | collective-permute-start | bytes 737288 | tf_op jit(solution)/shard_map/ppermute | solution.py:1204
  69.6 12.1 %collective-permute-start.5 = (bf16[192,640]{1,0:T(8,128)(2,1)}, bf16[192,640]{1,0:T(8,128)(2,1)}, u32[]{:S(2)}, u32[]{:S(2)}) collective-permute-start(bf16[192,640]{1,0:T(8,128)(2,1)} %get-tuple-element.90), channel_id=1, source_target_pairs={{0,3},{1,2},{2,1},{3,0},{4,7},{5,6},{6,5},{7,4},{8,11},{9,10},{10,... | collective-permute-start | bytes 737288 | tf_op jit(solution)/shard_map/ppermute | solution.py:1204
  73.3 8.4 %copy-start.57 = (bf16[192,640]{1,0:T(8,128)(2,1)}, bf16[192,640]{1,0:T(8,128)(2,1)S(1)}, u32[]{:S(2)}) copy-start(bf16[192,640]{1,0:T(8,128)(2,1)S(1)} %collective-permute-done.3.refs_1_.refs_20_) | copy-start | bytes 737284
  73.3 22.6 %collective-permute-start.9 = (bf16[768,768]{1,0:T(8,128)(2,1)}, bf16[768,768]{1,0:T(8,128)(2,1)}, u32[]{:S(2)}, u32[]{:S(2)}) collective-permute-start(bf16[768,768]{1,0:T(8,128)(2,1)} %collective-permute-done.7.refs_4_.refs_10_.refs_11_), channel_id=1, source_target_pairs={{0,1},{1,0},{2,3},{3,2},{4,5},{5,4},{6,7},{7,6},{8,9},{9,8},{10,11... | collective-permute-start | bytes 3538952 | tf_op jit(solution)/shard_map/ppermute | solution.py:1204
  78.0 3.6 %copy-start.58 = (bf16[192,640]{1,0:T(8,128)(2,1)}, bf16[192,640]{1,0:T(8,128)(2,1)S(1)}, u32[]{:S(2)}) copy-start(bf16[192,640]{1,0:T(8,128)(2,1)S(1)} %collective-permute-done.4.refs_2_.refs_21_) | copy-start | bytes 737284
  95.4 3.0 copy-start.56
  95.4 3.0 collective-permute-start.10
  95.5 43.3 %collective-permute-start.13 = (bf16[640,768]{1,0:T(8,128)(2,1)}, bf16[640,768]{1,0:T(8,128)(2,1)}, u32[]{:S(2)}, u32[]{:S(2)}) collective-permute-start(bf16[640,768]{1,0:T(8,128)(2,1)} %get-tuple-element.91.refs_0_.refs_2_), channel_id=1, source_target_pairs={{0,2},{1,3},{2,0},{3,1},{4,6},{5,7},{6,4},{7,5},{8,10},{9,11},{10,... | collective-permute-start | bytes 2949128 | tf_op jit(solution)/shard_map/ppermute | solution.py:1204
  117.8 24.2 %collective-permute-start.14 = (bf16[640,768]{1,0:T(8,128)(2,1)}, bf16[640,768]{1,0:T(8,128)(2,1)}, u32[]{:S(2)}, u32[]{:S(2)}) collective-permute-start(bf16[640,768]{1,0:T(8,128)(2,1)} %get-tuple-element.97.refs_0_.refs_3_), channel_id=1, source_target_pairs={{0,2},{1,3},{2,0},{3,1},{4,6},{5,7},{6,4},{7,5},{8,10},{9,11},{10,... | collective-permute-start | bytes 2949128 | tf_op jit(solution)/shard_map/ppermute | solution.py:1204
  118.2 18.4 %copy-start.47 = (f32[8,768]{1,0:T(8,128)S(1)}, f32[8,768]{1,0:T(8,128)}, u32[]{:S(2)}) copy-start(f32[8,768]{1,0:T(8,128)} %get-tuple-element.108) | copy-start | bytes 73732
  135.8 6.7 %copy-start = (bf16[768,768]{1,0:T(8,128)(2,1)S(1)}, bf16[768,768]{1,0:T(8,128)(2,1)}, u32[]{:S(2)}) copy-start(bf16[768,768]{1,0:T(8,128)(2,1)} %get-tuple-element.106) | copy-start | bytes 3538948
  138.1 3.9 %collective-permute-start.17 = (bf16[512,768]{1,0:T(8,128)(2,1)S(1)}, bf16[512,768]{1,0:T(8,128)(2,1)S(1)}, u32[]{:S(2)}, u32[]{:S(2)}) collective-permute-start(bf16[512,768]{1,0:T(8,128)(2,1)S(1)} %broadcast_select_fusion.2), channel_id=1, source_target_pairs={{0,1},{1,0},{2,3},{3,2},{4,5},{5,4},{6,7},{7,6},{8,9},{9,8},{10,11... | collective-permute-start | bytes 2359304 | tf_op jit(solution)/shard_map/ppermute | solution.py:1204
  138.2 4.7 %collective-permute-start.11 = (bf16[640,768]{1,0:T(8,128)(2,1)}, bf16[640,768]{1,0:T(8,128)(2,1)}, u32[]{:S(2)}, u32[]{:S(2)}) collective-permute-start(bf16[640,768]{1,0:T(8,128)(2,1)} %get-tuple-element.91.refs_0_.refs_2_), channel_id=1, source_target_pairs={{0,1},{1,0},{2,3},{3,2},{4,5},{5,4},{6,7},{7,6},{8,9},{9,8},{10,11... | collective-permute-start | bytes 2949128 | tf_op jit(solution)/shard_map/ppermute | solution.py:1204
  138.7 7.7 %collective-permute-start.12 = (bf16[640,768]{1,0:T(8,128)(2,1)}, bf16[640,768]{1,0:T(8,128)(2,1)}, u32[]{:S(2)}, u32[]{:S(2)}) collective-permute-start(bf16[640,768]{1,0:T(8,128)(2,1)} %get-tuple-element.97.refs_0_.refs_3_), channel_id=1, source_target_pairs={{0,1},{1,0},{2,3},{3,2},{4,5},{5,4},{6,7},{7,6},{8,9},{9,8},{10,11... | collective-permute-start | bytes 2949128 | tf_op jit(solution)/shard_map/ppermute | solution.py:1204
  138.8 6.3 %collective-permute-start.15 = (bf16[640,768]{1,0:T(8,128)(2,1)}, bf16[640,768]{1,0:T(8,128)(2,1)}, u32[]{:S(2)}, u32[]{:S(2)}) collective-permute-start(bf16[640,768]{1,0:T(8,128)(2,1)} %collective-permute-done.13.refs_6_), channel_id=1, source_target_pairs={{0,1},{1,0},{2,3},{3,2},{4,5},{5,4},{6,7},{7,6},{8,9},{9,8},{10,11... | collective-permute-start | bytes 2949128 | tf_op jit(solution)/shard_map/ppermute | solution.py:1204
  142.0 4.9 %collective-permute-start.16 = (bf16[640,768]{1,0:T(8,128)(2,1)}, bf16[640,768]{1,0:T(8,128)(2,1)}, u32[]{:S(2)}, u32[]{:S(2)}) collective-permute-start(bf16[640,768]{1,0:T(8,128)(2,1)} %collective-permute-done.14.refs_7_), channel_id=1, source_target_pairs={{0,1},{1,0},{2,3},{3,2},{4,5},{5,4},{6,7},{7,6},{8,9},{9,8},{10,11... | collective-permute-start | bytes 2949128 | tf_op jit(solution)/shard_map/ppermute | solution.py:1204
  142.0 33.9 %collective-permute-start.19 = (bf16[192,640]{1,0:T(8,128)(2,1)}, bf16[192,640]{1,0:T(8,128)(2,1)}, u32[]{:S(2)}, u32[]{:S(2)}) collective-permute-start(bf16[192,640]{1,0:T(8,128)(2,1)} %get-tuple-element.113), channel_id=1, source_target_pairs={{0,1},{1,0},{2,3},{3,2},{4,5},{5,4},{6,7},{7,6},{8,9},{9,8},{10,11... | collective-permute-start | bytes 737288 | tf_op jit(solution)/shard_map/ppermute | solution.py:1204
  142.9 33.0 %collective-permute-start.20 = (bf16[192,640]{1,0:T(8,128)(2,1)}, bf16[192,640]{1,0:T(8,128)(2,1)}, u32[]{:S(2)}, u32[]{:S(2)}) collective-permute-start(bf16[192,640]{1,0:T(8,128)(2,1)} %get-tuple-element.114), channel_id=1, source_target_pairs={{0,2},{1,3},{2,0},{3,1},{4,6},{5,7},{6,4},{7,5},{8,10},{9,11},{10,... | collective-permute-start | bytes 737288 | tf_op jit(solution)/shard_map/ppermute | solution.py:1204
  145.1 30.9 %collective-permute-start.21 = (bf16[192,640]{1,0:T(8,128)(2,1)}, bf16[192,640]{1,0:T(8,128)(2,1)}, u32[]{:S(2)}, u32[]{:S(2)}) collective-permute-start(bf16[192,640]{1,0:T(8,128)(2,1)} %get-tuple-element.115), channel_id=1, source_target_pairs={{0,3},{1,2},{2,1},{3,0},{4,7},{5,6},{6,5},{7,4},{8,11},{9,10},{10,... | collective-permute-start | bytes 737288 | tf_op jit(solution)/shard_map/ppermute | solution.py:1204
  146.5 24.3 %collective-permute-start.18 = (bf16[256,768]{1,0:T(8,128)(2,1)S(1)}, bf16[256,768]{1,0:T(8,128)(2,1)S(1)}, u32[]{:S(2)}, u32[]{:S(2)}) collective-permute-start(bf16[256,768]{1,0:T(8,128)(2,1)S(1)} %broadcast_select_fusion.13), channel_id=1, source_target_pairs={{0,2},{1,3},{2,0},{3,1},{4,6},{5,7},{6,4},{7,5},{8,10},{9,11},{10,... | collective-permute-start | bytes 1179656 | tf_op jit(solution)/shard_map/ppermute | solution.py:1204
  170.9 3.1 %copy-start.7 = (bf16[768,768]{1,0:T(8,128)(2,1)S(1)}, bf16[768,768]{1,0:T(8,128)(2,1)}, u32[]{:S(2)}) copy-start(bf16[768,768]{1,0:T(8,128)(2,1)} %get-tuple-element.105) | copy-start | bytes 3538948
  172.3 23.1 %collective-permute-start.23 = (bf16[448,768]{1,0:T(8,128)(2,1)S(1)}, bf16[448,768]{1,0:T(8,128)(2,1)S(1)}, u32[]{:S(2)}, u32[]{:S(2)}) collective-permute-start(bf16[448,768]{1,0:T(8,128)(2,1)S(1)} %bitcast.82), channel_id=1, source_target_pairs={{0,8},{4,12},{8,0},{12,4},{16,24},{20,28},{24,16},{28,20},{1,9},{5... | collective-permute-start | bytes 2064392 | tf_op jit(solution)/shard_map/ppermute | solution.py:1204
  174.3 21.3 %collective-permute-start.22 = (bf16[448,768]{1,0:T(8,128)(2,1)S(1)}, bf16[448,768]{1,0:T(8,128)(2,1)S(1)}, u32[]{:S(2)}, u32[]{:S(2)}) collective-permute-start(bf16[448,768]{1,0:T(8,128)(2,1)S(1)} %bitcast.83), channel_id=1, source_target_pairs={{0,4},{4,0},{8,12},{12,8},{16,20},{20,16},{24,28},{28,24},{1,5},{5... | collective-permute-start | bytes 2064392 | tf_op jit(solution)/shard_map/ppermute | solution.py:1204
  195.9 12.3 %collective-permute-start.24 = (bf16[224,768]{1,0:T(8,128)(2,1)S(1)}, bf16[224,768]{1,0:T(8,128)(2,1)S(1)}, u32[]{:S(2)}, u32[]{:S(2)}) collective-permute-start(bf16[224,768]{1,0:T(8,128)(2,1)S(1)} %broadcast_select_fusion.22), channel_id=1, source_target_pairs={{0,8},{4,12},{8,0},{12,4},{16,24},{20,28},{24,16},{28,20},{1,9},{5... | collective-permute-start | bytes 1032200 | tf_op jit(solution)/shard_map/ppermute | solution.py:1204
  196.4 11.9 %collective-permute-start.25 = (bf16[224,768]{1,0:T(8,128)(2,1)S(1)}, bf16[224,768]{1,0:T(8,128)(2,1)S(1)}, u32[]{:S(2)}, u32[]{:S(2)}) collective-permute-start(bf16[224,768]{1,0:T(8,128)(2,1)S(1)} %broadcast_select_fusion.19), channel_id=1, source_target_pairs={{0,4},{4,0},{8,12},{12,8},{16,20},{20,16},{24,28},{28,24},{1,5},{5... | collective-permute-start | bytes 1032200 | tf_op jit(solution)/shard_map/ppermute | solution.py:1204
  208.6 18.6 %collective-permute-start.28 = (bf16[224,768]{1,0:T(8,128)(2,1)S(1)}, bf16[224,768]{1,0:T(8,128)(2,1)S(1)}, u32[]{:S(2)}, u32[]{:S(2)}) collective-permute-start(bf16[224,768]{1,0:T(8,128)(2,1)S(1)} %bitcast.84), channel_id=1, source_target_pairs={{0,16},{4,20},{8,24},{12,28},{16,0},{20,4},{24,8},{28,12},{1,17},{... | collective-permute-start | bytes 1032200 | tf_op jit(solution)/shard_map/ppermute | solution.py:1204
  226.6 2.6 copy-start.4
  226.6 5.3 %copy-start.10 = (bf16[640,768]{1,0:T(8,128)(2,1)S(1)}, bf16[640,768]{1,0:T(8,128)(2,1)}, u32[]{:S(2)}) copy-start(bf16[640,768]{1,0:T(8,128)(2,1)} %get-tuple-element.140) | copy-start | bytes 2949124
  226.6 5.3 %collective-permute-start.27 = (bf16[640,768]{1,0:T(8,128)(2,1)}, bf16[640,768]{1,0:T(8,128)(2,1)S(1)}, u32[]{:S(2)}, u32[]{:S(2)}) collective-permute-start(bf16[640,768]{1,0:T(8,128)(2,1)} %get-tuple-element.141), channel_id=1, source_target_pairs={{0,1},{1,0},{2,3},{3,2},{4,5},{5,4},{6,7},{7,6},{8,9},{9,8},{10,11... | collective-permute-start | bytes 2949128 | tf_op jit(solution)/shard_map/ppermute | solution.py:1204
  226.7 43.0 %collective-permute-start.26 = (bf16[640,768]{1,0:T(8,128)(2,1)}, bf16[640,768]{1,0:T(8,128)(2,1)S(1)}, u32[]{:S(2)}, u32[]{:S(2)}) collective-permute-start(bf16[640,768]{1,0:T(8,128)(2,1)} %get-tuple-element.139), channel_id=1, source_target_pairs={{0,1},{1,0},{2,3},{3,2},{4,5},{5,4},{6,7},{7,6},{8,9},{9,8},{10,11... | collective-permute-start | bytes 2949128 | tf_op jit(solution)/shard_map/ppermute | solution.py:1204
  227.6 7.5 %collective-permute-start.30 = (bf16[152,768]{1,0:T(8,128)(2,1)S(1)}, bf16[152,768]{1,0:T(8,128)(2,1)S(1)}, u32[]{:S(2)}, u32[]{:S(2)}) collective-permute-start(bf16[152,768]{1,0:T(8,128)(2,1)S(1)} %broadcast_select_fusion.28), channel_id=1, source_target_pairs={{0,4},{4,0},{8,12},{12,8},{16,20},{20,16},{24,28},{28,24},{1,5},{5... | collective-permute-start | bytes 700424 | tf_op jit(solution)/shard_map/ppermute | solution.py:1204
  229.2 10.6 %collective-permute-start.32 = (bf16[152,768]{1,0:T(8,128)(2,1)S(1)}, bf16[152,768]{1,0:T(8,128)(2,1)S(1)}, u32[]{:S(2)}, u32[]{:S(2)}) collective-permute-start(bf16[152,768]{1,0:T(8,128)(2,1)S(1)} %broadcast_select_fusion.25), channel_id=1, source_target_pairs={{0,8},{4,12},{8,0},{12,4},{16,24},{20,28},{24,16},{28,20},{1,9},{5... | collective-permute-start | bytes 700424 | tf_op jit(solution)/shard_map/ppermute | solution.py:1204
  230.9 17.6 %collective-permute-start.35 = (bf16[224,768]{1,0:T(8,128)(2,1)S(1)}, bf16[224,768]{1,0:T(8,128)(2,1)S(1)}, u32[]{:S(2)}, u32[]{:S(2)}) collective-permute-start(bf16[224,768]{1,0:T(8,128)(2,1)S(1)} %bitcast.85), channel_id=1, source_target_pairs={{0,16},{4,20},{8,24},{12,28},{16,0},{20,4},{24,8},{28,12},{1,17},{... | collective-permute-start | bytes 1032200 | tf_op jit(solution)/shard_map/ppermute | solution.py:1204
  233.1 31.5 %collective-permute-start.29 = (bf16[640,768]{1,0:T(8,128)(2,1)}, bf16[640,768]{1,0:T(8,128)(2,1)S(1)}, u32[]{:S(2)}, u32[]{:S(2)}) collective-permute-start(bf16[640,768]{1,0:T(8,128)(2,1)} %add_convert_fusion), channel_id=1, source_target_pairs={{0,2},{1,3},{2,0},{3,1},{4,6},{5,7},{6,4},{7,5},{8,10},{9,11},{10,... | collective-permute-start | bytes 2949128 | tf_op jit(solution)/shard_map/ppermute | solution.py:1204
  239.9 9.4 %collective-permute-start.31 = (bf16[76,768]{1,0:T(8,128)(2,1)S(1)}, bf16[76,768]{1,0:T(8,128)(2,1)S(1)}, u32[]{:S(2)}, u32[]{:S(2)}) collective-permute-start(bf16[76,768]{1,0:T(8,128)(2,1)S(1)} %broadcast_select_fusion.34), channel_id=1, source_target_pairs={{0,8},{4,12},{8,0},{12,4},{16,24},{20,28},{24,16},{28,20},{1,9},{5... | collective-permute-start | bytes 350216 | tf_op jit(solution)/shard_map/ppermute | solution.py:1204
  240.0 9.4 %collective-permute-start.33 = (bf16[76,768]{1,0:T(8,128)(2,1)S(1)}, bf16[76,768]{1,0:T(8,128)(2,1)S(1)}, u32[]{:S(2)}, u32[]{:S(2)}) collective-permute-start(bf16[76,768]{1,0:T(8,128)(2,1)S(1)} %broadcast_select_fusion.31), channel_id=1, source_target_pairs={{0,4},{4,0},{8,12},{12,8},{16,20},{20,16},{24,28},{28,24},{1,5},{5... | collective-permute-start | bytes 350216 | tf_op jit(solution)/shard_map/ppermute | solution.py:1204
  248.8 8.3 %collective-permute-start.37 = (bf16[224,768]{1,0:T(8,128)(2,1)S(1)}, bf16[224,768]{1,0:T(8,128)(2,1)S(1)}, u32[]{:S(2)}, u32[]{:S(2)}) collective-permute-start(bf16[224,768]{1,0:T(8,128)(2,1)S(1)} %get-tuple-element.215), channel_id=1, source_target_pairs={{0,4},{4,0},{8,12},{12,8},{16,20},{20,16},{24,28},{28,24},{1,5},{5... | collective-permute-start | bytes 1032200 | tf_op jit(solution)/shard_map/ppermute | solution.py:1204
  249.3 15.3 %collective-permute-start.36 = (bf16[224,768]{1,0:T(8,128)(2,1)S(1)}, bf16[224,768]{1,0:T(8,128)(2,1)}, u32[]{:S(2)}, u32[]{:S(2)}) collective-permute-start(bf16[224,768]{1,0:T(8,128)(2,1)S(1)} %get-tuple-element.216), channel_id=1, source_target_pairs={{0,8},{4,12},{8,0},{12,4},{16,24},{20,28},{24,16},{28,20},{1,9},{5... | collective-permute-start | bytes 1032200 | tf_op jit(solution)/shard_map/ppermute | solution.py:1204
  250.3 12.7 %collective-permute-start.34 = (bf16[152,768]{1,0:T(8,128)(2,1)}, bf16[152,768]{1,0:T(8,128)(2,1)}, u32[]{:S(2)}, u32[]{:S(2)}) collective-permute-start(bf16[152,768]{1,0:T(8,128)(2,1)} %reshape.563), channel_id=1, source_target_pairs={{0,16},{4,20},{8,24},{12,28},{16,0},{20,4},{24,8},{28,12},{1,17},{... | collective-permute-start | bytes 700424 | tf_op jit(solution)/shard_map/ppermute | solution.py:1204
  257.3 28.6 %collective-permute-start.43 = (bf16[384,768]{1,0:T(8,128)(2,1)S(1)}, bf16[384,768]{1,0:T(8,128)(2,1)}, u32[]{:S(2)}, u32[]{:S(2)}) collective-permute-start(bf16[384,768]{1,0:T(8,128)(2,1)S(1)} %bitcast.72), channel_id=1, source_target_pairs={{0,8},{4,12},{8,0},{12,4},{16,24},{20,28},{24,16},{28,20},{1,9},{5... | collective-permute-start | bytes 1769480 | tf_op jit(solution)/shard_map/ppermute | solution.py:1204
  265.7 4.0 %copy-start.3 = (f32[640,768]{1,0:T(8,128)S(1)}, f32[640,768]{1,0:T(8,128)}, u32[]{:S(2)}) copy-start(f32[640,768]{1,0:T(8,128)} %get-tuple-element.101) | copy-start | bytes 5898244
  265.7 3.9 %copy-start.9 = (bf16[640,768]{1,0:T(8,128)(2,1)S(1)}, bf16[640,768]{1,0:T(8,128)(2,1)}, u32[]{:S(2)}) copy-start(bf16[640,768]{1,0:T(8,128)(2,1)} %get-tuple-element.138) | copy-start | bytes 2949124
  265.8 26.0 %collective-permute-start.40 = (bf16[384,768]{1,0:T(8,128)(2,1)S(1)}, bf16[384,768]{1,0:T(8,128)(2,1)S(1)}, u32[]{:S(2)}, u32[]{:S(2)}) collective-permute-start(bf16[384,768]{1,0:T(8,128)(2,1)S(1)} %bitcast.73), channel_id=1, source_target_pairs={{0,4},{4,0},{8,12},{12,8},{16,20},{20,16},{24,28},{28,24},{1,5},{5... | collective-permute-start | bytes 1769480 | tf_op jit(solution)/shard_map/ppermute | solution.py:1204
  267.6 14.0 %collective-permute-start.41 = (bf16[140,768]{1,0:T(8,128)(2,1)S(1)}, bf16[140,768]{1,0:T(8,128)(2,1)S(1)}, u32[]{:S(2)}, u32[]{:S(2)}) collective-permute-start(bf16[140,768]{1,0:T(8,128)(2,1)S(1)} %pad_maximum_fusion.18), channel_id=1, source_target_pairs={{0,4},{4,0},{8,12},{12,8},{16,20},{20,16},{24,28},{28,24},{1,5},{5... | collective-permute-start | bytes 645128 | tf_op jit(solution)/shard_map/ppermute | solution.py:1204
  268.1 13.5 %collective-permute-start.38 = (bf16[140,768]{1,0:T(8,128)(2,1)S(1)}, bf16[140,768]{1,0:T(8,128)(2,1)S(1)}, u32[]{:S(2)}, u32[]{:S(2)}) collective-permute-start(bf16[140,768]{1,0:T(8,128)(2,1)S(1)} %pad_maximum_fusion.17), channel_id=1, source_target_pairs={{0,8},{4,12},{8,0},{12,4},{16,24},{20,28},{24,16},{28,20},{1,9},{5... | collective-permute-start | bytes 645128 | tf_op jit(solution)/shard_map/ppermute | solution.py:1204
  281.7 11.8 %collective-permute-start.44 = (bf16[256,768]{1,0:T(8,128)(2,1)S(1)}, bf16[256,768]{1,0:T(8,128)(2,1)S(1)}, u32[]{:S(2)}, u32[]{:S(2)}) collective-permute-start(bf16[256,768]{1,0:T(8,128)(2,1)S(1)} %pad_maximum_fusion.11), channel_id=1, source_target_pairs={{0,2},{1,3},{2,0},{3,1},{4,6},{5,7},{6,4},{7,5},{8,10},{9,11},{10,... | collective-permute-start | bytes 1179656 | tf_op jit(solution)/shard_map/ppermute | solution.py:1204
  284.0 9.5 %collective-permute-start.39 = (bf16[152,768]{1,0:T(8,128)(2,1)S(1)}, bf16[152,768]{1,0:T(8,128)(2,1)S(1)}, u32[]{:S(2)}, u32[]{:S(2)}) collective-permute-start(bf16[152,768]{1,0:T(8,128)(2,1)S(1)} %pad_maximum_fusion.15), channel_id=1, source_target_pairs={{0,4},{4,0},{8,12},{12,8},{16,20},{20,16},{24,28},{28,24},{1,5},{5... | collective-permute-start | bytes 700424 | tf_op jit(solution)/shard_map/ppermute | solution.py:1204
  285.7 6.1 %collective-permute-start.42 = (bf16[152,768]{1,0:T(8,128)(2,1)S(1)}, bf16[152,768]{1,0:T(8,128)(2,1)S(1)}, u32[]{:S(2)}, u32[]{:S(2)}) collective-permute-start(bf16[152,768]{1,0:T(8,128)(2,1)S(1)} %pad_maximum_fusion.16), channel_id=1, source_target_pairs={{0,8},{4,12},{8,0},{12,4},{16,24},{20,28},{24,16},{28,20},{1,9},{5... | collective-permute-start | bytes 700424 | tf_op jit(solution)/shard_map/ppermute | solution.py:1204
  293.7 2.4 collective-permute-start.45
  (42 other events, 81.4 us)

commit v4 on v3

--- a/solution.py
+++ b/solution.py
@@ -390,6 +390,18 @@
         amongs.append(split_low(packed))
         approxes.append(fold(among.T) / column_top)
 
+    io.need(5)
+
+    def convolve(start):
+        same = jnp.where(layout.same(start), 1.0, 0.0).astype(BF16)
+        smooth = [
+            dot_nn(qkv_t[part_rows(2, h), start : start + BAND_IN], bands[h] * same)
+            for h in each
+        ]
+        for h in each:
+            context[part_rows(0, h), start : start + BAND_OUT] = smooth[h]
+
+    starts = list(range(0, group_size, BAND_OUT))
     for step in range(NS_ITERS):
         product = [
             dot_three(amongs[h], spread_split(approxes[h], mask_b)) for h in range(heads)
@@ -404,6 +416,8 @@
             13.0 * eye - dot_three(split[h], spread_split(second[h], mask_b))
             for h in range(heads)
         ]
+        for start in starts[step::NS_ITERS]:
+            convolve(start)
         for h in range(heads):
             steps_out[h, 4 * step] = approxes[h]
             steps_out[h, 4 * step + 1] = product[h]
@@ -424,19 +438,6 @@
             part = mark_values[s * LANDMARKS : (s + 1) * LANDMARKS, :]
             mvts[SEQS * h + s] = part.T.astype(BF16)
     io.send(6, 8, 9, 10)
-    io.need(5)
-
-    @pl.loop(0, group_size // BAND_OUT)
-    def _(i):
-        start = i * BAND_OUT
-        same = jnp.where(layout.same(start), 1.0, 0.0).astype(BF16)
-        smooth = [
-            dot_nn(qkv_t[part_rows(2, h), lane_slice(start, BAND_IN)], bands[h] * same)
-            for h in each
-        ]
-        for h in each:
-            context[part_rows(0, h), lane_slice(start, BAND_OUT)] = smooth[h]
-
     @pl.loop(0, layout.pairs)
     def _(p):
         sequence, tile, start, end = layout.pair(p)
@@ -960,6 +961,7 @@
 
 ROWS = 320
 UNITS = 768
+PART = 768
 
 
 def norm_in_kernel(io, scalars):
@@ -1139,24 +1141,23 @@
 
 
 def feed_weights_kernel(io, scalars, pre, grad_hidden, up_total, down_total):
-    up, down = io.inputs[0], io.inputs[1]
+    up_t, down = io.inputs[0], io.inputs[1]
     grad_up, grad_down = io.outputs
-    units = up.shape[1]
+    units = up_t.shape[0]
 
     def into(at, j):
         n, b = io.inputs[2 + 2 * at], io.inputs[3 + 2 * at]
-        columns = lane_slice(j * UNITS, UNITS)
-        pre[at % 2, :, columns] = dot_nn(n[...], up[:, columns])
-        grad_hidden[at % 2, :, columns] = dot_nt(b[...], down[row_block(j, UNITS), :])
+        rows = row_block(j, PART)
+        pre[at % 2, rows, :] = dot_nt(up_t[rows, :], n[...])
+        grad_hidden[at % 2, rows, :] = dot_nt(down[rows, :], b[...])
 
     def out_of(at, j):
         n, b = io.inputs[2 + 2 * at], io.inputs[3 + 2 * at]
-        columns = lane_slice(j * UNITS, UNITS)
-        rows = row_block(j, UNITS)
-        value, derivative = gelu_and_slope(pre[at % 2, :, columns])
-        grad_pre = (derivative * grad_hidden[at % 2, :, columns]).astype(BF16)
-        down_part = dot_tn(value.astype(BF16), b[...])
-        up_part = dot_tn(grad_pre, n[...])
+        rows = row_block(j, PART)
+        value, derivative = gelu_and_slope(pre[at % 2, rows, :])
+        grad_pre = (derivative * grad_hidden[at % 2, rows, :]).astype(BF16)
+        down_part = dot_nn(value.astype(BF16), b[...])
+        up_part = dot_nn(grad_pre, n[...])
         if at == 0:
             down_total[rows, :] = down_part
             up_total[rows, :] = up_part
@@ -1165,14 +1166,16 @@
             up_total[rows, :] += up_part
         else:
             grad_down[rows, :] = (down_total[rows, :] + down_part).astype(BF16)
-            grad_up[:, columns] = (up_total[rows, :] + up_part).T.astype(BF16)
+            grad_up[:, lane_slice(j * PART, PART)] = (
+                (up_total[rows, :] + up_part).T.astype(BF16)
+            )
 
     io.need(0, 1)
     for at in range(5):
         if at < 4:
             io.need(2 + 2 * at, 3 + 2 * at)
 
-        @pl.loop(0, units // UNITS)
+        @pl.loop(0, units // PART)
         def _(j):
             if at < 4:
                 into(at, j)
@@ -1180,19 +1183,19 @@
                 out_of(at - 1, j)
 
 
-def feed_weights(scalars, normeds, branch_grads, up, down):
-    features, units = up.shape
+def feed_weights(scalars, normeds, branch_grads, weights):
+    units, features = weights.shape[0] // 2, weights.shape[1]
     block = normeds[0].shape[0]
     between = [a for pair in zip(normeds, branch_grads, strict=True) for a in pair]
     return local_call(
         feed_weights_kernel,
         "feed_weights",
         scalars,
-        (up, down, *between),
+        (Joined((weights, 0, units)), Joined((weights, units, units)), *between),
         (shape_of(BF16, features, units), shape_of(BF16, units, features)),
         [
-            pltpu.VMEM((2, block, units), F32),
-            pltpu.VMEM((2, block, units), F32),
+            pltpu.VMEM((2, units, block), F32),
+            pltpu.VMEM((2, units, block), F32),
             pltpu.VMEM((units, features), F32),
             pltpu.VMEM((units, features), F32),
         ],
@@ -1365,7 +1368,7 @@
         small = add(small_kept, after(small_got, branch_two))
         small_kept, small_sent = halve(small, "tensor", 2)
         small_got = to_partner(small_sent, "tensor", 4, 2)
-        grad_up, grad_down = feed_weights(scalars, normeds, branch_grads, w_up, w_down)
+        grad_up, grad_down = feed_weights(scalars, normeds, branch_grads, weights)
         small = add(small_kept, after(small_got, grad_up))
 
         def with_part(grad, rows):

time: 296 us -> 290 us (0.980); the launches traced: 299 us -> 287 us
  Pallas kernels: 150 us -> 136 us
    pallas_call x8, Pallas kernels: 150 us -> 136 us  [local_call(): pl.pallas_call(body, name=name, out_shape=out_shape, in_specs=[pl.BlockSp...]
  transfers between devices with their start and end apart: 46 -> 46, of which waited for: 17 -> 17; matrix products, arithmetic and copies ran while one was open for 13% -> 14% of each run, Pallas kernels for 50% -> 48%
where the time goes in v4:
time: 290 us; the launch traced here: 287 us
  Pallas kernels  136 us (47%)
  waiting for transfers between devices  64.8 us (22%)
  starting transfers between devices  37.2 us (13%)
  other arithmetic  34.6 us (12%)
  local copies, waits for them, and re-layouts  11.9 us (4%)
    pallas_call x8, Pallas kernels, local_call(): pl.pallas_call(body, name=name, out_shape=out_shape, in_specs=[pl.BlockSp...  136 us
    ppermute x46, waiting for transfers between devices, to_partner(): return lax.ppermute(array, axis, [(i, i ^ bit) for i in range(size)])  64.8 us
    ppermute x46, starting transfers between devices, to_partner(): return lax.ppermute(array, axis, [(i, i ^ bit) for i in range(size)])  37.2 us
    convert_element_type x1, other arithmetic, make_bands(): return band.astype(BF16)  6.72 us
  transfers between devices with their start and end apart: 46, of which 17 were waited for; matrix products, arithmetic and copies ran while one was open for 14% of the time, Pallas kernels for 48%

profile of v4, /device:TPU:0, one launch (start us, length us, event | category | flops | bytes accessed | tf_op | source)
XLA Modules:
  0.0 287.0 jit_solution(6966202455390275782)
XLA Ops:
  0.6 3.0 %collective-permute-start.1 = (bf16[640,768]{1,0:T(8,128)(2,1)}, bf16[640,768]{1,0:T(8,128)(2,1)}, u32[]{:S(2)}, u32[]{:S(2)}) collective-permute-start(bf16[640,768]{1,0:T(8,128)(2,1)} %refs_6_.1), channel_id=1, source_target_pairs={{0,2},{1,3},{2,0},{3,1},{4,6},{5,7},{6,4},{7,5},{8,10},{9,11},{10,... | collective-permute-start | bytes 2949128 | tf_op jit(solution)/shard_map/ppermute | solution.py:1207
  3.7 2.5 slice_reduce_fusion.36
  6.1 2.2 slice_reduce_fusion.35
  8.3 4.5 %fusion.40 = (pred[512,256]{1,0:T(8,128)(4,1)}, pred[512,256]{1,0:T(8,128)(4,1)}, pred[512,256]{1,0:T(8,128)(4,1)}, pred[512,256]{1,0:T(8,128)(4,1)}, pred[512,2...) fusion(s32[512]{0:T(512)S(1)} %iota_add_fusion), kind=kLoop, calls=%fused_computation.91 | loop fusion | flops 4587520 | bytes 4327424 | tf_op jit(solution)/shard_map/eq | solution.py:1228
  12.8 0.8 copy.28
  14.4 1.6 pad_maximum_fusion.refs_2_.refs_8_.refs_9_.refs_0_.refs_1_
  16.0 1.6 fusion.6
  18.1 1.0 pad_maximum_fusion.3.refs_0_.refs_5_
  20.3 6.7 %select_convert_fusion.refs_5_.refs_11_ = bf16[3,512,256]{2,1,0:T(8,128)(2,1)} fusion(bf16[3]{0:T(256)(128)(2,1)} %get-tuple-element.194, bf16[3]{0:T(256)(128)(2,1)} %get-tuple-element.195, bf16[3]{0:T(256)(128)(2,1)S(1)} %copy-done.52, bf16[3]{0:T(256)(128)(2,1)S(1)} %copy-done.53, bf16[3]{0:T(256)(128)(2,1)S(1)} %copy-done.54, ...), kind=kLoop, calls=%fused_computation.8 | loop fusion | flops 12976128 | bytes 5112006 | tf_op jit(solution)/shard_map/convert_element_type | solution.py:1229
  28.2 1.9 collective-permute-done.2.refs_4_.refs_9_
  30.1 23.8 %attend.1 = (bf16[576,2816]{1,0:T(8,128)(2,1)}, bf16[192,640]{1,0:T(8,128)(2,1)}, bf16[192,640]{1,0:T(8,128)(2,1)}, bf16[192,640]{1,0:T(8,128)(2,1)}, bf16[192,6...) custom-call(s32[4]{0:T(128)} %pad_add_fusion.scalar_ref, ...), custom_call_target="tpu_custom_call" | custom-call | flops 30000001024 | bytes 14358528 | tf_op jit(solution)/shard_map/attend/pallas_call | solution.py:240
  53.9 2.2 collective-permute-done.7.refs_4_.refs_10_.refs_11_
  56.2 1.5 collective-permute-start.8
  58.7 0.8 collective-permute-start.5
  59.5 2.9 collective-permute-done.3.refs_1_.refs_20_
  62.8 4.4 %collective-permute-done.4.refs_2_.refs_21_ = bf16[192,640]{1,0:T(8,128)(2,1)S(1)} collective-permute-done((bf16[192,640]{1,0:T(8,128)(2,1)}, bf16[192,640]{1,0:T(8,128)(2,1)S(1)}, u32[]{:S(2)}, u32[]{:S(2)}) %collective-permute-start.4) | collective-permute-done | bytes 245792 | tf_op jit(solution)/shard_map/ppermute | solution.py:1207
  67.2 3.3 %collective-permute-done.5.refs_3_.refs_22_ = bf16[192,640]{1,0:T(8,128)(2,1)S(1)} collective-permute-done((bf16[192,640]{1,0:T(8,128)(2,1)}, bf16[192,640]{1,0:T(8,128)(2,1)S(1)}, u32[]{:S(2)}, u32[]{:S(2)}) %collective-permute-start.5) | collective-permute-done | bytes 245792 | tf_op jit(solution)/shard_map/ppermute | solution.py:1207
  71.3 6.3 %norm_in.1 = (bf16[640,768]{1,0:T(8,128)(2,1)}, f32[640,768]{1,0:T(8,128)}, f32[640,128]{1,0:T(8,128)}) custom-call(s32[4]{0:T(128)} %pad_add_fusion.scalar_ref, bf16[192,640]{1,0:T(8,128)(2,1)} %get-tuple-element.87.refs_0_.refs_19_, bf16[192,640]{1,0:T(8,128)(2,1)} %copy-done.55, bf16[192,640]{1,0:T(8,128)(2,1)} %copy-done.56, ...), custom_call_target="tpu_custom_call" | custom-call | flops 6000000000 | bytes 6434816 | tf_op jit(solution)/shard_map/norm_in/pallas_call | solution.py:240
  77.5 6.0 %collective-permute-done.8.refs_5_.refs_11_.refs_12_ = bf16[768,768]{1,0:T(8,128)(2,1)} collective-permute-done((bf16[768,768]{1,0:T(8,128)(2,1)}, bf16[768,768]{1,0:T(8,128)(2,1)}, u32[]{:S(2)}, u32[]{:S(2)}) %collective-permute-start.8) | collective-permute-done | bytes 1179680 | tf_op jit(solution)/shard_map/ppermute | solution.py:1207
  83.6 0.7 collective-permute-start.13
  84.3 2.4 collective-permute-done.10.refs_7_.refs_13_.refs_14_
  86.7 19.2 %feed.1 = (f32[640,768]{1,0:T(8,128)}, bf16[640,3072]{1,0:T(8,128)(2,1)}, f32[640,768]{1,0:T(8,128)}, bf16[640,768]{1,0:T(8,128)(2,1)}, f32[8,768]{1,0:T(8,128)}) custom-call(s32[4]{0:T(128)} %pad_add_fusion.scalar_ref, bf16[640,768]{1,0:T(8,128)(2,1)} %get-tuple-element.91.refs_0_.refs_2_, f32[4,768]{1,0:T(4,128)} %pad_maximum_fusion.19.refs_6_.refs_1_, ...), custom_call_target="tpu_custom_call" | custom-call | flops 22000001024 | bytes 31690752 | tf_op jit(solution)/shard_map/feed/pallas_call | solution.py:240
  105.9 0.8 collective-permute-start.14
  106.7 17.6 %feed_back.1 = (f32[640,768]{1,0:T(8,128)}, bf16[768,768]{1,0:T(8,128)(2,1)}, f32[8,768]{1,0:T(8,128)}, bf16[192,640]{1,0:T(8,128)(2,1)}, bf16[192,640]{1,0:T(8,...) custom-call(s32[4]{0:T(128)} %pad_add_fusion.scalar_ref, ...), custom_call_target="tpu_custom_call" | custom-call | flops 20000000000 | bytes 34377728 | tf_op jit(solution)/shard_map/feed_back/pallas_call | solution.py:240
  124.3 0.8 convert.8
  125.1 1.5 broadcast_select_fusion.2
  127.7 2.3 collective-permute-done.14.refs_7_
  131.0 1.0 collective-permute-start.20
  132.0 1.5 collective-permute-done.15.refs_8_
  133.5 1.0 collective-permute-start.21
  134.6 0.7 collective-permute-start.18
  135.3 23.7 %feed_weights.1 = (bf16[768,768]{1,0:T(8,128)(2,1)}, bf16[768,768]{1,0:T(8,128)(2,1)}) custom-call(s32[4]{0:T(128)} %pad_add_fusion.scalar_ref, bf16[1536,768]{1,0:T(8,128)(2,1)} %pad_maximum_fusion.refs_2_.refs_8_.refs_9_.refs_0_.refs_1_, bf16[1536,768]{1,0:T(8,128)(2,1)} %pad_maximum_fusion.refs_2_.refs_8_.refs_9_.refs_0_.refs_1_, ...), custom_call_target="tpu_custom_call" | custom-call | flops 24999999488 | bytes 14942208 | tf_op jit(solution)/shard_map/feed_weights/pallas_call | solution.py:240
  159.3 1.0 copy-done.8
  160.6 1.4 collective-permute-start.23
  162.3 1.6 collective-permute-start.22
  163.9 19.2 %attend_back.1 = (bf16[192,2560]{1,0:T(8,128)(2,1)}, f32[8,128]{1,0:T(8,128)}, f32[192,2560]{1,0:T(8,128)}, f32[192,2560]{1,0:T(8,128)}, f32[3,192,64]{2,1,0:T(8...) custom-call(s32[4]{0:T(128)} %pad_add_fusion.scalar_ref, bf16[192,640]{1,0:T(8,128)(2,1)} %get-tuple-element.112.refs_0_, ...), custom_call_target="tpu_custom_call" | custom-call | flops 8000000000 | bytes 11216896 | tf_op jit(solution)/shard_map/attend_back/pallas_call | solution.py:240
  184.9 11.4 %attend_steps.1.refs_4_ = bf16[2,9,64,64]{3,2,1,0:T(8,128)(2,1)} custom-call(s32[4]{0:T(128)} %pad_add_fusion.scalar_ref, f32[3,192,64]{2,1,0:T(8,128)} %get-tuple-element.130.refs_0_, f32[3,192,64]{2,1,0:T(8,128)} %get-tuple-element.119.refs_7_.refs_1_, f32[3,64,192]{2,1,0:T(8,128)} %get-tuple-element.131.refs_2_, ...), custom_call_target="tpu_custom_call" | custom-call | flops 5000000000 | bytes 4571136 | tf_op jit(solution)/shard_map/attend_steps/pallas_call | solution.py:240
  196.6 2.5 collective-permute-start.28
  199.1 15.2 %attend_grads.1 = (bf16[304,768]{1,0:T(8,128)(2,1)}, bf16[304,768]{1,0:T(8,128)(2,1)}, bf16[640,768]{1,0:T(8,128)(2,1)}, bf16[640,768]{1,0:T(8,128)(2,1)}, bf16[...) custom-call(s32[4]{0:T(128)} %pad_add_fusion.scalar_ref, bf16[192,2560]{1,0:T(8,128)(2,1)} %get-tuple-element.123.refs_0_, ...), custom_call_target="tpu_custom_call" | custom-call | flops 8000000000 | bytes 14749696 | tf_op jit(solution)/shard_map/attend_grads/pallas_call | solution.py:240
  215.3 1.6 collective-permute-start.30
  217.0 1.6 collective-permute-start.32
  218.6 1.0 collective-permute-start.35
  219.6 1.2 add_convert_fusion
  220.8 1.5 collective-permute-start.29
  222.9 4.6 %collective-permute-done.32 = bf16[152,768]{1,0:T(8,128)(2,1)S(1)} collective-permute-done((bf16[152,768]{1,0:T(8,128)(2,1)S(1)}, bf16[152,768]{1,0:T(8,128)(2,1)S(1)}, u32[]{:S(2)}, u32[]{:S(2)}) %collective-permute-start.32) | collective-permute-done | bytes 233504 | tf_op jit(solution)/shard_map/ppermute | solution.py:1207
  228.3 7.9 %collective-permute-done.35 = bf16[224,768]{1,0:T(8,128)(2,1)S(1)} collective-permute-done((bf16[224,768]{1,0:T(8,128)(2,1)S(1)}, bf16[224,768]{1,0:T(8,128)(2,1)S(1)}, u32[]{:S(2)}, u32[]{:S(2)}) %collective-permute-start.35) | collective-permute-done | bytes 344096 | tf_op jit(solution)/shard_map/ppermute | solution.py:1207
  237.4 1.7 collective-permute-start.34
  239.0 5.9 %collective-permute-done.37 = bf16[224,768]{1,0:T(8,128)(2,1)} collective-permute-done((bf16[224,768]{1,0:T(8,128)(2,1)S(1)}, bf16[224,768]{1,0:T(8,128)(2,1)}, u32[]{:S(2)}, u32[]{:S(2)}) %collective-permute-start.37) | collective-permute-done | bytes 344096 | tf_op jit(solution)/shard_map/ppermute | solution.py:1207
  245.0 1.0 broadcast_select_fusion.18
  246.2 4.4 %collective-permute-done.34 = bf16[152,768]{1,0:T(8,128)(2,1)} collective-permute-done((bf16[152,768]{1,0:T(8,128)(2,1)S(1)}, bf16[152,768]{1,0:T(8,128)(2,1)}, u32[]{:S(2)}, u32[]{:S(2)}) %collective-permute-start.34) | collective-permute-done | bytes 233504 | tf_op jit(solution)/shard_map/ppermute | solution.py:1207
  250.6 1.0 reshape.564
  251.6 1.0 broadcast_select_fusion.21
  252.8 1.6 collective-permute-start.40
  255.1 2.3 collective-permute-start.38
  257.4 1.8 convert_add_fusion
  259.2 11.0 %collective-permute-done.41 = bf16[140,768]{1,0:T(8,128)(2,1)S(1)} collective-permute-done((bf16[140,768]{1,0:T(8,128)(2,1)S(1)}, bf16[140,768]{1,0:T(8,128)(2,1)S(1)}, u32[]{:S(2)}, u32[]{:S(2)}) %collective-permute-start.41) | collective-permute-done | bytes 215072 | tf_op jit(solution)/shard_map/ppermute | solution.py:1207
  270.3 1.8 collective-permute-start.44
  272.2 1.6 collective-permute-start.39
  274.0 1.1 broadcast_select_fusion.8
  275.1 1.6 maximum_convert_fusion.1
  276.7 3.3 %collective-permute-done.42 = bf16[152,768]{1,0:T(8,128)(2,1)S(1)} collective-permute-done((bf16[152,768]{1,0:T(8,128)(2,1)S(1)}, bf16[152,768]{1,0:T(8,128)(2,1)S(1)}, u32[]{:S(2)}, u32[]{:S(2)}) %collective-permute-start.42) | collective-permute-done | bytes 233504 | tf_op jit(solution)/shard_map/ppermute | solution.py:1207
  280.1 1.6 maximum_convert_fusion
  282.9 1.2 slice_bitcast_fusion
  284.6 1.6 fusion.2
  (236 shorter events, 17.3 us)
Async XLA Ops:
  0.6 26.3 %collective-permute-start.1 = (bf16[640,768]{1,0:T(8,128)(2,1)}, bf16[640,768]{1,0:T(8,128)(2,1)}, u32[]{:S(2)}, u32[]{:S(2)}) collective-permute-start(bf16[640,768]{1,0:T(8,128)(2,1)} %refs_6_.1), channel_id=1, source_target_pairs={{0,2},{1,3},{2,0},{3,1},{4,6},{5,7},{6,4},{7,5},{8,10},{9,11},{10,... | collective-permute-start | bytes 2949128 | tf_op jit(solution)/shard_map/ppermute | solution.py:1207
  3.6 24.6 %collective-permute-start = (bf16[640,768]{1,0:T(8,128)(2,1)}, bf16[640,768]{1,0:T(8,128)(2,1)}, u32[]{:S(2)}, u32[]{:S(2)}) collective-permute-start(bf16[640,768]{1,0:T(8,128)(2,1)} %refs_6_.1), channel_id=1, source_target_pairs={{0,1},{1,0},{2,3},{3,2},{4,5},{5,4},{6,7},{7,6},{8,9},{9,8},{10,11... | collective-permute-start | bytes 2949128 | tf_op jit(solution)/shard_map/ppermute | solution.py:1207
  8.3 4.5 %copy-start.6 = (bf16[768,768]{1,0:T(8,128)(2,1)S(1)}, bf16[768,768]{1,0:T(8,128)(2,1)}, u32[]{:S(2)}) copy-start(bf16[768,768]{1,0:T(8,128)(2,1)} %param.22) | copy-start | bytes 3538948
  16.0 3.7 %copy-start.43 = (pred[512,256]{1,0:T(8,128)(4,1)S(1)}, pred[512,256]{1,0:T(8,128)(4,1)}, u32[]{:S(2)}) copy-start(pred[512,256]{1,0:T(8,128)(4,1)} %get-tuple-element.271) | copy-start | bytes 393220
  17.9 2.3 copy-start.42
  18.0 2.3 copy-start.51
  18.0 2.3 copy-start.52
  18.0 2.3 copy-start.53
  18.0 2.3 copy-start.54
  20.2 7.3 %copy-start.58 = (s32[1,3]{1,0:T(1,128)S(1)}, s32[1,3]{1,0:T(1,128)}, u32[]{:S(2)}) copy-start(s32[1,3]{1,0:T(1,128)} %param.26) | copy-start | bytes 40
  27.0 3.1 %collective-permute-start.2 = (bf16[640,768]{1,0:T(8,128)(2,1)}, bf16[640,768]{1,0:T(8,128)(2,1)}, u32[]{:S(2)}, u32[]{:S(2)}) collective-permute-start(bf16[640,768]{1,0:T(8,128)(2,1)} %collective-permute-done.1.refs_3_.refs_8_), channel_id=1, source_target_pairs={{0,1},{1,0},{2,3},{3,2},{4,5},{5,4},{6,7},{7,6},{8,9},{9,8},{10,11... | collective-permute-start | bytes 2949128 | tf_op jit(solution)/shard_map/ppermute | solution.py:1207
  28.1 29.5 %copy-start.2 = (bf16[1536,768]{1,0:T(8,128)(2,1)S(1)}, bf16[1536,768]{1,0:T(8,128)(2,1)}, u32[]{:S(2)}) copy-start(bf16[1536,768]{1,0:T(8,128)(2,1)} %pad_maximum_fusion.refs_2_.refs_8_.refs_9_.refs_0_.refs_1_) | copy-start | bytes 7077892
  28.1 28.0 %collective-permute-start.7 = (bf16[768,768]{1,0:T(8,128)(2,1)S(1)}, bf16[768,768]{1,0:T(8,128)(2,1)}, u32[]{:S(2)}, u32[]{:S(2)}) collective-permute-start(bf16[768,768]{1,0:T(8,128)(2,1)S(1)} %pad_maximum_fusion.2), channel_id=1, source_target_pairs={{0,2},{1,3},{2,0},{3,1},{4,6},{5,7},{6,4},{7,5},{8,10},{9,11},{10,... | collective-permute-start | bytes 3538952 | tf_op jit(solution)/shard_map/ppermute | solution.py:1207
  56.2 27.4 %collective-permute-start.8 = (bf16[768,768]{1,0:T(8,128)(2,1)}, bf16[768,768]{1,0:T(8,128)(2,1)}, u32[]{:S(2)}, u32[]{:S(2)}) collective-permute-start(bf16[768,768]{1,0:T(8,128)(2,1)} %collective-permute-done.7.refs_4_.refs_10_.refs_11_), channel_id=1, source_target_pairs={{0,4},{4,0},{8,12},{12,8},{16,20},{20,16},{24,28},{28,24},{1,5},{5... | collective-permute-start | bytes 3538952 | tf_op jit(solution)/shard_map/ppermute | solution.py:1207
  57.7 26.7 %collective-permute-start.6 = (bf16[1536,768]{1,0:T(8,128)(2,1)S(1)}, bf16[1536,768]{1,0:T(8,128)(2,1)}, u32[]{:S(2)}, u32[]{:S(2)}) collective-permute-start(bf16[1536,768]{1,0:T(8,128)(2,1)S(1)} %copy-done.2), channel_id=1, source_target_pairs={{0,1},{1,0},{2,3},{3,2},{4,5},{5,4},{6,7},{7,6},{8,9},{9,8},{10,11... | collective-permute-start | bytes 7077896 | tf_op jit(solution)/shard_map/ppermute | solution.py:1207
  57.7 4.7 %collective-permute-start.3 = (bf16[192,640]{1,0:T(8,128)(2,1)}, bf16[192,640]{1,0:T(8,128)(2,1)S(1)}, u32[]{:S(2)}, u32[]{:S(2)}) collective-permute-start(bf16[192,640]{1,0:T(8,128)(2,1)} %get-tuple-element.88), channel_id=1, source_target_pairs={{0,1},{1,0},{2,3},{3,2},{4,5},{5,4},{6,7},{7,6},{8,9},{9,8},{10,11... | collective-permute-start | bytes 737288 | tf_op jit(solution)/shard_map/ppermute | solution.py:1207
  58.2 9.0 %collective-permute-start.4 = (bf16[192,640]{1,0:T(8,128)(2,1)}, bf16[192,640]{1,0:T(8,128)(2,1)S(1)}, u32[]{:S(2)}, u32[]{:S(2)}) collective-permute-start(bf16[192,640]{1,0:T(8,128)(2,1)} %get-tuple-element.89), channel_id=1, source_target_pairs={{0,2},{1,3},{2,0},{3,1},{4,6},{5,7},{6,4},{7,5},{8,10},{9,11},{10,... | collective-permute-start | bytes 737288 | tf_op jit(solution)/shard_map/ppermute | solution.py:1207
  58.7 11.8 %collective-permute-start.5 = (bf16[192,640]{1,0:T(8,128)(2,1)}, bf16[192,640]{1,0:T(8,128)(2,1)S(1)}, u32[]{:S(2)}, u32[]{:S(2)}) collective-permute-start(bf16[192,640]{1,0:T(8,128)(2,1)} %get-tuple-element.90), channel_id=1, source_target_pairs={{0,3},{1,2},{2,1},{3,0},{4,7},{5,6},{6,5},{7,4},{8,11},{9,10},{10,... | collective-permute-start | bytes 737288 | tf_op jit(solution)/shard_map/ppermute | solution.py:1207
  62.4 8.2 %copy-start.55 = (bf16[192,640]{1,0:T(8,128)(2,1)}, bf16[192,640]{1,0:T(8,128)(2,1)S(1)}, u32[]{:S(2)}) copy-start(bf16[192,640]{1,0:T(8,128)(2,1)S(1)} %collective-permute-done.3.refs_1_.refs_20_) | copy-start | bytes 737284
  62.4 21.9 %collective-permute-start.9 = (bf16[768,768]{1,0:T(8,128)(2,1)}, bf16[768,768]{1,0:T(8,128)(2,1)}, u32[]{:S(2)}, u32[]{:S(2)}) collective-permute-start(bf16[768,768]{1,0:T(8,128)(2,1)} %collective-permute-done.7.refs_4_.refs_10_.refs_11_), channel_id=1, source_target_pairs={{0,1},{1,0},{2,3},{3,2},{4,5},{5,4},{6,7},{7,6},{8,9},{9,8},{10,11... | collective-permute-start | bytes 3538952 | tf_op jit(solution)/shard_map/ppermute | solution.py:1207
  67.2 3.3 %copy-start.56 = (bf16[192,640]{1,0:T(8,128)(2,1)}, bf16[192,640]{1,0:T(8,128)(2,1)S(1)}, u32[]{:S(2)}) copy-start(bf16[192,640]{1,0:T(8,128)(2,1)S(1)} %collective-permute-done.4.refs_2_.refs_21_) | copy-start | bytes 737284
  83.5 3.2 %collective-permute-start.10 = (bf16[768,768]{1,0:T(8,128)(2,1)}, bf16[768,768]{1,0:T(8,128)(2,1)}, u32[]{:S(2)}, u32[]{:S(2)}) collective-permute-start(bf16[768,768]{1,0:T(8,128)(2,1)} %collective-permute-done.8.refs_5_.refs_11_.refs_12_), channel_id=1, source_target_pairs={{0,1},{1,0},{2,3},{3,2},{4,5},{5,4},{6,7},{7,6},{8,9},{9,8},{10,11... | collective-permute-start | bytes 3538952 | tf_op jit(solution)/shard_map/ppermute | solution.py:1207
  83.6 43.7 %collective-permute-start.13 = (bf16[640,768]{1,0:T(8,128)(2,1)}, bf16[640,768]{1,0:T(8,128)(2,1)}, u32[]{:S(2)}, u32[]{:S(2)}) collective-permute-start(bf16[640,768]{1,0:T(8,128)(2,1)} %get-tuple-element.91.refs_0_.refs_2_), channel_id=1, source_target_pairs={{0,2},{1,3},{2,0},{3,1},{4,6},{5,7},{6,4},{7,5},{8,10},{9,11},{10,... | collective-permute-start | bytes 2949128 | tf_op jit(solution)/shard_map/ppermute | solution.py:1207
  105.9 24.2 %collective-permute-start.14 = (bf16[640,768]{1,0:T(8,128)(2,1)}, bf16[640,768]{1,0:T(8,128)(2,1)}, u32[]{:S(2)}, u32[]{:S(2)}) collective-permute-start(bf16[640,768]{1,0:T(8,128)(2,1)} %get-tuple-element.97.refs_0_.refs_3_), channel_id=1, source_target_pairs={{0,2},{1,3},{2,0},{3,1},{4,6},{5,7},{6,4},{7,5},{8,10},{9,11},{10,... | collective-permute-start | bytes 2949128 | tf_op jit(solution)/shard_map/ppermute | solution.py:1207
  106.7 18.4 %copy-start.47 = (f32[8,768]{1,0:T(8,128)S(1)}, f32[8,768]{1,0:T(8,128)}, u32[]{:S(2)}) copy-start(f32[8,768]{1,0:T(8,128)} %get-tuple-element.108) | copy-start | bytes 73732
  124.3 6.3 %copy-start = (bf16[768,768]{1,0:T(8,128)(2,1)S(1)}, bf16[768,768]{1,0:T(8,128)(2,1)}, u32[]{:S(2)}) copy-start(bf16[768,768]{1,0:T(8,128)(2,1)} %get-tuple-element.106) | copy-start | bytes 3538948
  126.6 3.4 %collective-permute-start.17 = (bf16[512,768]{1,0:T(8,128)(2,1)S(1)}, bf16[512,768]{1,0:T(8,128)(2,1)S(1)}, u32[]{:S(2)}, u32[]{:S(2)}) collective-permute-start(bf16[512,768]{1,0:T(8,128)(2,1)S(1)} %broadcast_select_fusion.2), channel_id=1, source_target_pairs={{0,1},{1,0},{2,3},{3,2},{4,5},{5,4},{6,7},{7,6},{8,9},{9,8},{10,11... | collective-permute-start | bytes 2359304 | tf_op jit(solution)/shard_map/ppermute | solution.py:1207
  126.7 4.3 %collective-permute-start.11 = (bf16[640,768]{1,0:T(8,128)(2,1)}, bf16[640,768]{1,0:T(8,128)(2,1)}, u32[]{:S(2)}, u32[]{:S(2)}) collective-permute-start(bf16[640,768]{1,0:T(8,128)(2,1)} %get-tuple-element.91.refs_0_.refs_2_), channel_id=1, source_target_pairs={{0,1},{1,0},{2,3},{3,2},{4,5},{5,4},{6,7},{7,6},{8,9},{9,8},{10,11... | collective-permute-start | bytes 2949128 | tf_op jit(solution)/shard_map/ppermute | solution.py:1207
  127.2 7.4 %collective-permute-start.12 = (bf16[640,768]{1,0:T(8,128)(2,1)}, bf16[640,768]{1,0:T(8,128)(2,1)}, u32[]{:S(2)}, u32[]{:S(2)}) collective-permute-start(bf16[640,768]{1,0:T(8,128)(2,1)} %get-tuple-element.97.refs_0_.refs_3_), channel_id=1, source_target_pairs={{0,1},{1,0},{2,3},{3,2},{4,5},{5,4},{6,7},{7,6},{8,9},{9,8},{10,11... | collective-permute-start | bytes 2949128 | tf_op jit(solution)/shard_map/ppermute | solution.py:1207
  127.3 6.3 %collective-permute-start.15 = (bf16[640,768]{1,0:T(8,128)(2,1)}, bf16[640,768]{1,0:T(8,128)(2,1)}, u32[]{:S(2)}, u32[]{:S(2)}) collective-permute-start(bf16[640,768]{1,0:T(8,128)(2,1)} %collective-permute-done.13.refs_6_), channel_id=1, source_target_pairs={{0,1},{1,0},{2,3},{3,2},{4,5},{5,4},{6,7},{7,6},{8,9},{9,8},{10,11... | collective-permute-start | bytes 2949128 | tf_op jit(solution)/shard_map/ppermute | solution.py:1207
  130.1 5.3 %collective-permute-start.16 = (bf16[640,768]{1,0:T(8,128)(2,1)}, bf16[640,768]{1,0:T(8,128)(2,1)}, u32[]{:S(2)}, u32[]{:S(2)}) collective-permute-start(bf16[640,768]{1,0:T(8,128)(2,1)} %collective-permute-done.14.refs_7_), channel_id=1, source_target_pairs={{0,1},{1,0},{2,3},{3,2},{4,5},{5,4},{6,7},{7,6},{8,9},{9,8},{10,11... | collective-permute-start | bytes 2949128 | tf_op jit(solution)/shard_map/ppermute | solution.py:1207
  130.1 33.8 %collective-permute-start.19 = (bf16[192,640]{1,0:T(8,128)(2,1)}, bf16[192,640]{1,0:T(8,128)(2,1)}, u32[]{:S(2)}, u32[]{:S(2)}) collective-permute-start(bf16[192,640]{1,0:T(8,128)(2,1)} %get-tuple-element.113), channel_id=1, source_target_pairs={{0,1},{1,0},{2,3},{3,2},{4,5},{5,4},{6,7},{7,6},{8,9},{9,8},{10,11... | collective-permute-start | bytes 737288 | tf_op jit(solution)/shard_map/ppermute | solution.py:1207
  131.0 32.9 %collective-permute-start.20 = (bf16[192,640]{1,0:T(8,128)(2,1)}, bf16[192,640]{1,0:T(8,128)(2,1)}, u32[]{:S(2)}, u32[]{:S(2)}) collective-permute-start(bf16[192,640]{1,0:T(8,128)(2,1)} %get-tuple-element.114), channel_id=1, source_target_pairs={{0,2},{1,3},{2,0},{3,1},{4,6},{5,7},{6,4},{7,5},{8,10},{9,11},{10,... | collective-permute-start | bytes 737288 | tf_op jit(solution)/shard_map/ppermute | solution.py:1207
  133.5 30.3 %collective-permute-start.21 = (bf16[192,640]{1,0:T(8,128)(2,1)}, bf16[192,640]{1,0:T(8,128)(2,1)}, u32[]{:S(2)}, u32[]{:S(2)}) collective-permute-start(bf16[192,640]{1,0:T(8,128)(2,1)} %get-tuple-element.115), channel_id=1, source_target_pairs={{0,3},{1,2},{2,1},{3,0},{4,7},{5,6},{6,5},{7,4},{8,11},{9,10},{10,... | collective-permute-start | bytes 737288 | tf_op jit(solution)/shard_map/ppermute | solution.py:1207
  134.6 24.5 %collective-permute-start.18 = (bf16[256,768]{1,0:T(8,128)(2,1)S(1)}, bf16[256,768]{1,0:T(8,128)(2,1)S(1)}, u32[]{:S(2)}, u32[]{:S(2)}) collective-permute-start(bf16[256,768]{1,0:T(8,128)(2,1)S(1)} %broadcast_select_fusion.13), channel_id=1, source_target_pairs={{0,2},{1,3},{2,0},{3,1},{4,6},{5,7},{6,4},{7,5},{8,10},{9,11},{10,... | collective-permute-start | bytes 1179656 | tf_op jit(solution)/shard_map/ppermute | solution.py:1207
  159.3 2.8 copy-start.7
  160.6 22.5 %collective-permute-start.23 = (bf16[448,768]{1,0:T(8,128)(2,1)S(1)}, bf16[448,768]{1,0:T(8,128)(2,1)S(1)}, u32[]{:S(2)}, u32[]{:S(2)}) collective-permute-start(bf16[448,768]{1,0:T(8,128)(2,1)S(1)} %bitcast.82), channel_id=1, source_target_pairs={{0,8},{4,12},{8,0},{12,4},{16,24},{20,28},{24,16},{28,20},{1,9},{5... | collective-permute-start | bytes 2064392 | tf_op jit(solution)/shard_map/ppermute | solution.py:1207
  162.3 21.1 %collective-permute-start.22 = (bf16[448,768]{1,0:T(8,128)(2,1)S(1)}, bf16[448,768]{1,0:T(8,128)(2,1)S(1)}, u32[]{:S(2)}, u32[]{:S(2)}) collective-permute-start(bf16[448,768]{1,0:T(8,128)(2,1)S(1)} %bitcast.83), channel_id=1, source_target_pairs={{0,4},{4,0},{8,12},{12,8},{16,20},{20,16},{24,28},{28,24},{1,5},{5... | collective-permute-start | bytes 2064392 | tf_op jit(solution)/shard_map/ppermute | solution.py:1207
  183.7 12.6 %collective-permute-start.24 = (bf16[224,768]{1,0:T(8,128)(2,1)S(1)}, bf16[224,768]{1,0:T(8,128)(2,1)S(1)}, u32[]{:S(2)}, u32[]{:S(2)}) collective-permute-start(bf16[224,768]{1,0:T(8,128)(2,1)S(1)} %broadcast_select_fusion.22), channel_id=1, source_target_pairs={{0,8},{4,12},{8,0},{12,4},{16,24},{20,28},{24,16},{28,20},{1,9},{5... | collective-permute-start | bytes 1032200 | tf_op jit(solution)/shard_map/ppermute | solution.py:1207
  184.2 12.2 %collective-permute-start.25 = (bf16[224,768]{1,0:T(8,128)(2,1)S(1)}, bf16[224,768]{1,0:T(8,128)(2,1)S(1)}, u32[]{:S(2)}, u32[]{:S(2)}) collective-permute-start(bf16[224,768]{1,0:T(8,128)(2,1)S(1)} %broadcast_select_fusion.19), channel_id=1, source_target_pairs={{0,4},{4,0},{8,12},{12,8},{16,20},{20,16},{24,28},{28,24},{1,5},{5... | collective-permute-start | bytes 1032200 | tf_op jit(solution)/shard_map/ppermute | solution.py:1207
  196.6 18.3 %collective-permute-start.28 = (bf16[224,768]{1,0:T(8,128)(2,1)S(1)}, bf16[224,768]{1,0:T(8,128)(2,1)S(1)}, u32[]{:S(2)}, u32[]{:S(2)}) collective-permute-start(bf16[224,768]{1,0:T(8,128)(2,1)S(1)} %bitcast.84), channel_id=1, source_target_pairs={{0,16},{4,20},{8,24},{12,28},{16,0},{20,4},{24,8},{28,12},{1,17},{... | collective-permute-start | bytes 1032200 | tf_op jit(solution)/shard_map/ppermute | solution.py:1207
  214.3 2.6 copy-start.4
  214.3 5.3 %copy-start.10 = (bf16[640,768]{1,0:T(8,128)(2,1)S(1)}, bf16[640,768]{1,0:T(8,128)(2,1)}, u32[]{:S(2)}) copy-start(bf16[640,768]{1,0:T(8,128)(2,1)} %get-tuple-element.140) | copy-start | bytes 2949124
  214.3 5.3 %collective-permute-start.27 = (bf16[640,768]{1,0:T(8,128)(2,1)}, bf16[640,768]{1,0:T(8,128)(2,1)S(1)}, u32[]{:S(2)}, u32[]{:S(2)}) collective-permute-start(bf16[640,768]{1,0:T(8,128)(2,1)} %get-tuple-element.141), channel_id=1, source_target_pairs={{0,1},{1,0},{2,3},{3,2},{4,5},{5,4},{6,7},{7,6},{8,9},{9,8},{10,11... | collective-permute-start | bytes 2949128 | tf_op jit(solution)/shard_map/ppermute | solution.py:1207
  214.4 43.0 %collective-permute-start.26 = (bf16[640,768]{1,0:T(8,128)(2,1)}, bf16[640,768]{1,0:T(8,128)(2,1)S(1)}, u32[]{:S(2)}, u32[]{:S(2)}) collective-permute-start(bf16[640,768]{1,0:T(8,128)(2,1)} %get-tuple-element.139), channel_id=1, source_target_pairs={{0,1},{1,0},{2,3},{3,2},{4,5},{5,4},{6,7},{7,6},{8,9},{9,8},{10,11... | collective-permute-start | bytes 2949128 | tf_op jit(solution)/shard_map/ppermute | solution.py:1207
  215.3 7.5 %collective-permute-start.30 = (bf16[152,768]{1,0:T(8,128)(2,1)S(1)}, bf16[152,768]{1,0:T(8,128)(2,1)S(1)}, u32[]{:S(2)}, u32[]{:S(2)}) collective-permute-start(bf16[152,768]{1,0:T(8,128)(2,1)S(1)} %broadcast_select_fusion.28), channel_id=1, source_target_pairs={{0,4},{4,0},{8,12},{12,8},{16,20},{20,16},{24,28},{28,24},{1,5},{5... | collective-permute-start | bytes 700424 | tf_op jit(solution)/shard_map/ppermute | solution.py:1207
  217.0 10.5 %collective-permute-start.32 = (bf16[152,768]{1,0:T(8,128)(2,1)S(1)}, bf16[152,768]{1,0:T(8,128)(2,1)S(1)}, u32[]{:S(2)}, u32[]{:S(2)}) collective-permute-start(bf16[152,768]{1,0:T(8,128)(2,1)S(1)} %broadcast_select_fusion.25), channel_id=1, source_target_pairs={{0,8},{4,12},{8,0},{12,4},{16,24},{20,28},{24,16},{28,20},{1,9},{5... | collective-permute-start | bytes 700424 | tf_op jit(solution)/shard_map/ppermute | solution.py:1207
  218.6 17.6 %collective-permute-start.35 = (bf16[224,768]{1,0:T(8,128)(2,1)S(1)}, bf16[224,768]{1,0:T(8,128)(2,1)S(1)}, u32[]{:S(2)}, u32[]{:S(2)}) collective-permute-start(bf16[224,768]{1,0:T(8,128)(2,1)S(1)} %bitcast.85), channel_id=1, source_target_pairs={{0,16},{4,20},{8,24},{12,28},{16,0},{20,4},{24,8},{28,12},{1,17},{... | collective-permute-start | bytes 1032200 | tf_op jit(solution)/shard_map/ppermute | solution.py:1207
  220.8 30.8 %collective-permute-start.29 = (bf16[640,768]{1,0:T(8,128)(2,1)}, bf16[640,768]{1,0:T(8,128)(2,1)S(1)}, u32[]{:S(2)}, u32[]{:S(2)}) collective-permute-start(bf16[640,768]{1,0:T(8,128)(2,1)} %add_convert_fusion), channel_id=1, source_target_pairs={{0,2},{1,3},{2,0},{3,1},{4,6},{5,7},{6,4},{7,5},{8,10},{9,11},{10,... | collective-permute-start | bytes 2949128 | tf_op jit(solution)/shard_map/ppermute | solution.py:1207
  227.6 9.5 %collective-permute-start.31 = (bf16[76,768]{1,0:T(8,128)(2,1)S(1)}, bf16[76,768]{1,0:T(8,128)(2,1)S(1)}, u32[]{:S(2)}, u32[]{:S(2)}) collective-permute-start(bf16[76,768]{1,0:T(8,128)(2,1)S(1)} %broadcast_select_fusion.34), channel_id=1, source_target_pairs={{0,8},{4,12},{8,0},{12,4},{16,24},{20,28},{24,16},{28,20},{1,9},{5... | collective-permute-start | bytes 350216 | tf_op jit(solution)/shard_map/ppermute | solution.py:1207
  227.8 9.4 %collective-permute-start.33 = (bf16[76,768]{1,0:T(8,128)(2,1)S(1)}, bf16[76,768]{1,0:T(8,128)(2,1)S(1)}, u32[]{:S(2)}, u32[]{:S(2)}) collective-permute-start(bf16[76,768]{1,0:T(8,128)(2,1)S(1)} %broadcast_select_fusion.31), channel_id=1, source_target_pairs={{0,4},{4,0},{8,12},{12,8},{16,20},{20,16},{24,28},{28,24},{1,5},{5... | collective-permute-start | bytes 350216 | tf_op jit(solution)/shard_map/ppermute | solution.py:1207
  236.5 8.4 %collective-permute-start.37 = (bf16[224,768]{1,0:T(8,128)(2,1)S(1)}, bf16[224,768]{1,0:T(8,128)(2,1)}, u32[]{:S(2)}, u32[]{:S(2)}) collective-permute-start(bf16[224,768]{1,0:T(8,128)(2,1)S(1)} %get-tuple-element.215), channel_id=1, source_target_pairs={{0,4},{4,0},{8,12},{12,8},{16,20},{20,16},{24,28},{28,24},{1,5},{5... | collective-permute-start | bytes 1032200 | tf_op jit(solution)/shard_map/ppermute | solution.py:1207
  237.1 14.5 %collective-permute-start.36 = (bf16[224,768]{1,0:T(8,128)(2,1)S(1)}, bf16[224,768]{1,0:T(8,128)(2,1)}, u32[]{:S(2)}, u32[]{:S(2)}) collective-permute-start(bf16[224,768]{1,0:T(8,128)(2,1)S(1)} %get-tuple-element.216), channel_id=1, source_target_pairs={{0,8},{4,12},{8,0},{12,4},{16,24},{20,28},{24,16},{28,20},{1,9},{5... | collective-permute-start | bytes 1032200 | tf_op jit(solution)/shard_map/ppermute | solution.py:1207
  237.4 13.3 %collective-permute-start.34 = (bf16[152,768]{1,0:T(8,128)(2,1)S(1)}, bf16[152,768]{1,0:T(8,128)(2,1)}, u32[]{:S(2)}, u32[]{:S(2)}) collective-permute-start(bf16[152,768]{1,0:T(8,128)(2,1)S(1)} %reshape.563), channel_id=1, source_target_pairs={{0,16},{4,20},{8,24},{12,28},{16,0},{20,4},{24,8},{28,12},{1,17},{... | collective-permute-start | bytes 700424 | tf_op jit(solution)/shard_map/ppermute | solution.py:1207
  246.1 27.8 %collective-permute-start.43 = (bf16[384,768]{1,0:T(8,128)(2,1)S(1)}, bf16[384,768]{1,0:T(8,128)(2,1)}, u32[]{:S(2)}, u32[]{:S(2)}) collective-permute-start(bf16[384,768]{1,0:T(8,128)(2,1)S(1)} %bitcast.72), channel_id=1, source_target_pairs={{0,8},{4,12},{8,0},{12,4},{16,24},{20,28},{24,16},{28,20},{1,9},{5... | collective-permute-start | bytes 1769480 | tf_op jit(solution)/shard_map/ppermute | solution.py:1207
  252.7 4.7 %copy-start.3 = (f32[640,768]{1,0:T(8,128)S(1)}, f32[640,768]{1,0:T(8,128)}, u32[]{:S(2)}) copy-start(f32[640,768]{1,0:T(8,128)} %get-tuple-element.101) | copy-start | bytes 5898244
  252.7 4.7 %copy-start.9 = (bf16[640,768]{1,0:T(8,128)(2,1)S(1)}, bf16[640,768]{1,0:T(8,128)(2,1)}, u32[]{:S(2)}) copy-start(bf16[640,768]{1,0:T(8,128)(2,1)} %get-tuple-element.138) | copy-start | bytes 2949124
  252.8 27.2 %collective-permute-start.40 = (bf16[384,768]{1,0:T(8,128)(2,1)S(1)}, bf16[384,768]{1,0:T(8,128)(2,1)S(1)}, u32[]{:S(2)}, u32[]{:S(2)}) collective-permute-start(bf16[384,768]{1,0:T(8,128)(2,1)S(1)} %bitcast.73), channel_id=1, source_target_pairs={{0,4},{4,0},{8,12},{12,8},{16,20},{20,16},{24,28},{28,24},{1,5},{5... | collective-permute-start | bytes 1769480 | tf_op jit(solution)/shard_map/ppermute | solution.py:1207
  254.5 15.6 %collective-permute-start.41 = (bf16[140,768]{1,0:T(8,128)(2,1)S(1)}, bf16[140,768]{1,0:T(8,128)(2,1)S(1)}, u32[]{:S(2)}, u32[]{:S(2)}) collective-permute-start(bf16[140,768]{1,0:T(8,128)(2,1)S(1)} %pad_maximum_fusion.18), channel_id=1, source_target_pairs={{0,4},{4,0},{8,12},{12,8},{16,20},{20,16},{24,28},{28,24},{1,5},{5... | collective-permute-start | bytes 645128 | tf_op jit(solution)/shard_map/ppermute | solution.py:1207
  255.1 15.1 %collective-permute-start.38 = (bf16[140,768]{1,0:T(8,128)(2,1)S(1)}, bf16[140,768]{1,0:T(8,128)(2,1)S(1)}, u32[]{:S(2)}, u32[]{:S(2)}) collective-permute-start(bf16[140,768]{1,0:T(8,128)(2,1)S(1)} %pad_maximum_fusion.17), channel_id=1, source_target_pairs={{0,8},{4,12},{8,0},{12,4},{16,24},{20,28},{24,16},{28,20},{1,9},{5... | collective-permute-start | bytes 645128 | tf_op jit(solution)/shard_map/ppermute | solution.py:1207
  270.3 11.4 %collective-permute-start.44 = (bf16[256,768]{1,0:T(8,128)(2,1)S(1)}, bf16[256,768]{1,0:T(8,128)(2,1)S(1)}, u32[]{:S(2)}, u32[]{:S(2)}) collective-permute-start(bf16[256,768]{1,0:T(8,128)(2,1)S(1)} %pad_maximum_fusion.11), channel_id=1, source_target_pairs={{0,2},{1,3},{2,0},{3,1},{4,6},{5,7},{6,4},{7,5},{8,10},{9,11},{10,... | collective-permute-start | bytes 1179656 | tf_op jit(solution)/shard_map/ppermute | solution.py:1207
  272.2 9.5 %collective-permute-start.39 = (bf16[152,768]{1,0:T(8,128)(2,1)S(1)}, bf16[152,768]{1,0:T(8,128)(2,1)S(1)}, u32[]{:S(2)}, u32[]{:S(2)}) collective-permute-start(bf16[152,768]{1,0:T(8,128)(2,1)S(1)} %pad_maximum_fusion.15), channel_id=1, source_target_pairs={{0,4},{4,0},{8,12},{12,8},{16,20},{20,16},{24,28},{28,24},{1,5},{5... | collective-permute-start | bytes 700424 | tf_op jit(solution)/shard_map/ppermute | solution.py:1207
  273.9 6.1 %collective-permute-start.42 = (bf16[152,768]{1,0:T(8,128)(2,1)S(1)}, bf16[152,768]{1,0:T(8,128)(2,1)S(1)}, u32[]{:S(2)}, u32[]{:S(2)}) collective-permute-start(bf16[152,768]{1,0:T(8,128)(2,1)S(1)} %pad_maximum_fusion.16), channel_id=1, source_target_pairs={{0,8},{4,12},{8,0},{12,4},{16,24},{20,28},{24,16},{28,20},{1,9},{5... | collective-permute-start | bytes 700424 | tf_op jit(solution)/shard_map/ppermute | solution.py:1207
  281.9 2.4 collective-permute-start.45
  (41 other events, 78.3 us)

commit v5 on v4

--- a/solution.py
+++ b/solution.py
@@ -960,7 +960,6 @@
 
 
 ROWS = 320
-UNITS = 768
 PART = 768
 
 
@@ -980,37 +979,47 @@
     normed_out[...] = (unit * norms[0:1, :] + norms[1:2, :]).astype(BF16)
 
 
+def feed_first_kernel(io, scalars, hidden):
+    count = len(io.outputs) - 1
+    normed_low, ups, downs = io.inputs[0], io.inputs[1 : 1 + count], io.inputs[1 + count :]
+    slopes, partial = io.outputs[:count], io.outputs[count]
+    block = normed_low.shape[0]
+    units = ups[0].shape[0]
+    io.need(0)
+    for s, up in enumerate(ups):
+        io.need(1 + s)
+        value, derivative = gelu_and_slope(dot_nt(normed_low[...], up[...]))
+        hidden[:, s * units : (s + 1) * units] = value.astype(BF16)
+        slopes[s][...] = derivative.astype(BF16)
+        io.send(s)
+    io.need(*range(1 + count, 1 + 2 * count))
+
+    @pl.loop(0, block // ROWS)
+    def _(i):
+        rows = row_block(i, ROWS)
+        total = dot_nn(hidden[rows, :units], downs[0][...])
+        for s in range(1, count):
+            total += dot_nn(hidden[rows, s * units : (s + 1) * units], downs[s][...])
+        partial[rows, :] = total
+
+
 def feed_kernel(io, scalars, hidden):
-    normed_low, norms = io.inputs[:2]
-    ups, downs = io.inputs[2:6], io.inputs[6:10]
-    unit_one, grad_output = io.inputs[10:]
+    normed_low, up, down, partial, unit_one, norms, grad_output = io.inputs
     output, slope, summed_grad, branch_grad, norm_grads = io.outputs
-    block, features = normed_low.shape
-    units = ups[0].shape[0]
+    block = normed_low.shape[0]
     norm_grads[...] = jnp.zeros_like(norm_grads)
     io.need(0, 1)
-
-    for s, up in enumerate(ups):
-        io.need(2 + s)
-
-        @pl.loop(0, units // UNITS)
-        def _(j):
-            target = lane_slice(s * units + j * UNITS, UNITS)
-            value, derivative = gelu_and_slope(
-                dot_nt(normed_low[...], up[row_block(j, UNITS), :])
-            )
-            hidden[:, target] = value.astype(BF16)
-            slope[:, target] = derivative.astype(BF16)
-
+    value, derivative = gelu_and_slope(dot_nt(normed_low[...], up[...]))
+    hidden[...] = value.astype(BF16)
+    slope[...] = derivative.astype(BF16)
     io.send(1)
-    io.need(*range(6, 12))
+    io.need(2, 3, 4, 5, 6)
 
     @pl.loop(0, block // ROWS)
     def _(i):
         rows = row_block(i, ROWS)
         total = unit_one[rows, :] * norms[0:1, :] + norms[1:2, :]
-        for s, down in enumerate(downs):
-            total += dot_nn(hidden[rows, s * units : (s + 1) * units], down[...])
+        total += partial[rows, :] + dot_nn(hidden[rows, :], down[...])
         unit, recip = unit_norm(total)
         output[rows, :] = unit * norms[2:3, :] + norms[3:4, :]
         top = grad_output[rows, :].astype(F32)
@@ -1023,28 +1032,24 @@
 
 def feed_back_kernel(io, scalars, grad_pre, attended_grad):
     branch_grad, norms = io.inputs[:2]
-    downs, slope = io.inputs[2:6], io.inputs[6]
-    ups = io.inputs[7:11]
-    summed_grad, unit_one, recip_one, w_out = io.inputs[11:15]
-    contexts = io.inputs[15:19]
+    downs, slopes = io.inputs[2:10:2], io.inputs[3:10:2]
+    ups = io.inputs[10:14]
+    summed_grad, unit_one, recip_one, w_out = io.inputs[14:18]
+    contexts = io.inputs[18:22]
     resid_grad, grad_w_out, norm_grads = io.outputs[:3]
     targets = io.outputs[3:]
     me = scalars[3]
     width, block = contexts[0].shape
     units = ups[0].shape[0]
     norm_grads[...] = jnp.zeros_like(norm_grads)
-    io.need(0, 1, 2, 6)
-
-    for s, down in enumerate(downs):
-        io.need(2 + s)
-
-        @pl.loop(0, units // UNITS)
-        def _(j):
-            target = lane_slice(s * units + j * UNITS, UNITS)
-            grad = dot_nt(branch_grad[...], down[row_block(j, UNITS), :])
-            grad_pre[:, target] = (slope[:, target] * grad).astype(BF16)
-
-    io.need(*range(7, 19))
+    io.need(0, 1)
+
+    for s, (down, slope) in enumerate(zip(downs, slopes, strict=True)):
+        io.need(2 + 2 * s, 3 + 2 * s)
+        grad = dot_nt(branch_grad[...], down[...])
+        grad_pre[:, s * units : (s + 1) * units] = (slope[...].astype(F32) * grad).astype(BF16)
+
+    io.need(*range(10, 22))
 
     @pl.loop(0, block // ROWS)
     def _(i):
@@ -1085,28 +1090,45 @@
     )
 
 
-def feed(scalars, normed_low, unit_one, grad_output, norms, ups, downs):
+def feed_first(scalars, normed_low, ups, downs):
     block, features = normed_low.shape
     units = ups[0].shape[0]
+    return local_call(
+        feed_first_kernel,
+        "feed_first",
+        scalars,
+        (normed_low, *ups, *downs),
+        (
+            *[shape_of(BF16, block, units) for _ in ups],
+            shape_of(F32, block, features),
+        ),
+        [pltpu.VMEM((block, len(ups) * units), BF16)],
+        15,
+    )
+
+
+def feed(scalars, normed_low, up, down, partial, unit_one, norms, grad_output):
+    block, features = normed_low.shape
+    units = up.shape[0]
     return local_call(
         feed_kernel,
         "feed",
         scalars,
-        (normed_low, norms, *ups, *downs, unit_one, grad_output),
+        (normed_low, up, down, partial, unit_one, norms, grad_output),
         (
             shape_of(F32, block, features),
-            shape_of(BF16, block, 4 * units),
+            shape_of(BF16, block, units),
             shape_of(F32, block, features),
             shape_of(BF16, block, features),
             shape_of(F32, 8, features),
         ),
-        [pltpu.VMEM((block, 4 * units), BF16)],
-        22,
+        [pltpu.VMEM((block, units), BF16)],
+        8,
     )
 
 
 def feed_back(scalars, fed, unit_one, recip_one, contexts, w_out, norms, ups, downs):
-    slope, summed_grad, branch_grad = fed
+    slopes, summed_grad, branch_grad = fed
     width, block = contexts[0].shape
     features = w_out.shape[0]
     units = ups[0].shape[0]
@@ -1117,8 +1139,7 @@
         (
             branch_grad,
             norms,
-            *downs,
-            slope,
+            *[a for pair in zip(downs, slopes, strict=True) for a in pair],
             *ups,
             summed_grad,
             unit_one,
@@ -1320,32 +1341,37 @@
         across = after(across, attended[1])
         on = to_partner(across, "dp", dp_size, 1)
         normed_low, unit_one, recip_one = norm_in(scalars, contexts, tokens, w_out, norms)
-        normed_two = to_partner(normed_low, "tensor", 4, 2)
-        on = after(on, normed_low)
+        row_half = tokens.shape[0] // 2
+        normed_a = to_partner(normed_low[:row_half], "tensor", 4, 2)
+        normed_b = to_partner(normed_low[row_half:], "tensor", 4, 2)
 
         def core_hop(array):
             return to_partner(array, "tensor", 4, 1)
 
-        across_one, on_one = core_hop(across), core_hop(on)
-        ups, downs = [
-            (
-                Joined((weights, which * units, units)),
-                Joined((weights_one, which * units, units)),
-                Joined(*[(a, which * half_units, half_units) for a in (across, on)]),
-                Joined(*[(a, which * half_units, half_units) for a in (across_one, on_one)]),
-            )
-            for which in (0, 1)
-        ]
+        across_one = core_hop(across)
+
+        def shards_of(which, pieces):
+            return [
+                Joined(*[(a, which * rows, rows) for a in group]) for group, rows in pieces
+            ]
+
+        here = [((weights,), units), ((weights_one,), units), ((across, across_one), half_units)]
+        ups, downs = shards_of(0, here), shards_of(1, here)
+        *slopes, partial = feed_first(scalars, normed_low, ups, downs)
+        on = after(on, partial, normed_a)
+        late = [((on, core_hop(on)), half_units)]
+        ups, downs = ups + shards_of(0, late), downs + shards_of(1, late)
         output, slope, summed_grad, branch_grad, norm_grads_two = feed(
-            scalars, normed_low, unit_one, grad_output, norms, ups, downs
+            scalars, normed_low, ups[3], downs[3], partial, unit_one, norms, grad_output
         )
+        normed_b = after(normed_b, branch_grad)
         branch_two = to_partner(branch_grad, "tensor", 4, 2)
         branch_one = core_hop(branch_grad)
         normed_one = core_hop(normed_low)
         resid_grad, grad_w_out, norm_grads_one, *context_grads = feed_back(
             scalars,
-            (slope, summed_grad, branch_grad),
-            unit_one,
+            ([*slopes, slope], summed_grad, branch_grad),
+            after(unit_one, normed_b),
             recip_one,
             contexts,
             w_out,
@@ -1362,8 +1388,10 @@
             jnp.concatenate([grad_w_out, norm_rows.astype(BF16), spare], axis=0), "tensor", 1
         )
         small_got = core_hop(small_sent)
-        normed_two, branch_two = after(normed_two, resid_grad), after(branch_two, resid_grad)
-        normeds = (normed_low, normed_one, normed_two, core_hop(normed_two))
+        branch_two = after(branch_two, resid_grad)
+        normed_twos = [(a, 0, row_half) for a in (normed_a, normed_b)]
+        normed_threes = [(core_hop(a), 0, row_half) for a in (normed_a, normed_b)]
+        normeds = (normed_low, normed_one, Joined(*normed_twos), Joined(*normed_threes))
         branch_grads = (branch_grad, branch_one, branch_two, core_hop(branch_two))
         small = add(small_kept, after(small_got, branch_two))
         small_kept, small_sent = halve(small, "tensor", 2)

time: 290 us -> 296 us (1.021)
  waiting for transfers between devices: 64.8 us -> 55.9 us
  local copies, waits for them, and re-layouts: 11.9 us -> 18.7 us
  other arithmetic: 34.6 us -> 37.8 us
  Pallas kernels: 136 us -> 139 us
    ppermute x46 -> x48, waiting for transfers between devices: 64.8 us -> 55.9 us  [to_partner(): return lax.ppermute(array, axis, [(i, i ^ bit) for i in range(size)])]
    unnamed x119 -> x139, local copies, waits for them, and re-layouts: 3.4 us -> 9.01 us
    pallas_call x8 -> x9, Pallas kernels: 136 us -> 139 us  [local_call(): pl.pallas_call(body, name=name, out_shape=out_shape, in_specs=[pl.BlockSp...]
    ppermute x46 -> x48, starting transfers between devices: 37.2 us -> 39.1 us  [to_partner(): return lax.ppermute(array, axis, [(i, i ^ bit) for i in range(size)])]
  transfers between devices with their start and end apart: 46 -> 48, of which waited for: 17 -> 16; matrix products, arithmetic and copies ran while one was open for 14% -> 15% of each run, Pallas kernels for 48% -> 47%
where the time goes in v5:
time: 296 us; the launch traced here: 292 us
  Pallas kernels  139 us (47%)
  waiting for transfers between devices  55.9 us (19%)
  starting transfers between devices  39.1 us (13%)
  other arithmetic  37.8 us (13%)
  local copies, waits for them, and re-layouts  18.7 us (6%)
    pallas_call x9, Pallas kernels, local_call(): pl.pallas_call(body, name=name, out_shape=out_shape, in_specs=[pl.BlockSp...  139 us
    ppermute x48, waiting for transfers between devices, to_partner(): return lax.ppermute(array, axis, [(i, i ^ bit) for i in range(size)])  55.9 us
    ppermute x48, starting transfers between devices, to_partner(): return lax.ppermute(array, axis, [(i, i ^ bit) for i in range(size)])  39.1 us
    unnamed x139, local copies, waits for them, and re-layouts  9.01 us
    convert_element_type x1, other arithmetic, make_bands(): return band.astype(BF16)  6.76 us
  transfers between devices with their start and end apart: 48, of which 16 were waited for; matrix products, arithmetic and copies ran while one was open for 15% of the time, Pallas kernels for 47%

profile of v5, /device:TPU:0, one launch (start us, length us, event | category | flops | bytes accessed | tf_op | source)
XLA Modules:
  0.0 292.4 jit_solution(8220177620945169876)
XLA Ops:
  0.6 3.0 %collective-permute-start.1 = (bf16[640,768]{1,0:T(8,128)(2,1)}, bf16[640,768]{1,0:T(8,128)(2,1)}, u32[]{:S(2)}, u32[]{:S(2)}) collective-permute-start(bf16[640,768]{1,0:T(8,128)(2,1)} %refs_6_.1), channel_id=1, source_target_pairs={{0,2},{1,3},{2,0},{3,1},{4,6},{5,7},{6,4},{7,5},{8,10},{9,11},{10,... | collective-permute-start | bytes 2949128 | tf_op jit(solution)/shard_map/ppermute | solution.py:1228
  3.7 2.5 slice_reduce_fusion.36
  6.1 2.2 slice_reduce_fusion.35
  8.3 4.5 %fusion.40 = (pred[512,256]{1,0:T(8,128)(4,1)}, pred[512,256]{1,0:T(8,128)(4,1)}, pred[512,256]{1,0:T(8,128)(4,1)}, pred[512,256]{1,0:T(8,128)(4,1)}, pred[512,2...) fusion(s32[512]{0:T(512)S(1)} %iota_add_fusion), kind=kLoop, calls=%fused_computation.91 | loop fusion | flops 4587520 | bytes 4327424 | tf_op jit(solution)/shard_map/eq | solution.py:1249
  14.4 1.6 pad_maximum_fusion.refs_1_.refs_5_.refs_2_.refs_12_.refs_0_
  16.0 1.6 fusion.6
  18.1 1.0 pad_maximum_fusion.3.refs_0_.refs_5_
  20.3 6.8 %select_convert_fusion.refs_5_.refs_11_ = bf16[3,512,256]{2,1,0:T(8,128)(2,1)} fusion(bf16[3]{0:T(256)(128)(2,1)} %get-tuple-element.204, bf16[3]{0:T(256)(128)(2,1)} %get-tuple-element.205, bf16[3]{0:T(256)(128)(2,1)S(1)} %copy-done.53, bf16[3]{0:T(256)(128)(2,1)S(1)} %copy-done.54, bf16[3]{0:T(256)(128)(2,1)S(1)} %copy-done.55, ...), kind=kLoop, calls=%fused_computation.8 | loop fusion | flops 12976128 | bytes 5112006 | tf_op jit(solution)/shard_map/convert_element_type | solution.py:1250
  28.6 2.2 collective-permute-done.2.refs_4_.refs_9_
  30.7 24.0 %attend.1 = (bf16[576,2816]{1,0:T(8,128)(2,1)}, bf16[192,640]{1,0:T(8,128)(2,1)}, bf16[192,640]{1,0:T(8,128)(2,1)}, bf16[192,640]{1,0:T(8,128)(2,1)}, bf16[192,6...) custom-call(s32[4]{0:T(128)} %pad_add_fusion.scalar_ref, ...), custom_call_target="tpu_custom_call" | custom-call | flops 30000001024 | bytes 14358528 | tf_op jit(solution)/shard_map/attend/pallas_call | solution.py:240
  54.8 1.9 collective-permute-done.6.refs_3_.refs_7_.refs_6_.refs_14_
  57.5 1.1 collective-permute-start.5
  58.6 1.2 collective-permute-done.3.refs_1_.refs_23_
  59.7 1.5 collective-permute-start.7
  61.3 5.0 %collective-permute-done.4.refs_2_.refs_24_ = bf16[192,640]{1,0:T(8,128)(2,1)S(1)} collective-permute-done((bf16[192,640]{1,0:T(8,128)(2,1)}, bf16[192,640]{1,0:T(8,128)(2,1)S(1)}, u32[]{:S(2)}, u32[]{:S(2)}) %collective-permute-start.4) | collective-permute-done | bytes 245792 | tf_op jit(solution)/shard_map/ppermute | solution.py:1228
  66.2 3.3 %collective-permute-done.5.refs_3_.refs_25_ = bf16[192,640]{1,0:T(8,128)(2,1)S(1)} collective-permute-done((bf16[192,640]{1,0:T(8,128)(2,1)}, bf16[192,640]{1,0:T(8,128)(2,1)S(1)}, u32[]{:S(2)}, u32[]{:S(2)}) %collective-permute-start.5) | collective-permute-done | bytes 245792 | tf_op jit(solution)/shard_map/ppermute | solution.py:1228
  70.3 6.3 %norm_in.1 = (bf16[640,768]{1,0:T(8,128)(2,1)}, f32[640,768]{1,0:T(8,128)}, f32[640,128]{1,0:T(8,128)}) custom-call(s32[4]{0:T(128)} %pad_add_fusion.scalar_ref, bf16[192,640]{1,0:T(8,128)(2,1)} %get-tuple-element.92.refs_0_.refs_22_, bf16[192,640]{1,0:T(8,128)(2,1)} %copy-done.63, bf16[192,640]{1,0:T(8,128)(2,1)} %copy-done.64, ...), custom_call_target="tpu_custom_call" | custom-call | flops 6000000000 | bytes 6434816 | tf_op jit(solution)/shard_map/norm_in/pallas_call | solution.py:240
  76.6 1.2 fusion.49
  78.5 1.4 copy-done.56
  79.9 13.6 %feed_first.1 = (bf16[640,768]{1,0:T(8,128)(2,1)}, bf16[640,768]{1,0:T(8,128)(2,1)}, bf16[640,768]{1,0:T(8,128)(2,1)}, f32[640,768]{1,0:T(8,128)}) custom-call(s32[4]{0:T(128)} %pad_add_fusion.scalar_ref, bf16[640,768]{1,0:T(8,128)(2,1)} %get-tuple-element.96.refs_0_.refs_2_, bf16[1536,768]{1,0:T(8,128)(2,1)} %pad_maximum_fusion.refs_1_.refs_5_.refs_2_.refs_12_.refs_0_, ...), custom_call_target="tpu_custom_call" | custom-call | flops 15000000512 | bytes 20054016 | tf_op jit(solution)/shard_map/feed_first/pallas_call | solution.py:240
  95.0 1.7 collective-permute-start.12
  97.6 1.0 copy-done.57
  98.6 9.5 %feed.1 = (f32[640,768]{1,0:T(8,128)}, bf16[640,768]{1,0:T(8,128)(2,1)}, f32[640,768]{1,0:T(8,128)}, bf16[640,768]{1,0:T(8,128)(2,1)}, f32[8,768]{1,0:T(8,128)}) custom-call(s32[4]{0:T(128)} %pad_add_fusion.scalar_ref, bf16[640,768]{1,0:T(8,128)(2,1)} %get-tuple-element.96.refs_0_.refs_2_, ...), custom_call_target="tpu_custom_call" | custom-call | flops 8000000000 | bytes 16551936 | tf_op jit(solution)/shard_map/feed/pallas_call | solution.py:240
  108.1 1.8 collective-permute-start.15
  110.7 15.8 %feed_back.1 = (f32[640,768]{1,0:T(8,128)}, bf16[768,768]{1,0:T(8,128)(2,1)}, f32[8,768]{1,0:T(8,128)}, bf16[192,640]{1,0:T(8,128)(2,1)}, bf16[192,640]{1,0:T(8,...) custom-call(s32[4]{0:T(128)} %pad_add_fusion.scalar_ref, ...), custom_call_target="tpu_custom_call" | custom-call | flops 20000000000 | bytes 34377728 | tf_op jit(solution)/shard_map/feed_back/pallas_call | solution.py:240
  127.4 2.4 broadcast_select_fusion.2
  130.3 2.1 collective-permute-done.15.refs_8_
  133.9 1.5 add_convert_fusion.1
  135.5 0.9 collective-permute-done.16.refs_9_
  136.5 1.7 collective-permute-start.22
  138.3 1.4 collective-permute-start.20
  139.7 23.7 %feed_weights.1 = (bf16[768,768]{1,0:T(8,128)(2,1)}, bf16[768,768]{1,0:T(8,128)(2,1)}) custom-call(s32[4]{0:T(128)} %pad_add_fusion.scalar_ref, bf16[1536,768]{1,0:T(8,128)(2,1)} %pad_maximum_fusion.refs_1_.refs_5_.refs_2_.refs_12_.refs_0_, bf16[1536,768]{1,0:T(8,128)(2,1)} %pad_maximum_fusion.refs_1_.refs_5_.refs_2_.refs_12_.refs_0_, ...), custom_call_target="tpu_custom_call" | custom-call | flops 24999999488 | bytes 14942208 | tf_op jit(solution)/shard_map/feed_weights/pallas_call | solution.py:240
  163.7 1.0 copy-done.7
  165.0 1.7 collective-permute-start.25
  167.0 1.6 collective-permute-start.24
  169.4 19.2 %attend_back.1 = (bf16[192,2560]{1,0:T(8,128)(2,1)}, f32[8,128]{1,0:T(8,128)}, f32[192,2560]{1,0:T(8,128)}, f32[192,2560]{1,0:T(8,128)}, f32[3,192,64]{2,1,0:T(8...) custom-call(s32[4]{0:T(128)} %pad_add_fusion.scalar_ref, bf16[192,640]{1,0:T(8,128)(2,1)} %get-tuple-element.122.refs_0_, ...), custom_call_target="tpu_custom_call" | custom-call | flops 8000000000 | bytes 11216896 | tf_op jit(solution)/shard_map/attend_back/pallas_call | solution.py:240
  188.9 1.3 fusion.1
  191.1 11.4 %attend_steps.1.refs_4_ = bf16[2,9,64,64]{3,2,1,0:T(8,128)(2,1)} custom-call(s32[4]{0:T(128)} %pad_add_fusion.scalar_ref, f32[3,192,64]{2,1,0:T(8,128)} %get-tuple-element.140.refs_0_, f32[3,192,64]{2,1,0:T(8,128)} %get-tuple-element.129.refs_7_.refs_1_, f32[3,64,192]{2,1,0:T(8,128)} %get-tuple-element.141.refs_2_, ...), custom_call_target="tpu_custom_call" | custom-call | flops 5000000000 | bytes 4571136 | tf_op jit(solution)/shard_map/attend_steps/pallas_call | solution.py:240
  202.9 2.8 collective-permute-start.30
  205.6 15.2 %attend_grads.1 = (bf16[304,768]{1,0:T(8,128)(2,1)}, bf16[304,768]{1,0:T(8,128)(2,1)}, bf16[640,768]{1,0:T(8,128)(2,1)}, bf16[640,768]{1,0:T(8,128)(2,1)}, bf16[...) custom-call(s32[4]{0:T(128)} %pad_add_fusion.scalar_ref, bf16[192,2560]{1,0:T(8,128)(2,1)} %get-tuple-element.133.refs_0_, ...), custom_call_target="tpu_custom_call" | custom-call | flops 8000000000 | bytes 14749696 | tf_op jit(solution)/shard_map/attend_grads/pallas_call | solution.py:240
  221.9 1.6 collective-permute-start.32
  223.5 1.6 collective-permute-start.34
  225.2 1.2 collective-permute-start.37
  226.4 1.2 add_convert_fusion
  227.9 1.4 collective-permute-done.32
  229.5 4.8 %collective-permute-done.34 = bf16[152,768]{1,0:T(8,128)(2,1)S(1)} collective-permute-done((bf16[152,768]{1,0:T(8,128)(2,1)S(1)}, bf16[152,768]{1,0:T(8,128)(2,1)S(1)}, u32[]{:S(2)}, u32[]{:S(2)}) %collective-permute-start.34) | collective-permute-done | bytes 233504 | tf_op jit(solution)/shard_map/ppermute | solution.py:1228
  235.1 7.7 %collective-permute-done.37 = bf16[224,768]{1,0:T(8,128)(2,1)S(1)} collective-permute-done((bf16[224,768]{1,0:T(8,128)(2,1)S(1)}, bf16[224,768]{1,0:T(8,128)(2,1)S(1)}, u32[]{:S(2)}, u32[]{:S(2)}) %collective-permute-start.37) | collective-permute-done | bytes 344096 | tf_op jit(solution)/shard_map/ppermute | solution.py:1228
  243.9 2.0 collective-permute-start.36
  245.9 5.7 %collective-permute-done.39 = bf16[224,768]{1,0:T(8,128)(2,1)} collective-permute-done((bf16[224,768]{1,0:T(8,128)(2,1)S(1)}, bf16[224,768]{1,0:T(8,128)(2,1)}, u32[]{:S(2)}, u32[]{:S(2)}) %collective-permute-start.39) | collective-permute-done | bytes 344096 | tf_op jit(solution)/shard_map/ppermute | solution.py:1228
  251.5 1.0 broadcast_select_fusion.18
  252.8 4.4 %collective-permute-done.36 = bf16[152,768]{1,0:T(8,128)(2,1)} collective-permute-done((bf16[152,768]{1,0:T(8,128)(2,1)S(1)}, bf16[152,768]{1,0:T(8,128)(2,1)}, u32[]{:S(2)}, u32[]{:S(2)}) %collective-permute-start.36) | collective-permute-done | bytes 233504 | tf_op jit(solution)/shard_map/ppermute | solution.py:1228
  257.2 1.0 reshape.564
  258.2 1.0 broadcast_select_fusion.21
  259.4 1.6 collective-permute-start.42
  261.7 2.5 collective-permute-start.40
  264.2 1.8 convert_add_fusion
  266.0 11.0 %collective-permute-done.43 = bf16[140,768]{1,0:T(8,128)(2,1)S(1)} collective-permute-done((bf16[140,768]{1,0:T(8,128)(2,1)S(1)}, bf16[140,768]{1,0:T(8,128)(2,1)S(1)}, u32[]{:S(2)}, u32[]{:S(2)}) %collective-permute-start.43) | collective-permute-done | bytes 215072 | tf_op jit(solution)/shard_map/ppermute | solution.py:1228
  277.6 1.6 collective-permute-start.41
  279.4 1.1 broadcast_select_fusion.8
  280.6 1.6 maximum_convert_fusion.1
  282.2 3.2 %collective-permute-done.44 = bf16[152,768]{1,0:T(8,128)(2,1)S(1)} collective-permute-done((bf16[152,768]{1,0:T(8,128)(2,1)S(1)}, bf16[152,768]{1,0:T(8,128)(2,1)S(1)}, u32[]{:S(2)}, u32[]{:S(2)}) %collective-permute-start.44) | collective-permute-done | bytes 233504 | tf_op jit(solution)/shard_map/ppermute | solution.py:1228
  285.5 1.6 maximum_convert_fusion
  288.3 1.2 slice_bitcast_fusion
  289.9 1.6 fusion.2
  (262 shorter events, 23.2 us)
Async XLA Ops:
  0.6 26.4 %collective-permute-start.1 = (bf16[640,768]{1,0:T(8,128)(2,1)}, bf16[640,768]{1,0:T(8,128)(2,1)}, u32[]{:S(2)}, u32[]{:S(2)}) collective-permute-start(bf16[640,768]{1,0:T(8,128)(2,1)} %refs_6_.1), channel_id=1, source_target_pairs={{0,2},{1,3},{2,0},{3,1},{4,6},{5,7},{6,4},{7,5},{8,10},{9,11},{10,... | collective-permute-start | bytes 2949128 | tf_op jit(solution)/shard_map/ppermute | solution.py:1228
  3.6 24.9 %collective-permute-start = (bf16[640,768]{1,0:T(8,128)(2,1)}, bf16[640,768]{1,0:T(8,128)(2,1)}, u32[]{:S(2)}, u32[]{:S(2)}) collective-permute-start(bf16[640,768]{1,0:T(8,128)(2,1)} %refs_6_.1), channel_id=1, source_target_pairs={{0,1},{1,0},{2,3},{3,2},{4,5},{5,4},{6,7},{7,6},{8,9},{9,8},{10,11... | collective-permute-start | bytes 2949128 | tf_op jit(solution)/shard_map/ppermute | solution.py:1228
  8.3 4.5 %copy-start.5 = (bf16[768,768]{1,0:T(8,128)(2,1)S(1)}, bf16[768,768]{1,0:T(8,128)(2,1)}, u32[]{:S(2)}) copy-start(bf16[768,768]{1,0:T(8,128)(2,1)} %param.22) | copy-start | bytes 3538948
  16.0 3.7 %copy-start.44 = (pred[512,256]{1,0:T(8,128)(4,1)S(1)}, pred[512,256]{1,0:T(8,128)(4,1)}, u32[]{:S(2)}) copy-start(pred[512,256]{1,0:T(8,128)(4,1)} %get-tuple-element.283) | copy-start | bytes 393220
  18.0 2.3 copy-start.43
  20.3 7.4 %copy-start.68 = (s32[1,3]{1,0:T(1,128)S(1)}, s32[1,3]{1,0:T(1,128)}, u32[]{:S(2)}) copy-start(s32[1,3]{1,0:T(1,128)} %param.26) | copy-start | bytes 40
  27.0 3.7 %collective-permute-start.2 = (bf16[640,768]{1,0:T(8,128)(2,1)}, bf16[640,768]{1,0:T(8,128)(2,1)}, u32[]{:S(2)}, u32[]{:S(2)}) collective-permute-start(bf16[640,768]{1,0:T(8,128)(2,1)} %collective-permute-done.1.refs_3_.refs_8_), channel_id=1, source_target_pairs={{0,1},{1,0},{2,3},{3,2},{4,5},{5,4},{6,7},{7,6},{8,9},{9,8},{10,11... | collective-permute-start | bytes 2949128 | tf_op jit(solution)/shard_map/ppermute | solution.py:1228
  27.6 50.9 %collective-permute-start.8 = (bf16[1536,768]{1,0:T(8,128)(2,1)}, bf16[1536,768]{1,0:T(8,128)(2,1)S(1)}, u32[]{:S(2)}, u32[]{:S(2)}) collective-permute-start(bf16[1536,768]{1,0:T(8,128)(2,1)} %pad_maximum_fusion.refs_1_.refs_5_.refs_2_.refs_12_.refs_0_), channel_id=1, source_target_pairs={{0,1},{1,0},{2,3},{3,2},{4,5},{5,4},{6,7},{7,6},{8,9},{9,8},{10,11... | collective-permute-start | bytes 7077896 | tf_op jit(solution)/shard_map/ppermute | solution.py:1228
  28.3 28.4 %collective-permute-start.6 = (bf16[768,768]{1,0:T(8,128)(2,1)S(1)}, bf16[768,768]{1,0:T(8,128)(2,1)}, u32[]{:S(2)}, u32[]{:S(2)}) collective-permute-start(bf16[768,768]{1,0:T(8,128)(2,1)S(1)} %pad_maximum_fusion.2), channel_id=1, source_target_pairs={{0,2},{1,3},{2,0},{3,1},{4,6},{5,7},{6,4},{7,5},{8,10},{9,11},{10,... | collective-permute-start | bytes 3538952 | tf_op jit(solution)/shard_map/ppermute | solution.py:1228
  56.7 21.8 %collective-permute-start.9 = (bf16[768,768]{1,0:T(8,128)(2,1)}, bf16[768,768]{1,0:T(8,128)(2,1)}, u32[]{:S(2)}, u32[]{:S(2)}) collective-permute-start(bf16[768,768]{1,0:T(8,128)(2,1)} %collective-permute-done.6.refs_3_.refs_7_.refs_6_.refs_14_), channel_id=1, source_target_pairs={{0,1},{1,0},{2,3},{3,2},{4,5},{5,4},{6,7},{7,6},{8,9},{9,8},{10,11... | collective-permute-start | bytes 3538952 | tf_op jit(solution)/shard_map/ppermute | solution.py:1228
  56.7 3.0 %collective-permute-start.3 = (bf16[192,640]{1,0:T(8,128)(2,1)}, bf16[192,640]{1,0:T(8,128)(2,1)S(1)}, u32[]{:S(2)}, u32[]{:S(2)}) collective-permute-start(bf16[192,640]{1,0:T(8,128)(2,1)} %get-tuple-element.93), channel_id=1, source_target_pairs={{0,1},{1,0},{2,3},{3,2},{4,5},{5,4},{6,7},{7,6},{8,9},{9,8},{10,11... | collective-permute-start | bytes 737288 | tf_op jit(solution)/shard_map/ppermute | solution.py:1228
  57.2 9.0 %collective-permute-start.4 = (bf16[192,640]{1,0:T(8,128)(2,1)}, bf16[192,640]{1,0:T(8,128)(2,1)S(1)}, u32[]{:S(2)}, u32[]{:S(2)}) collective-permute-start(bf16[192,640]{1,0:T(8,128)(2,1)} %get-tuple-element.94), channel_id=1, source_target_pairs={{0,2},{1,3},{2,0},{3,1},{4,6},{5,7},{6,4},{7,5},{8,10},{9,11},{10,... | collective-permute-start | bytes 737288 | tf_op jit(solution)/shard_map/ppermute | solution.py:1228
  57.5 12.1 %collective-permute-start.5 = (bf16[192,640]{1,0:T(8,128)(2,1)}, bf16[192,640]{1,0:T(8,128)(2,1)S(1)}, u32[]{:S(2)}, u32[]{:S(2)}) collective-permute-start(bf16[192,640]{1,0:T(8,128)(2,1)} %get-tuple-element.95), channel_id=1, source_target_pairs={{0,3},{1,2},{2,1},{3,0},{4,7},{5,6},{6,5},{7,4},{8,11},{9,10},{10,... | collective-permute-start | bytes 737288 | tf_op jit(solution)/shard_map/ppermute | solution.py:1228
  59.7 9.8 %copy-start.63 = (bf16[192,640]{1,0:T(8,128)(2,1)}, bf16[192,640]{1,0:T(8,128)(2,1)S(1)}, u32[]{:S(2)}) copy-start(bf16[192,640]{1,0:T(8,128)(2,1)S(1)} %collective-permute-done.3.refs_1_.refs_23_) | copy-start | bytes 737284
  59.7 33.8 %collective-permute-start.7 = (bf16[768,768]{1,0:T(8,128)(2,1)}, bf16[768,768]{1,0:T(8,128)(2,1)}, u32[]{:S(2)}, u32[]{:S(2)}) collective-permute-start(bf16[768,768]{1,0:T(8,128)(2,1)} %collective-permute-done.6.refs_3_.refs_7_.refs_6_.refs_14_), channel_id=1, source_target_pairs={{0,4},{4,0},{8,12},{12,8},{16,20},{20,16},{24,28},{28,24},{1,5},{5... | collective-permute-start | bytes 3538952 | tf_op jit(solution)/shard_map/ppermute | solution.py:1228
  66.2 3.3 %copy-start.64 = (bf16[192,640]{1,0:T(8,128)(2,1)}, bf16[192,640]{1,0:T(8,128)(2,1)S(1)}, u32[]{:S(2)}) copy-start(bf16[192,640]{1,0:T(8,128)(2,1)S(1)} %collective-permute-done.4.refs_2_.refs_24_) | copy-start | bytes 737284
  77.8 15.7 %collective-permute-start.10 = (bf16[320,768]{1,0:T(8,128)(2,1)S(1)}, bf16[320,768]{1,0:T(8,128)(2,1)S(1)}, u32[]{:S(2)}, u32[]{:S(2)}) collective-permute-start(bf16[320,768]{1,0:T(8,128)(2,1)S(1)} %get-tuple-element.222), channel_id=1, source_target_pairs={{0,2},{1,3},{2,0},{3,1},{4,6},{5,7},{6,4},{7,5},{8,10},{9,11},{10,... | collective-permute-start | bytes 1474568 | tf_op jit(solution)/shard_map/ppermute | solution.py:1228
  94.3 3.3 %collective-permute-start.11 = (bf16[768,768]{1,0:T(8,128)(2,1)}, bf16[768,768]{1,0:T(8,128)(2,1)S(1)}, u32[]{:S(2)}, u32[]{:S(2)}) collective-permute-start(bf16[768,768]{1,0:T(8,128)(2,1)} %collective-permute-done.7.refs_1_.refs_3_.refs_9_.refs_16_), channel_id=1, source_target_pairs={{0,1},{1,0},{2,3},{3,2},{4,5},{5,4},{6,7},{7,6},{8,9},{9,8},{10,11... | collective-permute-start | bytes 3538952 | tf_op jit(solution)/shard_map/ppermute | solution.py:1228
  95.0 14.9 %collective-permute-start.12 = (bf16[320,768]{1,0:T(8,128)(2,1)S(1)}, bf16[320,768]{1,0:T(8,128)(2,1)S(1)}, u32[]{:S(2)}, u32[]{:S(2)}) collective-permute-start(bf16[320,768]{1,0:T(8,128)(2,1)S(1)} %get-tuple-element.221), channel_id=1, source_target_pairs={{0,2},{1,3},{2,0},{3,1},{4,6},{5,7},{6,4},{7,5},{8,10},{9,11},{10,... | collective-permute-start | bytes 1474568 | tf_op jit(solution)/shard_map/ppermute | solution.py:1228
  108.1 24.4 %collective-permute-start.15 = (bf16[640,768]{1,0:T(8,128)(2,1)}, bf16[640,768]{1,0:T(8,128)(2,1)}, u32[]{:S(2)}, u32[]{:S(2)}) collective-permute-start(bf16[640,768]{1,0:T(8,128)(2,1)} %get-tuple-element.103.refs_0_.refs_3_), channel_id=1, source_target_pairs={{0,2},{1,3},{2,0},{3,1},{4,6},{5,7},{6,4},{7,5},{8,10},{9,11},{10,... | collective-permute-start | bytes 2949128 | tf_op jit(solution)/shard_map/ppermute | solution.py:1228
  110.7 16.7 %copy-start.48 = (f32[8,768]{1,0:T(8,128)S(1)}, f32[8,768]{1,0:T(8,128)}, u32[]{:S(2)}) copy-start(f32[8,768]{1,0:T(8,128)} %get-tuple-element.118) | copy-start | bytes 73732
  126.5 3.4 %copy-start.9 = (bf16[640,768]{1,0:T(8,128)(2,1)S(1)}, bf16[640,768]{1,0:T(8,128)(2,1)}, u32[]{:S(2)}) copy-start(bf16[640,768]{1,0:T(8,128)(2,1)} %get-tuple-element.96.refs_0_.refs_2_) | copy-start | bytes 2949124
  126.5 6.0 %copy-start.59 = (bf16[320,768]{1,0:T(8,128)(2,1)S(1)}, bf16[320,768]{1,0:T(8,128)(2,1)}, u32[]{:S(2)}) copy-start(bf16[320,768]{1,0:T(8,128)(2,1)} %copy-done.58) | copy-start | bytes 1474564
  126.5 7.4 %copy-start = (bf16[768,768]{1,0:T(8,128)(2,1)S(1)}, bf16[768,768]{1,0:T(8,128)(2,1)}, u32[]{:S(2)}) copy-start(bf16[768,768]{1,0:T(8,128)(2,1)} %get-tuple-element.116) | copy-start | bytes 3538948
  129.8 3.2 %collective-permute-start.19 = (bf16[512,768]{1,0:T(8,128)(2,1)}, bf16[512,768]{1,0:T(8,128)(2,1)S(1)}, u32[]{:S(2)}, u32[]{:S(2)}) collective-permute-start(bf16[512,768]{1,0:T(8,128)(2,1)} %broadcast_select_fusion.2), channel_id=1, source_target_pairs={{0,1},{1,0},{2,3},{3,2},{4,5},{5,4},{6,7},{7,6},{8,9},{9,8},{10,11... | collective-permute-start | bytes 2359304 | tf_op jit(solution)/shard_map/ppermute | solution.py:1228
  129.8 6.7 %collective-permute-start.13 = (bf16[640,768]{1,0:T(8,128)(2,1)S(1)}, bf16[640,768]{1,0:T(8,128)(2,1)}, u32[]{:S(2)}, u32[]{:S(2)}) collective-permute-start(bf16[640,768]{1,0:T(8,128)(2,1)S(1)} %copy-done.9), channel_id=1, source_target_pairs={{0,1},{1,0},{2,3},{3,2},{4,5},{5,4},{6,7},{7,6},{8,9},{9,8},{10,11... | collective-permute-start | bytes 2949128 | tf_op jit(solution)/shard_map/ppermute | solution.py:1228
  130.3 8.0 %collective-permute-start.14 = (bf16[640,768]{1,0:T(8,128)(2,1)}, bf16[640,768]{1,0:T(8,128)(2,1)}, u32[]{:S(2)}, u32[]{:S(2)}) collective-permute-start(bf16[640,768]{1,0:T(8,128)(2,1)} %get-tuple-element.103.refs_0_.refs_3_), channel_id=1, source_target_pairs={{0,1},{1,0},{2,3},{3,2},{4,5},{5,4},{6,7},{7,6},{8,9},{9,8},{10,11... | collective-permute-start | bytes 2949128 | tf_op jit(solution)/shard_map/ppermute | solution.py:1228
  132.5 7.2 %collective-permute-start.18 = (bf16[640,768]{1,0:T(8,128)(2,1)}, bf16[640,768]{1,0:T(8,128)(2,1)}, u32[]{:S(2)}, u32[]{:S(2)}) collective-permute-start(bf16[640,768]{1,0:T(8,128)(2,1)} %collective-permute-done.15.refs_8_), channel_id=1, source_target_pairs={{0,1},{1,0},{2,3},{3,2},{4,5},{5,4},{6,7},{7,6},{8,9},{9,8},{10,11... | collective-permute-start | bytes 2949128 | tf_op jit(solution)/shard_map/ppermute | solution.py:1228
  132.5 3.9 %collective-permute-start.16 = (bf16[320,768]{1,0:T(8,128)(2,1)S(1)}, bf16[320,768]{1,0:T(8,128)(2,1)S(1)}, u32[]{:S(2)}, u32[]{:S(2)}) collective-permute-start(bf16[320,768]{1,0:T(8,128)(2,1)S(1)} %copy-done.59), channel_id=1, source_target_pairs={{0,1},{1,0},{2,3},{3,2},{4,5},{5,4},{6,7},{7,6},{8,9},{9,8},{10,11... | collective-permute-start | bytes 1474568 | tf_op jit(solution)/shard_map/ppermute | solution.py:1228
  133.9 4.3 %collective-permute-start.17 = (bf16[320,768]{1,0:T(8,128)(2,1)}, bf16[320,768]{1,0:T(8,128)(2,1)S(1)}, u32[]{:S(2)}, u32[]{:S(2)}) collective-permute-start(bf16[320,768]{1,0:T(8,128)(2,1)} %copy-done.60), channel_id=1, source_target_pairs={{0,1},{1,0},{2,3},{3,2},{4,5},{5,4},{6,7},{7,6},{8,9},{9,8},{10,11... | collective-permute-start | bytes 1474568 | tf_op jit(solution)/shard_map/ppermute | solution.py:1228
  136.4 3.3 %copy-start.61 = (bf16[320,768]{1,0:T(8,128)(2,1)}, bf16[320,768]{1,0:T(8,128)(2,1)S(1)}, u32[]{:S(2)}) copy-start(bf16[320,768]{1,0:T(8,128)(2,1)S(1)} %collective-permute-done.16.refs_9_) | copy-start | bytes 1474564
  136.4 32.2 %collective-permute-start.21 = (bf16[192,640]{1,0:T(8,128)(2,1)}, bf16[192,640]{1,0:T(8,128)(2,1)S(1)}, u32[]{:S(2)}, u32[]{:S(2)}) collective-permute-start(bf16[192,640]{1,0:T(8,128)(2,1)} %get-tuple-element.123), channel_id=1, source_target_pairs={{0,1},{1,0},{2,3},{3,2},{4,5},{5,4},{6,7},{7,6},{8,9},{9,8},{10,11... | collective-permute-start | bytes 737288 | tf_op jit(solution)/shard_map/ppermute | solution.py:1228
  136.5 32.1 %collective-permute-start.22 = (bf16[192,640]{1,0:T(8,128)(2,1)}, bf16[192,640]{1,0:T(8,128)(2,1)S(1)}, u32[]{:S(2)}, u32[]{:S(2)}) collective-permute-start(bf16[192,640]{1,0:T(8,128)(2,1)} %get-tuple-element.124), channel_id=1, source_target_pairs={{0,2},{1,3},{2,0},{3,1},{4,6},{5,7},{6,4},{7,5},{8,10},{9,11},{10,... | collective-permute-start | bytes 737288 | tf_op jit(solution)/shard_map/ppermute | solution.py:1228
  138.2 30.4 %collective-permute-start.23 = (bf16[192,640]{1,0:T(8,128)(2,1)}, bf16[192,640]{1,0:T(8,128)(2,1)}, u32[]{:S(2)}, u32[]{:S(2)}) collective-permute-start(bf16[192,640]{1,0:T(8,128)(2,1)} %get-tuple-element.125), channel_id=1, source_target_pairs={{0,3},{1,2},{2,1},{3,0},{4,7},{5,6},{6,5},{7,4},{8,11},{9,10},{10,... | collective-permute-start | bytes 737288 | tf_op jit(solution)/shard_map/ppermute | solution.py:1228
  138.3 25.2 %collective-permute-start.20 = (bf16[256,768]{1,0:T(8,128)(2,1)S(1)}, bf16[256,768]{1,0:T(8,128)(2,1)S(1)}, u32[]{:S(2)}, u32[]{:S(2)}) collective-permute-start(bf16[256,768]{1,0:T(8,128)(2,1)S(1)} %broadcast_select_fusion.13), channel_id=1, source_target_pairs={{0,2},{1,3},{2,0},{3,1},{4,6},{5,7},{6,4},{7,5},{8,10},{9,11},{10,... | collective-permute-start | bytes 1179656 | tf_op jit(solution)/shard_map/ppermute | solution.py:1228
  163.7 3.1 %copy-start.6 = (bf16[768,768]{1,0:T(8,128)(2,1)S(1)}, bf16[768,768]{1,0:T(8,128)(2,1)}, u32[]{:S(2)}) copy-start(bf16[768,768]{1,0:T(8,128)(2,1)} %get-tuple-element.115) | copy-start | bytes 3538948
  165.0 23.6 %collective-permute-start.25 = (bf16[448,768]{1,0:T(8,128)(2,1)S(1)}, bf16[448,768]{1,0:T(8,128)(2,1)S(1)}, u32[]{:S(2)}, u32[]{:S(2)}) collective-permute-start(bf16[448,768]{1,0:T(8,128)(2,1)S(1)} %bitcast.82), channel_id=1, source_target_pairs={{0,8},{4,12},{8,0},{12,4},{16,24},{20,28},{24,16},{28,20},{1,9},{5... | collective-permute-start | bytes 2064392 | tf_op jit(solution)/shard_map/ppermute | solution.py:1228
  167.0 21.9 %collective-permute-start.24 = (bf16[448,768]{1,0:T(8,128)(2,1)S(1)}, bf16[448,768]{1,0:T(8,128)(2,1)}, u32[]{:S(2)}, u32[]{:S(2)}) collective-permute-start(bf16[448,768]{1,0:T(8,128)(2,1)S(1)} %bitcast.83), channel_id=1, source_target_pairs={{0,4},{4,0},{8,12},{12,8},{16,20},{20,16},{24,28},{28,24},{1,5},{5... | collective-permute-start | bytes 2064392 | tf_op jit(solution)/shard_map/ppermute | solution.py:1228
  190.2 12.3 %collective-permute-start.26 = (bf16[224,768]{1,0:T(8,128)(2,1)S(1)}, bf16[224,768]{1,0:T(8,128)(2,1)S(1)}, u32[]{:S(2)}, u32[]{:S(2)}) collective-permute-start(bf16[224,768]{1,0:T(8,128)(2,1)S(1)} %broadcast_select_fusion.22), channel_id=1, source_target_pairs={{0,8},{4,12},{8,0},{12,4},{16,24},{20,28},{24,16},{28,20},{1,9},{5... | collective-permute-start | bytes 1032200 | tf_op jit(solution)/shard_map/ppermute | solution.py:1228
  190.7 11.9 %collective-permute-start.27 = (bf16[224,768]{1,0:T(8,128)(2,1)S(1)}, bf16[224,768]{1,0:T(8,128)(2,1)S(1)}, u32[]{:S(2)}, u32[]{:S(2)}) collective-permute-start(bf16[224,768]{1,0:T(8,128)(2,1)S(1)} %broadcast_select_fusion.19), channel_id=1, source_target_pairs={{0,4},{4,0},{8,12},{12,8},{16,20},{20,16},{24,28},{28,24},{1,5},{5... | collective-permute-start | bytes 1032200 | tf_op jit(solution)/shard_map/ppermute | solution.py:1228
  202.9 18.6 %collective-permute-start.30 = (bf16[224,768]{1,0:T(8,128)(2,1)S(1)}, bf16[224,768]{1,0:T(8,128)(2,1)S(1)}, u32[]{:S(2)}, u32[]{:S(2)}) collective-permute-start(bf16[224,768]{1,0:T(8,128)(2,1)S(1)} %bitcast.84), channel_id=1, source_target_pairs={{0,16},{4,20},{8,24},{12,28},{16,0},{20,4},{24,8},{28,12},{1,17},{... | collective-permute-start | bytes 1032200 | tf_op jit(solution)/shard_map/ppermute | solution.py:1228
  220.9 2.6 copy-start.3
  220.9 5.5 %copy-start.10 = (bf16[640,768]{1,0:T(8,128)(2,1)S(1)}, bf16[640,768]{1,0:T(8,128)(2,1)}, u32[]{:S(2)}) copy-start(bf16[640,768]{1,0:T(8,128)(2,1)} %get-tuple-element.150) | copy-start | bytes 2949124
  220.9 5.5 %collective-permute-start.29 = (bf16[640,768]{1,0:T(8,128)(2,1)}, bf16[640,768]{1,0:T(8,128)(2,1)S(1)}, u32[]{:S(2)}, u32[]{:S(2)}) collective-permute-start(bf16[640,768]{1,0:T(8,128)(2,1)} %get-tuple-element.151), channel_id=1, source_target_pairs={{0,1},{1,0},{2,3},{3,2},{4,5},{5,4},{6,7},{7,6},{8,9},{9,8},{10,11... | collective-permute-start | bytes 2949128 | tf_op jit(solution)/shard_map/ppermute | solution.py:1228
  221.0 43.3 %collective-permute-start.28 = (bf16[640,768]{1,0:T(8,128)(2,1)}, bf16[640,768]{1,0:T(8,128)(2,1)S(1)}, u32[]{:S(2)}, u32[]{:S(2)}) collective-permute-start(bf16[640,768]{1,0:T(8,128)(2,1)} %get-tuple-element.149), channel_id=1, source_target_pairs={{0,1},{1,0},{2,3},{3,2},{4,5},{5,4},{6,7},{7,6},{8,9},{9,8},{10,11... | collective-permute-start | bytes 2949128 | tf_op jit(solution)/shard_map/ppermute | solution.py:1228
  221.9 7.5 %collective-permute-start.32 = (bf16[152,768]{1,0:T(8,128)(2,1)S(1)}, bf16[152,768]{1,0:T(8,128)(2,1)S(1)}, u32[]{:S(2)}, u32[]{:S(2)}) collective-permute-start(bf16[152,768]{1,0:T(8,128)(2,1)S(1)} %broadcast_select_fusion.28), channel_id=1, source_target_pairs={{0,4},{4,0},{8,12},{12,8},{16,20},{20,16},{24,28},{28,24},{1,5},{5... | collective-permute-start | bytes 700424 | tf_op jit(solution)/shard_map/ppermute | solution.py:1228
  223.5 10.8 %collective-permute-start.34 = (bf16[152,768]{1,0:T(8,128)(2,1)S(1)}, bf16[152,768]{1,0:T(8,128)(2,1)S(1)}, u32[]{:S(2)}, u32[]{:S(2)}) collective-permute-start(bf16[152,768]{1,0:T(8,128)(2,1)S(1)} %broadcast_select_fusion.25), channel_id=1, source_target_pairs={{0,8},{4,12},{8,0},{12,4},{16,24},{20,28},{24,16},{28,20},{1,9},{5... | collective-permute-start | bytes 700424 | tf_op jit(solution)/shard_map/ppermute | solution.py:1228
  225.2 17.6 %collective-permute-start.37 = (bf16[224,768]{1,0:T(8,128)(2,1)S(1)}, bf16[224,768]{1,0:T(8,128)(2,1)S(1)}, u32[]{:S(2)}, u32[]{:S(2)}) collective-permute-start(bf16[224,768]{1,0:T(8,128)(2,1)S(1)} %bitcast.85), channel_id=1, source_target_pairs={{0,16},{4,20},{8,24},{12,28},{16,0},{20,4},{24,8},{28,12},{1,17},{... | collective-permute-start | bytes 1032200 | tf_op jit(solution)/shard_map/ppermute | solution.py:1228
  227.6 30.5 %collective-permute-start.31 = (bf16[640,768]{1,0:T(8,128)(2,1)}, bf16[640,768]{1,0:T(8,128)(2,1)S(1)}, u32[]{:S(2)}, u32[]{:S(2)}) collective-permute-start(bf16[640,768]{1,0:T(8,128)(2,1)} %add_convert_fusion), channel_id=1, source_target_pairs={{0,2},{1,3},{2,0},{3,1},{4,6},{5,7},{6,4},{7,5},{8,10},{9,11},{10,... | collective-permute-start | bytes 2949128 | tf_op jit(solution)/shard_map/ppermute | solution.py:1228
  234.4 9.2 %collective-permute-start.33 = (bf16[76,768]{1,0:T(8,128)(2,1)S(1)}, bf16[76,768]{1,0:T(8,128)(2,1)S(1)}, u32[]{:S(2)}, u32[]{:S(2)}) collective-permute-start(bf16[76,768]{1,0:T(8,128)(2,1)S(1)} %broadcast_select_fusion.34), channel_id=1, source_target_pairs={{0,8},{4,12},{8,0},{12,4},{16,24},{20,28},{24,16},{28,20},{1,9},{5... | collective-permute-start | bytes 350216 | tf_op jit(solution)/shard_map/ppermute | solution.py:1228
  234.6 9.2 %collective-permute-start.35 = (bf16[76,768]{1,0:T(8,128)(2,1)S(1)}, bf16[76,768]{1,0:T(8,128)(2,1)S(1)}, u32[]{:S(2)}, u32[]{:S(2)}) collective-permute-start(bf16[76,768]{1,0:T(8,128)(2,1)S(1)} %broadcast_select_fusion.31), channel_id=1, source_target_pairs={{0,4},{4,0},{8,12},{12,8},{16,20},{20,16},{24,28},{28,24},{1,5},{5... | collective-permute-start | bytes 350216 | tf_op jit(solution)/shard_map/ppermute | solution.py:1228
  243.1 8.5 %collective-permute-start.39 = (bf16[224,768]{1,0:T(8,128)(2,1)S(1)}, bf16[224,768]{1,0:T(8,128)(2,1)}, u32[]{:S(2)}, u32[]{:S(2)}) collective-permute-start(bf16[224,768]{1,0:T(8,128)(2,1)S(1)} %get-tuple-element.227), channel_id=1, source_target_pairs={{0,4},{4,0},{8,12},{12,8},{16,20},{20,16},{24,28},{28,24},{1,5},{5... | collective-permute-start | bytes 1032200 | tf_op jit(solution)/shard_map/ppermute | solution.py:1228
  243.6 14.5 %collective-permute-start.38 = (bf16[224,768]{1,0:T(8,128)(2,1)S(1)}, bf16[224,768]{1,0:T(8,128)(2,1)}, u32[]{:S(2)}, u32[]{:S(2)}) collective-permute-start(bf16[224,768]{1,0:T(8,128)(2,1)S(1)} %get-tuple-element.228), channel_id=1, source_target_pairs={{0,8},{4,12},{8,0},{12,4},{16,24},{20,28},{24,16},{28,20},{1,9},{5... | collective-permute-start | bytes 1032200 | tf_op jit(solution)/shard_map/ppermute | solution.py:1228
  243.9 13.3 %collective-permute-start.36 = (bf16[152,768]{1,0:T(8,128)(2,1)S(1)}, bf16[152,768]{1,0:T(8,128)(2,1)}, u32[]{:S(2)}, u32[]{:S(2)}) collective-permute-start(bf16[152,768]{1,0:T(8,128)(2,1)S(1)} %reshape.563), channel_id=1, source_target_pairs={{0,16},{4,20},{8,24},{12,28},{16,0},{20,4},{24,8},{28,12},{1,17},{... | collective-permute-start | bytes 700424 | tf_op jit(solution)/shard_map/ppermute | solution.py:1228
  252.7 26.8 %collective-permute-start.45 = (bf16[384,768]{1,0:T(8,128)(2,1)S(1)}, bf16[384,768]{1,0:T(8,128)(2,1)}, u32[]{:S(2)}, u32[]{:S(2)}) collective-permute-start(bf16[384,768]{1,0:T(8,128)(2,1)S(1)} %bitcast.72), channel_id=1, source_target_pairs={{0,8},{4,12},{8,0},{12,4},{16,24},{20,28},{24,16},{28,20},{1,9},{5... | collective-permute-start | bytes 1769480 | tf_op jit(solution)/shard_map/ppermute | solution.py:1228
  259.3 4.9 %copy-start.2 = (f32[640,768]{1,0:T(8,128)S(1)}, f32[640,768]{1,0:T(8,128)}, u32[]{:S(2)}) copy-start(f32[640,768]{1,0:T(8,128)} %get-tuple-element.112) | copy-start | bytes 5898244
  259.3 4.9 %copy-start.8 = (bf16[640,768]{1,0:T(8,128)(2,1)S(1)}, bf16[640,768]{1,0:T(8,128)(2,1)}, u32[]{:S(2)}) copy-start(bf16[640,768]{1,0:T(8,128)(2,1)} %get-tuple-element.148) | copy-start | bytes 2949124
  259.4 26.0 %collective-permute-start.42 = (bf16[384,768]{1,0:T(8,128)(2,1)S(1)}, bf16[384,768]{1,0:T(8,128)(2,1)S(1)}, u32[]{:S(2)}, u32[]{:S(2)}) collective-permute-start(bf16[384,768]{1,0:T(8,128)(2,1)S(1)} %bitcast.73), channel_id=1, source_target_pairs={{0,4},{4,0},{8,12},{12,8},{16,20},{20,16},{24,28},{28,24},{1,5},{5... | collective-permute-start | bytes 1769480 | tf_op jit(solution)/shard_map/ppermute | solution.py:1228
  261.1 15.9 %collective-permute-start.43 = (bf16[140,768]{1,0:T(8,128)(2,1)S(1)}, bf16[140,768]{1,0:T(8,128)(2,1)S(1)}, u32[]{:S(2)}, u32[]{:S(2)}) collective-permute-start(bf16[140,768]{1,0:T(8,128)(2,1)S(1)} %pad_maximum_fusion.18), channel_id=1, source_target_pairs={{0,4},{4,0},{8,12},{12,8},{16,20},{20,16},{24,28},{28,24},{1,5},{5... | collective-permute-start | bytes 645128 | tf_op jit(solution)/shard_map/ppermute | solution.py:1228
  261.7 15.4 %collective-permute-start.40 = (bf16[140,768]{1,0:T(8,128)(2,1)S(1)}, bf16[140,768]{1,0:T(8,128)(2,1)S(1)}, u32[]{:S(2)}, u32[]{:S(2)}) collective-permute-start(bf16[140,768]{1,0:T(8,128)(2,1)S(1)} %pad_maximum_fusion.17), channel_id=1, source_target_pairs={{0,8},{4,12},{8,0},{12,4},{16,24},{20,28},{24,16},{28,20},{1,9},{5... | collective-permute-start | bytes 645128 | tf_op jit(solution)/shard_map/ppermute | solution.py:1228
  277.1 9.9 %collective-permute-start.46 = (bf16[256,768]{1,0:T(8,128)(2,1)S(1)}, bf16[256,768]{1,0:T(8,128)(2,1)S(1)}, u32[]{:S(2)}, u32[]{:S(2)}) collective-permute-start(bf16[256,768]{1,0:T(8,128)(2,1)S(1)} %pad_maximum_fusion.11), channel_id=1, source_target_pairs={{0,2},{1,3},{2,0},{3,1},{4,6},{5,7},{6,4},{7,5},{8,10},{9,11},{10,... | collective-permute-start | bytes 1179656 | tf_op jit(solution)/shard_map/ppermute | solution.py:1228
  277.6 9.5 %collective-permute-start.41 = (bf16[152,768]{1,0:T(8,128)(2,1)S(1)}, bf16[152,768]{1,0:T(8,128)(2,1)S(1)}, u32[]{:S(2)}, u32[]{:S(2)}) collective-permute-start(bf16[152,768]{1,0:T(8,128)(2,1)S(1)} %pad_maximum_fusion.15), channel_id=1, source_target_pairs={{0,4},{4,0},{8,12},{12,8},{16,20},{20,16},{24,28},{28,24},{1,5},{5... | collective-permute-start | bytes 700424 | tf_op jit(solution)/shard_map/ppermute | solution.py:1228
  279.2 6.1 %collective-permute-start.44 = (bf16[152,768]{1,0:T(8,128)(2,1)S(1)}, bf16[152,768]{1,0:T(8,128)(2,1)S(1)}, u32[]{:S(2)}, u32[]{:S(2)}) collective-permute-start(bf16[152,768]{1,0:T(8,128)(2,1)S(1)} %pad_maximum_fusion.16), channel_id=1, source_target_pairs={{0,8},{4,12},{8,0},{12,4},{16,24},{20,28},{24,16},{28,20},{1,9},{5... | collective-permute-start | bytes 700424 | tf_op jit(solution)/shard_map/ppermute | solution.py:1228
  287.3 2.4 collective-permute-start.47
  (53 other events, 95.0 us)
